TPU v7x, 32 devices: a whole 2x2x4 slice. The times are simulated.
32 devices in a mesh: dp: 8 (over y, x, core), mp: 4 (over z).
Axes of the slice: x: 2, y: 2, z: 4, core: 2. Of those that a mesh axis runs over, the one named last changes fastest.
Arguments:
- tokens: bfloat16 [8192, 2048], P(('dp', 'mp')), may hold values from -6 to 6
- input_gain: float32 [2048], replicated, may hold values from 0.5 to 1.5
- query_weight: bfloat16 [2048, 4096], P('dp', 'mp'), may hold values from -0.125 to 0.125
- key_value_weight: bfloat16 [2048, 1024], P('dp'), may hold values from -0.125 to 0.125
- query_gain: float32 [128], replicated, may hold values from 0.5 to 1.5
- key_gain: float32 [128], replicated, may hold values from 0.5 to 1.5
- out_weight: bfloat16 [4096, 2048], P('mp', 'dp'), may hold values from -0.75 to 0.75
- moe_gain: float32 [2048], replicated, may hold values from 0.5 to 1.5
- gate_weight: bfloat16 [32, 2048, 768], P(('dp', 'mp')), may hold values from -0.125 to 0.125
- up_weight: bfloat16 [32, 2048, 768], P(('dp', 'mp')), may hold values from -0.125 to 0.125
- down_weight: bfloat16 [32, 768, 2048], P(('dp', 'mp')), may hold values from -0.875 to 0.875
- gate_values: float32 [8192, 8], P(('dp', 'mp')), may hold values from 0 to 1, as said below
- routes: int32 [8192, 8], P(('dp', 'mp')), may hold values from 0 to 31, all different within a row; in each aligned block of 256 rows (0 to 255, 256 to 511, ...) at most 68 rows name the same one
- lengths: int32 [4, 4], replicated, may hold values from 1 to 1536, 2048 in all within a row
- cotangent: bfloat16 [8192, 2048], P(('dp', 'mp')), may hold values from -6 to 6
Outputs:
- block_out: bfloat16 [8192, 2048], P(('dp', 'mp'))
- tokens_grad: float32 [8192, 2048], P(('dp', 'mp'))
- input_gain_grad: float32 [2048], replicated
- query_weight_grad: float32 [2048, 4096], P('dp', 'mp')
- kv_weight_grad: float32 [2048, 1024], P('dp')
- query_gain_grad: float32 [128], replicated
- key_gain_grad: float32 [128], replicated
- out_weight_grad: float32 [4096, 2048], P('mp', 'dp')
- moe_gain_grad: float32 [2048], replicated
- gate_weight_grad: float32 [32, 2048, 768], P(('dp', 'mp'))
- up_weight_grad: float32 [32, 2048, 768], P(('dp', 'mp'))
- down_weight_grad: float32 [32, 768, 2048], P(('dp', 'mp'))
- gate_values_grad: float32 [8192, 8], P(('dp', 'mp'))
Inputs may be any that keep to these rules, and one draw needn't show every extreme that they name: `routes`: each row names 8 different experts; in the rows of one device (aligned blocks of 256 rows) no expert is named by more than 68 rows, a bound that some block reaches. `gate_values`: each row's 8 weights are positive and sum to 1. Each sequence's 4 lengths sum to 2048; the longest is exactly 1536.
All inputs are finite; a program needn't handle non-finite values.
Results may differ from a plain program's by a relative error of at most 0.02.
Values may be sent and summed in bfloat16 or wider, within the bound.
No kernel may reach another device: no remote copies, remote signals or barrier semaphores. Data moves between devices by JAX's collectives and lax.ppermute only.
A program may use at most 320 MiB of HBM per device.

v0:
```python
import math

import jax
import jax.numpy as jnp
from jax import lax
from jax.sharding import PartitionSpec as P

WINDOW = 1024


EPSILON = 1e-06
ROPE_BASE = 1000000.0
MASKED = -1e30


def passed_along(shard, axis, by):
    length = lax.axis_size(axis)
    pairs = [(i, i + by) for i in range(length) if 0 <= i + by < length]
    return lax.ppermute(shard, axis, pairs)


def rms_norm(value_rows, gain_vector):
    return (
        value_rows
        * lax.rsqrt(jnp.mean(value_rows * value_rows, axis=-1, keepdims=True) + EPSILON)
        * gain_vector
    )


def rope_tables(positions, head_width):
    half_width = head_width // 2
    frequency = jnp.exp(
        jnp.arange(half_width, dtype=jnp.float32) * (-2.0 * math.log(ROPE_BASE) / head_width)
    )
    angles = positions[:, None] * frequency[None, :]
    cosine = jnp.cos(angles)
    sine_table = jnp.sin(angles)
    return (
        jnp.concatenate([cosine, cosine], axis=-1),
        jnp.concatenate([sine_table, sine_table], axis=-1),
    )


def rotate(value_rows, cosine, sine_table):
    half_width = value_rows.shape[-1] // 2
    turned = jnp.concatenate([-value_rows[..., half_width:], value_rows[..., :half_width]], axis=-1)
    return value_rows * cosine[:, None, :] + turned * sine_table[:, None, :]


def doc_layout(doc_lengths, sequence_length):
    ends_at = jnp.cumsum(doc_lengths)
    starts_at = ends_at - doc_lengths
    places = jnp.arange(sequence_length, dtype=jnp.int32)
    doc_ids = jnp.sum((places[:, None] >= ends_at[None, :]).astype(jnp.int32), axis=1)
    matches = doc_ids[:, None] == jnp.arange(doc_lengths.shape[0], dtype=jnp.int32)[None, :]
    begins = jnp.sum(jnp.where(matches, starts_at[None, :], 0), axis=1)
    return (doc_ids, places - begins)


def contract_last(left_side, right_side):
    return lax.dot_general(
        left_side, right_side, (((1,), (1,)), ((), ())), preferred_element_type=jnp.float32
    )


def contract_first(left_side, right_side):
    return lax.dot_general(
        left_side, right_side, (((0,), (0,)), ((), ())), preferred_element_type=jnp.float32
    )


def on_device(
    tokens,
    input_gain,
    query_weight,
    key_value_weight,
    query_gain,
    key_gain,
    out_weight,
    moe_gain,
    gate_weight,
    up_weight,
    down_weight,
    gate_values,
    routes,
    lengths,
    cotangent,
):
    row_count, model_width = tokens.shape
    head_width = query_gain.shape[0]
    kv_width = key_value_weight.shape[1] // 2
    local_width = query_weight.shape[1]
    local_heads = local_width // head_width
    mp_count = lax.axis_size("mp")
    dp_count = lax.axis_size("dp")
    device_count = mp_count * dp_count
    heads_per_group = local_heads * mp_count * head_width // kv_width
    kv_offset = lax.axis_index("mp") * local_heads // heads_per_group * head_width
    sequence_length = row_count * mp_count
    score_scale = 1.0 / math.sqrt(head_width)
    dp_place = lax.axis_index("dp")
    half_index = dp_place % 2
    seq_index = dp_place // 2
    resid_in = tokens.astype(jnp.float32)
    normed_one, norm_one_back = jax.vjp(rms_norm, resid_in, input_gain)
    sequence = lax.all_gather(normed_one.astype(jnp.bfloat16), "mp", axis=0, tiled=True)
    wq_whole, wkv_whole = (
        lax.all_gather(query_weight, "dp", axis=0, tiled=True),
        lax.all_gather(key_value_weight, "dp", axis=0, tiled=True),
    )
    kv_own = jnp.concatenate(
        [
            lax.dynamic_slice_in_dim(wkv_whole, kv_offset, head_width, 1),
            lax.dynamic_slice_in_dim(wkv_whole, kv_width + kv_offset, head_width, 1),
        ],
        axis=1,
    )
    query_pre = jnp.dot(sequence, wq_whole, preferred_element_type=jnp.float32).reshape(
        sequence_length, local_heads, head_width
    )
    key_value_projected = jnp.dot(sequence, kv_own, preferred_element_type=jnp.float32)
    value_rows = key_value_projected[:, head_width:].astype(jnp.bfloat16)
    seq_lengths = lax.dynamic_index_in_dim(lengths, seq_index, 0, keepdims=False)
    docs_whole, places_whole = doc_layout(seq_lengths, 2 * sequence_length)
    doc_ids = lax.dynamic_slice_in_dim(docs_whole, half_index * sequence_length, sequence_length, 0)
    positions = lax.dynamic_slice_in_dim(
        places_whole, half_index * sequence_length, sequence_length, 0
    )
    prior_docs = jnp.where(half_index == 1, docs_whole[:sequence_length], -1)
    cosine, sine_table = rope_tables(positions.astype(jnp.float32), head_width)

    def head_prep(pre_values, gain_vector):
        return rotate(rms_norm(pre_values, gain_vector), cosine, sine_table)

    query_rot, query_back = jax.vjp(head_prep, query_pre, query_gain)
    key_rot, key_back = jax.vjp(
        head_prep,
        key_value_projected[:, :head_width].reshape(sequence_length, 1, head_width),
        key_gain,
    )
    queries = query_rot.astype(jnp.bfloat16)
    keys = key_rot[:, 0, :].astype(jnp.bfloat16)
    block_rows = min(512, sequence_length)
    block_count = sequence_length // block_rows
    reach_tiles = -(-WINDOW // block_rows)
    margin = reach_tiles * block_rows
    key_span = margin + block_rows
    tail_rows = jnp.concatenate([keys, value_rows], axis=1)
    prior = passed_along(tail_rows, "dp", 1)
    keys_pad = jnp.concatenate([prior[:, :head_width], keys], axis=0)
    values_pad = jnp.concatenate([prior[:, head_width:], value_rows], axis=0)
    docs_pad = jnp.concatenate([prior_docs, doc_ids])
    offsets = jnp.arange(block_rows, dtype=jnp.int32)
    key_offsets = jnp.arange(key_span, dtype=jnp.int32)

    def block_scores(block_index):
        first_row = block_index * block_rows
        query_block = lax.dynamic_slice_in_dim(queries, first_row, block_rows, 0)
        key_block = lax.dynamic_slice_in_dim(keys_pad, first_row, key_span, 0)
        value_block = lax.dynamic_slice_in_dim(values_pad, first_row, key_span, 0)
        query_docs = lax.dynamic_slice_in_dim(doc_ids, first_row, block_rows, 0)
        key_docs = lax.dynamic_slice_in_dim(docs_pad, first_row, key_span, 0)
        query_places = first_row + offsets
        key_places = first_row - margin + key_offsets
        allowed = (
            (key_docs[None, :] == query_docs[:, None])
            & (key_places[None, :] <= query_places[:, None])
            & (query_places[:, None] - key_places[None, :] < WINDOW)
        )
        raw_scores = (
            jnp.einsum("qhd,kd->hqk", query_block, key_block, preferred_element_type=jnp.float32)
            * score_scale
        )
        return (jnp.where(allowed[None], raw_scores, MASKED), query_block, key_block, value_block)

    def forward_block(block_index):
        scores, query_block, key_block, value_block = block_scores(block_index)
        log_totals = jax.nn.logsumexp(scores, axis=-1)
        soft_low = jnp.exp(scores - log_totals[..., None]).astype(jnp.bfloat16)
        attended_block = jnp.einsum(
            "hqk,kd->qhd", soft_low, value_block, preferred_element_type=jnp.float32
        )
        return (attended_block.astype(jnp.bfloat16), log_totals)

    attended_blocks, total_blocks = lax.map(forward_block, jnp.arange(block_count, dtype=jnp.int32))
    attended = attended_blocks.reshape(sequence_length, local_width)
    wo_whole = lax.all_gather(out_weight, "dp", axis=1, tiled=True)
    resid = resid_in + lax.psum_scatter(
        jnp.dot(attended, wo_whole, preferred_element_type=jnp.float32).astype(jnp.bfloat16),
        "mp",
        scatter_dimension=0,
        tiled=True,
    ).astype(jnp.float32)
    normed_two, norm_two_back = jax.vjp(rms_norm, resid, moe_gain)
    normed_low = normed_two.astype(jnp.bfloat16)
    top_count = routes.shape[1]
    local_experts = gate_weight.shape[0]
    expert_count = local_experts * device_count
    routed_mean = row_count * top_count // expert_count
    capacity = max(2, routed_mean + routed_mean // 16)
    slot_count = local_experts * capacity
    flat_routes = routes.reshape(-1)
    one_hot = (flat_routes[:, None] == jnp.arange(expert_count, dtype=jnp.int32)[None, :]).astype(
        jnp.int32
    )
    ranks = jnp.sum((jnp.cumsum(one_hot, axis=0) - one_hot) * one_hot, axis=1)
    targets = flat_routes // local_experts
    slot_index = flat_routes % local_experts * capacity + ranks
    sources = jnp.arange(row_count * top_count, dtype=jnp.int32) // top_count

    def route_rows(buffer):
        return lax.all_to_all(buffer, ("dp", "mp"), split_axis=0, concat_axis=0, tiled=True)

    def send_out(per_pick):
        buffer = (
            jnp.zeros((device_count, slot_count, model_width), jnp.bfloat16)
            .at[targets, slot_index]
            .set(per_pick, mode="drop")
        )
        arrived = route_rows(buffer)
        return (
            arrived.reshape(device_count, local_experts, capacity, model_width)
            .transpose(1, 0, 2, 3)
            .reshape(local_experts, device_count * capacity, model_width)
        )

    def bring_back(per_expert):
        buffer = (
            per_expert.reshape(local_experts, device_count, capacity, model_width)
            .transpose(1, 0, 2, 3)
            .reshape(device_count, slot_count, model_width)
        )
        arrived = route_rows(buffer)
        return arrived[targets, slot_index].reshape(row_count, top_count, model_width)

    expert_in = send_out(normed_low[sources])
    gate_pre = jnp.einsum(
        "erd,edf->erf", expert_in, gate_weight, preferred_element_type=jnp.float32
    )
    up_pre = jnp.einsum("erd,edf->erf", expert_in, up_weight, preferred_element_type=jnp.float32)
    sigmoid_gate = jax.nn.sigmoid(gate_pre)
    silu_gate = gate_pre * sigmoid_gate
    hidden = (silu_gate * up_pre).astype(jnp.bfloat16)
    expert_out = jnp.einsum(
        "erf,efd->erd", hidden, down_weight, preferred_element_type=jnp.float32
    ).astype(jnp.bfloat16)
    picked = bring_back(expert_out)
    moe_sum = jnp.sum(gate_values[:, :, None] * picked, axis=1)
    block_out = (resid + moe_sum).astype(jnp.bfloat16)
    grad_out = cotangent.astype(jnp.float32)
    gate_values_grad = jnp.sum(grad_out[:, None, :] * picked, axis=2)
    grad_picked = (gate_values[:, :, None] * grad_out[:, None, :]).astype(jnp.bfloat16)
    grad_expert_out = send_out(grad_picked.reshape(row_count * top_count, model_width))
    grad_hidden = jnp.einsum(
        "erd,efd->erf", grad_expert_out, down_weight, preferred_element_type=jnp.float32
    )
    down_weight_grad = jnp.einsum(
        "erf,erd->efd", hidden, grad_expert_out, preferred_element_type=jnp.float32
    )
    grad_gate_pre = (
        grad_hidden * up_pre * sigmoid_gate * (1.0 + gate_pre * (1.0 - sigmoid_gate))
    ).astype(jnp.bfloat16)
    grad_up_pre = (grad_hidden * silu_gate).astype(jnp.bfloat16)
    gate_weight_grad = jnp.einsum(
        "erd,erf->edf", expert_in, grad_gate_pre, preferred_element_type=jnp.float32
    )
    up_weight_grad = jnp.einsum(
        "erd,erf->edf", expert_in, grad_up_pre, preferred_element_type=jnp.float32
    )
    grad_expert_in = (
        jnp.einsum("erf,edf->erd", grad_gate_pre, gate_weight, preferred_element_type=jnp.float32)
        + jnp.einsum("erf,edf->erd", grad_up_pre, up_weight, preferred_element_type=jnp.float32)
    ).astype(jnp.bfloat16)
    grad_moe_normed = jnp.sum(bring_back(grad_expert_in).astype(jnp.float32), axis=1)
    grad_resid_norm, moe_gain_part = norm_two_back(grad_moe_normed)
    grad_resid = grad_out + grad_resid_norm
    back_seq = lax.all_gather(grad_resid.astype(jnp.bfloat16), "mp", axis=0, tiled=True)
    out_weight_grad = lax.psum_scatter(
        contract_first(attended, back_seq).astype(jnp.bfloat16),
        "dp",
        scatter_dimension=1,
        tiled=True,
    ).astype(jnp.float32)
    grad_attended = (
        contract_last(back_seq, wo_whole)
        .astype(jnp.bfloat16)
        .reshape(sequence_length, local_heads, head_width)
    )

    def backward_block(carried, block_index):
        key_accum, value_accum = carried
        scores, query_block, key_block, value_block = block_scores(block_index)
        first_row = block_index * block_rows
        soft_full = jnp.exp(scores - total_blocks[block_index][..., None])
        grad_block = lax.dynamic_slice_in_dim(grad_attended, first_row, block_rows, 0)
        grad_soft = jnp.einsum(
            "qhd,kd->hqk", grad_block, value_block, preferred_element_type=jnp.float32
        )
        row_dots = jnp.sum(soft_full * grad_soft, axis=-1, keepdims=True)
        grad_scores = (soft_full * (grad_soft - row_dots)).astype(jnp.bfloat16)
        grad_query = (
            jnp.einsum("hqk,kd->qhd", grad_scores, key_block, preferred_element_type=jnp.float32)
            * score_scale
        )
        grad_key = (
            jnp.einsum("hqk,qhd->kd", grad_scores, query_block, preferred_element_type=jnp.float32)
            * score_scale
        )
        grad_value = jnp.einsum(
            "hqk,qhd->kd",
            soft_full.astype(jnp.bfloat16),
            grad_block,
            preferred_element_type=jnp.float32,
        )
        key_accum = lax.dynamic_update_slice_in_dim(
            key_accum,
            lax.dynamic_slice_in_dim(key_accum, first_row, key_span, 0) + grad_key,
            first_row,
            0,
        )
        value_accum = lax.dynamic_update_slice_in_dim(
            value_accum,
            lax.dynamic_slice_in_dim(value_accum, first_row, key_span, 0) + grad_value,
            first_row,
            0,
        )
        return ((key_accum, value_accum), grad_query)

    zeros_pad = jnp.zeros((sequence_length + margin, head_width), jnp.float32)
    (key_accum, value_accum), query_blocks = lax.scan(
        backward_block, (zeros_pad, zeros_pad), jnp.arange(block_count, dtype=jnp.int32)
    )
    returned = passed_along(
        jnp.concatenate([key_accum[:margin], value_accum[:margin]], axis=1).astype(jnp.bfloat16),
        "dp",
        -1,
    ).astype(jnp.float32)
    returned = returned * (half_index == 0).astype(jnp.float32)
    tail_add = jnp.concatenate(
        [jnp.zeros((sequence_length - margin, 2 * head_width), jnp.float32), returned], axis=0
    )
    key_total = key_accum[margin:] + tail_add[:, :head_width]
    value_total = value_accum[margin:] + tail_add[:, head_width:]
    grad_query_pre, query_gain_part = query_back(
        query_blocks.reshape(sequence_length, local_heads, head_width)
    )
    grad_key_pre, key_gain_part = key_back(key_total.reshape(sequence_length, 1, head_width))
    query_low = grad_query_pre.reshape(sequence_length, local_width).astype(jnp.bfloat16)
    kv_low = jnp.concatenate(
        [grad_key_pre.reshape(sequence_length, head_width), value_total], axis=1
    ).astype(jnp.bfloat16)
    grad_normed_one = lax.psum_scatter(
        (contract_last(query_low, wq_whole) + contract_last(kv_low, kv_own)).astype(jnp.bfloat16),
        "mp",
        scatter_dimension=0,
        tiled=True,
    ).astype(jnp.float32)
    grad_in_norm, input_gain_part = norm_one_back(grad_normed_one)
    tokens_grad = grad_resid + grad_in_norm
    joined = jnp.concatenate([query_low, kv_low], axis=1)
    shard_rows = query_weight.shape[0]
    summed_rows = lax.psum_scatter(
        contract_first(sequence, joined).astype(jnp.bfloat16), "dp", scatter_dimension=0, tiled=True
    ).astype(jnp.float32)
    query_weight_grad = summed_rows[:, :local_width]
    own_rows = summed_rows[:, local_width:]
    placed = jnp.zeros((shard_rows, 2 * kv_width), jnp.float32)
    placed = lax.dynamic_update_slice_in_dim(placed, own_rows[:, :head_width], kv_offset, 1)
    placed = lax.dynamic_update_slice_in_dim(
        placed, own_rows[:, head_width:], kv_width + kv_offset, 1
    )
    kv_weight_grad = lax.psum(placed.astype(jnp.bfloat16), "mp").astype(jnp.float32)
    input_gain_grad, moe_gain_grad, query_gain_grad, key_gain_grad = lax.psum(
        (input_gain_part, moe_gain_part, query_gain_part, key_gain_part), ("dp", "mp")
    )
    return (
        block_out,
        tokens_grad,
        input_gain_grad,
        query_weight_grad,
        kv_weight_grad,
        query_gain_grad,
        key_gain_grad,
        out_weight_grad,
        moe_gain_grad,
        gate_weight_grad,
        up_weight_grad,
        down_weight_grad,
        gate_values_grad,
    )


def solution(mesh):
    return jax.shard_map(
        on_device,
        mesh=mesh,
        in_specs=(
            P(("dp", "mp"), None),
            P(),
            P("dp", "mp"),
            P("dp", None),
            P(),
            P(),
            P("mp", "dp"),
            P(),
            P(("dp", "mp"), None, None),
            P(("dp", "mp"), None, None),
            P(("dp", "mp"), None, None),
            P(("dp", "mp"), None),
            P(("dp", "mp"), None),
            P(),
            P(("dp", "mp"), None),
        ),
        out_specs=(
            P(("dp", "mp"), None),
            P(("dp", "mp"), None),
            P(),
            P("dp", "mp"),
            P("dp", None),
            P(),
            P(),
            P("mp", "dp"),
            P(),
            P(("dp", "mp"), None, None),
            P(("dp", "mp"), None, None),
            P(("dp", "mp"), None, None),
            P(("dp", "mp"), None),
        ),
        check_vma=False,
    )
```

profile of v0, /device:TPU:0, one launch (start us, length us, event | category | flops | bytes accessed | tf_op | source)
XLA Modules:
  0.0 1947.7 jit_solution(6953492462160106966)
XLA Ops:
  16.0 15.9 reduce-window.11
  38.8 18.9 scatter_custom_fusion.1
  57.7 12.9 copy.201
  70.6 7.2 all-to-all-start.2
  83.2 131.1 %all-gather.6.cloned.1.call-done = bf16[1024,2048]{1,0:T(8,128)(2,1)} async-done(((bf16[256,2048]{1,0:T(8,128)(2,1)}), bf16[1024,2048]{1,0:T(8,128)(2,1)}) %all-gather.6.cloned.1.call-update) | async-done | bytes 4194320 | tf_op jit(solution)/shard_map/all_gather | solution.py:106
  224.0 47.7 %all-gather.10.cloned.1.call-done = bf16[2048,1024]{1,0:T(8,128)(2,1)} async-done(((bf16[256,1024]{1,0:T(8,128)(2,1)}), bf16[2048,1024]{1,0:T(8,128)(2,1)}) %all-gather.10.cloned.1.call-update) | async-done | bytes 4194320 | tf_op jit(solution)/shard_map/all_gather | solution.py:108
  271.6 10.1 multiply_reduce_fusion.2
  281.7 5.5 copy.186
  301.0 8.2 fusion.69
  315.1 93.8 %while.32 = (s32[]{:T(128)}, bf16[2,512,8,128]{3,2,1,0:T(8,128)(2,1)}, f32[2,8,512]{2,1,0:T(8,128)S(1)}, s32[2]{0:T(128)S(1)}, bf16[2048,128]{0,1:T(8,128)(2,1)}...) while((s32[]{:T(128)}, ...), condition=%wide.region_9.10_spmd.clone, body=%wide.region_6.9_spmd.clone.sunk | while | flops 3270543360 | bytes 86483248 | solution.py:185
  319.7 14.1 fusion.179
  333.8 10.3 exponential_reduce_fusion.2
  344.1 13.5 fusion.181
  366.5 13.9 fusion.179
  380.4 10.3 exponential_reduce_fusion.2
  390.7 13.5 fusion.181
  408.9 9.3 convolution_convert_fusion.3
  418.3 79.9 %reduce-scatter.5.cloned.1.call-done = bf16[256,2048]{1,0:T(8,128)(2,1)} async-done(((bf16[1024,2048]{1,0:T(8,128)(2,1)}), bf16[256,2048]{1,0:T(8,128)(2,1)}) %reduce-scatter.5.cloned.1.call-update) | async-done | bytes 1048592 | tf_op jit(solution)/shard_map/reduce_scatter | solution.py:188
  503.6 45.3 %scatter_custom_fusion = bf16[2176,2048]{1,0:T(8,128)(2,1)} fusion(s32[2048]{0:T(1024)} %copy-done.72, bf16[256,2048]{1,0:T(8,128)(2,1)} %multiply_convert_fusion.3, s32[2048]{0:T(1024)} %get-tuple-element.640, bf16[]{:T(256)} %constant.234.clone.1), kind=kCustom, calls=%fused_computation.86 | custom fusion | bytes 8913408
  548.9 12.1 copy.198
  561.1 5.2 all-to-all-start
  566.4 12.8 reshape.626
  579.2 191.0 %all-to-all-done = bf16[32,68,2048]{2,1,0:T(8,128)(2,1)} async-done(((bf16[32,68,2048]{2,1,0:T(8,128)(2,1)}), bf16[32,68,2048]{2,1,0:T(8,128)(2,1)}, u32[]{:S(2)}, u32[]{:S(2)}) %all-to-all-start) | async-done | bytes 8912928 | tf_op jit(solution)/shard_map/all_to_all | solution.py:212
  770.2 12.8 reshape.622
  783.0 12.5 fusion.76
  795.5 9.1 fusion.80
  804.5 17.0 multiply_convert_fusion
  821.6 13.4 fusion.78
  835.0 14.0 add_convert_fusion
  849.0 12.8 reshape_transpose_reshape.9
  861.8 214.2 %all_to_all.20 = bf16[32,68,2048]{2,1,0:T(8,128)(2,1)} all-to-all(bf16[32,68,2048]{2,1,0:T(8,128)(2,1)} %reshape_transpose_reshape.9), channel_id=1, replica_groups=mesh['dp'=8,'mp'=4] {'dp','mp'}, dimensions={0} | all-to-all | bytes 17825792 | tf_op jit(solution)/shard_map/all_to_all | solution.py:212
  1076.0 12.1 copy.202
  1088.1 50.5 %gather_fusion.1 = bf16[2048,2048]{1,0:T(8,128)(2,1)} fusion(bf16[32,68,2048]{2,0,1:T(8,128)(2,1)} %copy.202, s32[2048]{0:T(1024)S(1)} %bitcast.243), kind=kCustom, calls=%fused_computation.2 | custom fusion | bytes 16793600 | tf_op jit(solution)/shard_map/gather | solution.py:234
  1138.6 11.3 convert_reduce_fusion
  1157.4 80.7 %all-gather.14.cloned.1.call-done = bf16[1024,2048]{1,0:T(8,128)(2,1)} async-done(((bf16[256,2048]{1,0:T(8,128)(2,1)}), bf16[1024,2048]{1,0:T(8,128)(2,1)}) %all-gather.14.cloned.1.call-update) | async-done | bytes 4194320 | tf_op jit(solution)/shard_map/all_gather | solution.py:277
  1238.0 9.3 convolution_convert_fusion.4
  1249.5 207.2 %while.33 = (s32[]{:T(128)}, f32[2048,128]{0,1:T(8,128)}, f32[2048,128]{0,1:T(8,128)}, f32[2,512,8,128]{3,2,1,0:T(8,128)}, s32[2]{0:T(128)S(1)}, /*index=5*/s32[...) while((s32[]{:T(128)}, f32[2048,128]{0,1:T(8,128)}, ...), condition=%wide.region_22.23_spmd.clone, body=%wide.region_20.22_spmd.clone.sunk | while | flops 8115517440 | bytes 305914432 | solution.py:330
  1265.7 13.1 fusion.191
  1278.8 17.0 fusion.193
  1295.8 22.4 %fusion.195 = bf16[8,512,1536]{1,2,0:T(8,128)(2,1)} fusion(f32[8,512,1536]{1,2,0:T(8,128)} %get-tuple-element.778, f32[1536,512,8]{1,0,2:T(8,128)} %fusion.191, f32[8,512]{1,0:T(8,128)S(1)} %get-tuple-element.779), kind=kLoop, calls=%fused_computation.38.clone.1 | loop fusion | flops 18874368 | bytes 62930944 | tf_op jit(solution)/shard_map/while/body/eval_jaxpr/convert_element_type | solution.py:300
  1318.2 11.1 fusion.194
  1329.3 9.1 fusion.196
  1369.0 13.1 fusion.191
  1382.1 17.0 fusion.193
  1399.1 22.4 %fusion.195 = bf16[8,512,1536]{1,2,0:T(8,128)(2,1)} fusion(f32[8,512,1536]{1,2,0:T(8,128)} %get-tuple-element.778, f32[1536,512,8]{1,0,2:T(8,128)} %fusion.191, f32[8,512]{1,0:T(8,128)S(1)} %get-tuple-element.779), kind=kLoop, calls=%fused_computation.38.clone.1 | loop fusion | flops 18874368 | bytes 62930944 | tf_op jit(solution)/shard_map/while/body/eval_jaxpr/convert_element_type | solution.py:300
  1421.5 11.1 fusion.194
  1432.6 9.1 fusion.196
  1468.5 5.6 fusion.71
  1474.1 6.4 multiply_reduce_fusion
  1482.8 7.3 fusion.67
  1499.0 7.4 convolution_convert_fusion.1
  1506.4 11.4 convolution_convert_fusion
  1517.8 13.1 reshape_transpose_reshape.8
  1535.9 9.6 convolution_convert_fusion.2
  1545.6 7.1 fusion.132
  1556.6 12.9 convolution_bitcast_fusion.1
  1569.5 12.1 convolution_bitcast_fusion.2
  1581.7 10.0 convolution_bitcast_fusion.3
  1591.7 193.1 %all-to-all-done.1 = bf16[32,68,2048]{2,1,0:T(8,128)(2,1)} async-done(((bf16[32,68,2048]{2,1,0:T(8,128)(2,1)}), bf16[32,68,2048]{2,1,0:T(8,128)(2,1)}, u32[]{:S(2)}, u32[]{:S(2)}) %all-to-all-start.1) | async-done | bytes 8912928 | tf_op jit(solution)/shard_map/all_to_all | solution.py:212
  1784.8 12.1 copy.199
  1796.9 50.1 %gather_fusion = bf16[2048,2048]{1,0:T(8,128)(2,1)} fusion(bf16[32,68,2048]{2,0,1:T(8,128)(2,1)} %copy.199, s32[2048]{0:T(1024)S(1)} %bitcast.244), kind=kCustom, calls=%fused_computation.1 | custom fusion | bytes 16793600 | tf_op jit(solution)/shard_map/gather | solution.py:234
  1850.9 9.7 fusion.56
  1868.0 63.8 %all-reduce.4 = (f32[2048]{0:T(1024)}, f32[128]{0:T(128)}, f32[128]{0:T(128)}, f32[2048]{0:T(1024)}) all-reduce(f32[2048]{0:T(1024)S(1)} %get-tuple-element.550, f32[128]{0:T(128)S(1)} %get-tuple-element.546, f32[128]{0:T(128)S(1)} %get-tuple-element.552, f32[2048]{0:T(1024)S(1)} %copy-done.56), channel_id=1, replica_groups=mesh['dp'=8,'mp'=4] {'dp','mp'}, use_global_device_ids=true, to_apply=%region_28.29 | all-reduce | flops 4352 | bytes 34816 | tf_op jit(solution)/shard_map/psum | solution.py:373
  1934.0 6.6 fusion.92
  (365 shorter events, 182.8 us)
Async XLA Ops:
  7.2 797.4 %copy-start = (bf16[1,768,2048]{2,1,0:T(8,128)(2,1)S(1)}, bf16[1,768,2048]{2,1,0:T(8,128)(2,1)}, u32[]{:S(2)}) copy-start(bf16[1,768,2048]{2,1,0:T(8,128)(2,1)} %param.29) | copy-start | bytes 9437188
  7.2 7.3 copy-start.71
  7.2 73.6 %all-gather.8.cloned.1.call-start = ((), (), s32[]{:S(2)}) async-start(), calls=%async_computation.9 | async-start | bytes 4718592 | tf_op jit(solution)/shard_map/all_gather | solution.py:109
  7.9 206.3 %all-gather.6.cloned.1.call-start = ((), (), s32[]{:S(2)}) async-start(), calls=%async_computation.8 | async-start | bytes 5242880 | tf_op jit(solution)/shard_map/all_gather | solution.py:106
  13.2 24.7 %copy-start.76 = (s32[2]{0:T(128)S(1)}, s32[2]{0:T(128)}, u32[]{:S(2)}) copy-start(s32[2]{0:T(128)} %constant.271) | copy-start | bytes 28
  13.2 24.8 %copy-start.75 = (s32[2]{0:T(128)S(1)}, s32[2]{0:T(128)}, u32[]{:S(2)}) copy-start(s32[2]{0:T(128)} %constant.274) | copy-start | bytes 28
  13.3 258.4 %all-gather.10.cloned.1.call-start = ((), (), s32[]{:S(2)}) async-start(), calls=%async_computation.10 | async-start | bytes 4718592 | tf_op jit(solution)/shard_map/all_gather | solution.py:108
  38.8 18.9 copy-start.72
  70.6 8.0 copy-start.77
  70.6 490.5 %all-to-all-start.2 = ((bf16[32,68,2048]{2,1,0:T(8,128)(2,1)}), bf16[32,68,2048]{2,1,0:T(8,128)(2,1)}, u32[]{:S(2)}, u32[]{:S(2)}) async-start(bf16[32,68,2048]{2,1,0:T(8,128)(2,1)} %copy.201), calls=%async_computation.3 | async-start | bytes 18874368 | tf_op jit(solution)/shard_map/all_to_all | solution.py:212
  77.8 331.1 %all-gather.12.cloned.1.call-start = ((), (), s32[]{:S(2)}) async-start(), calls=%async_computation.11 | async-start | bytes 4718592 | tf_op jit(solution)/shard_map/all_gather | solution.py:187
  78.4 419.8 %reduce-scatter.5.cloned.1.call-start = ((), (), s32[]{:S(2)}) async-start(), calls=%async_computation.12 | async-start | bytes 5242880 | tf_op jit(solution)/shard_map/reduce_scatter | solution.py:188
  80.8 138.1 %copy-start.23 = (f32[1024,64]{0,1:T(8,128)}, f32[1024,64]{0,1:T(8,128)S(1)}, u32[]{:S(2)}) copy-start(f32[1024,64]{0,1:T(8,128)S(1)} %get-tuple-element.635) | copy-start | bytes 786436
  221.7 89.2 %collective-permute-start = (bf16[1024,256]{0,1:T(8,128)(2,1)}, bf16[1024,256]{0,1:T(8,128)(2,1)}, u32[]{:S(2)}, u32[]{:S(2)}) collective-permute-start(bf16[1024,256]{0,1:T(8,128)(2,1)} %pad_maximum_fusion.5), channel_id=1, source_target_pairs={{0,4},{4,8},{8,12},{12,16},{16,20},{20,24},{24,28},{1,5},{5,9},{9,... | collective-permute-start | bytes 1572872 | tf_op jit(solution)/shard_map/ppermute | solution.py:19
  333.8 10.3 copy-start.11
  380.4 10.3 copy-start.11
  408.9 9.4 copy-start.40
  408.9 9.4 copy-start.42
  408.9 9.4 copy-start.44
  418.3 82.4 %copy-start.48 = (f32[2048]{0:T(1024)S(1)}, f32[2048]{0:T(1024)}, u32[]{:S(2)}) copy-start(f32[2048]{0:T(1024)} %param.26) | copy-start | bytes 24580
  561.1 209.1 %all-to-all-start = ((bf16[32,68,2048]{2,1,0:T(8,128)(2,1)}), bf16[32,68,2048]{2,1,0:T(8,128)(2,1)}, u32[]{:S(2)}, u32[]{:S(2)}) async-start(bf16[32,68,2048]{2,1,0:T(8,128)(2,1)} %copy.198), calls=%async_computation.1 | async-start | bytes 18874368 | tf_op jit(solution)/shard_map/all_to_all | solution.py:212
  566.3 671.7 %all-gather.14.cloned.1.call-start = ((), (), s32[]{:S(2)}) async-start(), calls=%async_computation.13 | async-start | bytes 5242880 | tf_op jit(solution)/shard_map/all_gather | solution.py:277
  783.0 12.5 copy-start.19
  783.0 12.5 copy-start.79
  821.6 13.4 copy-start.80
  1076.0 12.1 copy-start.2
  1138.6 11.3 copy-start.49
  1138.6 11.3 copy-start.58
  1157.3 689.8 %reduce-scatter.9.cloned.1.call-start = ((), (), s32[]{:S(2)}) async-start(), calls=%async_computation.15 | async-start | bytes 5898240 | tf_op jit(solution)/shard_map/reduce_scatter | solution.py:362
  1157.3 92.2 %copy-start.41 = (s32[2048]{0:T(1024)S(1)}, s32[2048]{0:T(1024)}, u32[]{:S(2)}) copy-start(s32[2048]{0:T(1024)} %copy-done.40) | copy-start | bytes 24580
  1157.4 92.2 %copy-start.43 = (f32[2,8,512]{2,1,0:T(8,128)S(1)}, f32[2,8,512]{2,1,0:T(8,128)}, u32[]{:S(2)}) copy-start(f32[2,8,512]{2,1,0:T(8,128)} %copy-done.42) | copy-start | bytes 98308
  1157.4 92.2 %copy-start.45 = (s32[1024]{0:T(1024)S(1)}, s32[1024]{0:T(1024)}, u32[]{:S(2)}) copy-start(s32[1024]{0:T(1024)} %copy-done.44) | copy-start | bytes 12292
  1295.8 22.4 %copy-start.5 = (f32[1536,128]{1,0:T(8,128)S(1)}, f32[1536,128]{1,0:T(8,128)}, u32[]{:S(2)}) copy-start(f32[1536,128]{1,0:T(8,128)} %copy.272) | copy-start | bytes 2359300 | tf_op jit(solution)/shard_map/while
  1295.8 22.4 %copy-start.10 = (bf16[1024,8,128]{0,2,1:T(8,128)(2,1)S(1)}, bf16[1024,8,128]{0,2,1:T(8,128)(2,1)}, u32[]{:S(2)}) copy-start(bf16[1024,8,128]{0,2,1:T(8,128)(2,1)} %get-tuple-element.876) | copy-start | bytes 6291460 | tf_op jit(solution)/shard_map/while
  1318.2 11.1 copy-start.8
  1318.2 11.1 copy-start.16
  1329.3 9.1 copy-start.1
  1329.3 9.1 copy-start.7
  1399.1 22.4 %copy-start.5 = (f32[1536,128]{1,0:T(8,128)S(1)}, f32[1536,128]{1,0:T(8,128)}, u32[]{:S(2)}) copy-start(f32[1536,128]{1,0:T(8,128)} %copy.272) | copy-start | bytes 2359300 | tf_op jit(solution)/shard_map/while
  1399.1 22.4 %copy-start.10 = (bf16[1024,8,128]{0,2,1:T(8,128)(2,1)S(1)}, bf16[1024,8,128]{0,2,1:T(8,128)(2,1)}, u32[]{:S(2)}) copy-start(bf16[1024,8,128]{0,2,1:T(8,128)(2,1)} %get-tuple-element.876) | copy-start | bytes 6291460 | tf_op jit(solution)/shard_map/while
  1421.5 11.1 copy-start.8
  1421.5 11.1 copy-start.16
  1432.6 9.1 copy-start.1
  1432.6 9.1 copy-start.7
  1459.7 34.5 %collective-permute-start.1 = (bf16[1024,256]{0,1:T(8,128)(2,1)}, bf16[1024,256]{0,1:T(8,128)(2,1)}, u32[]{:S(2)}, u32[]{:S(2)}) collective-permute-start(bf16[1024,256]{0,1:T(8,128)(2,1)} %pad_maximum_fusion.8), channel_id=1, source_target_pairs={{4,0},{8,4},{12,8},{16,12},{20,16},{24,20},{28,24},{5,1},{9,5},{13... | collective-permute-start | bytes 1572872 | tf_op jit(solution)/shard_map/ppermute | solution.py:19
  1474.1 7.7 copy-start.47
  1530.9 253.9 %all-to-all-start.1 = ((bf16[32,68,2048]{2,1,0:T(8,128)(2,1)}), bf16[32,68,2048]{2,1,0:T(8,128)(2,1)}, u32[]{:S(2)}, u32[]{:S(2)}) async-start(bf16[32,68,2048]{2,1,0:T(8,128)(2,1)} %reshape_transpose_reshape.8), calls=%async_computation.2 | async-start | bytes 18874368 | tf_op jit(solution)/shard_map/all_to_all | solution.py:212
  1535.6 325.6 %reduce-scatter.11.cloned.1.call-start = ((), (), s32[]{:S(2)}) async-start(), calls=%async_computation.17 | async-start | bytes 4718592 | tf_op jit(solution)/shard_map/reduce_scatter | solution.py:278
  1545.5 320.0 %reduce-scatter.7.cloned.1.call-start = ((), (), s32[]{:S(2)}) async-start(), calls=%async_computation.14 | async-start | bytes 5242880 | tf_op jit(solution)/shard_map/reduce_scatter | solution.py:352
  1556.1 375.7 %all-reduce.7.cloned.1.call-start = ((), (), s32[]{:S(2)}) async-start(), calls=%async_computation.16 | async-start | bytes 1048576 | tf_op jit(solution)/shard_map/psum | solution.py:372
  1556.6 12.9 copy-start.82
  1556.6 25.0 %slice-start = ((s8[8912896]{0:T(1024)(128)(4,1)}), s8[4194304]{0:T(1024)(128)(4,1)S(1)}, s32[]{:S(2)}) async-start(s8[8912896]{0:T(1024)(128)(4,1)} %bitcast.248), calls=%async_computation.18 | async-start | bytes 8388608
  1556.6 25.0 %slice-start.1 = ((s8[8912896]{0:T(1024)(128)(4,1)}), s8[4194304]{0:T(1024)(128)(4,1)S(1)}, s32[]{:S(2)}) async-start(s8[8912896]{0:T(1024)(128)(4,1)} %bitcast.248), calls=%async_computation.19 | async-start | bytes 8388608
  1569.5 12.1 slice-start.2
  1569.5 12.1 copy-start.81
  1591.7 205.2 %copy-start.3 = (s32[2048,1]{0,1:T(1,128)S(1)}, s32[2048,1]{0,1:T(1,128)}, u32[]{:S(2)}) copy-start(s32[2048,1]{0,1:T(1,128)} %get-tuple-element.629) | copy-start | bytes 24580
  1796.9 54.0 %copy-start.35 = (f32[256,8]{1,0:T(8,128)S(1)}, f32[256,8]{1,0:T(8,128)}, u32[]{:S(2)}) copy-start(f32[256,8]{1,0:T(8,128)} %copy-done.34) | copy-start | bytes 24580
  1850.9 14.6 copy-start.53
  1850.9 14.6 copy-start.61
  1860.5 7.5 copy-start.56
  1860.5 71.3 %copy-start.63 = (f32[256]{0:T(256)S(1)}, f32[256]{0:T(256)}, u32[]{:S(2)}) copy-start(f32[256]{0:T(256)} %copy-done.62) | copy-start | bytes 3076
  1860.5 73.5 %copy-start.50 = (f32[2048]{0:T(1024)S(1)}, f32[2048]{0:T(1024)}, u32[]{:S(2)}) copy-start(f32[2048]{0:T(1024)} %param.26) | copy-start | bytes 24580
  1860.5 73.5 %copy-start.59 = (f32[256]{0:T(256)S(1)}, f32[256]{0:T(256)}, u32[]{:S(2)}) copy-start(f32[256]{0:T(256)} %copy-done.57) | copy-start | bytes 3076
  1860.5 73.5 %copy-start.67 = (f32[256]{0:T(256)S(1)}, f32[256]{0:T(256)}, u32[]{:S(2)}) copy-start(f32[256]{0:T(256)} %copy-done.66) | copy-start | bytes 3076
  (45 other events, 170.9 us)
Sparse Core Ops, SparseCore 0:
  9.9 39.4 all-gather.7
  51.5 162.6 all-gather.5
  216.1 55.4 all-gather.9
  273.4 48.4 all-gather.11
  418.4 79.6 reduce-scatter.4
  1157.4 80.5 all-gather.13
  1506.6 120.2 reduce-scatter.8
  1630.2 69.2 reduce-scatter.10
  1701.8 101.8 reduce-scatter.6
  1851.0 60.7 all-reduce.6
where the time goes:
time: 1960 us; the launch traced here: 1950 us
  waiting for transfers between devices  725 us (37%)
  local copies, waits for them, and re-layouts  343 us (18%)
  matrix products  334 us (17%)
  blocking collectives  278 us (14%)
  other arithmetic  222 us (11%)
  starting transfers between devices  21.7 us (1%)
    all_to_all x3, waiting for transfers between devices, route_rows(): lax.all_to_all(buffer, ('dp', 'mp'), split_axis=0, concat_axis=0, tiled=T...  384 us
    all_to_all x1, blocking collectives, route_rows(): lax.all_to_all(buffer, ('dp', 'mp'), split_axis=0, concat_axis=0, tiled=T...  214 us
    all_gather x1, waiting for transfers between devices, on_device(): lax.all_gather(normed_one.astype(jnp.bfloat16), 'mp', axis=0, tiled=True)  131 us
    gather x2, local copies, waits for them, and re-layouts, bring_back(): arrived[targets, slot_index].reshape(row_count, top_count, model_width)  101 us
    all_gather x1, waiting for transfers between devices, on_device(): lax.all_gather(grad_resid.astype(jnp.bfloat16), 'mp', axis=0, tiled=True)  80.7 us
    reduce_scatter x1, waiting for transfers between devices, on_device(): lax.psum_scatter(jnp.dot(attended, wo_whole, preferred_element_type=jnp.f...  79.9 us
    psum x1, blocking collectives, on_device(): lax.psum((input_gain_part, moe_gain_part, query_gain_part, key_gain_part)...  63.8 us
    dot_general x4, matrix products, block_scores(): jnp.einsum('qhd,kd->hqk', query_block, key_block, preferred_element_type=...  62 us
  transfers between devices with their start and end apart: 15, of which 6 were waited for; matrix products, arithmetic and copies ran while one was open for 25% of the time, Pallas kernels for 0%

commit v1 on v0

v1 whole, which is shorter than its diff:
```python
import functools
import math

import jax
import jax.numpy as jnp
from jax import lax
from jax.experimental import pallas as pl
from jax.experimental.pallas import tpu as pltpu
from jax.sharding import PartitionSpec as P

WINDOW = 1024
EPSILON = 1e-06
ROPE_BASE = 1000000.0
FAR = 16384.0
VMEM = 56 * 1024 * 1024
LOW = jnp.bfloat16
FULL = jnp.float32


def rms_norm(value_rows, gain_vector):
    return (
        value_rows
        * lax.rsqrt(jnp.mean(value_rows * value_rows, axis=-1, keepdims=True) + EPSILON)
        * gain_vector
    )


def rope_tables(positions, head_width):
    half_width = head_width // 2
    frequency = jnp.exp(
        jnp.arange(half_width, dtype=FULL) * (-2.0 * math.log(ROPE_BASE) / head_width)
    )
    angles = positions[:, None] * frequency[None, :]
    cosine = jnp.cos(angles)
    sine = jnp.sin(angles)
    return (
        jnp.concatenate([cosine, cosine], axis=-1),
        jnp.concatenate([-sine, sine], axis=-1),
    )


def doc_layout(doc_lengths, sequence_length):
    ends_at = jnp.cumsum(doc_lengths)
    starts_at = ends_at - doc_lengths
    places = jnp.arange(sequence_length, dtype=jnp.int32)
    doc_ids = jnp.sum((places[:, None] >= ends_at[None, :]).astype(jnp.int32), axis=1)
    matches = doc_ids[:, None] == jnp.arange(doc_lengths.shape[0], dtype=jnp.int32)[None, :]
    begins = jnp.sum(jnp.where(matches, starts_at[None, :], 0), axis=1)
    return (doc_ids, places - begins)


def matmul(left, right):
    return jnp.dot(left, right, preferred_element_type=FULL)


def contract_last(left, right):
    return lax.dot_general(left, right, (((1,), (1,)), ((), ())), preferred_element_type=FULL)


def contract_first(left, right):
    return lax.dot_general(left, right, (((0,), (0,)), ((), ())), preferred_element_type=FULL)


def ring_shift(shard, axis="mp"):
    length = lax.axis_size(axis)
    return lax.ppermute(shard, axis, [(i, (i + 1) % length) for i in range(length)])


def swap(shard, axis, bit):
    length = lax.axis_size(axis)
    return lax.ppermute(shard, axis, [(i, i ^ bit) for i in range(length)])


def split_rows(rows, count):
    size = rows.shape[0] // count
    return [rows[k * size : (k + 1) * size] for k in range(count)]


def joined_rows(pieces):
    return pieces[0] if len(pieces) == 1 else jnp.concatenate(pieces, axis=0)


def exchange(rows, order):
    pieces = [rows]
    for bit in order:
        half = pieces[0].shape[0] // 2
        came = swap(joined_rows([p[half:] for p in pieces]), "dp", bit)
        pieces = [p[:half] for p in pieces] + split_rows(came, len(pieces))
    return joined_rows(pieces)


def give_back(rows, order):
    pieces = split_rows(rows, 1 << len(order))
    for bit in reversed(order):
        count = len(pieces) // 2
        came = split_rows(swap(joined_rows(pieces[count:]), "dp", bit), count)
        pieces = [joined_rows([k, c]) for k, c in zip(pieces[:count], came)]
    return pieces[0]


def by_place(table, me, order):
    count = len(order)
    rest = table.shape[1:]
    table = table.reshape((2,) * count + rest)
    for axis in range(count):
        turned = (me >> (count - 1 - axis)) & 1
        table = jnp.where(turned == 1, jnp.flip(table, axis), table)
    axes = [count - 1 - (bit.bit_length() - 1) for bit in order]
    axes += list(range(count, count + len(rest)))
    return table.transpose(axes).reshape((1 << count,) + rest)


def by_index(table, me, order):
    count = len(order)
    rest = table.shape[1:]
    table = table.reshape((2,) * count + rest)
    axes = [count - 1 - (bit.bit_length() - 1) for bit in order]
    back = [axes.index(k) for k in range(count)] + list(range(count, count + len(rest)))
    table = table.transpose(back)
    for axis in range(count):
        turned = (me >> (count - 1 - axis)) & 1
        table = jnp.where(turned == 1, jnp.flip(table, axis), table)
    return table.reshape((1 << count,) + rest)


def sum_scatter_rows(rows, order):
    me = lax.axis_index("dp")
    count = len(order)
    size = rows.shape[0] >> count
    parts = rows.reshape((2,) * count + (size, rows.shape[1]))
    axis_of = {bit: count - bit.bit_length() for bit in order}
    left = sorted(order, reverse=True)
    for bit in order:
        axis = left.index(bit)
        side = (me // bit) % 2
        own = lax.dynamic_index_in_dim(parts, side, axis, keepdims=False)
        other = lax.dynamic_index_in_dim(parts, 1 - side, axis, keepdims=False)
        parts = (own.astype(FULL) + swap(other, "dp", bit).astype(FULL)).astype(LOW)
        left.remove(bit)
    return parts


def ring_sum(parts):
    total = None
    for b in list(range(1, len(parts))) + [0]:
        if total is None:
            total = parts[b]
        else:
            total = parts[b] + ring_shift(total.astype(LOW)).astype(FULL)
    return total


def ring_blocks(shard, count):
    blocks = [shard]
    for _ in range(1, count):
        blocks.append(ring_shift(blocks[-1]))
    return blocks


def turned(values):
    return pltpu.roll(values, values.shape[1] // 2, axis=1)


def prep_kernel(at_ref, query_ref, kv_ref, cos_ref, sin_ref, qg_ref, kg_ref, out_ref, kvo_ref):
    width = cos_ref.shape[1]
    cosine, sine = cos_ref[...], sin_ref[...]

    def one(pre, gain):
        rate = lax.rsqrt(jnp.mean(pre * pre, axis=1, keepdims=True) + EPSILON)
        normed = pre * rate * gain
        return (normed * cosine + turned(normed) * sine).astype(LOW)

    for h in range(query_ref.shape[1] // width):
        cols = slice(h * width, (h + 1) * width)
        out_ref[:, cols] = one(query_ref[:, cols], qg_ref[...])
    kvo_ref[:, :width] = one(kv_ref[:, :width], kg_ref[...])
    kvo_ref[:, width:] = kv_ref[:, width:].astype(LOW)


def prepare(at, query_pre, kv_pre, cosine, sine, query_gain, key_gain):
    rows, wide = query_pre.shape
    width = cosine.shape[1]
    step = min(128, rows)
    count = rows // step
    own = lambda i, at: (i, 0)
    table = pl.BlockSpec((step, width), lambda i, at: (at[0] * count + i, 0))
    gain = pl.BlockSpec((1, width), lambda i, at: (0, 0))
    return pl.pallas_call(
        prep_kernel,
        out_shape=(
            jax.ShapeDtypeStruct((rows, wide), LOW),
            jax.ShapeDtypeStruct((rows, 2 * width), LOW),
        ),
        grid_spec=pltpu.PrefetchScalarGridSpec(
            num_scalar_prefetch=1,
            grid=(count,),
            in_specs=[
                pl.BlockSpec((step, wide), own),
                pl.BlockSpec((step, 2 * width), own),
                table,
                table,
                gain,
                gain,
            ],
            out_specs=[pl.BlockSpec((step, wide), own), pl.BlockSpec((step, 2 * width), own)],
        ),
        compiler_params=pltpu.CompilerParams(vmem_limit_bytes=VMEM),
        cost_estimate=pl.CostEstimate(
            flops=rows * wide * 10, bytes_accessed=rows * wide * 8, transcendentals=rows * 16
        ),
    )(at, query_pre, kv_pre, cosine, sine, query_gain, key_gain)


def thirds(values):
    first = values.astype(LOW)
    rest = values - first.astype(FULL)
    second = rest.astype(LOW)
    return first, second, (rest - second.astype(FULL)).astype(LOW)


def attend_kernel(score_scale, docs, at_ref, q_ref, qa_ref, kx_ref, vx_ref, out_ref, aug_ref):
    rows, width = q_ref.shape
    window = WINDOW
    start = pl.multiple_of(at_ref[0] * rows, rows)
    rate = score_scale * math.log2(math.e)
    far = pl.ds(start, rows)
    mid = pl.ds(pl.multiple_of(start + rows, rows), window - rows)
    near = pl.ds(pl.multiple_of(start + window, rows), rows)
    query = jnp.concatenate([q_ref[...], qa_ref[...]], axis=1)
    key_at = lax.broadcasted_iota(jnp.int32, (rows, rows), 1)
    row_at = lax.broadcasted_iota(jnp.int32, (rows, rows), 0)
    upper = key_at > row_at
    corner = jnp.where(
        upper, contract_last(query, kx_ref[far, :]), contract_last(query, kx_ref[near, :])
    )
    corner = jnp.exp2(corner * rate)
    total = matmul(jnp.where(upper, corner, 0.0).astype(LOW), vx_ref[far, :])
    total += matmul(jnp.where(upper, 0.0, corner).astype(LOW), vx_ref[near, :])
    inner = jnp.exp2(contract_last(query, kx_ref[mid, :]) * rate).astype(LOW)
    total += matmul(inner, vx_ref[mid, :])
    sums = total[:, width:]
    out_ref[...] = (total[:, :width] / sums).astype(LOW)
    first, second, third = thirds(jnp.log(sums) * (-1.0 / score_scale))
    lane = lax.broadcasted_iota(jnp.int32, (rows, width), 1)
    aug = qa_ref[...].astype(FULL)
    aug = jnp.where(lane == docs + 1, first.astype(FULL), aug)
    aug = jnp.where(lane == docs + 2, second.astype(FULL), aug)
    aug = jnp.where(lane == docs + 3, third.astype(FULL), aug)
    aug_ref[...] = aug.astype(LOW)


def attend(at, queries, query_aug, keys_wide, values_wide, score_scale, docs):
    rows, wide = queries.shape
    width = query_aug.shape[1]
    heads = wide // width
    head = pl.BlockSpec((rows, width), lambda h, at: (0, h))
    fixed = lambda array: pl.BlockSpec(array.shape, lambda h, at: (0, 0))
    table = pl.BlockSpec((rows, width), lambda h, at: (at[0], 0))
    return pl.pallas_call(
        functools.partial(attend_kernel, score_scale, docs),
        out_shape=(jax.ShapeDtypeStruct((rows, wide), LOW), jax.ShapeDtypeStruct((rows, wide), LOW)),
        grid_spec=pltpu.PrefetchScalarGridSpec(
            num_scalar_prefetch=1,
            grid=(heads,),
            in_specs=[head, table, fixed(keys_wide), fixed(values_wide)],
            out_specs=[head, head],
        ),
        compiler_params=pltpu.CompilerParams(vmem_limit_bytes=VMEM),
        cost_estimate=pl.CostEstimate(
            flops=heads * rows * (WINDOW + rows) * 1024,
            bytes_accessed=rows * wide * 8 + keys_wide.size * 4,
            transcendentals=heads * rows * WINDOW,
        ),
    )(at, queries, query_aug, keys_wide, values_wide)


def attend_back_kernel(
    score_scale,
    at_ref,
    q_ref,
    qa_ref,
    grad_ref,
    out_ref,
    pre_ref,
    cos_ref,
    sin_ref,
    gain_ref,
    kx_ref,
    vx_ref,
    kt_ref,
    low_ref,
    kv_ref,
    gain_grad_ref,
):
    rows, width = q_ref.shape
    window = WINDOW
    start = pl.multiple_of(at_ref[0] * rows, rows)
    rate = score_scale * math.log2(math.e)

    @pl.when(pl.program_id(0) == 0)
    def _():
        kv_ref[...] = jnp.zeros_like(kv_ref)
        gain_grad_ref[...] = jnp.zeros_like(gain_grad_ref)

    query = q_ref[...]
    grad = grad_ref[...]
    query_wide = jnp.concatenate([query, qa_ref[...]], axis=1)
    dots = jnp.sum(grad.astype(FULL) * out_ref[...].astype(FULL), axis=1, keepdims=True)
    first, second, third = thirds(jnp.broadcast_to(-dots, (rows, width)))
    lane = lax.broadcasted_iota(jnp.int32, (rows, width), 1)
    aug = jnp.where(lane == 0, first.astype(FULL), 0.0)
    aug = jnp.where(lane == 1, second.astype(FULL), aug)
    aug = jnp.where(lane == 2, third.astype(FULL), aug)
    grad_wide = jnp.concatenate([grad, aug.astype(LOW)], axis=1)

    def add(part, soft, scores):
        kv_ref[part, :width] += matmul(scores, query)
        kv_ref[part, width:] += matmul(soft, grad)

    mid_size = window - rows
    mid = pl.ds(pl.multiple_of(start + rows, rows), mid_size)
    soft = jnp.exp2(contract_last(kx_ref[mid, :], query_wide) * rate)
    scores = (soft * contract_last(vx_ref[mid, :], grad_wide)).astype(LOW)
    add(slice(rows, rows + mid_size), soft.astype(LOW), scores)
    query_grad = matmul(kt_ref[:, mid], scores)

    far = pl.ds(start, rows)
    near = pl.ds(pl.multiple_of(start + window, rows), rows)
    key_at = lax.broadcasted_iota(jnp.int32, (rows, rows), 0)
    row_at = lax.broadcasted_iota(jnp.int32, (rows, rows), 1)
    upper = key_at > row_at
    corner = jnp.where(
        upper,
        contract_last(kx_ref[far, :], query_wide),
        contract_last(kx_ref[near, :], query_wide),
    )
    soft = jnp.exp2(corner * rate)
    slopes = jnp.where(
        upper, contract_last(vx_ref[far, :], grad_wide), contract_last(vx_ref[near, :], grad_wide)
    )
    scores = soft * slopes
    scores_far = jnp.where(upper, scores, 0.0).astype(LOW)
    scores_near = jnp.where(upper, 0.0, scores).astype(LOW)
    add(slice(0, rows), jnp.where(upper, soft, 0.0).astype(LOW), scores_far)
    add(slice(window, window + rows), jnp.where(upper, 0.0, soft).astype(LOW), scores_near)
    query_grad += matmul(kt_ref[:, far], scores_far)
    query_grad += matmul(kt_ref[:, near], scores_near)

    spread = query_grad.T * score_scale
    spread = spread * cos_ref[...] - sin_ref[...] * turned(spread)
    pre = pre_ref[...]
    pace = lax.rsqrt(jnp.mean(pre * pre, axis=1, keepdims=True) + EPSILON)
    normed = pre * pace
    gain_grad_ref[...] += jnp.sum(spread * normed, axis=0, keepdims=True)
    spread = spread * gain_ref[...]
    low_ref[...] = (
        pace * (spread - normed * jnp.mean(spread * normed, axis=1, keepdims=True))
    ).astype(LOW)


def attend_back(
    at, queries, query_aug, grads, outs, pre, cosine, sine, gain, keys_wide, values_wide, keys_turned, score_scale
):
    rows, wide = queries.shape
    width = cosine.shape[1]
    heads = wide // width
    span = WINDOW + rows
    head = pl.BlockSpec((rows, width), lambda h, at: (0, h))
    fixed = lambda shape: pl.BlockSpec(shape, lambda h, at: (0, 0))
    table = pl.BlockSpec((rows, width), lambda h, at: (at[0], 0))
    return pl.pallas_call(
        functools.partial(attend_back_kernel, score_scale),
        out_shape=(
            jax.ShapeDtypeStruct((rows, wide), LOW),
            jax.ShapeDtypeStruct((span, 2 * width), FULL),
            jax.ShapeDtypeStruct((1, width), FULL),
        ),
        grid_spec=pltpu.PrefetchScalarGridSpec(
            num_scalar_prefetch=1,
            grid=(heads,),
            in_specs=[
                head,
                head,
                head,
                head,
                head,
                table,
                table,
                fixed((1, width)),
                fixed(keys_wide.shape),
                fixed(values_wide.shape),
                fixed(keys_turned.shape),
            ],
            out_specs=[head, fixed((span, 2 * width)), fixed((1, width))],
        ),
        compiler_params=pltpu.CompilerParams(vmem_limit_bytes=VMEM),
        cost_estimate=pl.CostEstimate(
            flops=heads * rows * span * 2048,
            bytes_accessed=rows * wide * 16 + keys_wide.size * 8,
            transcendentals=heads * rows * WINDOW,
        ),
    )(at, queries, query_aug, grads, outs, pre, cosine, sine, gain, keys_wide, values_wide, keys_turned)


def on_device(
    tokens,
    input_gain,
    query_weight,
    key_value_weight,
    query_gain,
    key_gain,
    out_weight,
    moe_gain,
    gate_weight,
    up_weight,
    down_weight,
    gate_values,
    routes,
    lengths,
    cotangent,
):
    row_count, model_width = tokens.shape
    head_width = query_gain.shape[0]
    kv_width = key_value_weight.shape[1] // 2
    local_width = query_weight.shape[1]
    local_heads = local_width // head_width
    mp_count = lax.axis_size("mp")
    dp_count = lax.axis_size("dp")
    expert_count = mp_count * dp_count
    heads_per_group = local_heads * mp_count * head_width // kv_width
    kv_offsets = [m * local_heads // heads_per_group * head_width for m in range(mp_count)]
    mp_place = lax.axis_index("mp")
    dp_place = lax.axis_index("dp")
    kv_offset = mp_place * local_heads // heads_per_group * head_width
    sequence_length = row_count * mp_count
    docs = lengths.shape[1]
    score_scale = 1.0 / math.sqrt(head_width)
    half_index = dp_place % 2
    seq_index = dp_place // 2
    shard_rows = query_weight.shape[0]
    blocks = range(mp_count)
    places = [(mp_place - b) % mp_count for b in blocks]
    spots = [p.reshape((1,)).astype(jnp.int32) for p in places]

    resid_in = tokens.astype(FULL)
    normed_one, norm_one_back = jax.vjp(rms_norm, resid_in, input_gain)
    sequence = ring_blocks(normed_one.astype(LOW), mp_count)
    wq_whole = lax.all_gather(query_weight, "dp", axis=0, tiled=True)
    kv_own = lax.all_gather(
        jnp.concatenate(
            [
                lax.dynamic_slice_in_dim(key_value_weight, kv_offset, head_width, 1),
                lax.dynamic_slice_in_dim(key_value_weight, kv_width + kv_offset, head_width, 1),
            ],
            axis=1,
        ),
        "dp",
        axis=0,
        tiled=True,
    )
    wo_whole = lax.all_gather(out_weight, "dp", axis=1, tiled=True)
    wkv_whole = lax.all_gather(key_value_weight, "dp", axis=0, tiled=True)

    top_count = routes.shape[1]
    routed_mean = row_count * top_count // expert_count
    capacity = max(2, routed_mean + routed_mean // 16)
    capacity = -(-capacity // 8) * 8
    bits = [1 << k for k in range(dp_count.bit_length() - 1)]
    if capacity >= 32:
        cut = (capacity // 2 + 7) // 8 * 8
        streams = [(0, cut, bits[1:] + bits[:1]), (cut, capacity, bits[1:][::-1] + bits[:1])]
    else:
        streams = [(0, capacity, bits[1:] + bits[:1])]
    routes_turned = routes.T
    gates_turned = gate_values.T
    expert_ids = lax.broadcasted_iota(jnp.int32, (expert_count, row_count), 0)
    picked = [routes_turned[k][None, :] == expert_ids for k in range(top_count)]
    member = sum(p.astype(FULL) for p in picked)
    gate_of = sum(jnp.where(picked[k], gates_turned[k][None, :], 0.0) for k in range(top_count))
    ahead = (
        lax.broadcasted_iota(jnp.int32, (row_count, row_count), 0)
        < lax.broadcasted_iota(jnp.int32, (row_count, row_count), 1)
    ).astype(LOW)
    counts = jnp.where(member > 0, matmul(member.astype(LOW), ahead), -1.0)
    plane_counts = lax.all_to_all(
        counts.astype(LOW).reshape(dp_count, mp_count, row_count).transpose(1, 0, 2),
        "mp",
        split_axis=0,
        concat_axis=0,
        tiled=True,
    )
    expert_view = lax.all_to_all(
        jnp.stack([counts, gate_of], axis=1), ("dp", "mp"), split_axis=0, concat_axis=0, tiled=True
    ).reshape(dp_count, mp_count, 2, row_count)

    def slots(table, low, high):
        at = lax.broadcasted_iota(jnp.int32, (1, high - low, 1), 1) + low
        return table[:, None, :] == at.astype(FULL)

    sends = []
    seen = []
    row_gates = []
    for b in blocks:
        here = lax.dynamic_index_in_dim(plane_counts, places[b], 0, keepdims=False).astype(FULL)
        there = lax.dynamic_index_in_dim(expert_view, places[b], 1, keepdims=False)
        picks, finds, weights = [], [], []
        for low, high, order in streams:
            hot = slots(by_place(here, dp_place, order), low, high)
            picks.append(hot.astype(LOW).reshape(dp_count * (high - low), row_count))
            turned_view = by_place(there, dp_place, order[::-1])
            hot = slots(turned_view[:, 0], low, high)
            finds.append(hot)
            weights.append(
                jnp.sum(jnp.where(hot, turned_view[:, 1][:, None, :], 0.0), axis=2).reshape(-1, 1)
            )
        sends.append(picks)
        seen.append(finds)
        row_gates.append(jnp.concatenate(weights, axis=0))

    def dispatch(block, b):
        arrived = [
            exchange(matmul(pick, block).astype(LOW), order)
            for pick, (_, _, order) in zip(sends[b], streams)
        ]
        return joined_rows(arrived)

    def combine(rows, b):
        ends = [dp_count * (high - low) for low, high, _ in streams]
        came = [
            give_back(rows[(sum(ends[:n])) : sum(ends[: n + 1])], streams[n][2])
            for n in range(len(streams))
        ]
        return contract_first(joined_rows(sends[b]), joined_rows(came))

    seq_lengths = lax.dynamic_index_in_dim(lengths, seq_index, 0, keepdims=False)
    docs_whole, places_whole = doc_layout(seq_lengths, 2 * sequence_length)
    doc_ids = lax.dynamic_slice_in_dim(docs_whole, half_index * sequence_length, sequence_length, 0)
    positions = lax.dynamic_slice_in_dim(
        places_whole, half_index * sequence_length, sequence_length, 0
    )
    prior_docs = jnp.where(half_index == 1, docs_whole[:sequence_length], -1)
    docs_pad = jnp.concatenate([prior_docs, doc_ids])
    cosine, sine = rope_tables(positions.astype(FULL), head_width)
    lane = jnp.arange(head_width, dtype=jnp.int32)[None, :]
    query_aug = jnp.where(lane < docs, doc_ids[:, None] != lane, lane == docs).astype(LOW)
    key_hit = jnp.where(lane == docs, docs_pad[:, None] == -1, docs_pad[:, None] == lane)
    key_aug = jnp.where(
        lane <= docs, jnp.where(key_hit, -FAR, 0.0), jnp.where(lane <= docs + 3, 1.0, 0.0)
    ).astype(LOW)
    query_gain_row = query_gain.reshape(1, head_width)
    key_gain_row = key_gain.reshape(1, head_width)

    query_pre, queries = [], []
    kv_rows = jnp.zeros((sequence_length, 2 * head_width), LOW)
    key_pre = jnp.zeros((sequence_length, head_width), FULL)
    for b in blocks:
        pre_b = matmul(sequence[b], wq_whole)
        kv_b = matmul(sequence[b], kv_own)
        queries_b, kv_low = prepare(
            spots[b], pre_b, kv_b, cosine, sine, query_gain_row, key_gain_row
        )
        query_pre.append(pre_b)
        queries.append(queries_b)
        kv_rows = lax.dynamic_update_slice_in_dim(kv_rows, kv_low, places[b] * row_count, 0)
        key_pre = lax.dynamic_update_slice_in_dim(
            key_pre, kv_b[:, :head_width], places[b] * row_count, 0
        )
    prior = lax.ppermute(kv_rows, "dp", [(i, i + 1) for i in range(0, dp_count, 2)])
    keys_pad = jnp.concatenate([prior[:, :head_width], kv_rows[:, :head_width]], axis=0)
    values_pad = jnp.concatenate([prior[:, head_width:], kv_rows[:, head_width:]], axis=0)
    keys_wide = jnp.concatenate([keys_pad, key_aug], axis=1)
    values_wide = jnp.concatenate([values_pad, jnp.ones_like(values_pad)], axis=1)
    keys_turned = keys_pad.T

    attended, augs, head_parts = [None] * mp_count, [None] * mp_count, [None] * mp_count
    for b in list(range(1, mp_count)) + [0]:
        attended[b], augs[b] = attend(
            spots[b], queries[b], query_aug, keys_wide, values_wide, score_scale, docs
        )
        head_parts[b] = matmul(attended[b], wo_whole)
    resid = resid_in + ring_sum(head_parts)
    normed_two, norm_two_back = jax.vjp(rms_norm, resid, moe_gain)

    gate_one, up_one, down_one = gate_weight[0], up_weight[0], down_weight[0]
    cot_blocks = ring_blocks(cotangent, mp_count)
    normed_blocks = ring_blocks(normed_two.astype(LOW), mp_count)
    inputs, hiddens, scaled, gate_grads, up_grads, outs, gate_rows = [], [], [], [], [], [], []
    resid_parts = []
    cot_rows = [dispatch(cot_blocks[b], b) for b in blocks]
    for b in blocks:
        rows_b = dispatch(normed_blocks[b], b)
        gate_pre = matmul(rows_b, gate_one)
        up_pre = matmul(rows_b, up_one)
        sigmoid_gate = jax.nn.sigmoid(gate_pre)
        silu_gate = gate_pre * sigmoid_gate
        hidden = (silu_gate * up_pre).astype(LOW)
        scaled_b = (row_gates[b] * cot_rows[b].astype(FULL)).astype(LOW)
        grad_hidden = contract_last(scaled_b, down_one)
        gate_grad = (
            grad_hidden * up_pre * sigmoid_gate * (1.0 + gate_pre * (1.0 - sigmoid_gate))
        ).astype(LOW)
        up_grad = (grad_hidden * silu_gate).astype(LOW)
        grad_in = (contract_last(gate_grad, gate_one) + contract_last(up_grad, up_one)).astype(LOW)
        resid_parts.append(combine(grad_in, b))
        inputs.append(rows_b)
        hiddens.append(hidden)
        scaled.append(scaled_b)
        gate_grads.append(gate_grad)
        up_grads.append(up_grad)
    grad_moe_normed = ring_sum(resid_parts)
    grad_resid_norm, moe_gain_part = norm_two_back(grad_moe_normed)
    grad_resid = cotangent.astype(FULL) + grad_resid_norm
    back = ring_blocks(grad_resid.astype(LOW), mp_count)

    out_parts = []
    gate_grad_parts = []
    for b in blocks:
        out_b = matmul(hiddens[b], down_one)
        dots = jnp.sum(out_b * cot_rows[b].astype(FULL), axis=1, keepdims=True)
        out_low = (row_gates[b] * out_b).astype(LOW)
        out_low, _ = lax.optimization_barrier((out_low, grad_moe_normed))
        out_parts.append(combine(out_low, b))
        found = 0.0
        base = 0
        for (low, high, order), hot in zip(streams, seen[b]):
            size = dp_count * (high - low)
            mine = dots[base : base + size].reshape(dp_count, high - low, 1)
            base += size
            found += by_index(jnp.sum(jnp.where(hot, mine, 0.0), axis=1), dp_place, order[::-1])
        gate_grad_parts.append(found)
    block_out = (resid + ring_sum(out_parts)).astype(LOW)
    spread = jnp.stack(
        [
            sum(jnp.where(places[b] == p, gate_grad_parts[b], 0.0) for b in blocks)
            for p in range(mp_count)
        ],
        axis=1,
    ).reshape(expert_count, row_count)
    spread = lax.all_to_all(spread, ("dp", "mp"), split_axis=0, concat_axis=0, tiled=True)
    gate_values_grad = jnp.stack(
        [jnp.sum(jnp.where(picked[k], spread, 0.0), axis=0) for k in range(top_count)], axis=1
    )
    inputs_all = joined_rows(inputs)
    down_weight_grad = contract_first(joined_rows(hiddens), joined_rows(scaled))[None]
    gate_weight_grad = contract_first(inputs_all, joined_rows(gate_grads))[None]
    up_weight_grad = contract_first(inputs_all, joined_rows(up_grads))[None]

    out_weight_grad = lax.psum_scatter(
        contract_first(joined_rows(attended), joined_rows(back)).astype(LOW),
        "dp",
        scatter_dimension=1,
        tiled=True,
    ).astype(FULL)
    kv_grads = jnp.zeros((2 * sequence_length, 2 * head_width), FULL)
    query_low, query_gain_part, input_parts = [], 0.0, []
    for b in blocks:
        grad_attended = contract_last(back[b], wo_whole).astype(LOW)
        low_b, kv_b, gain_b = attend_back(
            spots[b],
            queries[b],
            augs[b],
            grad_attended,
            attended[b],
            query_pre[b],
            cosine,
            sine,
            query_gain_row,
            keys_wide,
            values_wide,
            keys_turned,
            score_scale,
        )
        at = places[b] * row_count
        kv_grads = lax.dynamic_update_slice_in_dim(
            kv_grads, lax.dynamic_slice_in_dim(kv_grads, at, kv_b.shape[0], 0) + kv_b, at, 0
        )
        query_low.append(low_b)
        query_gain_part += gain_b[0]
        input_parts.append(contract_last(low_b, wq_whole))
    returned = lax.ppermute(
        kv_grads[:sequence_length].astype(LOW), "dp", [(i + 1, i) for i in range(0, dp_count, 2)]
    )
    kv_total = kv_grads[sequence_length:] + jnp.where(half_index == 0, returned.astype(FULL), 0.0)

    def key_prep(pre, gain):
        normed = rms_norm(pre, gain)
        return normed * cosine + jnp.roll(normed, head_width // 2, axis=1) * sine

    _, key_back = jax.vjp(key_prep, key_pre, key_gain)
    grad_key_pre, key_gain_part = key_back(kv_total[:, :head_width] * score_scale)
    kv_low = jnp.concatenate([grad_key_pre, kv_total[:, head_width:]], axis=1).astype(LOW)
    kv_spread = lax.all_to_all(
        kv_low.reshape(mp_count, row_count, 2 * head_width),
        "mp",
        split_axis=0,
        concat_axis=0,
        tiled=True,
    )
    grad_normed_one = ring_sum(input_parts)
    for m in blocks:
        cols = kv_offsets[m]
        grad_normed_one += contract_last(
            kv_spread[m, :, :head_width], wkv_whole[:, cols : cols + head_width]
        )
        cols += kv_width
        grad_normed_one += contract_last(
            kv_spread[m, :, head_width:], wkv_whole[:, cols : cols + head_width]
        )
    grad_in_norm, input_gain_part = norm_one_back(grad_normed_one)
    tokens_grad = grad_resid + grad_in_norm

    kv_blocks = [
        lax.dynamic_slice_in_dim(kv_low, places[b] * row_count, row_count, 0) for b in blocks
    ]
    joined = jnp.concatenate([joined_rows(query_low), joined_rows(kv_blocks)], axis=1)
    weight_part = contract_first(joined_rows(sequence), joined).astype(LOW)
    half = (weight_part.shape[1] // 256) * 128
    summed_rows = jnp.concatenate(
        [
            sum_scatter_rows(weight_part[:, :half], bits),
            sum_scatter_rows(weight_part[:, half:], bits[:1] + bits[1:][::-1]),
        ],
        axis=1,
    )
    query_weight_grad = summed_rows[:, :local_width].astype(FULL)
    own_cols = lax.all_gather(summed_rows[:, local_width:], "mp", axis=0).astype(FULL)
    kv_parts = [None] * (2 * kv_width // head_width)
    for m in blocks:
        for side in range(2):
            at = (kv_offsets[m] + side * kv_width) // head_width
            term = own_cols[m, :, side * head_width : (side + 1) * head_width]
            kv_parts[at] = term if kv_parts[at] is None else kv_parts[at] + term
    kv_weight_grad = jnp.concatenate(kv_parts, axis=1)

    gains = jnp.concatenate([moe_gain_part, query_gain_part, key_gain_part, input_gain_part])
    for bit in bits:
        gains += swap(gains, "dp", bit)
    step = 1
    while step < mp_count:
        gains += swap(gains, "mp", step)
        step *= 2
    ends = [model_width, model_width + head_width, model_width + 2 * head_width]
    return (
        block_out,
        tokens_grad,
        gains[ends[2] :],
        query_weight_grad,
        kv_weight_grad,
        gains[ends[0] : ends[1]],
        gains[ends[1] : ends[2]],
        out_weight_grad,
        gains[: ends[0]],
        gate_weight_grad,
        up_weight_grad,
        down_weight_grad,
        gate_values_grad,
    )


def solution(mesh):
    both = ("dp", "mp")
    rows = P(both, None)
    experts = P(both, None, None)
    return jax.shard_map(
        on_device,
        mesh=mesh,
        in_specs=(
            rows,
            P(),
            P("dp", "mp"),
            P("dp", None),
            P(),
            P(),
            P("mp", "dp"),
            P(),
            experts,
            experts,
            experts,
            rows,
            rows,
            P(),
            rows,
        ),
        out_specs=(
            rows,
            rows,
            P(),
            P("dp", "mp"),
            P("dp", None),
            P(),
            P(),
            P("mp", "dp"),
            P(),
            experts,
            experts,
            experts,
            rows,
        ),
        check_vma=False,
    )
```

time: 1960 us -> 1420 us (0.72)
  blocking collectives: 278 us -> 17.9 us
  waiting for transfers between devices: 725 us -> 548 us
  other arithmetic: 222 us -> 85.9 us
  starting transfers between devices: 21.7 us -> 141 us
  Pallas kernels: 0 us -> 111 us
  local copies, waits for them, and re-layouts: 343 us -> 243 us
  matrix products: 334 us -> 248 us
    ppermute x2 -> x133, waiting for transfers between devices: 0.01 us -> 505 us  [the longest x107 391 us: swap(): return lax.ppermute(shard, axis, [(i, i ^ bit) for i in range(length)])]
    all_to_all x3 -> x4, waiting for transfers between devices: 384 us -> 41.3 us  [the longest x1 32.7 us: on_device(): lax.all_to_all(counts.astype(LOW).reshape(dp_count, mp_count, row_count)....]
    all_gather x4 -> x3, waiting for transfers between devices: 259 us -> 0.01 us  [the longest x1 0.01 us: on_device(): lax.all_gather(jnp.concatenate([lax.dynamic_slice_in_dim(key_value_weight...]
    all_to_all x1 -> x0, blocking collectives: 214 us -> none  [route_rows(): lax.all_to_all(buffer, ('dp', 'mp'), split_axis=0, concat_axis=0, tiled=T...]
    ppermute x2 -> x133, starting transfers between devices: 3.54 us -> 124 us  [the longest x107 89 us: swap(): return lax.ppermute(shard, axis, [(i, i ^ bit) for i in range(length)])]
    pallas_call x0 -> x12, Pallas kernels: none -> 111 us  [the longest x4 60.6 us: attend_back(): pl.pallas_call(functools.partial(attend_back_kernel, score_scale), out_sh...]
    gather x2 -> x0, local copies, waits for them, and re-layouts: 101 us -> none  [bring_back(): arrived[targets, slot_index].reshape(row_count, top_count, model_width)]
    slice x6 -> x174, local copies, waits for them, and re-layouts: 6.21 us -> 102 us  [the longest x64 59 us: split_rows(): return [rows[k * size:(k + 1) * size] for k in range(count)]]
  transfers between devices with their start and end apart: 15 -> 142, of which waited for: 6 -> 60; matrix products, arithmetic and copies ran while one was open for 25% -> 39% of each run, Pallas kernels for 0% -> 8%
where the time goes in v1:
time: 1420 us; the launch traced here: 1410 us
  waiting for transfers between devices  548 us (39%)
  matrix products  248 us (17%)
  local copies, waits for them, and re-layouts  243 us (17%)
  starting transfers between devices  141 us (10%)
  Pallas kernels  111 us (8%)
  other arithmetic  85.9 us (6%)
  between operations  19.1 us (1%)
  blocking collectives  17.9 us (1%)
    ppermute x107, waiting for transfers between devices, swap(): return lax.ppermute(shard, axis, [(i, i ^ bit) for i in range(length)])  391 us
    ppermute x24, waiting for transfers between devices, ring_shift(): lax.ppermute(shard, axis, [(i, (i + 1) % length) for i in range(length)])  114 us
    dot_general x41, matrix products, matmul(): return jnp.dot(left, right, preferred_element_type=FULL)  106 us
    ppermute x107, starting transfers between devices, swap(): return lax.ppermute(shard, axis, [(i, i ^ bit) for i in range(length)])  89 us
    unnamed x627, local copies, waits for them, and re-layouts  85 us
    dot_general x28, matrix products, contract_last(): lax.dot_general(left, right, (((1,), (1,)), ((), ())), preferred_element_...  75.6 us
    dot_general x13, matrix products, contract_first(): lax.dot_general(left, right, (((0,), (0,)), ((), ())), preferred_element_...  67 us
    pallas_call x4, Pallas kernels, attend_back(): pl.pallas_call(functools.partial(attend_back_kernel, score_scale), out_sh...  60.6 us
  transfers between devices with their start and end apart: 142, of which 60 were waited for; matrix products, arithmetic and copies ran while one was open for 39% of the time, Pallas kernels for 8%

profile of v1, /device:TPU:0, one launch (start us, length us, event | category | flops | bytes accessed | tf_op | source)
XLA Modules:
  0.0 1414.2 jit_solution(10095995191383536545)
XLA Ops:
  33.6 32.7 %all-to-all-done = bf16[4,8,256]{2,1,0:T(8,128)(2,1)S(1)} async-done(((bf16[4,8,256]{2,1,0:T(8,128)(2,1)}), bf16[4,8,256]{2,1,0:T(8,128)(2,1)S(1)}, u32[]{:S(2)}, u32[]{:S(2)}) %all-to-all-start) | async-done | bytes 16416 | tf_op jit(solution)/shard_map/all_to_all | solution.py:485
  91.8 7.3 collective-permute-done.16
  115.3 16.6 %collective-permute-done.14 = bf16[160,2048]{1,0:T(8,128)(2,1)S(1)} collective-permute-done((bf16[160,2048]{1,0:T(8,128)(2,1)S(1)}, bf16[160,2048]{1,0:T(8,128)(2,1)S(1)}, u32[]{:S(2)}, u32[]{:S(2)}) %collective-permute-start.14) | collective-permute-done | bytes 655392 | tf_op jit(solution)/shard_map/ppermute | solution.py:71
  167.2 6.7 collective-permute-done.68
  178.9 10.0 collective-permute-done.52
  199.4 20.8 %collective-permute-done.27 = bf16[256,2048]{1,0:T(8,128)(2,1)S(1)} collective-permute-done((bf16[256,2048]{1,0:T(8,128)(2,1)}, bf16[256,2048]{1,0:T(8,128)(2,1)S(1)}, u32[]{:S(2)}, u32[]{:S(2)}) %collective-permute-start.27) | collective-permute-done | bytes 1048608 | tf_op jit(solution)/shard_map/ppermute | solution.py:66
  294.4 12.2 collective-permute-start.3
  318.5 8.9 shard_map.253
  333.4 8.8 shard_map.252
  342.2 15.1 %collective-permute-done.4 = bf16[256,2048]{1,0:T(8,128)(2,1)S(1)} collective-permute-done((bf16[256,2048]{1,0:T(8,128)(2,1)S(1)}, bf16[256,2048]{1,0:T(8,128)(2,1)S(1)}, u32[]{:S(2)}, u32[]{:S(2)}) %collective-permute-start.4) | collective-permute-done | bytes 1048608 | tf_op jit(solution)/shard_map/ppermute | solution.py:66
  362.9 8.9 shard_map.251
  375.3 11.0 collective-permute-done.5
  389.5 8.8 shard_map.250
  402.0 9.0 collective-permute-done.6
  417.6 6.9 collective-permute-done.10
  430.0 10.0 collective-permute-done.34
  445.8 7.8 collective-permute-done.76
  459.9 8.6 collective-permute-done.11
  535.1 6.1 fusion.15
  549.3 11.1 collective-permute-done.38
  574.3 5.9 fusion.13
  591.0 6.2 fusion.11
  600.3 6.1 fusion.8
  646.0 6.1 multiply_convert_fusion
  676.2 6.5 multiply_convert_fusion.13
  686.9 9.6 convolution_bitcast_fusion
  699.5 9.8 convolution_bitcast_fusion.1
  724.8 5.5 all-to-all-start.3
  738.5 15.0 %collective-permute-done.20 = bf16[160,2048]{1,0:T(8,128)(2,1)S(1)} collective-permute-done((bf16[160,2048]{1,0:T(8,128)(2,1)S(1)}, bf16[160,2048]{1,0:T(8,128)(2,1)S(1)}, u32[]{:S(2)}, u32[]{:S(2)}) %collective-permute-start.20) | collective-permute-done | bytes 655392 | tf_op jit(solution)/shard_map/ppermute | solution.py:71
  756.0 13.5 collective-permute-done.80
  771.3 13.3 collective-permute-done.62
  786.3 12.4 collective-permute-done.44
  800.4 13.2 collective-permute-done.81
  817.0 14.3 %collective-permute-done.63 = bf16[160,2048]{1,0:T(8,128)(2,1)S(1)} collective-permute-done((bf16[160,2048]{1,0:T(8,128)(2,1)S(1)}, bf16[160,2048]{1,0:T(8,128)(2,1)S(1)}, u32[]{:S(2)}, u32[]{:S(2)}) %collective-permute-start.63) | collective-permute-done | bytes 655392 | tf_op jit(solution)/shard_map/ppermute | solution.py:71
  834.8 24.7 %collective-permute-done.45 = bf16[160,2048]{1,0:T(8,128)(2,1)S(1)} collective-permute-done((bf16[160,2048]{1,0:T(8,128)(2,1)S(1)}, bf16[160,2048]{1,0:T(8,128)(2,1)S(1)}, u32[]{:S(2)}, u32[]{:S(2)}) %collective-permute-start.45) | collective-permute-done | bytes 655392 | tf_op jit(solution)/shard_map/ppermute | solution.py:71
  864.4 6.2 collective-permute-done.83
  873.1 8.8 collective-permute-done.65
  893.2 5.9 collective-permute-done.66
  899.1 11.1 collective-permute-done.85
  915.0 5.6 collective-permute-done.48
  920.7 15.5 %collective-permute-done.86 = bf16[256,2048]{1,0:T(8,128)(2,1)S(1)} collective-permute-done((bf16[256,2048]{1,0:T(8,128)(2,1)S(1)}, bf16[256,2048]{1,0:T(8,128)(2,1)S(1)}, u32[]{:S(2)}, u32[]{:S(2)}) %collective-permute-start.86) | collective-permute-done | bytes 1048608 | tf_op jit(solution)/shard_map/ppermute | solution.py:66
  938.7 13.7 fusion.34
  980.0 15.2 %shard_map.254 = (bf16[256,1024]{1,0:T(8,128)(2,1)}, f32[1280,256]{1,0:T(8,128)}, f32[1,128]{1,0:T(1,128)}) custom-call(s32[1]{0:T(128)} %bitcast.at_ref, bf16[256,1024]{1,0:T(8,128)(2,1)} %get-tuple-element.45.q_ref, bf16[256,1024]{1,0:T(8,128)(2,1)} %get-tuple-element.61.qa_ref, bf16[256,1024]{1,0:T(8,128)(2,1)} %convolution_convert_fusion.24.grad_ref, ...), custom_call_target="tpu_custom_call" | custom-call | flops 5368709120 | bytes 8388608 | tf_op jit(solution)/shard_map/pallas_call | solution.py:371
  1016.7 15.1 %shard_map.257 = (bf16[256,1024]{1,0:T(8,128)(2,1)}, f32[1280,256]{1,0:T(8,128)}, f32[1,128]{1,0:T(1,128)}) custom-call(s32[1]{0:T(128)} %bitcast.7.at_ref, bf16[256,1024]{1,0:T(8,128)(2,1)} %get-tuple-element.55.q_ref, bf16[256,1024]{1,0:T(8,128)(2,1)} %get-tuple-element.67.qa_ref, bf16[256,1024]{1,0:T(8,128)(2,1)} %convolution_convert_fusion.21.grad_ref, ...), custom_call_target="tpu_custom_call" | custom-call | flops 5368709120 | bytes 8388608 | tf_op jit(solution)/shard_map/pallas_call | solution.py:371
  1040.2 13.9 collective-permute-done.101
  1055.5 14.2 %collective-permute-done.95 = bf16[160,2048]{1,0:T(8,128)(2,1)S(1)} collective-permute-done((bf16[160,2048]{1,0:T(8,128)(2,1)S(1)}, bf16[160,2048]{1,0:T(8,128)(2,1)S(1)}, u32[]{:S(2)}, u32[]{:S(2)}) %collective-permute-start.95) | collective-permute-done | bytes 655392 | tf_op jit(solution)/shard_map/ppermute | solution.py:71
  1071.1 13.2 collective-permute-done.89
  1086.7 12.5 collective-permute-done.108
  1103.5 10.6 collective-permute-done.102
  1118.3 7.8 collective-permute-done.96
  1138.1 8.0 collective-permute-done.90
  1156.9 13.2 collective-permute-done.116
  1173.8 15.2 %shard_map.256 = (bf16[256,1024]{1,0:T(8,128)(2,1)}, f32[1280,256]{1,0:T(8,128)}, f32[1,128]{1,0:T(1,128)}) custom-call(s32[1]{0:T(128)} %bitcast.8.at_ref, bf16[256,1024]{1,0:T(8,128)(2,1)} %get-tuple-element.53.q_ref, bf16[256,1024]{1,0:T(8,128)(2,1)} %get-tuple-element.65.qa_ref, bf16[256,1024]{1,0:T(8,128)(2,1)} %convolution_convert_fusion.22.grad_ref, ...), custom_call_target="tpu_custom_call" | custom-call | flops 5368709120 | bytes 8388608 | tf_op jit(solution)/shard_map/pallas_call | solution.py:371
  1204.3 7.8 collective-permute-done.111
  1214.5 8.8 collective-permute-done.105
  1224.9 7.5 collective-permute-done.99
  1238.8 5.7 collective-permute-done.117
  1246.7 15.2 %shard_map.255 = (bf16[256,1024]{1,0:T(8,128)(2,1)}, f32[1280,256]{1,0:T(8,128)}, f32[1,128]{1,0:T(1,128)}) custom-call(s32[1]{0:T(128)} %bitcast.9.at_ref, bf16[256,1024]{1,0:T(8,128)(2,1)} %get-tuple-element.51.q_ref, bf16[256,1024]{1,0:T(8,128)(2,1)} %get-tuple-element.63.qa_ref, bf16[256,1024]{1,0:T(8,128)(2,1)} %convolution_convert_fusion.23.grad_ref, ...), custom_call_target="tpu_custom_call" | custom-call | flops 5368709120 | bytes 8388608 | tf_op jit(solution)/shard_map/pallas_call | solution.py:371
  1269.6 8.1 fusion.31
  1287.3 9.1 convolution_convert_fusion
  1299.1 8.5 all-to-all-done.2
  1328.1 23.1 %collective-permute-done.125 = f32[4352]{0:T(1024)S(1)} collective-permute-done((f32[4352]{0:T(1024)S(1)}, f32[4352]{0:T(1024)S(1)}, u32[]{:S(2)}, u32[]{:S(2)}) %collective-permute-start.125) | collective-permute-done | bytes 17440 | tf_op jit(solution)/shard_map/ppermute | solution.py:71
  1362.5 9.6 collective-permute-done.131
  1381.2 17.9 %all-gather = bf16[1024,256]{1,0:T(8,128)(2,1)S(1)} all-gather(bf16[256,256]{1,0:T(8,128)(2,1)S(1)} %slice.2725), channel_id=2, replica_groups=mesh['dp'=8,'mp'=4] {'mp'}, dimensions={0}, use_global_device_ids=true | all-gather | bytes 655360 | tf_op jit(solution)/shard_map/all_gather | solution.py:726
  (1431 shorter events, 678.9 us)
Async XLA Ops:
  7.2 137.8 %all-gather.8.cloned.1.call-start = ((), (), s32[]{:S(2)}) async-start(), calls=%async_computation.6 | async-start | bytes 1179648 | tf_op jit(solution)/shard_map/all_gather | solution.py:449
  9.0 244.1 %all-gather.6.cloned.1.call-start = ((), (), s32[]{:S(2)}) async-start(), calls=%async_computation.5 | async-start | bytes 4718592 | tf_op jit(solution)/shard_map/all_gather | solution.py:448
  9.8 317.6 %all-gather.10.cloned.1.call-start = ((), (), s32[]{:S(2)}) async-start(), calls=%async_computation.7 | async-start | bytes 4718592 | tf_op jit(solution)/shard_map/all_gather | solution.py:461
  15.1 98.7 %collective-permute-start = (bf16[256,2048]{1,0:T(8,128)(2,1)}, bf16[256,2048]{1,0:T(8,128)(2,1)}, u32[]{:S(2)}, u32[]{:S(2)}) collective-permute-start(bf16[256,2048]{1,0:T(8,128)(2,1)} %fusion.139), channel_id=1, source_target_pairs={{0,1},{1,2},{2,3},{3,0},{4,5},{5,6},{6,7},{7,4},{8,9},{9,10},{10,1... | collective-permute-start | bytes 3145736 | tf_op jit(solution)/shard_map/ppermute | solution.py:66
  19.0 47.3 %all-to-all-start = ((bf16[4,8,256]{2,1,0:T(8,128)(2,1)}), bf16[4,8,256]{2,1,0:T(8,128)(2,1)S(1)}, u32[]{:S(2)}, u32[]{:S(2)}) async-start(bf16[4,8,256]{2,1,0:T(8,128)(2,1)} %bitcast.472), calls=%async_computation | async-start | bytes 32768 | tf_op jit(solution)/shard_map/all_to_all | solution.py:485
  22.9 1276.3 %all-gather.12.cloned.1.call-start = ((), (), s32[]{:S(2)}) async-start(), calls=%async_computation.8 | async-start | bytes 4718592 | tf_op jit(solution)/shard_map/all_gather | solution.py:462
  22.9 83.9 %collective-permute-start.25 = (bf16[256,2048]{1,0:T(8,128)(2,1)}, bf16[256,2048]{1,0:T(8,128)(2,1)}, u32[]{:S(2)}, u32[]{:S(2)}) collective-permute-start(bf16[256,2048]{1,0:T(8,128)(2,1)} %param.29), channel_id=1, source_target_pairs={{0,1},{1,2},{2,3},{3,0},{4,5},{5,6},{6,7},{7,4},{8,9},{9,10},{10,1... | collective-permute-start | bytes 3145736 | tf_op jit(solution)/shard_map/ppermute | solution.py:66
  101.9 54.8 %collective-permute-start.17 = (bf16[128,2048]{1,0:T(8,128)(2,1)}, bf16[128,2048]{1,0:T(8,128)(2,1)}, u32[]{:S(2)}, u32[]{:S(2)}) collective-permute-start(bf16[128,2048]{1,0:T(8,128)(2,1)} %pad_maximum_fusion.39), channel_id=1, source_target_pairs={{0,8},{4,12},{8,0},{12,4},{16,24},{20,28},{24,16},{28,20},{1,9},{5... | collective-permute-start | bytes 1572872 | tf_op jit(solution)/shard_map/ppermute | solution.py:71
  103.1 28.8 %collective-permute-start.14 = (bf16[160,2048]{1,0:T(8,128)(2,1)S(1)}, bf16[160,2048]{1,0:T(8,128)(2,1)S(1)}, u32[]{:S(2)}, u32[]{:S(2)}) collective-permute-start(bf16[160,2048]{1,0:T(8,128)(2,1)S(1)} %pad_maximum_fusion.3), channel_id=1, source_target_pairs={{0,16},{4,20},{8,24},{12,28},{16,0},{20,4},{24,8},{28,12},{1,17},{... | collective-permute-start | bytes 1966088 | tf_op jit(solution)/shard_map/ppermute | solution.py:71
  110.8 30.8 %collective-permute-start.67 = (bf16[160,2048]{1,0:T(8,128)(2,1)S(1)}, bf16[160,2048]{1,0:T(8,128)(2,1)S(1)}, u32[]{:S(2)}, u32[]{:S(2)}) collective-permute-start(bf16[160,2048]{1,0:T(8,128)(2,1)S(1)} %slice.2585), channel_id=1, source_target_pairs={{0,8},{4,12},{8,0},{12,4},{16,24},{20,28},{24,16},{28,20},{1,9},{5... | collective-permute-start | bytes 1966088 | tf_op jit(solution)/shard_map/ppermute | solution.py:71
  112.3 28.3 %collective-permute-start.70 = (bf16[128,2048]{1,0:T(8,128)(2,1)S(1)}, bf16[128,2048]{1,0:T(8,128)(2,1)S(1)}, u32[]{:S(2)}, u32[]{:S(2)}) collective-permute-start(bf16[128,2048]{1,0:T(8,128)(2,1)S(1)} %slice.2596), channel_id=1, source_target_pairs={{0,16},{4,20},{8,24},{12,28},{16,0},{20,4},{24,8},{28,12},{1,17},{... | collective-permute-start | bytes 1572872 | tf_op jit(solution)/shard_map/ppermute | solution.py:71
  113.7 46.5 %collective-permute-start.26 = (bf16[256,2048]{1,0:T(8,128)(2,1)}, bf16[256,2048]{1,0:T(8,128)(2,1)}, u32[]{:S(2)}, u32[]{:S(2)}) collective-permute-start(bf16[256,2048]{1,0:T(8,128)(2,1)} %collective-permute-done.25), channel_id=1, source_target_pairs={{0,1},{1,2},{2,3},{3,0},{4,5},{5,6},{6,7},{7,4},{8,9},{9,10},{10,1... | collective-permute-start | bytes 3145736 | tf_op jit(solution)/shard_map/ppermute | solution.py:66
  131.9 32.9 %collective-permute-start.1 = (bf16[256,2048]{1,0:T(8,128)(2,1)}, bf16[256,2048]{1,0:T(8,128)(2,1)}, u32[]{:S(2)}, u32[]{:S(2)}) collective-permute-start(bf16[256,2048]{1,0:T(8,128)(2,1)} %collective-permute-done), channel_id=1, source_target_pairs={{0,1},{1,2},{2,3},{3,0},{4,5},{5,6},{6,7},{7,4},{8,9},{9,10},{10,1... | collective-permute-start | bytes 3145736 | tf_op jit(solution)/shard_map/ppermute | solution.py:66
  141.6 54.4 %collective-permute-start.71 = (bf16[128,2048]{1,0:T(8,128)(2,1)}, bf16[128,2048]{1,0:T(8,128)(2,1)}, u32[]{:S(2)}, u32[]{:S(2)}) collective-permute-start(bf16[128,2048]{1,0:T(8,128)(2,1)} %pad_maximum_fusion.55), channel_id=1, source_target_pairs={{0,8},{4,12},{8,0},{12,4},{16,24},{20,28},{24,16},{28,20},{1,9},{5... | collective-permute-start | bytes 1572872 | tf_op jit(solution)/shard_map/ppermute | solution.py:71
  174.0 47.4 %collective-permute-start.2 = (bf16[256,2048]{1,0:T(8,128)(2,1)}, bf16[256,2048]{1,0:T(8,128)(2,1)S(1)}, u32[]{:S(2)}, u32[]{:S(2)}) collective-permute-start(bf16[256,2048]{1,0:T(8,128)(2,1)} %collective-permute-done.1), channel_id=1, source_target_pairs={{0,1},{1,2},{2,3},{3,0},{4,5},{5,6},{6,7},{7,4},{8,9},{9,10},{10,1... | collective-permute-start | bytes 3145736 | tf_op jit(solution)/shard_map/ppermute | solution.py:66
  176.3 43.8 %collective-permute-start.27 = (bf16[256,2048]{1,0:T(8,128)(2,1)}, bf16[256,2048]{1,0:T(8,128)(2,1)S(1)}, u32[]{:S(2)}, u32[]{:S(2)}) collective-permute-start(bf16[256,2048]{1,0:T(8,128)(2,1)} %collective-permute-done.26), channel_id=1, source_target_pairs={{0,1},{1,2},{2,3},{3,0},{4,5},{5,6},{6,7},{7,4},{8,9},{9,10},{10,1... | collective-permute-start | bytes 3145736 | tf_op jit(solution)/shard_map/ppermute | solution.py:66
  188.9 54.0 %collective-permute-start.53 = (bf16[128,2048]{1,0:T(8,128)(2,1)S(1)}, bf16[128,2048]{1,0:T(8,128)(2,1)S(1)}, u32[]{:S(2)}, u32[]{:S(2)}) collective-permute-start(bf16[128,2048]{1,0:T(8,128)(2,1)S(1)} %pad_maximum_fusion.49), channel_id=1, source_target_pairs={{0,8},{4,12},{8,0},{12,4},{16,24},{20,28},{24,16},{28,20},{1,9},{5... | collective-permute-start | bytes 1572872 | tf_op jit(solution)/shard_map/ppermute | solution.py:71
  190.9 35.1 %collective-permute-start.50 = (bf16[160,2048]{1,0:T(8,128)(2,1)S(1)}, bf16[160,2048]{1,0:T(8,128)(2,1)S(1)}, u32[]{:S(2)}, u32[]{:S(2)}) collective-permute-start(bf16[160,2048]{1,0:T(8,128)(2,1)S(1)} %pad_maximum_fusion.13), channel_id=1, source_target_pairs={{0,16},{4,20},{8,24},{12,28},{16,0},{20,4},{24,8},{28,12},{1,17},{... | collective-permute-start | bytes 1966088 | tf_op jit(solution)/shard_map/ppermute | solution.py:71
  199.3 28.3 %collective-permute-start.72 = (bf16[128,2048]{1,0:T(8,128)(2,1)S(1)}, bf16[128,2048]{1,0:T(8,128)(2,1)S(1)}, u32[]{:S(2)}, u32[]{:S(2)}) collective-permute-start(bf16[128,2048]{1,0:T(8,128)(2,1)S(1)} %pad_maximum_fusion.56), channel_id=1, source_target_pairs={{0,4},{4,0},{8,12},{12,8},{16,20},{20,16},{24,28},{28,24},{1,5},{5... | collective-permute-start | bytes 1572872 | tf_op jit(solution)/shard_map/ppermute | solution.py:71
  232.9 98.9 %collective-permute-start.32 = (bf16[128,2048]{1,0:T(8,128)(2,1)}, bf16[128,2048]{1,0:T(8,128)(2,1)}, u32[]{:S(2)}, u32[]{:S(2)}) collective-permute-start(bf16[128,2048]{1,0:T(8,128)(2,1)} %pad_maximum_fusion.43), channel_id=1, source_target_pairs={{0,8},{4,12},{8,0},{12,4},{16,24},{20,28},{24,16},{28,20},{1,9},{5... | collective-permute-start | bytes 1572872 | tf_op jit(solution)/shard_map/ppermute | solution.py:71
  251.6 135.1 %collective-permute-start.54 = (bf16[128,2048]{1,0:T(8,128)(2,1)}, bf16[128,2048]{1,0:T(8,128)(2,1)}, u32[]{:S(2)}, u32[]{:S(2)}) collective-permute-start(bf16[128,2048]{1,0:T(8,128)(2,1)} %pad_maximum_fusion.50), channel_id=1, source_target_pairs={{0,4},{4,0},{8,12},{12,8},{16,20},{20,16},{24,28},{28,24},{1,5},{5... | collective-permute-start | bytes 1572872 | tf_op jit(solution)/shard_map/ppermute | solution.py:71
  331.0 26.3 %collective-permute-start.4 = (bf16[256,2048]{1,0:T(8,128)(2,1)S(1)}, bf16[256,2048]{1,0:T(8,128)(2,1)S(1)}, u32[]{:S(2)}, u32[]{:S(2)}) collective-permute-start(bf16[256,2048]{1,0:T(8,128)(2,1)S(1)} %convolution_convert_fusion.20), channel_id=1, source_target_pairs={{0,1},{1,2},{2,3},{3,0},{4,5},{5,6},{6,7},{7,4},{8,9},{9,10},{10,1... | collective-permute-start | bytes 3145736 | tf_op jit(solution)/shard_map/ppermute | solution.py:66
  445.7 27.2 %collective-permute-start.35 = (bf16[256,2048]{1,0:T(8,128)(2,1)S(1)}, bf16[256,2048]{1,0:T(8,128)(2,1)}, u32[]{:S(2)}, u32[]{:S(2)}) collective-permute-start(bf16[256,2048]{1,0:T(8,128)(2,1)S(1)} %collective-permute-done.34), channel_id=1, source_target_pairs={{0,1},{1,2},{2,3},{3,0},{4,5},{5,6},{6,7},{7,4},{8,9},{9,10},{10,1... | collective-permute-start | bytes 3145736 | tf_op jit(solution)/shard_map/ppermute | solution.py:66
  454.4 51.5 %collective-permute-start.77 = (bf16[128,2048]{1,0:T(8,128)(2,1)}, bf16[128,2048]{1,0:T(8,128)(2,1)}, u32[]{:S(2)}, u32[]{:S(2)}) collective-permute-start(bf16[128,2048]{1,0:T(8,128)(2,1)} %pad_maximum_fusion.57), channel_id=1, source_target_pairs={{0,8},{4,12},{8,0},{12,4},{16,24},{20,28},{24,16},{28,20},{1,9},{5... | collective-permute-start | bytes 1572872 | tf_op jit(solution)/shard_map/ppermute | solution.py:71
  457.4 27.7 %collective-permute-start.74 = (bf16[160,2048]{1,0:T(8,128)(2,1)S(1)}, bf16[160,2048]{1,0:T(8,128)(2,1)S(1)}, u32[]{:S(2)}, u32[]{:S(2)}) collective-permute-start(bf16[160,2048]{1,0:T(8,128)(2,1)S(1)} %pad_maximum_fusion.21), channel_id=1, source_target_pairs={{0,16},{4,20},{8,24},{12,28},{16,0},{20,4},{24,8},{28,12},{1,17},{... | collective-permute-start | bytes 1966088 | tf_op jit(solution)/shard_map/ppermute | solution.py:71
  482.2 27.2 %collective-permute-start.36 = (bf16[256,2048]{1,0:T(8,128)(2,1)}, bf16[256,2048]{1,0:T(8,128)(2,1)}, u32[]{:S(2)}, u32[]{:S(2)}) collective-permute-start(bf16[256,2048]{1,0:T(8,128)(2,1)} %collective-permute-done.35), channel_id=1, source_target_pairs={{0,1},{1,2},{2,3},{3,0},{4,5},{5,6},{6,7},{7,4},{8,9},{9,10},{10,1... | collective-permute-start | bytes 3145736 | tf_op jit(solution)/shard_map/ppermute | solution.py:66
  499.4 33.0 %collective-permute-start.59 = (bf16[128,2048]{1,0:T(8,128)(2,1)S(1)}, bf16[128,2048]{1,0:T(8,128)(2,1)S(1)}, u32[]{:S(2)}, u32[]{:S(2)}) collective-permute-start(bf16[128,2048]{1,0:T(8,128)(2,1)S(1)} %pad_maximum_fusion.51), channel_id=1, source_target_pairs={{0,8},{4,12},{8,0},{12,4},{16,24},{20,28},{24,16},{28,20},{1,9},{5... | collective-permute-start | bytes 1572872 | tf_op jit(solution)/shard_map/ppermute | solution.py:71
  514.3 28.5 %collective-permute-start.37 = (bf16[160,2048]{1,0:T(8,128)(2,1)}, bf16[160,2048]{1,0:T(8,128)(2,1)}, u32[]{:S(2)}, u32[]{:S(2)}) collective-permute-start(bf16[160,2048]{1,0:T(8,128)(2,1)} %slice.2467), channel_id=1, source_target_pairs={{0,8},{4,12},{8,0},{12,4},{16,24},{20,28},{24,16},{28,20},{1,9},{5... | collective-permute-start | bytes 1966088 | tf_op jit(solution)/shard_map/ppermute | solution.py:71
  542.3 27.4 %collective-permute-start.41 = (bf16[128,2048]{1,0:T(8,128)(2,1)}, bf16[128,2048]{1,0:T(8,128)(2,1)}, u32[]{:S(2)}, u32[]{:S(2)}) collective-permute-start(bf16[128,2048]{1,0:T(8,128)(2,1)} %pad_maximum_fusion.45), channel_id=1, source_target_pairs={{0,8},{4,12},{8,0},{12,4},{16,24},{20,28},{24,16},{28,20},{1,9},{5... | collective-permute-start | bytes 1572872 | tf_op jit(solution)/shard_map/ppermute | solution.py:71
  696.5 35.1 %collective-permute-start.19 = (bf16[160,2048]{1,0:T(8,128)(2,1)}, bf16[160,2048]{1,0:T(8,128)(2,1)}, u32[]{:S(2)}, u32[]{:S(2)}) collective-permute-start(bf16[160,2048]{1,0:T(8,128)(2,1)} %slice.2419), channel_id=1, source_target_pairs={{0,4},{4,0},{8,12},{12,8},{16,20},{20,16},{24,28},{28,24},{1,5},{5... | collective-permute-start | bytes 1966088 | tf_op jit(solution)/shard_map/ppermute | solution.py:71
  724.8 227.6 %all-to-all-start.3 = ((f32[32,1,256]{2,1,0:T(1,128)}), f32[32,1,256]{2,1,0:T(1,128)}, u32[]{:S(2)}, u32[]{:S(2)}) async-start(f32[32,1,256]{2,1,0:T(1,128)} %all_to_all.23), calls=%async_computation.4 | async-start | bytes 65536 | tf_op jit(solution)/shard_map/all_to_all | solution.py:639
  730.3 675.0 %reduce-scatter.2.cloned.1.call-start = ((), (), s32[]{:S(2)}) async-start(), calls=%async_computation.9 | async-start | bytes 4718592 | tf_op jit(solution)/shard_map/reduce_scatter | solution.py:648
  730.4 141.9 %collective-permute-start.22 = (bf16[128,2048]{1,0:T(8,128)(2,1)}, bf16[128,2048]{1,0:T(8,128)(2,1)S(1)}, u32[]{:S(2)}, u32[]{:S(2)}) collective-permute-start(bf16[128,2048]{1,0:T(8,128)(2,1)} %slice.2430), channel_id=1, source_target_pairs={{0,4},{4,0},{8,12},{12,8},{16,20},{20,16},{24,28},{28,24},{1,5},{5... | collective-permute-start | bytes 1572872 | tf_op jit(solution)/shard_map/ppermute | solution.py:71
  731.0 85.4 %collective-permute-start.82 = (bf16[128,2048]{1,0:T(8,128)(2,1)}, bf16[128,2048]{1,0:T(8,128)(2,1)S(1)}, u32[]{:S(2)}, u32[]{:S(2)}) collective-permute-start(bf16[128,2048]{1,0:T(8,128)(2,1)} %slice.2640), channel_id=1, source_target_pairs={{0,4},{4,0},{8,12},{12,8},{16,20},{20,16},{24,28},{28,24},{1,5},{5... | collective-permute-start | bytes 1572872 | tf_op jit(solution)/shard_map/ppermute | solution.py:71
  731.6 102.5 %collective-permute-start.64 = (bf16[128,2048]{1,0:T(8,128)(2,1)}, bf16[128,2048]{1,0:T(8,128)(2,1)S(1)}, u32[]{:S(2)}, u32[]{:S(2)}) collective-permute-start(bf16[128,2048]{1,0:T(8,128)(2,1)} %slice.2570), channel_id=1, source_target_pairs={{0,4},{4,0},{8,12},{12,8},{16,20},{20,16},{24,28},{28,24},{1,5},{5... | collective-permute-start | bytes 1572872 | tf_op jit(solution)/shard_map/ppermute | solution.py:71
  735.2 125.8 %collective-permute-start.46 = (bf16[128,2048]{1,0:T(8,128)(2,1)S(1)}, bf16[128,2048]{1,0:T(8,128)(2,1)S(1)}, u32[]{:S(2)}, u32[]{:S(2)}) collective-permute-start(bf16[128,2048]{1,0:T(8,128)(2,1)S(1)} %copy-done.122), channel_id=1, source_target_pairs={{0,4},{4,0},{8,12},{12,8},{16,20},{20,16},{24,28},{28,24},{1,5},{5... | collective-permute-start | bytes 1572872 | tf_op jit(solution)/shard_map/ppermute | solution.py:71
  816.4 45.3 %collective-permute-start.21 = (bf16[160,2048]{1,0:T(8,128)(2,1)S(1)}, bf16[160,2048]{1,0:T(8,128)(2,1)S(1)}, u32[]{:S(2)}, u32[]{:S(2)}) collective-permute-start(bf16[160,2048]{1,0:T(8,128)(2,1)S(1)} %pad_maximum_fusion.6), channel_id=1, source_target_pairs={{0,8},{4,12},{8,0},{12,4},{16,24},{20,28},{24,16},{28,20},{1,9},{5... | collective-permute-start | bytes 1966088 | tf_op jit(solution)/shard_map/ppermute | solution.py:71
  831.3 28.1 %collective-permute-start.45 = (bf16[160,2048]{1,0:T(8,128)(2,1)S(1)}, bf16[160,2048]{1,0:T(8,128)(2,1)S(1)}, u32[]{:S(2)}, u32[]{:S(2)}) collective-permute-start(bf16[160,2048]{1,0:T(8,128)(2,1)S(1)} %pad_maximum_fusion.12), channel_id=1, source_target_pairs={{0,8},{4,12},{8,0},{12,4},{16,24},{20,28},{24,16},{28,20},{1,9},{5... | collective-permute-start | bytes 1966088 | tf_op jit(solution)/shard_map/ppermute | solution.py:71
  834.1 36.5 %collective-permute-start.83 = (bf16[128,2048]{1,0:T(8,128)(2,1)S(1)}, bf16[128,2048]{1,0:T(8,128)(2,1)S(1)}, u32[]{:S(2)}, u32[]{:S(2)}) collective-permute-start(bf16[128,2048]{1,0:T(8,128)(2,1)S(1)} %pad_maximum_fusion.59), channel_id=1, source_target_pairs={{0,8},{4,12},{8,0},{12,4},{16,24},{20,28},{24,16},{28,20},{1,9},{5... | collective-permute-start | bytes 1572872 | tf_op jit(solution)/shard_map/ppermute | solution.py:71
  861.2 31.9 %collective-permute-start.47 = (bf16[128,2048]{1,0:T(8,128)(2,1)S(1)}, bf16[128,2048]{1,0:T(8,128)(2,1)S(1)}, u32[]{:S(2)}, u32[]{:S(2)}) collective-permute-start(bf16[128,2048]{1,0:T(8,128)(2,1)S(1)} %pad_maximum_fusion.47), channel_id=1, source_target_pairs={{0,8},{4,12},{8,0},{12,4},{16,24},{20,28},{24,16},{28,20},{1,9},{5... | collective-permute-start | bytes 1572872 | tf_op jit(solution)/shard_map/ppermute | solution.py:71
  914.5 40.7 %collective-permute-start.24 = (bf16[128,2048]{1,0:T(8,128)(2,1)}, bf16[128,2048]{1,0:T(8,128)(2,1)}, u32[]{:S(2)}, u32[]{:S(2)}) collective-permute-start(bf16[128,2048]{1,0:T(8,128)(2,1)} %pad_maximum_fusion.42), channel_id=1, source_target_pairs={{0,16},{4,20},{8,24},{12,28},{16,0},{20,4},{24,8},{28,12},{1,17},{... | collective-permute-start | bytes 1572872 | tf_op jit(solution)/shard_map/ppermute | solution.py:71
  973.1 38.8 %collective-permute-start.115 = (bf16[256,2048]{1,0:T(8,128)(2,1)}, bf16[256,2048]{1,0:T(8,128)(2,1)}, u32[]{:S(2)}, u32[]{:S(2)}) collective-permute-start(bf16[256,2048]{1,0:T(8,128)(2,1)} %fusion.249), channel_id=1, source_target_pairs={{0,1},{1,2},{2,3},{3,0},{4,5},{5,6},{6,7},{7,4},{8,9},{9,10},{10,1... | collective-permute-start | bytes 3145736 | tf_op jit(solution)/shard_map/ppermute | solution.py:66
  975.7 25.9 %collective-permute-start.106 = (bf16[160,2048]{1,0:T(8,128)(2,1)}, bf16[160,2048]{1,0:T(8,128)(2,1)}, u32[]{:S(2)}, u32[]{:S(2)}) collective-permute-start(bf16[160,2048]{1,0:T(8,128)(2,1)} %slice.2280), channel_id=1, source_target_pairs={{0,4},{4,0},{8,12},{12,8},{16,20},{20,16},{24,28},{28,24},{1,5},{5... | collective-permute-start | bytes 1966088 | tf_op jit(solution)/shard_map/ppermute | solution.py:71
  975.7 155.8 %collective-permute-start.109 = (bf16[128,2048]{1,0:T(8,128)(2,1)}, bf16[128,2048]{1,0:T(8,128)(2,1)}, u32[]{:S(2)}, u32[]{:S(2)}) collective-permute-start(bf16[128,2048]{1,0:T(8,128)(2,1)} %slice.2291), channel_id=1, source_target_pairs={{0,4},{4,0},{8,12},{12,8},{16,20},{20,16},{24,28},{28,24},{1,5},{5... | collective-permute-start | bytes 1572872 | tf_op jit(solution)/shard_map/ppermute | solution.py:71
  976.2 27.5 %collective-permute-start.100 = (bf16[160,2048]{1,0:T(8,128)(2,1)}, bf16[160,2048]{1,0:T(8,128)(2,1)}, u32[]{:S(2)}, u32[]{:S(2)}) collective-permute-start(bf16[160,2048]{1,0:T(8,128)(2,1)} %slice.2258), channel_id=1, source_target_pairs={{0,4},{4,0},{8,12},{12,8},{16,20},{20,16},{24,28},{28,24},{1,5},{5... | collective-permute-start | bytes 1966088 | tf_op jit(solution)/shard_map/ppermute | solution.py:71
  976.2 159.5 %collective-permute-start.103 = (bf16[128,2048]{1,0:T(8,128)(2,1)}, bf16[128,2048]{1,0:T(8,128)(2,1)}, u32[]{:S(2)}, u32[]{:S(2)}) collective-permute-start(bf16[128,2048]{1,0:T(8,128)(2,1)} %slice.2269), channel_id=1, source_target_pairs={{0,4},{4,0},{8,12},{12,8},{16,20},{20,16},{24,28},{28,24},{1,5},{5... | collective-permute-start | bytes 1572872 | tf_op jit(solution)/shard_map/ppermute | solution.py:71
  1003.8 146.5 %collective-permute-start.97 = (bf16[128,2048]{1,0:T(8,128)(2,1)}, bf16[128,2048]{1,0:T(8,128)(2,1)}, u32[]{:S(2)}, u32[]{:S(2)}) collective-permute-start(bf16[128,2048]{1,0:T(8,128)(2,1)} %slice.2247), channel_id=1, source_target_pairs={{0,4},{4,0},{8,12},{12,8},{16,20},{20,16},{24,28},{28,24},{1,5},{5... | collective-permute-start | bytes 1572872 | tf_op jit(solution)/shard_map/ppermute | solution.py:71
  1009.8 143.0 %collective-permute-start.91 = (bf16[128,2048]{1,0:T(8,128)(2,1)}, bf16[128,2048]{1,0:T(8,128)(2,1)}, u32[]{:S(2)}, u32[]{:S(2)}) collective-permute-start(bf16[128,2048]{1,0:T(8,128)(2,1)} %slice.2225), channel_id=1, source_target_pairs={{0,4},{4,0},{8,12},{12,8},{16,20},{20,16},{24,28},{28,24},{1,5},{5... | collective-permute-start | bytes 1572872 | tf_op jit(solution)/shard_map/ppermute | solution.py:71
  1126.1 62.8 %collective-permute-start.118 = (bf16[256,2048]{1,0:T(8,128)(2,1)}, bf16[256,2048]{1,0:T(8,128)(2,1)}, u32[]{:S(2)}, u32[]{:S(2)}) collective-permute-start(bf16[256,2048]{1,0:T(8,128)(2,1)} %convolution_convert_fusion.11), channel_id=1, source_target_pairs={{0,1},{1,2},{2,3},{3,0},{4,5},{5,6},{6,7},{7,4},{8,9},{9,10},{10,1... | collective-permute-start | bytes 3145736 | tf_op jit(solution)/shard_map/ppermute | solution.py:66
  1135.8 34.3 %collective-permute-start.116 = (bf16[256,2048]{1,0:T(8,128)(2,1)}, bf16[256,2048]{1,0:T(8,128)(2,1)S(1)}, u32[]{:S(2)}, u32[]{:S(2)}) collective-permute-start(bf16[256,2048]{1,0:T(8,128)(2,1)} %collective-permute-done.115), channel_id=1, source_target_pairs={{0,1},{1,2},{2,3},{3,0},{4,5},{5,6},{6,7},{7,4},{8,9},{9,10},{10,1... | collective-permute-start | bytes 3145736 | tf_op jit(solution)/shard_map/ppermute | solution.py:66
  1146.1 48.8 %collective-permute-start.110 = (bf16[128,2048]{1,0:T(8,128)(2,1)}, bf16[128,2048]{1,0:T(8,128)(2,1)}, u32[]{:S(2)}, u32[]{:S(2)}) collective-permute-start(bf16[128,2048]{1,0:T(8,128)(2,1)} %pad_maximum_fusion.67), channel_id=1, source_target_pairs={{0,8},{4,12},{8,0},{12,4},{16,24},{20,28},{24,16},{28,20},{1,9},{5... | collective-permute-start | bytes 1572872 | tf_op jit(solution)/shard_map/ppermute | solution.py:71
  1150.2 46.9 %collective-permute-start.104 = (bf16[128,2048]{1,0:T(8,128)(2,1)}, bf16[128,2048]{1,0:T(8,128)(2,1)S(1)}, u32[]{:S(2)}, u32[]{:S(2)}) collective-permute-start(bf16[128,2048]{1,0:T(8,128)(2,1)} %pad_maximum_fusion.65), channel_id=1, source_target_pairs={{0,8},{4,12},{8,0},{12,4},{16,24},{20,28},{24,16},{28,20},{1,9},{5... | collective-permute-start | bytes 1572872 | tf_op jit(solution)/shard_map/ppermute | solution.py:71
  1152.8 45.6 %collective-permute-start.98 = (bf16[128,2048]{1,0:T(8,128)(2,1)S(1)}, bf16[128,2048]{1,0:T(8,128)(2,1)}, u32[]{:S(2)}, u32[]{:S(2)}) collective-permute-start(bf16[128,2048]{1,0:T(8,128)(2,1)S(1)} %pad_maximum_fusion.63), channel_id=1, source_target_pairs={{0,8},{4,12},{8,0},{12,4},{16,24},{20,28},{24,16},{28,20},{1,9},{5... | collective-permute-start | bytes 1572872 | tf_op jit(solution)/shard_map/ppermute | solution.py:71
  1170.1 31.9 %collective-permute-start.92 = (bf16[128,2048]{1,0:T(8,128)(2,1)}, bf16[128,2048]{1,0:T(8,128)(2,1)}, u32[]{:S(2)}, u32[]{:S(2)}) collective-permute-start(bf16[128,2048]{1,0:T(8,128)(2,1)} %pad_maximum_fusion.61), channel_id=1, source_target_pairs={{0,8},{4,12},{8,0},{12,4},{16,24},{20,28},{24,16},{28,20},{1,9},{5... | collective-permute-start | bytes 1572872 | tf_op jit(solution)/shard_map/ppermute | solution.py:71
  1194.0 73.2 %collective-permute-start.119 = (bf16[256,2048]{1,0:T(8,128)(2,1)}, bf16[256,2048]{1,0:T(8,128)(2,1)S(1)}, u32[]{:S(2)}, u32[]{:S(2)}) collective-permute-start(bf16[256,2048]{1,0:T(8,128)(2,1)} %add_convert_fusion.5), channel_id=1, source_target_pairs={{0,1},{1,2},{2,3},{3,0},{4,5},{5,6},{6,7},{7,4},{8,9},{9,10},{10,1... | collective-permute-start | bytes 3145736 | tf_op jit(solution)/shard_map/ppermute | solution.py:66
  1195.2 49.4 %collective-permute-start.117 = (bf16[256,2048]{1,0:T(8,128)(2,1)S(1)}, bf16[256,2048]{1,0:T(8,128)(2,1)S(1)}, u32[]{:S(2)}, u32[]{:S(2)}) collective-permute-start(bf16[256,2048]{1,0:T(8,128)(2,1)S(1)} %copy-done.232), channel_id=1, source_target_pairs={{0,1},{1,2},{2,3},{3,0},{4,5},{5,6},{6,7},{7,4},{8,9},{9,10},{10,1... | collective-permute-start | bytes 3145736 | tf_op jit(solution)/shard_map/ppermute | solution.py:66
  1202.0 30.4 %collective-permute-start.99 = (bf16[128,2048]{1,0:T(8,128)(2,1)S(1)}, bf16[128,2048]{1,0:T(8,128)(2,1)S(1)}, u32[]{:S(2)}, u32[]{:S(2)}) collective-permute-start(bf16[128,2048]{1,0:T(8,128)(2,1)S(1)} %pad_maximum_fusion.64), channel_id=1, source_target_pairs={{0,16},{4,20},{8,24},{12,28},{16,0},{20,4},{24,8},{28,12},{1,17},{... | collective-permute-start | bytes 1572872 | tf_op jit(solution)/shard_map/ppermute | solution.py:71
  1212.0 25.9 %collective-permute-start.93 = (bf16[128,2048]{1,0:T(8,128)(2,1)S(1)}, bf16[128,2048]{1,0:T(8,128)(2,1)S(1)}, u32[]{:S(2)}, u32[]{:S(2)}) collective-permute-start(bf16[128,2048]{1,0:T(8,128)(2,1)S(1)} %pad_maximum_fusion.62), channel_id=1, source_target_pairs={{0,16},{4,20},{8,24},{12,28},{16,0},{20,4},{24,8},{28,12},{1,17},{... | collective-permute-start | bytes 1572872 | tf_op jit(solution)/shard_map/ppermute | solution.py:71
  1223.3 101.1 %collective-permute-start.112 = (bf16[256,2048]{1,0:T(8,128)(2,1)}, bf16[256,2048]{1,0:T(8,128)(2,1)}, u32[]{:S(2)}, u32[]{:S(2)}) collective-permute-start(bf16[256,2048]{1,0:T(8,128)(2,1)} %convolution_convert_fusion.9), channel_id=1, source_target_pairs={{0,1},{1,2},{2,3},{3,0},{4,5},{5,6},{6,7},{7,4},{8,9},{9,10},{10,1... | collective-permute-start | bytes 3145736 | tf_op jit(solution)/shard_map/ppermute | solution.py:66
  1268.4 43.4 %collective-permute-start.120 = (bf16[256,2048]{1,0:T(8,128)(2,1)}, bf16[256,2048]{1,0:T(8,128)(2,1)}, u32[]{:S(2)}, u32[]{:S(2)}) collective-permute-start(bf16[256,2048]{1,0:T(8,128)(2,1)} %add_convert_fusion.4), channel_id=1, source_target_pairs={{0,1},{1,2},{2,3},{3,0},{4,5},{5,6},{6,7},{7,4},{8,9},{9,10},{10,1... | collective-permute-start | bytes 3145736 | tf_op jit(solution)/shard_map/ppermute | solution.py:66
  1318.9 38.9 %collective-permute-start.130 = (bf16[2,2,256,640]{3,2,1,0:T(8,128)(2,1)S(1)}, bf16[2,2,256,640]{3,2,1,0:T(8,128)(2,1)S(1)}, u32[]{:S(2)}, u32[]{:S(2)}) collective-permute-start(bf16[2,2,256,640]{3,2,1,0:T(8,128)(2,1)S(1)} %dynamic-slice_bitcast_fusion), channel_id=1, source_target_pairs={{0,4},{4,0},{8,12},{12,8},{16,20},{20,16},{24,28},{28,24},{1,5},{5... | collective-permute-start | bytes 3932168 | tf_op jit(solution)/shard_map/ppermute | solution.py:71
  1320.7 39.0 %collective-permute-start.127 = (bf16[2,2,256,640]{3,2,0,1:T(8,128)(2,1)S(1)}, bf16[2,2,256,640]{3,2,0,1:T(8,128)(2,1)S(1)}, u32[]{:S(2)}, u32[]{:S(2)}) collective-permute-start(bf16[2,2,256,640]{3,2,0,1:T(8,128)(2,1)S(1)} %bitcast.507), channel_id=1, source_target_pairs={{0,4},{4,0},{8,12},{12,8},{16,20},{20,16},{24,28},{28,24},{1,5},{5... | collective-permute-start | bytes 3932168 | tf_op jit(solution)/shard_map/ppermute | solution.py:71
  1326.9 33.8 %collective-permute-start.113 = (bf16[256,2048]{1,0:T(8,128)(2,1)S(1)}, bf16[256,2048]{1,0:T(8,128)(2,1)S(1)}, u32[]{:S(2)}, u32[]{:S(2)}) collective-permute-start(bf16[256,2048]{1,0:T(8,128)(2,1)S(1)} %fusion.135), channel_id=1, source_target_pairs={{0,1},{1,2},{2,3},{3,0},{4,5},{5,6},{6,7},{7,4},{8,9},{9,10},{10,1... | collective-permute-start | bytes 3145736 | tf_op jit(solution)/shard_map/ppermute | solution.py:66
  1362.4 39.1 %collective-permute-start.114 = (bf16[256,2048]{1,0:T(8,128)(2,1)S(1)}, bf16[256,2048]{1,0:T(8,128)(2,1)S(1)}, u32[]{:S(2)}, u32[]{:S(2)}) collective-permute-start(bf16[256,2048]{1,0:T(8,128)(2,1)S(1)} %fusion.134), channel_id=1, source_target_pairs={{0,1},{1,2},{2,3},{3,0},{4,5},{5,6},{6,7},{7,4},{8,9},{9,10},{10,1... | collective-permute-start | bytes 3145736 | tf_op jit(solution)/shard_map/ppermute | solution.py:66
  (362 other events, 4061.8 us)
Sparse Core Ops, SparseCore 0:
  9.9 26.1 all-gather.7
  38.0 36.7 all-gather.5
  76.8 54.7 all-gather.9
  133.4 51.9 all-gather.11
  1277.9 51.4 reduce-scatter.1

commit v2 on v1

--- a/solution.py
+++ b/solution.py
@@ -71,56 +71,16 @@
     return lax.ppermute(shard, axis, [(i, i ^ bit) for i in range(length)])
 
 
-def split_rows(rows, count):
-    size = rows.shape[0] // count
-    return [rows[k * size : (k + 1) * size] for k in range(count)]
-
-
 def joined_rows(pieces):
     return pieces[0] if len(pieces) == 1 else jnp.concatenate(pieces, axis=0)
 
 
-def exchange(rows, order):
-    pieces = [rows]
-    for bit in order:
-        half = pieces[0].shape[0] // 2
-        came = swap(joined_rows([p[half:] for p in pieces]), "dp", bit)
-        pieces = [p[:half] for p in pieces] + split_rows(came, len(pieces))
-    return joined_rows(pieces)
-
-
-def give_back(rows, order):
-    pieces = split_rows(rows, 1 << len(order))
-    for bit in reversed(order):
-        count = len(pieces) // 2
-        came = split_rows(swap(joined_rows(pieces[count:]), "dp", bit), count)
-        pieces = [joined_rows([k, c]) for k, c in zip(pieces[:count], came)]
-    return pieces[0]
-
-
-def by_place(table, me, order):
-    count = len(order)
-    rest = table.shape[1:]
-    table = table.reshape((2,) * count + rest)
-    for axis in range(count):
-        turned = (me >> (count - 1 - axis)) & 1
-        table = jnp.where(turned == 1, jnp.flip(table, axis), table)
-    axes = [count - 1 - (bit.bit_length() - 1) for bit in order]
-    axes += list(range(count, count + len(rest)))
-    return table.transpose(axes).reshape((1 << count,) + rest)
-
-
-def by_index(table, me, order):
-    count = len(order)
-    rest = table.shape[1:]
-    table = table.reshape((2,) * count + rest)
-    axes = [count - 1 - (bit.bit_length() - 1) for bit in order]
-    back = [axes.index(k) for k in range(count)] + list(range(count, count + len(rest)))
-    table = table.transpose(back)
-    for axis in range(count):
-        turned = (me >> (count - 1 - axis)) & 1
-        table = jnp.where(turned == 1, jnp.flip(table, axis), table)
-    return table.reshape((1 << count,) + rest)
+def nought(array):
+    return jnp.minimum(jnp.abs(array[(0,) * array.ndim].astype(FULL)), 0.0)
+
+
+def behind(array, *others):
+    return (array.astype(FULL) + sum(nought(o) for o in others)).astype(array.dtype)
 
 
 def sum_scatter_rows(rows, order):
@@ -464,13 +424,10 @@
     top_count = routes.shape[1]
     routed_mean = row_count * top_count // expert_count
     capacity = max(2, routed_mean + routed_mean // 16)
-    capacity = -(-capacity // 8) * 8
+    group_size = 2
+    groups = [list(range(b, b + group_size)) for b in range(0, mp_count, group_size)]
+    group_rows = group_size * capacity
     bits = [1 << k for k in range(dp_count.bit_length() - 1)]
-    if capacity >= 32:
-        cut = (capacity // 2 + 7) // 8 * 8
-        streams = [(0, cut, bits[1:] + bits[:1]), (cut, capacity, bits[1:][::-1] + bits[:1])]
-    else:
-        streams = [(0, capacity, bits[1:] + bits[:1])]
     routes_turned = routes.T
     gates_turned = gate_values.T
     expert_ids = lax.broadcasted_iota(jnp.int32, (expert_count, row_count), 0)
@@ -493,44 +450,52 @@
         jnp.stack([counts, gate_of], axis=1), ("dp", "mp"), split_axis=0, concat_axis=0, tiled=True
     ).reshape(dp_count, mp_count, 2, row_count)
 
-    def slots(table, low, high):
-        at = lax.broadcasted_iota(jnp.int32, (1, high - low, 1), 1) + low
-        return table[:, None, :] == at.astype(FULL)
-
-    sends = []
-    seen = []
-    row_gates = []
-    for b in blocks:
-        here = lax.dynamic_index_in_dim(plane_counts, places[b], 0, keepdims=False).astype(FULL)
-        there = lax.dynamic_index_in_dim(expert_view, places[b], 1, keepdims=False)
-        picks, finds, weights = [], [], []
-        for low, high, order in streams:
-            hot = slots(by_place(here, dp_place, order), low, high)
-            picks.append(hot.astype(LOW).reshape(dp_count * (high - low), row_count))
-            turned_view = by_place(there, dp_place, order[::-1])
-            hot = slots(turned_view[:, 0], low, high)
-            finds.append(hot)
-            weights.append(
-                jnp.sum(jnp.where(hot, turned_view[:, 1][:, None, :], 0.0), axis=2).reshape(-1, 1)
-            )
-        sends.append(picks)
-        seen.append(finds)
-        row_gates.append(jnp.concatenate(weights, axis=0))
-
-    def dispatch(block, b):
-        arrived = [
-            exchange(matmul(pick, block).astype(LOW), order)
-            for pick, (_, _, order) in zip(sends[b], streams)
-        ]
-        return joined_rows(arrived)
-
-    def combine(rows, b):
-        ends = [dp_count * (high - low) for low, high, _ in streams]
-        came = [
-            give_back(rows[(sum(ends[:n])) : sum(ends[: n + 1])], streams[n][2])
-            for n in range(len(streams))
-        ]
-        return contract_first(joined_rows(sends[b]), joined_rows(came))
+    row_ids = lax.broadcasted_iota(jnp.int32, (dp_count * group_rows, dp_count), 0)
+    widen = (
+        row_ids // group_rows == lax.broadcasted_iota(jnp.int32, row_ids.shape, 1)
+    ).astype(LOW)
+    row_ids = lax.broadcasted_iota(jnp.int32, (dp_count * group_rows, group_size * row_count), 0)
+    token_ids = lax.broadcasted_iota(jnp.int32, row_ids.shape, 1)
+    aim = jnp.where(
+        row_ids % group_rows // capacity == token_ids // row_count, row_ids % capacity, -5
+    ).astype(FULL)
+
+    def hot_rows(table):
+        return matmul(widen, table.astype(LOW)) == aim
+
+    sends, seen, row_gates = [], [], []
+    for group in groups:
+        here = jnp.concatenate(
+            [lax.dynamic_index_in_dim(plane_counts, places[b], 0, keepdims=False) for b in group],
+            axis=1,
+        )
+        there = jnp.concatenate(
+            [lax.dynamic_index_in_dim(expert_view, places[b], 1, keepdims=False) for b in group],
+            axis=2,
+        )
+        sends.append(hot_rows(here).astype(LOW))
+        hot = hot_rows(there[:, 0])
+        seen.append(hot)
+        spread_gates = jnp.dot(
+            widen.astype(FULL), there[:, 1], precision=lax.Precision.HIGHEST
+        )
+        row_gates.append(jnp.sum(jnp.where(hot, spread_gates, 0.0), axis=1, keepdims=True))
+
+    def plane_turn(rows):
+        return lax.all_to_all(
+            rows.reshape(dp_count, group_rows, model_width),
+            "dp",
+            split_axis=0,
+            concat_axis=0,
+            tiled=True,
+        ).reshape(dp_count * group_rows, model_width)
+
+    def dispatch(pieces, g):
+        return plane_turn(matmul(sends[g], joined_rows(pieces)).astype(LOW))
+
+    def place(came, g):
+        sums = contract_first(sends[g], came)
+        return [sums[k * row_count : (k + 1) * row_count] for k in range(group_size)]
 
     seq_lengths = lax.dynamic_index_in_dim(lengths, seq_index, 0, keepdims=False)
     docs_whole, places_whole = doc_layout(seq_lengths, 2 * sequence_length)
@@ -572,39 +537,46 @@
     values_wide = jnp.concatenate([values_pad, jnp.ones_like(values_pad)], axis=1)
     keys_turned = keys_pad.T
 
+    cot_blocks = [cotangent]
+    cot_rows = []
+
     attended, augs, head_parts = [None] * mp_count, [None] * mp_count, [None] * mp_count
     for b in list(range(1, mp_count)) + [0]:
         attended[b], augs[b] = attend(
             spots[b], queries[b], query_aug, keys_wide, values_wide, score_scale, docs
         )
         head_parts[b] = matmul(attended[b], wo_whole)
+        if b > 0:
+            waits = sequence[-1] if b == 1 else keys_wide if b == 2 else attended[b - 2]
+            cot_blocks.append(ring_shift(behind(cot_blocks[-1], waits)))
+    for g, group in enumerate(groups):
+        cot_rows.append(dispatch([cot_blocks[b] for b in group], g))
     resid = resid_in + ring_sum(head_parts)
     normed_two, norm_two_back = jax.vjp(rms_norm, resid, moe_gain)
 
     gate_one, up_one, down_one = gate_weight[0], up_weight[0], down_weight[0]
-    cot_blocks = ring_blocks(cotangent, mp_count)
     normed_blocks = ring_blocks(normed_two.astype(LOW), mp_count)
-    inputs, hiddens, scaled, gate_grads, up_grads, outs, gate_rows = [], [], [], [], [], [], []
-    resid_parts = []
-    cot_rows = [dispatch(cot_blocks[b], b) for b in blocks]
-    for b in blocks:
-        rows_b = dispatch(normed_blocks[b], b)
-        gate_pre = matmul(rows_b, gate_one)
-        up_pre = matmul(rows_b, up_one)
+    inputs, hiddens, scaled, gate_grads, up_grads = [], [], [], [], []
+    resid_parts, came = [], None
+    for g, group in enumerate(groups):
+        rows_g = dispatch([normed_blocks[b] for b in group], g)
+        gate_pre = matmul(rows_g, gate_one)
+        up_pre = matmul(rows_g, up_one)
         sigmoid_gate = jax.nn.sigmoid(gate_pre)
         silu_gate = gate_pre * sigmoid_gate
         hidden = (silu_gate * up_pre).astype(LOW)
-        scaled_b = (row_gates[b] * cot_rows[b].astype(FULL)).astype(LOW)
-        grad_hidden = contract_last(scaled_b, down_one)
+        scaled_g = (row_gates[g] * cot_rows[g].astype(FULL)).astype(LOW)
+        grad_hidden = contract_last(scaled_g, down_one)
         gate_grad = (
             grad_hidden * up_pre * sigmoid_gate * (1.0 + gate_pre * (1.0 - sigmoid_gate))
         ).astype(LOW)
         up_grad = (grad_hidden * silu_gate).astype(LOW)
         grad_in = (contract_last(gate_grad, gate_one) + contract_last(up_grad, up_one)).astype(LOW)
-        resid_parts.append(combine(grad_in, b))
-        inputs.append(rows_b)
+        came = plane_turn(grad_in)
+        resid_parts += place(came, g)
+        inputs.append(rows_g)
         hiddens.append(hidden)
-        scaled.append(scaled_b)
+        scaled.append(scaled_g)
         gate_grads.append(gate_grad)
         up_grads.append(up_grad)
     grad_moe_normed = ring_sum(resid_parts)
@@ -614,20 +586,20 @@
 
     out_parts = []
     gate_grad_parts = []
-    for b in blocks:
-        out_b = matmul(hiddens[b], down_one)
-        dots = jnp.sum(out_b * cot_rows[b].astype(FULL), axis=1, keepdims=True)
-        out_low = (row_gates[b] * out_b).astype(LOW)
-        out_low, _ = lax.optimization_barrier((out_low, grad_moe_normed))
-        out_parts.append(combine(out_low, b))
-        found = 0.0
-        base = 0
-        for (low, high, order), hot in zip(streams, seen[b]):
-            size = dp_count * (high - low)
-            mine = dots[base : base + size].reshape(dp_count, high - low, 1)
-            base += size
-            found += by_index(jnp.sum(jnp.where(hot, mine, 0.0), axis=1), dp_place, order[::-1])
-        gate_grad_parts.append(found)
+    for g, group in enumerate(groups):
+        out_g = matmul(hiddens[g], down_one)
+        dots = jnp.sum(out_g * cot_rows[g].astype(FULL), axis=1, keepdims=True)
+        out_low = (behind(row_gates[g], came) * out_g).astype(LOW)
+        out_parts += [p + nought(back[-1]) for p in place(plane_turn(out_low), g)]
+        found = lax.dot_general(
+            widen.astype(FULL),
+            jnp.where(seen[g], dots, 0.0),
+            (((0,), (0,)), ((), ())),
+            precision=lax.Precision.HIGHEST,
+        )
+        gate_grad_parts += [
+            found[:, k * row_count : (k + 1) * row_count] for k in range(group_size)
+        ]
     block_out = (resid + ring_sum(out_parts)).astype(LOW)
     spread = jnp.stack(
         [
@@ -641,9 +613,10 @@
         [jnp.sum(jnp.where(picked[k], spread, 0.0), axis=0) for k in range(top_count)], axis=1
     )
     inputs_all = joined_rows(inputs)
-    down_weight_grad = contract_first(joined_rows(hiddens), joined_rows(scaled))[None]
-    gate_weight_grad = contract_first(inputs_all, joined_rows(gate_grads))[None]
-    up_weight_grad = contract_first(inputs_all, joined_rows(up_grads))[None]
+    late = nought(grad_in)
+    down_weight_grad = (contract_first(joined_rows(hiddens), joined_rows(scaled)) + late)[None]
+    gate_weight_grad = (contract_first(inputs_all, joined_rows(gate_grads)) + late)[None]
+    up_weight_grad = (contract_first(inputs_all, joined_rows(up_grads)) + late)[None]
 
     out_weight_grad = lax.psum_scatter(
         contract_first(joined_rows(attended), joined_rows(back)).astype(LOW),
@@ -712,18 +685,18 @@
     kv_blocks = [
         lax.dynamic_slice_in_dim(kv_low, places[b] * row_count, row_count, 0) for b in blocks
     ]
-    joined = jnp.concatenate([joined_rows(query_low), joined_rows(kv_blocks)], axis=1)
-    weight_part = contract_first(joined_rows(sequence), joined).astype(LOW)
-    half = (weight_part.shape[1] // 256) * 128
-    summed_rows = jnp.concatenate(
+    sequence_all = joined_rows(sequence)
+    kv_part = contract_first(sequence_all, joined_rows(kv_blocks)).astype(LOW)
+    weight_part = contract_first(sequence_all, joined_rows(query_low)).astype(LOW)
+    half = local_width // 2
+    own_cols = lax.all_gather(sum_scatter_rows(kv_part, bits), "mp", axis=0).astype(FULL)
+    query_weight_grad = jnp.concatenate(
         [
             sum_scatter_rows(weight_part[:, :half], bits),
             sum_scatter_rows(weight_part[:, half:], bits[:1] + bits[1:][::-1]),
         ],
         axis=1,
-    )
-    query_weight_grad = summed_rows[:, :local_width].astype(FULL)
-    own_cols = lax.all_gather(summed_rows[:, local_width:], "mp", axis=0).astype(FULL)
+    ).astype(FULL)
     kv_parts = [None] * (2 * kv_width // head_width)
     for m in blocks:
         for side in range(2):

time: 1420 us -> 1020 us (0.72)
  waiting for transfers between devices: 548 us -> 342 us
  local copies, waits for them, and re-layouts: 243 us -> 76 us
  starting transfers between devices: 141 us -> 82.4 us
  matrix products: 248 us -> 272 us
    ppermute x107 -> x14, waiting for transfers between devices: 391 us -> 27.4 us  [swap(): return lax.ppermute(shard, axis, [(i, i ^ bit) for i in range(length)])]
    ppermute x24, waiting for transfers between devices: 114 us -> 233 us  [ring_shift(): lax.ppermute(shard, axis, [(i, (i + 1) % length) for i in range(length)])]
    slice x165 -> x7, local copies, waits for them, and re-layouts: 96.3 us -> 6.9 us  [the longest x6 5.77 us: nought(): return jnp.minimum(jnp.abs(array[(0,) * array.ndim].astype(FULL)), 0.0)]
    ppermute x107 -> x14, starting transfers between devices: 89 us -> 13.1 us  [swap(): return lax.ppermute(shard, axis, [(i, i ^ bit) for i in range(length)])]
    unnamed x627 -> x312, local copies, waits for them, and re-layouts: 85 us -> 23.5 us
    all_to_all x0 -> x8, waiting for transfers between devices: none -> 53.6 us  [plane_turn(): lax.all_to_all(rows.reshape(dp_count, group_rows, model_width), 'dp', spl...]
    all_to_all x0 -> x8, starting transfers between devices: none -> 38.7 us  [plane_turn(): lax.all_to_all(rows.reshape(dp_count, group_rows, model_width), 'dp', spl...]
    all_to_all x1, waiting for transfers between devices: 32.7 us -> 0.01 us  [on_device(): lax.all_to_all(counts.astype(LOW).reshape(dp_count, mp_count, row_count)....]
  transfers between devices with their start and end apart: 142 -> 57, of which waited for: 60 -> 24; matrix products, arithmetic and copies ran while one was open for 39% -> 42% of each run, Pallas kernels for 8% -> 11%
where the time goes in v2:
time: 1020 us; the launch traced here: 1010 us
  waiting for transfers between devices  342 us (34%)
  matrix products  272 us (27%)
  Pallas kernels  112 us (11%)
  other arithmetic  88.3 us (9%)
  starting transfers between devices  82.4 us (8%)
  local copies, waits for them, and re-layouts  76 us (7%)
  between operations  20.6 us (2%)
  blocking collectives  16.1 us (2%)
    ppermute x24, waiting for transfers between devices, ring_shift(): lax.ppermute(shard, axis, [(i, (i + 1) % length) for i in range(length)])  233 us
    dot_general x27, matrix products, matmul(): return jnp.dot(left, right, preferred_element_type=FULL)  120 us
    dot_general x10, matrix products, contract_first(): lax.dot_general(left, right, (((0,), (0,)), ((), ())), preferred_element_...  80 us
    dot_general x22, matrix products, contract_last(): lax.dot_general(left, right, (((1,), (1,)), ((), ())), preferred_element_...  65.3 us
    pallas_call x4, Pallas kernels, attend_back(): pl.pallas_call(functools.partial(attend_back_kernel, score_scale), out_sh...  60.9 us
    all_to_all x8, waiting for transfers between devices, plane_turn(): lax.all_to_all(rows.reshape(dp_count, group_rows, model_width), 'dp', spl...  53.6 us
    all_to_all x8, starting transfers between devices, plane_turn(): lax.all_to_all(rows.reshape(dp_count, group_rows, model_width), 'dp', spl...  38.7 us
    pallas_call x4, Pallas kernels, attend(): pl.pallas_call(functools.partial(attend_kernel, score_scale, docs), out_s...  35.8 us
  transfers between devices with their start and end apart: 57, of which 24 were waited for; matrix products, arithmetic and copies ran while one was open for 42% of the time, Pallas kernels for 11%

profile of v2, /device:TPU:0, one launch (start us, length us, event | category | flops | bytes accessed | tf_op | source)
XLA Modules:
  0.0 1009.3 jit_solution(10895565113103644489)
XLA Ops:
  13.0 6.3 all-to-all-start
  34.3 18.1 %collective-permute-done = bf16[256,2048]{0,1:T(8,128)(2,1)} collective-permute-done((bf16[256,2048]{0,1:T(8,128)(2,1)}, bf16[256,2048]{0,1:T(8,128)(2,1)}, u32[]{:S(2)}, u32[]{:S(2)}) %collective-permute-start) | collective-permute-done | bytes 1048608 | tf_op jit(solution)/shard_map/ppermute | solution.py:66
  56.4 6.2 all-to-all-start.1
  65.5 13.3 %collective-permute-done.1 = bf16[256,2048]{0,1:T(8,128)(2,1)} collective-permute-done((bf16[256,2048]{0,1:T(8,128)(2,1)}, bf16[256,2048]{0,1:T(8,128)(2,1)}, u32[]{:S(2)}, u32[]{:S(2)}) %collective-permute-start.1) | collective-permute-done | bytes 1048608 | tf_op jit(solution)/shard_map/ppermute | solution.py:66
  89.8 13.4 %collective-permute-done.2 = bf16[256,2048]{0,1:T(8,128)(2,1)} collective-permute-done((bf16[256,2048]{0,1:T(8,128)(2,1)}, bf16[256,2048]{0,1:T(8,128)(2,1)}, u32[]{:S(2)}, u32[]{:S(2)}) %collective-permute-start.2) | collective-permute-done | bytes 1048608 | tf_op jit(solution)/shard_map/ppermute | solution.py:66
  108.8 4.9 fusion.273.query_ref.pre_ref
  147.6 6.3 convolution_convert_fusion
  165.4 8.9 shard_map.253
  174.3 5.0 all-to-all-start.7
  179.3 5.1 convolution_convert_fusion.7
  192.2 9.0 shard_map.252
  201.3 11.3 %collective-permute-done.4 = bf16[256,2048]{0,1:T(8,128)(2,1)} collective-permute-done((bf16[256,2048]{0,1:T(8,128)(2,1)}, bf16[256,2048]{0,1:T(8,128)(2,1)}, u32[]{:S(2)}, u32[]{:S(2)}) %collective-permute-start.4) | collective-permute-done | bytes 1048608 | tf_op jit(solution)/shard_map/ppermute | solution.py:66
  216.7 18.4 %collective-permute-done.8 = bf16[256,2048]{0,1:T(8,128)(2,1)} collective-permute-done((bf16[256,2048]{0,1:T(8,128)(2,1)}, bf16[256,2048]{0,1:T(8,128)(2,1)}, u32[]{:S(2)}, u32[]{:S(2)}) %collective-permute-start.8) | collective-permute-done | bytes 1048608 | tf_op jit(solution)/shard_map/ppermute | solution.py:66
  236.5 8.8 shard_map.251
  249.5 7.9 collective-permute-done.5
  258.6 21.3 %collective-permute-done.9 = bf16[256,2048]{0,1:T(8,128)(2,1)S(1)} collective-permute-done((bf16[256,2048]{0,1:T(8,128)(2,1)S(1)}, bf16[256,2048]{0,1:T(8,128)(2,1)S(1)}, u32[]{:S(2)}, u32[]{:S(2)}) %collective-permute-start.9) | collective-permute-done | bytes 1048608 | tf_op jit(solution)/shard_map/ppermute | solution.py:66
  279.9 5.8 convolution_convert_fusion.3
  285.8 4.8 all-to-all-start.2
  292.9 9.1 shard_map.250
  317.0 19.8 %collective-permute-done.10 = bf16[256,2048]{0,1:T(8,128)(2,1)} collective-permute-done((bf16[256,2048]{0,1:T(8,128)(2,1)}, bf16[256,2048]{0,1:T(8,128)(2,1)}, u32[]{:S(2)}, u32[]{:S(2)}) %collective-permute-start.10) | collective-permute-done | bytes 1048608 | tf_op jit(solution)/shard_map/ppermute | solution.py:66
  336.8 6.3 convolution_convert_fusion.1
  355.4 5.1 multiply_convert_fusion.3
  360.6 19.4 %collective-permute-done.11 = bf16[256,2048]{0,1:T(8,128)(2,1)S(1)} collective-permute-done((bf16[256,2048]{0,1:T(8,128)(2,1)}, bf16[256,2048]{0,1:T(8,128)(2,1)S(1)}, u32[]{:S(2)}, u32[]{:S(2)}) %collective-permute-start.11) | collective-permute-done | bytes 1048608 | tf_op jit(solution)/shard_map/ppermute | solution.py:66
  383.2 5.5 fusion.51
  388.7 17.8 %collective-permute-done.12 = bf16[256,2048]{0,1:T(8,128)(2,1)S(1)} collective-permute-done((bf16[256,2048]{0,1:T(8,128)(2,1)S(1)}, bf16[256,2048]{0,1:T(8,128)(2,1)S(1)}, u32[]{:S(2)}, u32[]{:S(2)}) %collective-permute-start.12) | collective-permute-done | bytes 1048608 | tf_op jit(solution)/shard_map/ppermute | solution.py:66
  411.2 5.0 all-to-all-start.3
  416.2 6.5 fusion.40
  422.8 5.5 fusion.33
  428.3 5.8 multiply_convert_fusion.7
  437.8 5.3 fusion.4
  443.1 25.0 %all-to-all-done.3 = bf16[8,136,2048]{2,1,0:T(8,128)(2,1)} async-done(((bf16[8,136,2048]{2,1,0:T(8,128)(2,1)}), bf16[8,136,2048]{2,1,0:T(8,128)(2,1)}, u32[]{:S(2)}, u32[]{:S(2)}) %all-to-all-start.3) | async-done | bytes 4456480 | tf_op jit(solution)/shard_map/all_to_all | solution.py:485
  472.9 6.5 fusion.37
  479.5 8.5 multiply_convert_fusion.6
  491.7 5.3 convolution_add_fusion.1
  496.9 6.4 copy.357
  503.4 6.6 copy.358
  510.0 14.9 %all-to-all-done.8 = bf16[8,136,2048]{2,1,0:T(8,128)(2,1)} async-done(((bf16[8,136,2048]{2,1,0:T(8,128)(2,1)}), bf16[8,136,2048]{2,1,0:T(8,128)(2,1)}, u32[]{:S(2)}, u32[]{:S(2)}) %all-to-all-start.8) | async-done | bytes 4456480 | tf_op jit(solution)/shard_map/all_to_all | solution.py:485
  529.6 8.0 multiply_convert_fusion.1
  537.7 8.0 multiply_convert_fusion
  547.6 12.2 %add_bitcast_fusion.1 = f32[1,2048,768]{2,1,0:T(8,128)} fusion(bf16[1088,2048]{1,0:T(8,128)(2,1)} %bitcast.50, bf16[1088,2048]{1,0:T(8,128)(2,1)} %bitcast.57, bf16[1088,768]{1,0:T(8,128)(2,1)S(1)} %copy-done.145, bf16[1088,768]{1,0:T(8,128)(2,1)S(1)} %copy-done.143, f32[]{:T(128)} %bitcast.110), kind=kOutput, calls=%fused_computation.21 | convolution fusion | flops 6871187456 | bytes 18546692 | tf_op jit(solution)/shard_map/dot_general | solution.py:61
  559.8 4.8 fusion.282
  567.9 13.7 %all-to-all-done.4 = bf16[8,136,2048]{2,1,0:T(8,128)(2,1)} async-done(((bf16[8,136,2048]{2,1,0:T(8,128)(2,1)}), bf16[8,136,2048]{2,1,0:T(8,128)(2,1)}, u32[]{:S(2)}, u32[]{:S(2)}) %all-to-all-start.4) | async-done | bytes 4456480 | tf_op jit(solution)/shard_map/all_to_all | solution.py:485
  583.5 8.3 multiply_reduce_fusion.1
  593.1 7.8 multiply_reduce_fusion
  605.6 4.9 fusion.283
  615.9 5.2 all-to-all-start.6
  621.1 13.0 %add_bitcast_fusion.2 = f32[1,2048,768]{2,1,0:T(8,128)} fusion(bf16[1088,2048]{1,0:T(8,128)(2,1)} %bitcast.50, bf16[1088,2048]{1,0:T(8,128)(2,1)} %bitcast.57, bf16[1088,768]{1,0:T(8,128)(2,1)} %copy-done.136, bf16[1088,768]{1,0:T(8,128)(2,1)} %copy-done.135, f32[]{:T(128)} %bitcast.110), kind=kOutput, calls=%fused_computation.22 | convolution fusion | flops 6871187456 | bytes 18546692 | tf_op jit(solution)/shard_map/dot_general | solution.py:61
  634.1 7.2 collective-permute-done.14
  642.9 11.4 %add_bitcast_fusion = f32[1,768,2048]{2,1,0:T(8,128)} fusion(bf16[1088,2048]{1,0:T(8,128)(2,1)} %get-tuple-element.163, bf16[1088,2048]{1,0:T(8,128)(2,1)S(1)} %bitcast.371, bf16[1088,768]{1,0:T(8,128)(2,1)S(1)} %copy-done.134, bf16[1088,768]{1,0:T(8,128)(2,1)S(1)} %copy-done.132, f32[]{:T(128)} %bitcast.110), kind=kOutput, calls=%fused_computation.20 | convolution fusion | flops 6871187456 | bytes 18546692 | tf_op jit(solution)/shard_map/dot_general | solution.py:61
  655.0 14.3 %collective-permute-done.15 = bf16[256,2048]{0,1:T(8,128)(2,1)} collective-permute-done((bf16[256,2048]{0,1:T(8,128)(2,1)}, bf16[256,2048]{0,1:T(8,128)(2,1)}, u32[]{:S(2)}, u32[]{:S(2)}) %collective-permute-start.15) | collective-permute-done | bytes 1048608 | tf_op jit(solution)/shard_map/ppermute | solution.py:66
  685.2 15.2 %shard_map.254 = (bf16[256,1024]{1,0:T(8,128)(2,1)}, f32[1280,256]{1,0:T(8,128)}, f32[1,128]{1,0:T(1,128)}) custom-call(s32[1]{0:T(128)} %bitcast.at_ref, bf16[256,1024]{1,0:T(8,128)(2,1)} %get-tuple-element.41.q_ref, bf16[256,1024]{1,0:T(8,128)(2,1)} %get-tuple-element.53.qa_ref, bf16[256,1024]{1,0:T(8,128)(2,1)} %convolution_convert_fusion.11.grad_ref, ...), custom_call_target="tpu_custom_call" | custom-call | flops 5368709120 | bytes 8388608 | tf_op jit(solution)/shard_map/pallas_call | solution.py:331
  707.9 15.1 %shard_map.257 = (bf16[256,1024]{1,0:T(8,128)(2,1)}, f32[1280,256]{1,0:T(8,128)}, f32[1,128]{1,0:T(1,128)}) custom-call(s32[1]{0:T(128)} %bitcast.7.at_ref, bf16[256,1024]{1,0:T(8,128)(2,1)} %get-tuple-element.51.q_ref, bf16[256,1024]{1,0:T(8,128)(2,1)} %get-tuple-element.59.qa_ref, bf16[256,1024]{1,0:T(8,128)(2,1)} %convolution_convert_fusion.8.grad_ref, ...), custom_call_target="tpu_custom_call" | custom-call | flops 5368709120 | bytes 8388608 | tf_op jit(solution)/shard_map/pallas_call | solution.py:331
  728.1 7.7 fusion.281
  735.8 7.5 fusion.284
  743.3 33.4 %collective-permute-done.17 = bf16[256,2048]{0,1:T(8,128)(2,1)} collective-permute-done((bf16[256,2048]{0,1:T(8,128)(2,1)S(1)}, bf16[256,2048]{0,1:T(8,128)(2,1)}, u32[]{:S(2)}, u32[]{:S(2)}) %collective-permute-start.17) | collective-permute-done | bytes 1048608 | tf_op jit(solution)/shard_map/ppermute | solution.py:66
  780.1 15.4 %shard_map.256 = (bf16[256,1024]{1,0:T(8,128)(2,1)}, f32[1280,256]{1,0:T(8,128)}, f32[1,128]{1,0:T(1,128)}) custom-call(s32[1]{0:T(128)} %bitcast.8.at_ref, bf16[256,1024]{1,0:T(8,128)(2,1)} %get-tuple-element.49.q_ref, bf16[256,1024]{1,0:T(8,128)(2,1)} %get-tuple-element.57.qa_ref, bf16[256,1024]{1,0:T(8,128)(2,1)} %convolution_convert_fusion.9.grad_ref, ...), custom_call_target="tpu_custom_call" | custom-call | flops 5368709120 | bytes 8388608 | tf_op jit(solution)/shard_map/pallas_call | solution.py:331
  805.7 15.2 %shard_map.255 = (bf16[256,1024]{1,0:T(8,128)(2,1)}, f32[1280,256]{1,0:T(8,128)}, f32[1,128]{1,0:T(1,128)}) custom-call(s32[1]{0:T(128)} %bitcast.9.at_ref, bf16[256,1024]{1,0:T(8,128)(2,1)} %get-tuple-element.47.q_ref, bf16[256,1024]{1,0:T(8,128)(2,1)} %get-tuple-element.55.qa_ref, bf16[256,1024]{1,0:T(8,128)(2,1)} %convolution_convert_fusion.10.grad_ref, ...), custom_call_target="tpu_custom_call" | custom-call | flops 5368709120 | bytes 8388608 | tf_op jit(solution)/shard_map/pallas_call | solution.py:331
  825.2 6.7 convolution_convert_fusion.4
  849.8 8.2 fusion.15
  859.5 4.8 all-to-all-start.10
  874.8 26.5 %all-to-all-done.10 = bf16[4,256,256]{2,1,0:T(8,128)(2,1)} async-done(((bf16[4,256,256]{2,1,0:T(8,128)(2,1)}), bf16[4,256,256]{2,1,0:T(8,128)(2,1)}, u32[]{:S(2)}, u32[]{:S(2)}) %all-to-all-start.10) | async-done | bytes 524320 | tf_op jit(solution)/shard_map/all_to_all | solution.py:665
  924.9 20.1 %collective-permute-done.29 = f32[4352]{0:T(1024)S(1)} collective-permute-done((f32[4352]{0:T(1024)S(1)}, f32[4352]{0:T(1024)S(1)}, u32[]{:S(2)}, u32[]{:S(2)}) %collective-permute-start.29) | collective-permute-done | bytes 17440 | tf_op jit(solution)/shard_map/ppermute | solution.py:71
  953.1 16.1 %all-gather = bf16[1024,256]{1,0:T(8,128)(2,1)S(1)} all-gather(bf16[256,256]{1,0:T(8,128)(2,1)S(1)} %fusion.167), channel_id=2, replica_groups=mesh['dp'=8,'mp'=4] {'mp'}, dimensions={0}, use_global_device_ids=true | all-gather | bytes 655360 | tf_op jit(solution)/shard_map/all_gather | solution.py:692
  983.2 13.5 %collective-permute-done.21 = bf16[256,2048]{0,1:T(8,128)(2,1)S(1)} collective-permute-done((bf16[256,2048]{0,1:T(8,128)(2,1)S(1)}, bf16[256,2048]{0,1:T(8,128)(2,1)S(1)}, u32[]{:S(2)}, u32[]{:S(2)}) %collective-permute-start.21) | collective-permute-done | bytes 1048608 | tf_op jit(solution)/shard_map/ppermute | solution.py:66
  (601 shorter events, 305.4 us)
Async XLA Ops:
  7.2 376.0 %copy-start = (bf16[1,768,2048]{2,1,0:T(8,128)(2,1)S(1)}, bf16[1,768,2048]{2,1,0:T(8,128)(2,1)}, u32[]{:S(2)}) copy-start(bf16[1,768,2048]{2,1,0:T(8,128)(2,1)} %param.25) | copy-start | bytes 9437188
  7.2 74.5 %all-gather.8.cloned.1.call-start = ((), (), s32[]{:S(2)}) async-start(), calls=%async_computation.14 | async-start | bytes 1179648 | tf_op jit(solution)/shard_map/all_gather | solution.py:409
  9.0 99.8 %all-gather.6.cloned.1.call-start = ((), (), s32[]{:S(2)}) async-start(), calls=%async_computation.13 | async-start | bytes 4718592 | tf_op jit(solution)/shard_map/all_gather | solution.py:408
  9.8 169.5 %all-gather.10.cloned.1.call-start = ((), (), s32[]{:S(2)}) async-start(), calls=%async_computation.15 | async-start | bytes 4718592 | tf_op jit(solution)/shard_map/all_gather | solution.py:421
  10.5 864.3 %all-gather.12.cloned.1.call-start = ((), (), s32[]{:S(2)}) async-start(), calls=%async_computation.16 | async-start | bytes 4718592 | tf_op jit(solution)/shard_map/all_gather | solution.py:422
  13.0 43.4 %all-to-all-start = ((bf16[4,8,256]{2,1,0:T(8,128)(2,1)}), bf16[4,8,256]{2,1,0:T(8,128)(2,1)S(1)}, u32[]{:S(2)}, u32[]{:S(2)}) async-start(bf16[4,8,256]{2,1,0:T(8,128)(2,1)} %bitcast.357), calls=%async_computation | async-start | bytes 32768 | tf_op jit(solution)/shard_map/all_to_all | solution.py:442
  25.7 26.7 %collective-permute-start = (bf16[256,2048]{0,1:T(8,128)(2,1)}, bf16[256,2048]{0,1:T(8,128)(2,1)}, u32[]{:S(2)}, u32[]{:S(2)}) collective-permute-start(bf16[256,2048]{0,1:T(8,128)(2,1)} %fusion.63), channel_id=1, source_target_pairs={{0,1},{1,2},{2,3},{3,0},{4,5},{5,6},{6,7},{7,4},{8,9},{9,10},{10,1... | collective-permute-start | bytes 3145736 | tf_op jit(solution)/shard_map/ppermute | solution.py:66
  27.8 51.0 %copy-start.88 = (s32[512]{0:T(512)}, s32[512]{0:T(512)S(1)}, u32[]{:S(2)}) copy-start(s32[512]{0:T(512)S(1)} %get-tuple-element.245) | copy-start | bytes 6148
  27.8 51.0 %copy-start.90 = (s32[512]{0:T(512)}, s32[512]{0:T(512)S(1)}, u32[]{:S(2)}) copy-start(s32[512]{0:T(512)S(1)} %get-tuple-element.246) | copy-start | bytes 6148
  27.8 51.0 %copy-start.85 = (pred[1088]{0:T(1024)(128)(4,1)}, pred[1088]{0:T(1024)(128)(4,1)S(1)}, u32[]{:S(2)}) copy-start(pred[1088]{0:T(1024)(128)(4,1)S(1)} %get-tuple-element.237) | copy-start | bytes 3268
  27.8 51.0 %copy-start.92 = (pred[1088]{0:T(1024)(128)(4,1)}, pred[1088]{0:T(1024)(128)(4,1)S(1)}, u32[]{:S(2)}) copy-start(pred[1088]{0:T(1024)(128)(4,1)S(1)} %get-tuple-element.236) | copy-start | bytes 3268
  28.3 285.4 %copy-start.73 = (s32[1088]{0:T(1024)}, s32[1088]{0:T(1024)S(1)}, u32[]{:S(2)}) copy-start(s32[1088]{0:T(1024)S(1)} %broadcast_add_fusion.2) | copy-start | bytes 13060
  28.4 285.4 %copy-start.75 = (s32[1088]{0:T(1024)}, s32[1088]{0:T(1024)S(1)}, u32[]{:S(2)}) copy-start(s32[1088]{0:T(1024)S(1)} %get-tuple-element.241) | copy-start | bytes 13060
  52.4 26.4 %collective-permute-start.1 = (bf16[256,2048]{0,1:T(8,128)(2,1)}, bf16[256,2048]{0,1:T(8,128)(2,1)}, u32[]{:S(2)}, u32[]{:S(2)}) collective-permute-start(bf16[256,2048]{0,1:T(8,128)(2,1)} %collective-permute-done), channel_id=1, source_target_pairs={{0,1},{1,2},{2,3},{3,0},{4,5},{5,6},{6,7},{7,4},{8,9},{9,10},{10,1... | collective-permute-start | bytes 3145736 | tf_op jit(solution)/shard_map/ppermute | solution.py:66
  56.4 117.9 %all-to-all-start.1 = ((f32[32,2,256]{2,1,0:T(2,128)}), f32[32,2,256]{2,1,0:T(2,128)}, u32[]{:S(2)}, u32[]{:S(2)}) async-start(f32[32,2,256]{2,1,0:T(2,128)} %copy.350), calls=%async_computation.1 | async-start | bytes 131072 | tf_op jit(solution)/shard_map/all_to_all | solution.py:449
  78.8 24.4 %collective-permute-start.2 = (bf16[256,2048]{0,1:T(8,128)(2,1)}, bf16[256,2048]{0,1:T(8,128)(2,1)}, u32[]{:S(2)}, u32[]{:S(2)}) collective-permute-start(bf16[256,2048]{0,1:T(8,128)(2,1)} %collective-permute-done.1), channel_id=1, source_target_pairs={{0,1},{1,2},{2,3},{3,0},{4,5},{5,6},{6,7},{7,4},{8,9},{9,10},{10,1... | collective-permute-start | bytes 3145736 | tf_op jit(solution)/shard_map/ppermute | solution.py:66
  106.2 41.4 %collective-permute-start.7 = (bf16[256,2048]{0,1:T(8,128)(2,1)}, bf16[256,2048]{0,1:T(8,128)(2,1)}, u32[]{:S(2)}, u32[]{:S(2)}) collective-permute-start(bf16[256,2048]{0,1:T(8,128)(2,1)} %fusion.65), channel_id=1, source_target_pairs={{0,1},{1,2},{2,3},{3,0},{4,5},{5,6},{6,7},{7,4},{8,9},{9,10},{10,1... | collective-permute-start | bytes 3145736 | tf_op jit(solution)/shard_map/ppermute | solution.py:66
  146.3 7.7 collective-permute-start.3
  174.3 111.4 %all-to-all-start.7 = ((bf16[8,136,2048]{2,1,0:T(8,128)(2,1)}), bf16[8,136,2048]{2,1,0:T(8,128)(2,1)}, u32[]{:S(2)}, u32[]{:S(2)}) async-start(bf16[8,136,2048]{2,1,0:T(8,128)(2,1)} %bitcast.372), calls=%async_computation.7 | async-start | bytes 8912896 | tf_op jit(solution)/shard_map/all_to_all | solution.py:485
  184.4 28.2 %collective-permute-start.4 = (bf16[256,2048]{0,1:T(8,128)(2,1)}, bf16[256,2048]{0,1:T(8,128)(2,1)}, u32[]{:S(2)}, u32[]{:S(2)}) collective-permute-start(bf16[256,2048]{0,1:T(8,128)(2,1)} %convolution_convert_fusion.7), channel_id=1, source_target_pairs={{0,1},{1,2},{2,3},{3,0},{4,5},{5,6},{6,7},{7,4},{8,9},{9,10},{10,1... | collective-permute-start | bytes 3145736 | tf_op jit(solution)/shard_map/ppermute | solution.py:66
  186.8 48.2 %collective-permute-start.8 = (bf16[256,2048]{0,1:T(8,128)(2,1)}, bf16[256,2048]{0,1:T(8,128)(2,1)}, u32[]{:S(2)}, u32[]{:S(2)}) collective-permute-start(bf16[256,2048]{0,1:T(8,128)(2,1)} %add_convert_fusion.3), channel_id=1, source_target_pairs={{0,1},{1,2},{2,3},{3,0},{4,5},{5,6},{6,7},{7,4},{8,9},{9,10},{10,1... | collective-permute-start | bytes 3145736 | tf_op jit(solution)/shard_map/ppermute | solution.py:66
  216.7 40.7 %collective-permute-start.5 = (bf16[256,2048]{0,1:T(8,128)(2,1)}, bf16[256,2048]{0,1:T(8,128)(2,1)S(1)}, u32[]{:S(2)}, u32[]{:S(2)}) collective-permute-start(bf16[256,2048]{0,1:T(8,128)(2,1)} %add_convert_fusion.5), channel_id=1, source_target_pairs={{0,1},{1,2},{2,3},{3,0},{4,5},{5,6},{6,7},{7,4},{8,9},{9,10},{10,1... | collective-permute-start | bytes 3145736 | tf_op jit(solution)/shard_map/ppermute | solution.py:66
  236.4 43.4 %collective-permute-start.9 = (bf16[256,2048]{0,1:T(8,128)(2,1)S(1)}, bf16[256,2048]{0,1:T(8,128)(2,1)S(1)}, u32[]{:S(2)}, u32[]{:S(2)}) collective-permute-start(bf16[256,2048]{0,1:T(8,128)(2,1)S(1)} %add_convert_fusion.2), channel_id=1, source_target_pairs={{0,1},{1,2},{2,3},{3,0},{4,5},{5,6},{6,7},{7,4},{8,9},{9,10},{10,1... | collective-permute-start | bytes 3145736 | tf_op jit(solution)/shard_map/ppermute | solution.py:66
  258.6 46.2 %collective-permute-start.6 = (bf16[256,2048]{0,1:T(8,128)(2,1)}, bf16[256,2048]{0,1:T(8,128)(2,1)}, u32[]{:S(2)}, u32[]{:S(2)}) collective-permute-start(bf16[256,2048]{0,1:T(8,128)(2,1)} %add_convert_fusion.4), channel_id=1, source_target_pairs={{0,1},{1,2},{2,3},{3,0},{4,5},{5,6},{6,7},{7,4},{8,9},{9,10},{10,1... | collective-permute-start | bytes 3145736 | tf_op jit(solution)/shard_map/ppermute | solution.py:66
  285.8 57.4 %all-to-all-start.2 = ((bf16[8,136,2048]{2,1,0:T(8,128)(2,1)}), bf16[8,136,2048]{2,1,0:T(8,128)(2,1)}, u32[]{:S(2)}, u32[]{:S(2)}) async-start(bf16[8,136,2048]{2,1,0:T(8,128)(2,1)} %bitcast.373), calls=%async_computation.2 | async-start | bytes 8912896 | tf_op jit(solution)/shard_map/all_to_all | solution.py:485
  309.2 27.6 %collective-permute-start.10 = (bf16[256,2048]{0,1:T(8,128)(2,1)}, bf16[256,2048]{0,1:T(8,128)(2,1)}, u32[]{:S(2)}, u32[]{:S(2)}) collective-permute-start(bf16[256,2048]{0,1:T(8,128)(2,1)} %multiply_convert_fusion.12), channel_id=1, source_target_pairs={{0,1},{1,2},{2,3},{3,0},{4,5},{5,6},{6,7},{7,4},{8,9},{9,10},{10,1... | collective-permute-start | bytes 3145736 | tf_op jit(solution)/shard_map/ppermute | solution.py:66
  343.1 68.1 %all-to-all-start.5 = ((bf16[8,136,2048]{2,1,0:T(8,128)(2,1)}), bf16[8,136,2048]{2,1,0:T(8,128)(2,1)}, u32[]{:S(2)}, u32[]{:S(2)}) async-start(bf16[8,136,2048]{2,1,0:T(8,128)(2,1)} %bitcast.374), calls=%async_computation.5 | async-start | bytes 8912896 | tf_op jit(solution)/shard_map/all_to_all | solution.py:485
  352.5 27.5 %collective-permute-start.11 = (bf16[256,2048]{0,1:T(8,128)(2,1)}, bf16[256,2048]{0,1:T(8,128)(2,1)S(1)}, u32[]{:S(2)}, u32[]{:S(2)}) collective-permute-start(bf16[256,2048]{0,1:T(8,128)(2,1)} %collective-permute-done.10), channel_id=1, source_target_pairs={{0,1},{1,2},{2,3},{3,0},{4,5},{5,6},{6,7},{7,4},{8,9},{9,10},{10,1... | collective-permute-start | bytes 3145736 | tf_op jit(solution)/shard_map/ppermute | solution.py:66
  380.0 26.6 %collective-permute-start.12 = (bf16[256,2048]{0,1:T(8,128)(2,1)S(1)}, bf16[256,2048]{0,1:T(8,128)(2,1)S(1)}, u32[]{:S(2)}, u32[]{:S(2)}) collective-permute-start(bf16[256,2048]{0,1:T(8,128)(2,1)S(1)} %collective-permute-done.11), channel_id=1, source_target_pairs={{0,1},{1,2},{2,3},{3,0},{4,5},{5,6},{6,7},{7,4},{8,9},{9,10},{10,1... | collective-permute-start | bytes 3145736 | tf_op jit(solution)/shard_map/ppermute | solution.py:66
  411.2 56.9 %all-to-all-start.3 = ((bf16[8,136,2048]{2,1,0:T(8,128)(2,1)}), bf16[8,136,2048]{2,1,0:T(8,128)(2,1)}, u32[]{:S(2)}, u32[]{:S(2)}) async-start(bf16[8,136,2048]{2,1,0:T(8,128)(2,1)} %bitcast.375), calls=%async_computation.3 | async-start | bytes 8912896 | tf_op jit(solution)/shard_map/all_to_all | solution.py:485
  468.1 56.7 %all-to-all-start.8 = ((bf16[8,136,2048]{2,1,0:T(8,128)(2,1)}), bf16[8,136,2048]{2,1,0:T(8,128)(2,1)}, u32[]{:S(2)}, u32[]{:S(2)}) async-start(bf16[8,136,2048]{2,1,0:T(8,128)(2,1)} %bitcast.376), calls=%async_computation.8 | async-start | bytes 8912896 | tf_op jit(solution)/shard_map/all_to_all | solution.py:485
  524.8 56.8 %all-to-all-start.4 = ((bf16[8,136,2048]{2,1,0:T(8,128)(2,1)}), bf16[8,136,2048]{2,1,0:T(8,128)(2,1)}, u32[]{:S(2)}, u32[]{:S(2)}) async-start(bf16[8,136,2048]{2,1,0:T(8,128)(2,1)} %bitcast.358), calls=%async_computation.4 | async-start | bytes 8912896 | tf_op jit(solution)/shard_map/all_to_all | solution.py:485
  567.7 42.9 %collective-permute-start.13 = (bf16[256,2048]{0,1:T(8,128)(2,1)}, bf16[256,2048]{0,1:T(8,128)(2,1)}, u32[]{:S(2)}, u32[]{:S(2)}) collective-permute-start(bf16[256,2048]{0,1:T(8,128)(2,1)} %slice.585), channel_id=1, source_target_pairs={{0,1},{1,2},{2,3},{3,0},{4,5},{5,6},{6,7},{7,4},{8,9},{9,10},{10,1... | collective-permute-start | bytes 3145736 | tf_op jit(solution)/shard_map/ppermute | solution.py:66
  603.0 12.9 %all-to-all-start.11 = ((f32[32,1,256]{2,1,0:T(1,128)}), f32[32,1,256]{2,1,0:T(1,128)S(1)}, u32[]{:S(2)}, u32[]{:S(2)}) async-start(f32[32,1,256]{2,1,0:T(1,128)} %all_to_all.55), calls=%async_computation.12 | async-start | bytes 65536 | tf_op jit(solution)/shard_map/all_to_all | solution.py:611
  614.2 27.1 %collective-permute-start.14 = (bf16[256,2048]{0,1:T(8,128)(2,1)S(1)}, bf16[256,2048]{0,1:T(8,128)(2,1)S(1)}, u32[]{:S(2)}, u32[]{:S(2)}) collective-permute-start(bf16[256,2048]{0,1:T(8,128)(2,1)S(1)} %fusion.74), channel_id=1, source_target_pairs={{0,1},{1,2},{2,3},{3,0},{4,5},{5,6},{6,7},{7,4},{8,9},{9,10},{10,1... | collective-permute-start | bytes 3145736 | tf_op jit(solution)/shard_map/ppermute | solution.py:66
  615.9 59.9 %all-to-all-start.6 = ((bf16[8,136,2048]{2,1,0:T(8,128)(2,1)}), bf16[8,136,2048]{2,1,0:T(8,128)(2,1)}, u32[]{:S(2)}, u32[]{:S(2)}) async-start(bf16[8,136,2048]{2,1,0:T(8,128)(2,1)} %bitcast.369), calls=%async_computation.6 | async-start | bytes 8912896 | tf_op jit(solution)/shard_map/all_to_all | solution.py:485
  642.8 26.6 %collective-permute-start.15 = (bf16[256,2048]{0,1:T(8,128)(2,1)}, bf16[256,2048]{0,1:T(8,128)(2,1)}, u32[]{:S(2)}, u32[]{:S(2)}) collective-permute-start(bf16[256,2048]{0,1:T(8,128)(2,1)} %fusion.75), channel_id=1, source_target_pairs={{0,1},{1,2},{2,3},{3,0},{4,5},{5,6},{6,7},{7,4},{8,9},{9,10},{10,1... | collective-permute-start | bytes 3145736 | tf_op jit(solution)/shard_map/ppermute | solution.py:66
  675.8 30.0 %collective-permute-start.16 = (bf16[256,2048]{0,1:T(8,128)(2,1)}, bf16[256,2048]{0,1:T(8,128)(2,1)S(1)}, u32[]{:S(2)}, u32[]{:S(2)}) collective-permute-start(bf16[256,2048]{0,1:T(8,128)(2,1)} %get-tuple-element.166), channel_id=1, source_target_pairs={{0,1},{1,2},{2,3},{3,0},{4,5},{5,6},{6,7},{7,4},{8,9},{9,10},{10,1... | collective-permute-start | bytes 3145736 | tf_op jit(solution)/shard_map/ppermute | solution.py:66
  675.8 60.0 %all-to-all-start.9 = ((bf16[8,136,2048]{2,1,0:T(8,128)(2,1)}), bf16[8,136,2048]{2,1,0:T(8,128)(2,1)}, u32[]{:S(2)}, u32[]{:S(2)}) async-start(bf16[8,136,2048]{2,1,0:T(8,128)(2,1)} %bitcast.368), calls=%async_computation.9 | async-start | bytes 8912896 | tf_op jit(solution)/shard_map/all_to_all | solution.py:485
  680.4 320.1 %reduce-scatter.2.cloned.1.call-start = ((), (), s32[]{:S(2)}) async-start(), calls=%async_computation.17 | async-start | bytes 4718592 | tf_op jit(solution)/shard_map/reduce_scatter | solution.py:621
  726.4 69.0 %collective-permute-start.22 = (bf16[256,2048]{0,1:T(8,128)(2,1)}, bf16[256,2048]{0,1:T(8,128)(2,1)}, u32[]{:S(2)}, u32[]{:S(2)}) collective-permute-start(bf16[256,2048]{0,1:T(8,128)(2,1)} %convolution_convert_fusion.6), channel_id=1, source_target_pairs={{0,1},{1,2},{2,3},{3,0},{4,5},{5,6},{6,7},{7,4},{8,9},{9,10},{10,1... | collective-permute-start | bytes 3145736 | tf_op jit(solution)/shard_map/ppermute | solution.py:66
  726.4 50.3 %collective-permute-start.17 = (bf16[256,2048]{0,1:T(8,128)(2,1)S(1)}, bf16[256,2048]{0,1:T(8,128)(2,1)}, u32[]{:S(2)}, u32[]{:S(2)}) collective-permute-start(bf16[256,2048]{0,1:T(8,128)(2,1)S(1)} %collective-permute-done.16), channel_id=1, source_target_pairs={{0,1},{1,2},{2,3},{3,0},{4,5},{5,6},{6,7},{7,4},{8,9},{9,10},{10,1... | collective-permute-start | bytes 3145736 | tf_op jit(solution)/shard_map/ppermute | solution.py:66
  776.7 26.9 %collective-permute-start.18 = (bf16[256,2048]{0,1:T(8,128)(2,1)}, bf16[256,2048]{0,1:T(8,128)(2,1)S(1)}, u32[]{:S(2)}, u32[]{:S(2)}) collective-permute-start(bf16[256,2048]{0,1:T(8,128)(2,1)} %collective-permute-done.17), channel_id=1, source_target_pairs={{0,1},{1,2},{2,3},{3,0},{4,5},{5,6},{6,7},{7,4},{8,9},{9,10},{10,1... | collective-permute-start | bytes 3145736 | tf_op jit(solution)/shard_map/ppermute | solution.py:66
  799.3 39.0 %collective-permute-start.23 = (bf16[256,2048]{0,1:T(8,128)(2,1)}, bf16[256,2048]{0,1:T(8,128)(2,1)S(1)}, u32[]{:S(2)}, u32[]{:S(2)}) collective-permute-start(bf16[256,2048]{0,1:T(8,128)(2,1)} %add_convert_fusion.1), channel_id=1, source_target_pairs={{0,1},{1,2},{2,3},{3,0},{4,5},{5,6},{6,7},{7,4},{8,9},{9,10},{10,1... | collective-permute-start | bytes 3145736 | tf_op jit(solution)/shard_map/ppermute | solution.py:66
  823.9 18.7 %collective-permute-start.25 = (bf16[1024,256]{1,0:T(8,128)(2,1)S(1)}, bf16[1024,256]{1,0:T(8,128)(2,1)S(1)}, u32[]{:S(2)}, u32[]{:S(2)}) collective-permute-start(bf16[1024,256]{1,0:T(8,128)(2,1)S(1)} %slice.586), channel_id=1, source_target_pairs={{4,0},{12,8},{20,16},{28,24},{5,1},{13,9},{21,17},{29,25},{6,2},{1... | collective-permute-start | bytes 1572872 | tf_op jit(solution)/shard_map/ppermute | solution.py:653
  834.6 32.9 %collective-permute-start.31 = (bf16[2,2,256,512]{3,2,0,1:T(8,128)(2,1)}, bf16[2,2,256,512]{3,2,0,1:T(8,128)(2,1)}, u32[]{:S(2)}, u32[]{:S(2)}) collective-permute-start(bf16[2,2,256,512]{3,2,0,1:T(8,128)(2,1)} %bitcast.356), channel_id=1, source_target_pairs={{0,4},{4,0},{8,12},{12,8},{16,20},{20,16},{24,28},{28,24},{1,5},{5... | collective-permute-start | bytes 3145736 | tf_op jit(solution)/shard_map/ppermute | solution.py:71
  836.9 33.9 %collective-permute-start.34 = (bf16[2,2,256,512]{3,2,1,0:T(8,128)(2,1)}, bf16[2,2,256,512]{3,2,1,0:T(8,128)(2,1)}, u32[]{:S(2)}, u32[]{:S(2)}) collective-permute-start(bf16[2,2,256,512]{3,2,1,0:T(8,128)(2,1)} %dynamic-slice_bitcast_fusion), channel_id=1, source_target_pairs={{0,4},{4,0},{8,12},{12,8},{16,20},{20,16},{24,28},{28,24},{1,5},{5... | collective-permute-start | bytes 3145736 | tf_op jit(solution)/shard_map/ppermute | solution.py:71
  839.6 67.6 %collective-permute-start.24 = (bf16[256,2048]{0,1:T(8,128)(2,1)}, bf16[256,2048]{0,1:T(8,128)(2,1)}, u32[]{:S(2)}, u32[]{:S(2)}) collective-permute-start(bf16[256,2048]{0,1:T(8,128)(2,1)} %add_convert_fusion), channel_id=1, source_target_pairs={{0,1},{1,2},{2,3},{3,0},{4,5},{5,6},{6,7},{7,4},{8,9},{9,10},{10,1... | collective-permute-start | bytes 3145736 | tf_op jit(solution)/shard_map/ppermute | solution.py:66
  842.1 72.1 %collective-permute-start.19 = (bf16[256,2048]{0,1:T(8,128)(2,1)}, bf16[256,2048]{0,1:T(8,128)(2,1)}, u32[]{:S(2)}, u32[]{:S(2)}) collective-permute-start(bf16[256,2048]{0,1:T(8,128)(2,1)} %fusion.69), channel_id=1, source_target_pairs={{0,1},{1,2},{2,3},{3,0},{4,5},{5,6},{6,7},{7,4},{8,9},{9,10},{10,1... | collective-permute-start | bytes 3145736 | tf_op jit(solution)/shard_map/ppermute | solution.py:66
  849.0 15.4 %collective-permute-start.37 = (bf16[2,2,256,256]{3,2,1,0:T(8,128)(2,1)}, bf16[2,2,256,256]{3,2,1,0:T(8,128)(2,1)}, u32[]{:S(2)}, u32[]{:S(2)}) collective-permute-start(bf16[2,2,256,256]{3,2,1,0:T(8,128)(2,1)} %dynamic-slice_bitcast_fusion.1), channel_id=1, source_target_pairs={{0,4},{4,0},{8,12},{12,8},{16,20},{20,16},{24,28},{28,24},{1,5},{5... | collective-permute-start | bytes 1572872 | tf_op jit(solution)/shard_map/ppermute | solution.py:71
  859.5 41.7 %all-to-all-start.10 = ((bf16[4,256,256]{2,1,0:T(8,128)(2,1)}), bf16[4,256,256]{2,1,0:T(8,128)(2,1)}, u32[]{:S(2)}, u32[]{:S(2)}) async-start(bf16[4,256,256]{2,1,0:T(8,128)(2,1)} %pad_maximum_fusion.14), calls=%async_computation.10 | async-start | bytes 1048576 | tf_op jit(solution)/shard_map/all_to_all | solution.py:665
  865.9 52.6 %collective-permute-start.38 = (bf16[2,256,256]{2,1,0:T(8,128)(2,1)S(1)}, bf16[2,256,256]{2,1,0:T(8,128)(2,1)}, u32[]{:S(2)}, u32[]{:S(2)}) collective-permute-start(bf16[2,256,256]{2,1,0:T(8,128)(2,1)S(1)} %dynamic-slice_bitcast_fusion.4), channel_id=1, source_target_pairs={{0,8},{4,12},{8,0},{12,4},{16,24},{20,28},{24,16},{28,20},{1,9},{5... | collective-permute-start | bytes 786440 | tf_op jit(solution)/shard_map/ppermute | solution.py:71
  870.1 99.4 %collective-permute-start.32 = (bf16[2,256,512]{2,1,0:T(8,128)(2,1)}, bf16[2,256,512]{2,1,0:T(8,128)(2,1)}, u32[]{:S(2)}, u32[]{:S(2)}) collective-permute-start(bf16[2,256,512]{2,1,0:T(8,128)(2,1)} %dynamic-slice_bitcast_fusion.3), channel_id=1, source_target_pairs={{0,8},{4,12},{8,0},{12,4},{16,24},{20,28},{24,16},{28,20},{1,9},{5... | collective-permute-start | bytes 1572872 | tf_op jit(solution)/shard_map/ppermute | solution.py:71
  873.4 100.9 %collective-permute-start.35 = (bf16[2,256,512]{2,1,0:T(8,128)(2,1)}, bf16[2,256,512]{2,1,0:T(8,128)(2,1)}, u32[]{:S(2)}, u32[]{:S(2)}) collective-permute-start(bf16[2,256,512]{2,1,0:T(8,128)(2,1)} %dynamic-slice_bitcast_fusion.2), channel_id=1, source_target_pairs={{0,16},{4,20},{8,24},{12,28},{16,0},{20,4},{24,8},{28,12},{1,17},{... | collective-permute-start | bytes 1572872 | tf_op jit(solution)/shard_map/ppermute | solution.py:71
  914.2 2.9 collective-permute-start.26
  917.0 55.3 %collective-permute-start.20 = (bf16[256,2048]{0,1:T(8,128)(2,1)}, bf16[256,2048]{0,1:T(8,128)(2,1)}, u32[]{:S(2)}, u32[]{:S(2)}) collective-permute-start(bf16[256,2048]{0,1:T(8,128)(2,1)} %fusion.71), channel_id=1, source_target_pairs={{0,1},{1,2},{2,3},{3,0},{4,5},{5,6},{6,7},{7,4},{8,9},{9,10},{10,1... | collective-permute-start | bytes 3145736 | tf_op jit(solution)/shard_map/ppermute | solution.py:66
  917.1 3.8 collective-permute-start.27
  920.9 3.8 collective-permute-start.28
  923.1 30.0 %collective-permute-start.39 = (bf16[256,256]{1,0:T(8,128)(2,1)}, bf16[256,256]{1,0:T(8,128)(2,1)S(1)}, u32[]{:S(2)}, u32[]{:S(2)}) collective-permute-start(bf16[256,256]{1,0:T(8,128)(2,1)} %dynamic-slice_bitcast_fusion.7), channel_id=1, source_target_pairs={{0,16},{4,20},{8,24},{12,28},{16,0},{20,4},{24,8},{28,12},{1,17},{... | collective-permute-start | bytes 393224 | tf_op jit(solution)/shard_map/ppermute | solution.py:71
  924.7 20.3 %collective-permute-start.29 = (f32[4352]{0:T(1024)S(1)}, f32[4352]{0:T(1024)S(1)}, u32[]{:S(2)}, u32[]{:S(2)}) collective-permute-start(f32[4352]{0:T(1024)S(1)} %add.667), channel_id=1, source_target_pairs={{0,1},{1,0},{2,3},{3,2},{4,5},{5,4},{6,7},{7,6},{8,9},{9,8},{10,11... | collective-permute-start | bytes 52232 | tf_op jit(solution)/shard_map/ppermute | solution.py:71
  945.6 5.5 collective-permute-start.30
  970.8 6.4 collective-permute-start.33
  974.2 22.5 %collective-permute-start.21 = (bf16[256,2048]{0,1:T(8,128)(2,1)S(1)}, bf16[256,2048]{0,1:T(8,128)(2,1)S(1)}, u32[]{:S(2)}, u32[]{:S(2)}) collective-permute-start(bf16[256,2048]{0,1:T(8,128)(2,1)S(1)} %fusion.73), channel_id=1, source_target_pairs={{0,1},{1,2},{2,3},{3,0},{4,5},{5,6},{6,7},{7,4},{8,9},{9,10},{10,1... | collective-permute-start | bytes 3145736 | tf_op jit(solution)/shard_map/ppermute | solution.py:66
  975.6 6.4 collective-permute-start.36
  (143 other events, 1537.6 us)
Sparse Core Ops, SparseCore 0:
  10.5 26.1 all-gather.7
  38.6 36.9 all-gather.5
  77.5 37.5 all-gather.9
  116.8 36.7 all-gather.11
  858.2 56.3 reduce-scatter.1

commit v3 on v2

--- a/solution.py
+++ b/solution.py
@@ -5,6 +5,7 @@
 import jax.numpy as jnp
 from jax import lax
 from jax.experimental import pallas as pl
+from jax.experimental.layout import Layout, with_layout_constraint
 from jax.experimental.pallas import tpu as pltpu
 from jax.sharding import PartitionSpec as P
 
@@ -49,6 +50,10 @@
     return (doc_ids, places - begins)
 
 
+def row_major(array):
+    return with_layout_constraint(array, Layout(tuple(range(array.ndim))))
+
+
 def matmul(left, right):
     return jnp.dot(left, right, preferred_element_type=FULL)
 
@@ -76,7 +81,18 @@
 
 
 def nought(array):
-    return jnp.minimum(jnp.abs(array[(0,) * array.ndim].astype(FULL)), 0.0)
+    return jnp.minimum(jnp.min(jnp.abs(array[:16, :128].astype(FULL))), 0.0)
+
+
+def pinned(spot, *others):
+    return spot + sum(nought(o) for o in others).astype(jnp.int32)
+
+
+def stage(flag, work):
+    shapes = jax.eval_shape(work)
+    return lax.cond(
+        flag, work, lambda: jax.tree.map(lambda s: jnp.zeros(s.shape, s.dtype), shapes)
+    )
 
 
 def behind(array, *others):
@@ -100,14 +116,30 @@
     return parts
 
 
-def ring_sum(parts):
-    total = None
-    for b in list(range(1, len(parts))) + [0]:
-        if total is None:
-            total = parts[b]
-        else:
-            total = parts[b] + ring_shift(total.astype(LOW)).astype(FULL)
-    return total
+def ring_sums(parts):
+    sums = [parts[1]]
+    for b in list(range(2, len(parts))) + [0]:
+        sums.append(parts[b] + ring_shift(sums[-1].astype(LOW)).astype(FULL))
+    return sums
+
+
+def far_order(count):
+    order = [0]
+    for step in range(1, count // 2 + 1):
+        order += [step] if 2 * step == count else [step, count - step]
+    return order
+
+
+def shift_by(shard, by, axis="mp"):
+    length = lax.axis_size(axis)
+    return lax.ppermute(shard, axis, [(i, (i + by) % length) for i in range(length)])
+
+
+def direct_blocks(shard, count):
+    blocks = [shard] + [None] * (count - 1)
+    for b in far_order(count)[1:]:
+        blocks[b] = shift_by(shard, b)
+    return blocks
 
 
 def ring_blocks(shard, count):
@@ -121,7 +153,7 @@
     return pltpu.roll(values, values.shape[1] // 2, axis=1)
 
 
-def prep_kernel(at_ref, query_ref, kv_ref, cos_ref, sin_ref, qg_ref, kg_ref, out_ref, kvo_ref):
+def prep_kernel(at_ref, pre_ref, cos_ref, sin_ref, qg_ref, kg_ref, out_ref, kvo_ref):
     width = cos_ref.shape[1]
     cosine, sine = cos_ref[...], sin_ref[...]
 
@@ -130,15 +162,16 @@
         normed = pre * rate * gain
         return (normed * cosine + turned(normed) * sine).astype(LOW)
 
-    for h in range(query_ref.shape[1] // width):
+    wide = out_ref.shape[1]
+    for h in range(wide // width):
         cols = slice(h * width, (h + 1) * width)
-        out_ref[:, cols] = one(query_ref[:, cols], qg_ref[...])
-    kvo_ref[:, :width] = one(kv_ref[:, :width], kg_ref[...])
-    kvo_ref[:, width:] = kv_ref[:, width:].astype(LOW)
-
-
-def prepare(at, query_pre, kv_pre, cosine, sine, query_gain, key_gain):
-    rows, wide = query_pre.shape
+        out_ref[:, cols] = one(pre_ref[:, cols], qg_ref[...])
+    kvo_ref[:, :width] = one(pre_ref[:, wide : wide + width], kg_ref[...])
+    kvo_ref[:, width:] = pre_ref[:, wide + width :].astype(LOW)
+
+
+def prepare(at, pre, wide, cosine, sine, query_gain, key_gain):
+    rows = pre.shape[0]
     width = cosine.shape[1]
     step = min(128, rows)
     count = rows // step
@@ -155,8 +188,7 @@
             num_scalar_prefetch=1,
             grid=(count,),
             in_specs=[
-                pl.BlockSpec((step, wide), own),
-                pl.BlockSpec((step, 2 * width), own),
+                pl.BlockSpec((step, pre.shape[1]), own),
                 table,
                 table,
                 gain,
@@ -165,10 +197,8 @@
             out_specs=[pl.BlockSpec((step, wide), own), pl.BlockSpec((step, 2 * width), own)],
         ),
         compiler_params=pltpu.CompilerParams(vmem_limit_bytes=VMEM),
-        cost_estimate=pl.CostEstimate(
-            flops=rows * wide * 10, bytes_accessed=rows * wide * 8, transcendentals=rows * 16
-        ),
-    )(at, query_pre, kv_pre, cosine, sine, query_gain, key_gain)
+        cost_estimate=pl.CostEstimate(flops=1, bytes_accessed=1, transcendentals=0),
+    )(at, pre, cosine, sine, query_gain, key_gain)
 
 
 def thirds(values):
@@ -178,7 +208,17 @@
     return first, second, (rest - second.astype(FULL)).astype(LOW)
 
 
-def attend_kernel(score_scale, docs, at_ref, q_ref, qa_ref, kx_ref, vx_ref, out_ref, aug_ref):
+def keys_of(kv_ref, ka_ref, part):
+    width = ka_ref.shape[1]
+    return jnp.concatenate([kv_ref[part, :width], ka_ref[part, :]], axis=1)
+
+
+def values_of(kv_ref, part):
+    values = kv_ref[part, kv_ref.shape[1] // 2 :]
+    return jnp.concatenate([values, jnp.ones_like(values)], axis=1)
+
+
+def attend_kernel(score_scale, docs, at_ref, q_ref, qa_ref, kv_ref, ka_ref, out_ref, aug_ref):
     rows, width = q_ref.shape
     window = WINDOW
     start = pl.multiple_of(at_ref[0] * rows, rows)
@@ -191,13 +231,15 @@
     row_at = lax.broadcasted_iota(jnp.int32, (rows, rows), 0)
     upper = key_at > row_at
     corner = jnp.where(
-        upper, contract_last(query, kx_ref[far, :]), contract_last(query, kx_ref[near, :])
+        upper,
+        contract_last(query, keys_of(kv_ref, ka_ref, far)),
+        contract_last(query, keys_of(kv_ref, ka_ref, near)),
     )
     corner = jnp.exp2(corner * rate)
-    total = matmul(jnp.where(upper, corner, 0.0).astype(LOW), vx_ref[far, :])
-    total += matmul(jnp.where(upper, 0.0, corner).astype(LOW), vx_ref[near, :])
-    inner = jnp.exp2(contract_last(query, kx_ref[mid, :]) * rate).astype(LOW)
-    total += matmul(inner, vx_ref[mid, :])
+    total = matmul(jnp.where(upper, corner, 0.0).astype(LOW), values_of(kv_ref, far))
+    total += matmul(jnp.where(upper, 0.0, corner).astype(LOW), values_of(kv_ref, near))
+    inner = jnp.exp2(contract_last(query, keys_of(kv_ref, ka_ref, mid)) * rate).astype(LOW)
+    total += matmul(inner, values_of(kv_ref, mid))
     sums = total[:, width:]
     out_ref[...] = (total[:, :width] / sums).astype(LOW)
     first, second, third = thirds(jnp.log(sums) * (-1.0 / score_scale))
@@ -209,7 +251,7 @@
     aug_ref[...] = aug.astype(LOW)
 
 
-def attend(at, queries, query_aug, keys_wide, values_wide, score_scale, docs):
+def attend(at, queries, query_aug, kv_all, key_aug, score_scale, docs):
     rows, wide = queries.shape
     width = query_aug.shape[1]
     heads = wide // width
@@ -222,16 +264,12 @@
         grid_spec=pltpu.PrefetchScalarGridSpec(
             num_scalar_prefetch=1,
             grid=(heads,),
-            in_specs=[head, table, fixed(keys_wide), fixed(values_wide)],
+            in_specs=[head, table, fixed(kv_all), fixed(key_aug)],
             out_specs=[head, head],
         ),
         compiler_params=pltpu.CompilerParams(vmem_limit_bytes=VMEM),
-        cost_estimate=pl.CostEstimate(
-            flops=heads * rows * (WINDOW + rows) * 1024,
-            bytes_accessed=rows * wide * 8 + keys_wide.size * 4,
-            transcendentals=heads * rows * WINDOW,
-        ),
-    )(at, queries, query_aug, keys_wide, values_wide)
+        cost_estimate=pl.CostEstimate(flops=1, bytes_accessed=1, transcendentals=0),
+    )(at, queries, query_aug, kv_all, key_aug)
 
 
 def attend_back_kernel(
@@ -245,12 +283,13 @@
     cos_ref,
     sin_ref,
     gain_ref,
-    kx_ref,
-    vx_ref,
-    kt_ref,
+    kva_ref,
+    ka_ref,
+    before_ref,
     low_ref,
     kv_ref,
     gain_grad_ref,
+    kt_ref,
 ):
     rows, width = q_ref.shape
     window = WINDOW
@@ -259,8 +298,10 @@
 
     @pl.when(pl.program_id(0) == 0)
     def _():
-        kv_ref[...] = jnp.zeros_like(kv_ref)
+        kv_ref[...] = before_ref[...]
         gain_grad_ref[...] = jnp.zeros_like(gain_grad_ref)
+        span = pl.ds(start, rows + window)
+        kt_ref[...] = kva_ref[span, :width].astype(FULL).T.astype(LOW)
 
     query = q_ref[...]
     grad = grad_ref[...]
@@ -279,10 +320,10 @@
 
     mid_size = window - rows
     mid = pl.ds(pl.multiple_of(start + rows, rows), mid_size)
-    soft = jnp.exp2(contract_last(kx_ref[mid, :], query_wide) * rate)
-    scores = (soft * contract_last(vx_ref[mid, :], grad_wide)).astype(LOW)
-    add(slice(rows, rows + mid_size), soft.astype(LOW), scores)
-    query_grad = matmul(kt_ref[:, mid], scores)
+    soft = jnp.exp2(contract_last(keys_of(kva_ref, ka_ref, mid), query_wide) * rate)
+    scores = (soft * contract_last(values_of(kva_ref, mid), grad_wide)).astype(LOW)
+    add(mid, soft.astype(LOW), scores)
+    query_grad = matmul(kt_ref[:, rows:window], scores)
 
     far = pl.ds(start, rows)
     near = pl.ds(pl.multiple_of(start + window, rows), rows)
@@ -291,20 +332,22 @@
     upper = key_at > row_at
     corner = jnp.where(
         upper,
-        contract_last(kx_ref[far, :], query_wide),
-        contract_last(kx_ref[near, :], query_wide),
+        contract_last(keys_of(kva_ref, ka_ref, far), query_wide),
+        contract_last(keys_of(kva_ref, ka_ref, near), query_wide),
     )
     soft = jnp.exp2(corner * rate)
     slopes = jnp.where(
-        upper, contract_last(vx_ref[far, :], grad_wide), contract_last(vx_ref[near, :], grad_wide)
+        upper,
+        contract_last(values_of(kva_ref, far), grad_wide),
+        contract_last(values_of(kva_ref, near), grad_wide),
     )
     scores = soft * slopes
     scores_far = jnp.where(upper, scores, 0.0).astype(LOW)
     scores_near = jnp.where(upper, 0.0, scores).astype(LOW)
-    add(slice(0, rows), jnp.where(upper, soft, 0.0).astype(LOW), scores_far)
-    add(slice(window, window + rows), jnp.where(upper, 0.0, soft).astype(LOW), scores_near)
-    query_grad += matmul(kt_ref[:, far], scores_far)
-    query_grad += matmul(kt_ref[:, near], scores_near)
+    add(far, jnp.where(upper, soft, 0.0).astype(LOW), scores_far)
+    add(near, jnp.where(upper, 0.0, soft).astype(LOW), scores_near)
+    query_grad += matmul(kt_ref[:, :rows], scores_far)
+    query_grad += matmul(kt_ref[:, window:], scores_near)
 
     spread = query_grad.T * score_scale
     spread = spread * cos_ref[...] - sin_ref[...] * turned(spread)
@@ -319,7 +362,7 @@
 
 
 def attend_back(
-    at, queries, query_aug, grads, outs, pre, cosine, sine, gain, keys_wide, values_wide, keys_turned, score_scale
+    at, queries, query_aug, grads, outs, pre, cosine, sine, gain, kv_all, key_aug, before, score_scale
 ):
     rows, wide = queries.shape
     width = cosine.shape[1]
@@ -332,7 +375,7 @@
         functools.partial(attend_back_kernel, score_scale),
         out_shape=(
             jax.ShapeDtypeStruct((rows, wide), LOW),
-            jax.ShapeDtypeStruct((span, 2 * width), FULL),
+            jax.ShapeDtypeStruct(before.shape, FULL),
             jax.ShapeDtypeStruct((1, width), FULL),
         ),
         grid_spec=pltpu.PrefetchScalarGridSpec(
@@ -347,19 +390,75 @@
                 table,
                 table,
                 fixed((1, width)),
-                fixed(keys_wide.shape),
-                fixed(values_wide.shape),
-                fixed(keys_turned.shape),
+                fixed(kv_all.shape),
+                fixed(key_aug.shape),
+                fixed(before.shape),
             ],
-            out_specs=[head, fixed((span, 2 * width)), fixed((1, width))],
+            out_specs=[head, fixed(before.shape), fixed((1, width))],
+            scratch_shapes=[pltpu.VMEM((width, span), LOW)],
         ),
         compiler_params=pltpu.CompilerParams(vmem_limit_bytes=VMEM),
-        cost_estimate=pl.CostEstimate(
-            flops=heads * rows * span * 2048,
-            bytes_accessed=rows * wide * 16 + keys_wide.size * 8,
-            transcendentals=heads * rows * WINDOW,
+        cost_estimate=pl.CostEstimate(flops=1, bytes_accessed=1, transcendentals=0),
+    )(at, queries, query_aug, grads, outs, pre, cosine, sine, gain, kv_all, key_aug, before)
+
+
+def key_back_kernel(
+    score_scale, at_ref, kv_ref, more_ref, pre_ref, cos_ref, sin_ref, gain_ref, low_ref, gain_grad_ref
+):
+    width = cos_ref.shape[1]
+    more = jnp.where(at_ref[1] == 0, more_ref[...].astype(FULL), 0.0)
+    total = kv_ref[...] + more
+    spread = total[:, :width] * score_scale
+    spread = spread * cos_ref[...] - sin_ref[...] * turned(spread)
+    pre = pre_ref[...]
+    pace = lax.rsqrt(jnp.mean(pre * pre, axis=1, keepdims=True) + EPSILON)
+    normed = pre * pace
+    gain_grad_ref[...] = jnp.sum(spread * normed, axis=0, keepdims=True)
+    spread = spread * gain_ref[...]
+    low_ref[:, :width] = (
+        pace * (spread - normed * jnp.mean(spread * normed, axis=1, keepdims=True))
+    ).astype(LOW)
+    low_ref[:, width:] = total[:, width:].astype(LOW)
+
+
+def key_back(spot, half_index, kv_grads, returned, pre, local_width, cosine, sine, gain, score_scale):
+    rows = pre.shape[0]
+    width = cosine.shape[1]
+    ahead = returned.shape[0] // rows
+    table = pl.BlockSpec((rows, width), lambda i, at: (at[0], 0))
+    return pl.pallas_call(
+        functools.partial(key_back_kernel, score_scale),
+        out_shape=(
+            jax.ShapeDtypeStruct((rows, 2 * width), LOW),
+            jax.ShapeDtypeStruct((1, width), FULL),
         ),
-    )(at, queries, query_aug, grads, outs, pre, cosine, sine, gain, keys_wide, values_wide, keys_turned)
+        grid_spec=pltpu.PrefetchScalarGridSpec(
+            num_scalar_prefetch=1,
+            grid=(1,),
+            in_specs=[
+                pl.BlockSpec((rows, 2 * width), lambda i, at: (at[0] + ahead, 0)),
+                pl.BlockSpec((rows, 2 * width), lambda i, at: (at[0], 0)),
+                pl.BlockSpec((rows, width), lambda i, at: (0, local_width // width)),
+                table,
+                table,
+                pl.BlockSpec((1, width), lambda i, at: (0, 0)),
+            ],
+            out_specs=[
+                pl.BlockSpec((rows, 2 * width), lambda i, at: (0, 0)),
+                pl.BlockSpec((1, width), lambda i, at: (0, 0)),
+            ],
+        ),
+        compiler_params=pltpu.CompilerParams(vmem_limit_bytes=VMEM),
+        cost_estimate=pl.CostEstimate(flops=1, bytes_accessed=1, transcendentals=0),
+    )(
+        jnp.concatenate([spot, half_index.reshape((1,)).astype(jnp.int32)]),
+        kv_grads,
+        returned,
+        pre,
+        cosine,
+        sine,
+        gain,
+    )
 
 
 def on_device(
@@ -404,11 +503,13 @@
 
     resid_in = tokens.astype(FULL)
     normed_one, norm_one_back = jax.vjp(rms_norm, resid_in, input_gain)
-    sequence = ring_blocks(normed_one.astype(LOW), mp_count)
-    wq_whole = lax.all_gather(query_weight, "dp", axis=0, tiled=True)
-    kv_own = lax.all_gather(
+    sequence = [normed_one.astype(LOW)]
+    for _ in range(1, mp_count - 1):
+        sequence.append(ring_shift(sequence[-1]))
+    own_whole = lax.all_gather(
         jnp.concatenate(
             [
+                query_weight,
                 lax.dynamic_slice_in_dim(key_value_weight, kv_offset, head_width, 1),
                 lax.dynamic_slice_in_dim(key_value_weight, kv_width + kv_offset, head_width, 1),
             ],
@@ -418,8 +519,8 @@
         axis=0,
         tiled=True,
     )
+    wq_whole = own_whole[:, :local_width]
     wo_whole = lax.all_gather(out_weight, "dp", axis=1, tiled=True)
-    wkv_whole = lax.all_gather(key_value_weight, "dp", axis=0, tiled=True)
 
     top_count = routes.shape[1]
     routed_mean = row_count * top_count // expert_count
@@ -490,8 +591,8 @@
             tiled=True,
         ).reshape(dp_count * group_rows, model_width)
 
-    def dispatch(pieces, g):
-        return plane_turn(matmul(sends[g], joined_rows(pieces)).astype(LOW))
+    def placed(pieces, g):
+        return matmul(sends[g], joined_rows(pieces)).astype(LOW)
 
     def place(came, g):
         sums = contract_first(sends[g], came)
@@ -517,49 +618,49 @@
 
     query_pre, queries = [], []
     kv_rows = jnp.zeros((sequence_length, 2 * head_width), LOW)
-    key_pre = jnp.zeros((sequence_length, head_width), FULL)
     for b in blocks:
-        pre_b = matmul(sequence[b], wq_whole)
-        kv_b = matmul(sequence[b], kv_own)
+        if b == mp_count - 1:
+            sequence.append(ring_shift(last_sent))
+        pre_b = matmul(sequence[b], own_whole)
         queries_b, kv_low = prepare(
-            spots[b], pre_b, kv_b, cosine, sine, query_gain_row, key_gain_row
+            spots[b], pre_b, local_width, cosine, sine, query_gain_row, key_gain_row
         )
+        if b == 0:
+            last_sent = behind(sequence[mp_count - 2], kv_low)
+        if b == 1:
+            second_kv = kv_low
         query_pre.append(pre_b)
         queries.append(queries_b)
         kv_rows = lax.dynamic_update_slice_in_dim(kv_rows, kv_low, places[b] * row_count, 0)
-        key_pre = lax.dynamic_update_slice_in_dim(
-            key_pre, kv_b[:, :head_width], places[b] * row_count, 0
-        )
     prior = lax.ppermute(kv_rows, "dp", [(i, i + 1) for i in range(0, dp_count, 2)])
-    keys_pad = jnp.concatenate([prior[:, :head_width], kv_rows[:, :head_width]], axis=0)
-    values_pad = jnp.concatenate([prior[:, head_width:], kv_rows[:, head_width:]], axis=0)
-    keys_wide = jnp.concatenate([keys_pad, key_aug], axis=1)
-    values_wide = jnp.concatenate([values_pad, jnp.ones_like(values_pad)], axis=1)
-    keys_turned = keys_pad.T
-
-    cot_blocks = [cotangent]
+    kv_all = jnp.concatenate([prior, kv_rows], axis=0)
+
+    cot_blocks = [cotangent, ring_shift(behind(cotangent, sequence[-1], second_kv))]
+    for b in blocks[2:]:
+        cot_blocks.append(ring_shift(cot_blocks[-1]))
     cot_rows = []
 
     attended, augs, head_parts = [None] * mp_count, [None] * mp_count, [None] * mp_count
     for b in list(range(1, mp_count)) + [0]:
+        spot = pinned(spots[b], cot_blocks[b]) if b else spots[b]
         attended[b], augs[b] = attend(
-            spots[b], queries[b], query_aug, keys_wide, values_wide, score_scale, docs
+            spot, queries[b], query_aug, kv_all, key_aug, score_scale, docs
         )
         head_parts[b] = matmul(attended[b], wo_whole)
-        if b > 0:
-            waits = sequence[-1] if b == 1 else keys_wide if b == 2 else attended[b - 2]
-            cot_blocks.append(ring_shift(behind(cot_blocks[-1], waits)))
     for g, group in enumerate(groups):
-        cot_rows.append(dispatch([cot_blocks[b] for b in group], g))
-    resid = resid_in + ring_sum(head_parts)
+        cot_rows.append(plane_turn(placed([cot_blocks[k] for k in group], g)))
+    resid = resid_in + ring_sums(head_parts)[-1]
     normed_two, norm_two_back = jax.vjp(rms_norm, resid, moe_gain)
 
     gate_one, up_one, down_one = gate_weight[0], up_weight[0], down_weight[0]
     normed_blocks = ring_blocks(normed_two.astype(LOW), mp_count)
+    kv_all_weights = lax.all_gather(
+        behind(own_whole[:, local_width:], normed_blocks[-1]), "mp", axis=1, tiled=True
+    )
     inputs, hiddens, scaled, gate_grads, up_grads = [], [], [], [], []
     resid_parts, came = [], None
     for g, group in enumerate(groups):
-        rows_g = dispatch([normed_blocks[b] for b in group], g)
+        rows_g = plane_turn(placed([normed_blocks[b] for b in group], g))
         gate_pre = matmul(rows_g, gate_one)
         up_pre = matmul(rows_g, up_one)
         sigmoid_gate = jax.nn.sigmoid(gate_pre)
@@ -573,130 +674,197 @@
         up_grad = (grad_hidden * silu_gate).astype(LOW)
         grad_in = (contract_last(gate_grad, gate_one) + contract_last(up_grad, up_one)).astype(LOW)
         came = plane_turn(grad_in)
-        resid_parts += place(came, g)
+        if group != groups[-1]:
+            resid_parts += place(came, g)
         inputs.append(rows_g)
         hiddens.append(hidden)
         scaled.append(scaled_g)
         gate_grads.append(gate_grad)
         up_grads.append(up_grad)
-    grad_moe_normed = ring_sum(resid_parts)
-    grad_resid_norm, moe_gain_part = norm_two_back(grad_moe_normed)
-    grad_resid = cotangent.astype(FULL) + grad_resid_norm
-    back = ring_blocks(grad_resid.astype(LOW), mp_count)
-
-    out_parts = []
-    gate_grad_parts = []
-    for g, group in enumerate(groups):
+    flag = routes[0, 0] >= 0
+    last = groups[-1]
+    sums = [resid_parts[1]]
+    for b in range(2, last[0]):
+        sums.append(resid_parts[b] + ring_shift(sums[-1].astype(LOW)).astype(FULL))
+    passed = ring_shift(sums[-1].astype(LOW))
+    late = nought(sums[0])
+    pairs = [(hiddens, scaled), (inputs, gate_grads), (inputs, up_grads)]
+    weight_parts = []
+    for left, right in pairs:
+        part = late
+        for g in range(len(groups) - 1):
+            part = row_major(contract_first(left[g], right[g]) + part)
+        weight_parts.append(part)
+
+    def expert_outs(g, tie):
         out_g = matmul(hiddens[g], down_one)
         dots = jnp.sum(out_g * cot_rows[g].astype(FULL), axis=1, keepdims=True)
-        out_low = (behind(row_gates[g], came) * out_g).astype(LOW)
-        out_parts += [p + nought(back[-1]) for p in place(plane_turn(out_low), g)]
         found = lax.dot_general(
             widen.astype(FULL),
             jnp.where(seen[g], dots, 0.0),
             (((0,), (0,)), ((), ())),
             precision=lax.Precision.HIGHEST,
         )
-        gate_grad_parts += [
-            found[:, k * row_count : (k + 1) * row_count] for k in range(group_size)
-        ]
-    block_out = (resid + ring_sum(out_parts)).astype(LOW)
-    spread = jnp.stack(
-        [
-            sum(jnp.where(places[b] == p, gate_grad_parts[b], 0.0) for b in blocks)
-            for p in range(mp_count)
-        ],
-        axis=1,
-    ).reshape(expert_count, row_count)
-    spread = lax.all_to_all(spread, ("dp", "mp"), split_axis=0, concat_axis=0, tiled=True)
+        return ((row_gates[g] + tie) * out_g).astype(LOW), found
+
+    outs = [expert_outs(g, late) for g in range(len(groups) - 1)]
+    own_part = resid_parts[0]
+
+    def sum_work():
+        first_out = plane_turn(outs[0][0])
+        parts = place(came, len(groups) - 1)
+        total = parts[0] + passed.astype(FULL)
+        for part in parts[1:] + [own_part]:
+            total = part + ring_shift(total.astype(LOW)).astype(FULL)
+        grad_norm, gain_part = norm_two_back(total)
+        grad = cotangent.astype(FULL) + grad_norm
+        return (
+            grad,
+            grad.astype(LOW),
+            gain_part,
+            first_out,
+            [
+                row_major(contract_first(left[-1], right[-1]) + part)
+                for (left, right), part in zip(pairs, weight_parts)
+            ],
+            expert_outs(len(groups) - 1, 0.0),
+        )
+
+    grad_resid, back_own, moe_gain_part, first_out, weight_grads, last_outs = stage(flag, sum_work)
+    down_weight_grad, gate_weight_grad, up_weight_grad = weight_grads
+    outs.append(last_outs)
+    back = [back_own]
+    out_came = [first_out] + [plane_turn(rows) for rows, _ in outs[1:]]
+    gate_grad_parts = [
+        found[:, k * row_count : (k + 1) * row_count] for _, found in outs for k in range(group_size)
+    ]
+
+    kv_grads = jnp.zeros((2 * sequence_length, 2 * head_width), FULL)
+    query_low, input_parts = [], []
+    query_gain_part = 0.0
+    for b in blocks:
+        ended = b == mp_count - 1
+        spot = pinned(spots[b], *out_came[1:]) if ended else spots[b]
+
+        def block_work():
+            extra = ()
+            if not ended:
+                extra += (ring_shift(back[b]),)
+            else:
+                extra += (ring_shift(input_parts[1].astype(LOW)),)
+                out_part = place(out_came[0], 0)
+                extra += (out_part[0], ring_shift(out_part[1].astype(LOW)))
+                extra += (contract_first(joined_rows(attended), joined_rows(back)).astype(LOW),)
+            if b == 0:
+                spread = jnp.stack(
+                    [
+                        sum(jnp.where(places[k] == p, gate_grad_parts[k], 0.0) for k in blocks)
+                        for p in blocks
+                    ],
+                    axis=1,
+                ).reshape(expert_count, row_count)
+                extra += (
+                    lax.all_to_all(spread, ("dp", "mp"), split_axis=0, concat_axis=0, tiled=True),
+                )
+            low, kv, gain = attend_back(
+                spot,
+                queries[b],
+                augs[b],
+                contract_last(back[b], wo_whole).astype(LOW),
+                attended[b],
+                query_pre[b],
+                cosine,
+                sine,
+                query_gain_row,
+                kv_all,
+                key_aug,
+                kv_grads,
+                score_scale,
+            )
+            return (low, kv, gain, contract_last(low, wq_whole)) + extra
+
+        low_b, kv_b, gain_b, input_b, *extra = stage(flag, block_work)
+        kv_grads = kv_b
+        query_low.append(low_b)
+        input_parts.append(input_b)
+        query_gain_part += gain_b[0]
+        if not ended:
+            back.append(extra[0])
+        if b == 0:
+            spread = extra[1]
+    input_passed, out_own, out_passed, out_weight_part = extra
     gate_values_grad = jnp.stack(
         [jnp.sum(jnp.where(picked[k], spread, 0.0), axis=0) for k in range(top_count)], axis=1
     )
-    inputs_all = joined_rows(inputs)
-    late = nought(grad_in)
-    down_weight_grad = (contract_first(joined_rows(hiddens), joined_rows(scaled)) + late)[None]
-    gate_weight_grad = (contract_first(inputs_all, joined_rows(gate_grads)) + late)[None]
-    up_weight_grad = (contract_first(inputs_all, joined_rows(up_grads)) + late)[None]
+
+    def dp_turn(parts):
+        return lax.all_to_all(parts, "dp", split_axis=0, concat_axis=0, tiled=True)
 
     out_weight_grad = lax.psum_scatter(
-        contract_first(joined_rows(attended), joined_rows(back)).astype(LOW),
-        "dp",
-        scatter_dimension=1,
-        tiled=True,
+        out_weight_part, "dp", scatter_dimension=1, tiled=True
     ).astype(FULL)
-    kv_grads = jnp.zeros((2 * sequence_length, 2 * head_width), FULL)
-    query_low, query_gain_part, input_parts = [], 0.0, []
-    for b in blocks:
-        grad_attended = contract_last(back[b], wo_whole).astype(LOW)
-        low_b, kv_b, gain_b = attend_back(
-            spots[b],
-            queries[b],
-            augs[b],
-            grad_attended,
-            attended[b],
-            query_pre[b],
-            cosine,
-            sine,
-            query_gain_row,
-            keys_wide,
-            values_wide,
-            keys_turned,
-            score_scale,
+    sequence_all = joined_rows(sequence)
+
+    def input_work():
+        weight_part = row_major(contract_first(sequence_all, joined_rows(query_low)).astype(LOW))
+        weight_came = dp_turn(weight_part.reshape(dp_count, shard_rows, local_width))
+        returned = lax.ppermute(
+            kv_grads[:sequence_length].astype(LOW),
+            "dp",
+            [(i + 1, i) for i in range(0, dp_count, 2)],
         )
-        at = places[b] * row_count
-        kv_grads = lax.dynamic_update_slice_in_dim(
-            kv_grads, lax.dynamic_slice_in_dim(kv_grads, at, kv_b.shape[0], 0) + kv_b, at, 0
+        total = input_parts[2] + input_passed.astype(FULL)
+        for part in input_parts[3:] + [input_parts[0]]:
+            total = part + ring_shift(total.astype(LOW)).astype(FULL)
+        kv_blocks, key_gain_part = [], 0.0
+        for b in blocks:
+            kv_low, gain_b = key_back(
+                spots[b],
+                half_index,
+                kv_grads,
+                returned,
+                query_pre[b],
+                local_width,
+                cosine,
+                sine,
+                key_gain_row,
+                score_scale,
+            )
+            kv_blocks.append(kv_low)
+            key_gain_part += gain_b[0]
+        kv_spread = jnp.zeros((mp_count, row_count, 2 * head_width), LOW)
+        for b in blocks:
+            kv_came = shift_by(kv_blocks[b], -b) if b else kv_blocks[0]
+            kv_spread = lax.dynamic_update_index_in_dim(
+                kv_spread, kv_came, (mp_place + b) % mp_count, 0
+            )
+        total += lax.dot_general(
+            kv_spread.transpose(1, 0, 2).reshape(row_count, -1),
+            kv_all_weights,
+            (((1,), (1,)), ((), ())),
+            preferred_element_type=FULL,
         )
-        query_low.append(low_b)
-        query_gain_part += gain_b[0]
-        input_parts.append(contract_last(low_b, wq_whole))
-    returned = lax.ppermute(
-        kv_grads[:sequence_length].astype(LOW), "dp", [(i + 1, i) for i in range(0, dp_count, 2)]
-    )
-    kv_total = kv_grads[sequence_length:] + jnp.where(half_index == 0, returned.astype(FULL), 0.0)
-
-    def key_prep(pre, gain):
-        normed = rms_norm(pre, gain)
-        return normed * cosine + jnp.roll(normed, head_width // 2, axis=1) * sine
-
-    _, key_back = jax.vjp(key_prep, key_pre, key_gain)
-    grad_key_pre, key_gain_part = key_back(kv_total[:, :head_width] * score_scale)
-    kv_low = jnp.concatenate([grad_key_pre, kv_total[:, head_width:]], axis=1).astype(LOW)
-    kv_spread = lax.all_to_all(
-        kv_low.reshape(mp_count, row_count, 2 * head_width),
-        "mp",
-        split_axis=0,
-        concat_axis=0,
-        tiled=True,
-    )
-    grad_normed_one = ring_sum(input_parts)
-    for m in blocks:
-        cols = kv_offsets[m]
-        grad_normed_one += contract_last(
-            kv_spread[m, :, :head_width], wkv_whole[:, cols : cols + head_width]
+        out_parts = []
+        for g in range(1, len(groups)):
+            out_parts += place(out_came[g], g)
+        return (
+            row_major(weight_came),
+            total,
+            key_gain_part,
+            row_major(contract_first(sequence_all, joined_rows(kv_blocks)).astype(LOW)),
+            out_parts,
         )
-        cols += kv_width
-        grad_normed_one += contract_last(
-            kv_spread[m, :, head_width:], wkv_whole[:, cols : cols + head_width]
-        )
+
+    weight_came, grad_normed_one, key_gain_part, kv_part, out_parts = stage(flag, input_work)
+    out_total = out_parts[0] + out_passed.astype(FULL)
+    for part in out_parts[1:] + [out_own]:
+        out_total = part + ring_shift(out_total.astype(LOW)).astype(FULL)
+    block_out = (resid + out_total).astype(LOW)
     grad_in_norm, input_gain_part = norm_one_back(grad_normed_one)
     tokens_grad = grad_resid + grad_in_norm
 
-    kv_blocks = [
-        lax.dynamic_slice_in_dim(kv_low, places[b] * row_count, row_count, 0) for b in blocks
-    ]
-    sequence_all = joined_rows(sequence)
-    kv_part = contract_first(sequence_all, joined_rows(kv_blocks)).astype(LOW)
-    weight_part = contract_first(sequence_all, joined_rows(query_low)).astype(LOW)
-    half = local_width // 2
+    query_weight_grad = jnp.sum(weight_came.astype(FULL), axis=0)
     own_cols = lax.all_gather(sum_scatter_rows(kv_part, bits), "mp", axis=0).astype(FULL)
-    query_weight_grad = jnp.concatenate(
-        [
-            sum_scatter_rows(weight_part[:, :half], bits),
-            sum_scatter_rows(weight_part[:, half:], bits[:1] + bits[1:][::-1]),
-        ],
-        axis=1,
-    ).astype(FULL)
     kv_parts = [None] * (2 * kv_width // head_width)
     for m in blocks:
         for side in range(2):
@@ -723,9 +891,9 @@
         gains[ends[1] : ends[2]],
         out_weight_grad,
         gains[: ends[0]],
-        gate_weight_grad,
-        up_weight_grad,
-        down_weight_grad,
+        gate_weight_grad[None],
+        up_weight_grad[None],
+        down_weight_grad[None],
         gate_values_grad,
     )
 

time: 1020 us -> 947 us (0.928)
  waiting for transfers between devices: 342 us -> 252 us
  local copies, waits for them, and re-layouts: 76 us -> 38.5 us
  starting transfers between devices: 82.4 us -> 104 us
  other arithmetic: 88.3 us -> 100 us
  matrix products: 272 us -> 283 us
    ppermute x24, waiting for transfers between devices: 233 us -> 183 us  [ring_shift(): lax.ppermute(shard, axis, [(i, (i + 1) % length) for i in range(length)])]
    all_to_all x2, waiting for transfers between devices: 26.5 us -> 0.01 us  [the longest x1 0.01 us: block_work(): lax.all_to_all(spread, ('dp', 'mp'), split_axis=0, concat_axis=0, tiled=T...]
    ppermute x14 -> x8, waiting for transfers between devices: 27.4 us -> 8.05 us  [swap(): return lax.ppermute(shard, axis, [(i, i ^ bit) for i in range(length)])]
    reduce_sum x0 -> x2, other arithmetic: none -> 15.2 us  [the longest x1 11.1 us: expert_outs(): dots = jnp.sum(out_g * cot_rows[g].astype(FULL), axis=1, keepdims=True)]
    unnamed x312 -> x233, local copies, waits for them, and re-layouts: 23.5 us -> 8.68 us
    ppermute x14 -> x8, starting transfers between devices: 13.1 us -> 25.5 us  [swap(): return lax.ppermute(shard, axis, [(i, i ^ bit) for i in range(length)])]
    dot_general x10 -> x13, matrix products: 80 us -> 92.2 us  [contract_first(): lax.dot_general(left, right, (((0,), (0,)), ((), ())), preferred_element_...]
    convert_element_type x4 -> x3, other arithmetic: 24.3 us -> 13.5 us  [on_device(): scaled_g = (row_gates[g] * cot_rows[g].astype(FULL)).astype(LOW)]
  transfers between devices with their start and end apart: 57 -> 53, of which waited for: 24 -> 27; matrix products, arithmetic and copies ran while one was open for 42% -> 42% of each run, Pallas kernels for 11% -> 12%
where the time goes in v3:
time: 947 us; the launch traced here: 935 us
  matrix products  283 us (30%)
  waiting for transfers between devices  252 us (27%)
  Pallas kernels  115 us (12%)
  starting transfers between devices  104 us (11%)
  other arithmetic  100 us (11%)
  local copies, waits for them, and re-layouts  38.5 us (4%)
  between operations  22.8 us (2%)
  blocking collectives  17.7 us (2%)
    ppermute x24, waiting for transfers between devices, ring_shift(): lax.ppermute(shard, axis, [(i, (i + 1) % length) for i in range(length)])  183 us
    dot_general x23, matrix products, matmul(): return jnp.dot(left, right, preferred_element_type=FULL)  113 us
    dot_general x13, matrix products, contract_first(): lax.dot_general(left, right, (((0,), (0,)), ((), ())), preferred_element_...  92.2 us
    dot_general x14, matrix products, contract_last(): lax.dot_general(left, right, (((1,), (1,)), ((), ())), preferred_element_...  67.7 us
    pallas_call x4, Pallas kernels, attend_back(): pl.pallas_call(functools.partial(attend_back_kernel, score_scale), out_sh...  59.8 us
    all_to_all x8, waiting for transfers between devices, plane_turn(): lax.all_to_all(rows.reshape(dp_count, group_rows, model_width), 'dp', spl...  58.4 us
    all_to_all x8, starting transfers between devices, plane_turn(): lax.all_to_all(rows.reshape(dp_count, group_rows, model_width), 'dp', spl...  37.4 us
    pallas_call x4, Pallas kernels, attend(): pl.pallas_call(functools.partial(attend_kernel, score_scale, docs), out_s...  34 us
  transfers between devices with their start and end apart: 53, of which 27 were waited for; matrix products, arithmetic and copies ran while one was open for 42% of the time, Pallas kernels for 12%

profile of v3, /device:TPU:0, one launch (start us, length us, event | category | flops | bytes accessed | tf_op | source)
XLA Modules:
  0.0 935.0 jit_solution(7503775585822990105)
XLA Ops:
  31.6 12.0 %collective-permute-done.13 = bf16[256,2048]{1,0:T(8,128)(2,1)} collective-permute-done((bf16[256,2048]{1,0:T(8,128)(2,1)}, bf16[256,2048]{1,0:T(8,128)(2,1)}, u32[]{:S(2)}, u32[]{:S(2)}) %collective-permute-start.13) | collective-permute-done | bytes 1048608 | tf_op jit(solution)/shard_map/ppermute | solution.py:71
  45.8 6.1 all-to-all-start.4
  63.4 7.1 collective-permute-done.14
  92.0 5.8 collective-permute-done.15
  116.2 9.1 collective-permute-done.17
  125.2 5.8 convolution_convert_fusion.9
  133.0 8.7 shard_map.253
  154.7 8.7 shard_map.252
  163.9 15.2 %collective-permute-done.20 = bf16[256,2048]{1,0:T(8,128)(2,1)} collective-permute-done((bf16[256,2048]{1,0:T(8,128)(2,1)}, bf16[256,2048]{1,0:T(8,128)(2,1)}, u32[]{:S(2)}, u32[]{:S(2)}) %collective-permute-start.20) | collective-permute-done | bytes 1048608 | tf_op jit(solution)/shard_map/ppermute | solution.py:71
  187.1 14.3 %collective-permute-done.19 = bf16[256,2048]{1,0:T(8,128)(2,1)S(1)} collective-permute-done((bf16[256,2048]{1,0:T(8,128)(2,1)}, bf16[256,2048]{1,0:T(8,128)(2,1)S(1)}, u32[]{:S(2)}, u32[]{:S(2)}) %collective-permute-start.19) | collective-permute-done | bytes 1048608 | tf_op jit(solution)/shard_map/ppermute | solution.py:71
  203.7 8.7 shard_map.251
  212.3 11.3 %collective-permute-done.21 = bf16[256,2048]{1,0:T(8,128)(2,1)} collective-permute-done((bf16[256,2048]{1,0:T(8,128)(2,1)}, bf16[256,2048]{1,0:T(8,128)(2,1)}, u32[]{:S(2)}, u32[]{:S(2)}) %collective-permute-start.21) | collective-permute-done | bytes 1048608 | tf_op jit(solution)/shard_map/ppermute | solution.py:71
  228.5 5.8 convolution_convert_fusion.7
  240.5 7.9 shard_map.250
  248.4 7.0 collective-permute-done.22
  272.5 5.2 multiply_convert_fusion.5
  277.7 10.2 %collective-permute-done.23 = bf16[256,2048]{1,0:T(8,128)(2,1)} collective-permute-done((bf16[256,2048]{1,0:T(8,128)(2,1)}, bf16[256,2048]{1,0:T(8,128)(2,1)}, u32[]{:S(2)}, u32[]{:S(2)}) %collective-permute-start.23) | collective-permute-done | bytes 1048608 | tf_op jit(solution)/shard_map/ppermute | solution.py:71
  287.9 6.1 convolution_convert_fusion.8
  298.7 8.6 fusion.202
  307.3 5.7 collective-permute-done.24
  313.3 5.1 multiply_convert_fusion.2
  321.6 5.4 fusion.200
  327.0 10.4 %collective-permute-done.25 = bf16[256,2048]{1,0:T(8,128)(2,1)S(1)} collective-permute-done((bf16[256,2048]{1,0:T(8,128)(2,1)}, bf16[256,2048]{1,0:T(8,128)(2,1)S(1)}, u32[]{:S(2)}, u32[]{:S(2)}) %collective-permute-start.25) | collective-permute-done | bytes 1048608 | tf_op jit(solution)/shard_map/ppermute | solution.py:71
  342.0 6.3 convolution_convert_fusion.6
  355.6 6.5 fusion.60
  362.1 7.3 multiply_convert_fusion.10
  373.2 6.0 fusion.198
  379.2 5.3 fusion.47
  384.5 23.0 %all-to-all-done.9 = bf16[8,136,2048]{2,1,0:T(8,128)(2,1)} async-done(((bf16[8,136,2048]{2,1,0:T(8,128)(2,1)}), bf16[8,136,2048]{2,1,0:T(8,128)(2,1)}, u32[]{:S(2)}, u32[]{:S(2)}) %all-to-all-start.9) | async-done | bytes 4456480 | tf_op jit(solution)/shard_map/all_to_all | solution.py:586
  412.3 6.5 fusion.56
  418.8 8.5 multiply_convert_fusion.9
  431.0 5.3 fusion.48
  436.3 27.9 %all-to-all-done.7 = bf16[8,136,2048]{2,1,0:T(8,128)(2,1)} async-done(((bf16[8,136,2048]{2,1,0:T(8,128)(2,1)}), bf16[8,136,2048]{2,1,0:T(8,128)(2,1)}, u32[]{:S(2)}, u32[]{:S(2)}) %all-to-all-start.7) | async-done | bytes 4456480 | tf_op jit(solution)/shard_map/all_to_all | solution.py:586
  477.1 9.8 %convolution_add_fusion.2 = f32[2048,768]{1,0:T(8,128)} fusion(bf16[1088,2048]{1,0:T(8,128)(2,1)} %bitcast.73, bf16[1088,768]{1,0:T(8,128)(2,1)} %copy-done.146, f32[]{:T(128)S(6)} %min.33), kind=kOutput, calls=%fused_computation.111 | convolution fusion | flops 3424124928 | bytes 12419076 | tf_op jit(solution)/shard_map/dot_general | solution.py:66
  486.8 11.1 %multiply_reduce_fusion.3 = (f32[1088]{0:T(1024)S(1)}, f32[1088,2048]{1,0:T(8,128)}, bf16[1088,2048]{1,0:T(8,128)(2,1)}) fusion(f32[1088,2048]{1,0:T(8,128)} %fusion.198, bf16[1088,2048]{1,0:T(8,128)(2,1)} %bitcast.209, f32[1088]{0:T(1024)S(1)} %broadcast_add_fusion), kind=kLoop, calls=%fused_computation.85 | loop fusion | flops 11140032 | bytes 26747392 | tf_op jit(solution)/shard_map/reduce_sum | solution.py:701
  499.0 9.9 %convolution_add_fusion.3 = f32[2048,768]{1,0:T(8,128)} fusion(bf16[1088,2048]{1,0:T(8,128)(2,1)} %bitcast.73, bf16[1088,768]{1,0:T(8,128)(2,1)} %copy-done.139, f32[]{:T(128)S(6)} %min.33), kind=kOutput, calls=%fused_computation.112 | convolution fusion | flops 3424124928 | bytes 12419076 | tf_op jit(solution)/shard_map/dot_general | solution.py:66
  509.0 6.7 fusion.51
  515.6 5.2 all-to-all-done.10
  521.0 76.3 %conditional.6 = (f32[256,2048]{1,0:T(8,128)}, bf16[256,2048]{1,0:T(8,128)(2,1)}, f32[2048]{0:T(1024)S(1)}, bf16[1088,2048]{1,0:T(8,128)(2,1)}, bf16[1088,2048]{...) conditional(s32[]{:T(128)} %bitcast.41, () %tuple.80, ...), branch_computations={%region_14.15_spmd, %region_15.19_spmd} | conditional | flops 16053860352 | bytes 276182528 | solution.py:93
  521.0 5.2 fusion.223
  534.1 9.7 %multiply_reduce_fusion = (f32[1088]{0:T(1024)S(1)}, bf16[1088,2048]{1,0:T(8,128)(2,1)}) fusion(bf16[1088,2048]{1,0:T(8,128)(2,1)} %get-tuple-element.291, f32[1088]{0:T(1024)S(1)} %get-tuple-element.287, bf16[1088,768]{1,0:T(8,128)(2,1)} %get-tuple-element.288, bf16[768,2048]{1,0:T(8,128)(2,1)} %get-tuple-element.289), kind=kOutput, calls=%fused_computation | convolution fusion | flops 3433692160 | bytes 13738496 | tf_op jit(solution)/shard_map/cond/branch_1_fun/dot_general | solution.py:58
  545.0 10.3 %add_bitcast_fusion = f32[1,2048,768]{2,1,0:T(8,128)} fusion(f32[2048,768]{1,0:T(8,128)} %get-tuple-element.299, bf16[1088,2048]{1,0:T(8,128)(2,1)} %get-tuple-element.295, bf16[1088,768]{1,0:T(8,128)(2,1)S(1)} %copy-done.141), kind=kOutput, calls=%fused_computation.2 | convolution fusion | flops 3424124928 | bytes 18710528 | tf_op jit(solution)/shard_map/cond/branch_1_fun/dot_general | solution.py:66
  555.4 8.7 add_bitcast_fusion.1
  566.6 6.4 add_bitcast_fusion.2
  573.0 20.3 %collective-permute-done.1 = bf16[256,2048]{1,0:T(8,128)(2,1)S(1)} collective-permute-done((bf16[256,2048]{1,0:T(8,128)(2,1)S(1)}, bf16[256,2048]{1,0:T(8,128)(2,1)S(1)}, u32[]{:S(2)}, u32[]{:S(2)}) %collective-permute-start.1) | collective-permute-done | bytes 1048608 | tf_op jit(solution)/shard_map/cond/branch_1_fun/ppermute | solution.py:71
  597.4 33.7 %conditional.7 = (bf16[256,1024]{1,0:T(8,128)(2,1)}, f32[2048,256]{1,0:T(8,128)}, f32[256,2048]{1,0:T(8,128)}, bf16[256,2048]{1,0:T(8,128)(2,1)}, f32[32,256]{1,0:T(8,128)S(1)}, /*index=5*/f32[128]{0:T(128)S(1)}) conditional(s32[]{:T(128)} %bitcast.41, () %tuple.84, (bf16[256,2048]{1,0:T(8,128)(2,1)}, bf16[1024,2048]{1,0:T(8,128)(2,1)}, ...), branch_computations={%region_20.21_spmd, %region_21.22_spmd} | conditional | flops 2147827712 | bytes 28770656 | solution.py:93
  598.6 5.8 all-to-all-start.1
  610.7 15.3 %branch_1_fun.8 = (bf16[256,1024]{1,0:T(8,128)(2,1)}, f32[2048,256]{1,0:T(8,128)}, f32[1,128]{1,0:T(1,128)S(1)}) custom-call(s32[1]{0:T(128)} %get-tuple-element.300.at_ref, bf16[256,1024]{1,0:T(8,128)(2,1)S(1)} %get-tuple-element.301.q_ref, bf16[256,1024]{1,0:T(8,128)(2,1)S(1)} %copy-done.64, bf16[256,1024]{1,0:T(8,128)(2,1)} %convolution_convert_fusion.grad_ref, ...), custom_call_target="tpu_custom_call" | custom-call | flops 1 | bytes 1 | tf_op jit(solution)/shard_map/cond/branch_1_fun/pallas_call | solution.py:374
  626.0 5.0 fusion.217
  641.6 27.5 %conditional.8 = (bf16[256,1024]{1,0:T(8,128)(2,1)}, f32[2048,256]{1,0:T(8,128)S(1)}, bf16[256,2048]{1,0:T(8,128)(2,1)}, bf16[256,2048]{1,0:T(8,128)(2,1)}, f32[128]{0:T(128)S(1)}) conditional(s32[]{:T(128)} %bitcast.41, () %tuple.83, (bf16[256,2048]{1,0:T(8,128)(2,1)}, bf16[1024,2048]{1,0:T(8,128)(2,1)S(1)}, s32[1]{0:T(128)}, ...), branch_computations={%region_22.23_spmd, %region_23.24_spmd} | conditional | flops 2147745792 | bytes 15728721 | solution.py:93
  646.7 14.7 %branch_1_fun.9 = (bf16[256,1024]{1,0:T(8,128)(2,1)}, f32[2048,256]{1,0:T(8,128)S(1)}, f32[1,128]{1,0:T(1,128)S(1)}) custom-call(s32[1]{0:T(128)} %get-tuple-element.323.at_ref, bf16[256,1024]{1,0:T(8,128)(2,1)S(1)} %get-tuple-element.324.q_ref, bf16[256,1024]{1,0:T(8,128)(2,1)S(1)} %get-tuple-element.325.qa_ref, ...), custom_call_target="tpu_custom_call" | custom-call | flops 1 | bytes 1 | tf_op jit(solution)/shard_map/cond/branch_1_fun/pallas_call | solution.py:374
  669.1 27.2 %conditional.9 = (bf16[256,1024]{1,0:T(8,128)(2,1)}, f32[2048,256]{1,0:T(8,128)}, f32[256,2048]{1,0:T(8,128)}, bf16[256,2048]{1,0:T(8,128)(2,1)}, f32[128]{0:T(128)S(1)}) conditional(s32[]{:T(128)} %bitcast.41, () %tuple.82, (bf16[256,2048]{1,0:T(8,128)(2,1)}, bf16[1024,2048]{1,0:T(8,128)(2,1)}, s32[1]{0:T(128)}, bf16[256,1024]{1,0:T(8,128)(2,1)S(1)}, ...), branch_computations={%region_24.25_spmd, %region_25.26_spmd} | conditional | flops 2147745792 | bytes 26214564 | solution.py:93
  674.3 14.5 %branch_1_fun.10 = (bf16[256,1024]{1,0:T(8,128)(2,1)}, f32[2048,256]{1,0:T(8,128)}, f32[1,128]{1,0:T(1,128)S(1)}) custom-call(s32[1]{0:T(128)} %get-tuple-element.340.at_ref, bf16[256,1024]{1,0:T(8,128)(2,1)S(1)} %get-tuple-element.341.q_ref, bf16[256,1024]{1,0:T(8,128)(2,1)S(1)} %copy-done.62, bf16[256,1024]{1,0:T(8,128)(2,1)} %convolution_convert_fusion.2.grad_ref, ...), custom_call_target="tpu_custom_call" | custom-call | flops 1 | bytes 1 | tf_op jit(solution)/shard_map/cond/branch_1_fun/pallas_call | solution.py:374
  698.3 54.6 %conditional.10 = (bf16[256,1024]{1,0:T(8,128)(2,1)}, f32[2048,256]{1,0:T(8,128)}, f32[256,2048]{1,0:T(8,128)}, bf16[256,2048]{1,0:T(8,128)(2,1)}, f32[256,2048]...) conditional(s32[]{:T(128)} %bitcast.41, () %tuple.79, (s32[]{:T(128)}, ...), branch_computations={%region_27.28_spmd, %region_28.29_spmd} | conditional | flops 8752201728 | bytes 77922632 | solution.py:93
  698.4 5.2 fusion.221
  708.5 15.3 %branch_1_fun.11 = (bf16[256,1024]{1,0:T(8,128)(2,1)}, f32[2048,256]{1,0:T(8,128)}, f32[1,128]{1,0:T(1,128)S(1)}) custom-call(s32[1]{0:T(128)S(6)} %add.403.at_ref, bf16[256,1024]{1,0:T(8,128)(2,1)S(1)} %copy-done.42, bf16[256,1024]{1,0:T(8,128)(2,1)} %get-tuple-element.360.qa_ref, bf16[256,1024]{1,0:T(8,128)(2,1)} %convolution_convert_fusion.3.grad_ref, ...), custom_call_target="tpu_custom_call" | custom-call | flops 1 | bytes 1 | tf_op jit(solution)/shard_map/cond/branch_1_fun/pallas_call | solution.py:374
  730.1 8.8 fusion.20
  741.7 11.2 %collective-permute-done.5 = bf16[256,2048]{1,0:T(8,128)(2,1)} collective-permute-done((bf16[256,2048]{1,0:T(8,128)(2,1)}, bf16[256,2048]{1,0:T(8,128)(2,1)}, u32[]{:S(2)}, u32[]{:S(2)}) %collective-permute-start.5) | collective-permute-done | bytes 1048608 | tf_op jit(solution)/shard_map/cond/branch_1_fun/ppermute | solution.py:71
  754.3 84.5 %conditional.11 = (f32[256,2048]{1,0:T(8,128)S(1)}, f32[128]{0:T(128)S(1)}, f32[256,2048]{1,0:T(8,128)}, f32[256,2048]{1,0:T(8,128)}, f32[256,1024]{1,0:T(8,128)}, /*index=5*/bf16[2,2,2,256,256]{4,3,2,1,0:T(8,128)(2,1)}) conditional(s32[]{:T(128)} %bitcast.41, () %tuple.89, (bf16[256,2048]{1,0:T(8,128)(2,1)}, f32[256,2048]{1,0:T(8,128)}, ...), branch_computations={%region_30.31_spmd, %region_31.33_spmd} | conditional | flops 8745910272 | bytes 151334864 | solution.py:93
  760.5 7.7 convolution_convert_fusion.4
  808.7 20.2 %collective-permute-done.8 = bf16[256,2048]{1,0:T(8,128)(2,1)S(1)} collective-permute-done((bf16[256,2048]{1,0:T(8,128)(2,1)}, bf16[256,2048]{1,0:T(8,128)(2,1)S(1)}, u32[]{:S(2)}, u32[]{:S(2)}) %collective-permute-start.8) | collective-permute-done | bytes 1048608 | tf_op jit(solution)/shard_map/cond/branch_1_fun/ppermute | solution.py:71
  854.6 21.5 %collective-permute-start.35 = (bf16[2,256,256]{2,1,0:T(8,128)(2,1)S(1)}, bf16[2,256,256]{2,1,0:T(8,128)(2,1)S(1)}, u32[]{:S(2)}, u32[]{:S(2)}) collective-permute-start(bf16[2,256,256]{2,1,0:T(8,128)(2,1)S(1)} %dynamic-slice_bitcast_fusion.1), channel_id=1, source_target_pairs={{0,8},{4,12},{8,0},{12,4},{16,24},{20,28},{24,16},{28,20},{1,9},{5... | collective-permute-start | bytes 786440 | tf_op jit(solution)/shard_map/ppermute | solution.py:76
  885.8 17.7 %all-gather = bf16[1024,256]{1,0:T(8,128)(2,1)S(1)} all-gather(bf16[256,256]{1,0:T(8,128)(2,1)S(1)} %fusion.104), channel_id=2, replica_groups=mesh['dp'=8,'mp'=4] {'mp'}, dimensions={0}, use_global_device_ids=true | all-gather | bytes 655360 | tf_op jit(solution)/shard_map/all_gather | solution.py:867
  906.9 17.6 %collective-permute-done.28 = bf16[256,2048]{1,0:T(8,128)(2,1)S(1)} collective-permute-done((bf16[256,2048]{1,0:T(8,128)(2,1)S(1)}, bf16[256,2048]{1,0:T(8,128)(2,1)S(1)}, u32[]{:S(2)}, u32[]{:S(2)}) %collective-permute-start.28) | collective-permute-done | bytes 1048608 | tf_op jit(solution)/shard_map/ppermute | solution.py:71
  (589 shorter events, 334.1 us)
Async XLA Ops:
  7.2 354.9 %copy-start = (bf16[1,2048,768]{2,1,0:T(8,128)(2,1)S(1)}, bf16[1,2048,768]{2,1,0:T(8,128)(2,1)}, u32[]{:S(2)}) copy-start(bf16[1,2048,768]{2,1,0:T(8,128)(2,1)} %param.36) | copy-start | bytes 9437188
  7.2 47.1 %all-gather.5.cloned.1.call-start = ((), (), s32[]{:S(2)}) async-start(), calls=%async_computation.13 | async-start | bytes 5898240 | tf_op jit(solution)/shard_map/all_gather | solution.py:509
  14.9 28.7 %collective-permute-start.13 = (bf16[256,2048]{1,0:T(8,128)(2,1)}, bf16[256,2048]{1,0:T(8,128)(2,1)}, u32[]{:S(2)}, u32[]{:S(2)}) collective-permute-start(bf16[256,2048]{1,0:T(8,128)(2,1)} %fusion.78), channel_id=1, source_target_pairs={{0,1},{1,2},{2,3},{3,0},{4,5},{5,6},{6,7},{7,4},{8,9},{9,10},{10,1... | collective-permute-start | bytes 3145736 | tf_op jit(solution)/shard_map/ppermute | solution.py:71
  18.8 27.0 %all-to-all-start.3 = ((bf16[4,8,256]{2,1,0:T(8,128)(2,1)}), bf16[4,8,256]{2,1,0:T(8,128)(2,1)S(1)}, u32[]{:S(2)}, u32[]{:S(2)}) async-start(bf16[4,8,256]{2,1,0:T(8,128)(2,1)} %bitcast.288), calls=%async_computation.3 | async-start | bytes 32768 | tf_op jit(solution)/shard_map/all_to_all | solution.py:543
  22.7 123.6 %all-gather.7.cloned.1.call-start = ((), (), s32[]{:S(2)}) async-start(), calls=%async_computation.14 | async-start | bytes 4718592 | tf_op jit(solution)/shard_map/all_gather | solution.py:523
  24.0 241.4 %copy-start.77 = (s32[1088]{0:T(1024)}, s32[1088]{0:T(1024)S(1)}, u32[]{:S(2)}) copy-start(s32[1088]{0:T(1024)S(1)} %broadcast_add_fusion.1) | copy-start | bytes 13060
  24.0 241.4 %copy-start.79 = (s32[1088]{0:T(1024)}, s32[1088]{0:T(1024)S(1)}, u32[]{:S(2)}) copy-start(s32[1088]{0:T(1024)S(1)} %iota_divide_fusion) | copy-start | bytes 13060
  24.0 241.4 %copy-start.105 = (pred[1088]{0:T(1024)(128)(4,1)}, pred[1088]{0:T(1024)(128)(4,1)S(1)}, u32[]{:S(2)}) copy-start(pred[1088]{0:T(1024)(128)(4,1)S(1)} %fusion.160) | copy-start | bytes 3268
  43.7 26.9 %collective-permute-start.14 = (bf16[256,2048]{1,0:T(8,128)(2,1)}, bf16[256,2048]{1,0:T(8,128)(2,1)}, u32[]{:S(2)}, u32[]{:S(2)}) collective-permute-start(bf16[256,2048]{1,0:T(8,128)(2,1)} %collective-permute-done.13), channel_id=1, source_target_pairs={{0,1},{1,2},{2,3},{3,0},{4,5},{5,6},{6,7},{7,4},{8,9},{9,10},{10,1... | collective-permute-start | bytes 3145736 | tf_op jit(solution)/shard_map/ppermute | solution.py:71
  45.8 95.9 %all-to-all-start.4 = ((f32[32,2,256]{2,1,0:T(2,128)}), f32[32,2,256]{2,1,0:T(2,128)S(1)}, u32[]{:S(2)}, u32[]{:S(2)}) async-start(f32[32,2,256]{2,1,0:T(2,128)} %copy.59), calls=%async_computation.4 | async-start | bytes 131072 | tf_op jit(solution)/shard_map/all_to_all | solution.py:550
  72.9 24.8 %collective-permute-start.15 = (bf16[256,2048]{1,0:T(8,128)(2,1)}, bf16[256,2048]{1,0:T(8,128)(2,1)}, u32[]{:S(2)}, u32[]{:S(2)}) collective-permute-start(bf16[256,2048]{1,0:T(8,128)(2,1)} %add_convert_fusion.7), channel_id=1, source_target_pairs={{0,1},{1,2},{2,3},{3,0},{4,5},{5,6},{6,7},{7,4},{8,9},{9,10},{10,1... | collective-permute-start | bytes 3145736 | tf_op jit(solution)/shard_map/ppermute | solution.py:71
  101.3 24.0 %collective-permute-start.17 = (bf16[256,2048]{1,0:T(8,128)(2,1)S(1)}, bf16[256,2048]{1,0:T(8,128)(2,1)}, u32[]{:S(2)}, u32[]{:S(2)}) collective-permute-start(bf16[256,2048]{1,0:T(8,128)(2,1)S(1)} %add_convert_fusion.6), channel_id=1, source_target_pairs={{0,1},{1,2},{2,3},{3,0},{4,5},{5,6},{6,7},{7,4},{8,9},{9,10},{10,1... | collective-permute-start | bytes 3145736 | tf_op jit(solution)/shard_map/ppermute | solution.py:71
  110.1 3.8 collective-permute-start.16
  125.2 27.5 %collective-permute-start.18 = (bf16[256,2048]{1,0:T(8,128)(2,1)}, bf16[256,2048]{1,0:T(8,128)(2,1)}, u32[]{:S(2)}, u32[]{:S(2)}) collective-permute-start(bf16[256,2048]{1,0:T(8,128)(2,1)} %collective-permute-done.17), channel_id=1, source_target_pairs={{0,1},{1,2},{2,3},{3,0},{4,5},{5,6},{6,7},{7,4},{8,9},{9,10},{10,1... | collective-permute-start | bytes 3145736 | tf_op jit(solution)/shard_map/ppermute | solution.py:71
  141.7 92.6 %all-to-all-start.5 = ((bf16[8,136,2048]{2,1,0:T(8,128)(2,1)}), bf16[8,136,2048]{2,1,0:T(8,128)(2,1)}, u32[]{:S(2)}, u32[]{:S(2)}) async-start(bf16[8,136,2048]{2,1,0:T(8,128)(2,1)} %bitcast.298), calls=%async_computation.5 | async-start | bytes 8912896 | tf_op jit(solution)/shard_map/all_to_all | solution.py:586
  150.9 28.2 %collective-permute-start.20 = (bf16[256,2048]{1,0:T(8,128)(2,1)}, bf16[256,2048]{1,0:T(8,128)(2,1)}, u32[]{:S(2)}, u32[]{:S(2)}) collective-permute-start(bf16[256,2048]{1,0:T(8,128)(2,1)} %convolution_convert_fusion.10), channel_id=1, source_target_pairs={{0,1},{1,2},{2,3},{3,0},{4,5},{5,6},{6,7},{7,4},{8,9},{9,10},{10,1... | collective-permute-start | bytes 3145736 | tf_op jit(solution)/shard_map/ppermute | solution.py:71
  163.3 38.1 %collective-permute-start.19 = (bf16[256,2048]{1,0:T(8,128)(2,1)}, bf16[256,2048]{1,0:T(8,128)(2,1)S(1)}, u32[]{:S(2)}, u32[]{:S(2)}) collective-permute-start(bf16[256,2048]{1,0:T(8,128)(2,1)} %collective-permute-done.18), channel_id=1, source_target_pairs={{0,1},{1,2},{2,3},{3,0},{4,5},{5,6},{6,7},{7,4},{8,9},{9,10},{10,1... | collective-permute-start | bytes 3145736 | tf_op jit(solution)/shard_map/ppermute | solution.py:71
  183.8 39.9 %collective-permute-start.21 = (bf16[256,2048]{1,0:T(8,128)(2,1)}, bf16[256,2048]{1,0:T(8,128)(2,1)}, u32[]{:S(2)}, u32[]{:S(2)}) collective-permute-start(bf16[256,2048]{1,0:T(8,128)(2,1)} %fusion.69), channel_id=1, source_target_pairs={{0,1},{1,2},{2,3},{3,0},{4,5},{5,6},{6,7},{7,4},{8,9},{9,10},{10,1... | collective-permute-start | bytes 3145736 | tf_op jit(solution)/shard_map/ppermute | solution.py:71
  228.5 27.0 %collective-permute-start.22 = (bf16[256,2048]{1,0:T(8,128)(2,1)}, bf16[256,2048]{1,0:T(8,128)(2,1)}, u32[]{:S(2)}, u32[]{:S(2)}) collective-permute-start(bf16[256,2048]{1,0:T(8,128)(2,1)} %fusion.68), channel_id=1, source_target_pairs={{0,1},{1,2},{2,3},{3,0},{4,5},{5,6},{6,7},{7,4},{8,9},{9,10},{10,1... | collective-permute-start | bytes 3145736 | tf_op jit(solution)/shard_map/ppermute | solution.py:71
  234.3 59.7 %all-to-all-start.8 = ((bf16[8,136,2048]{2,1,0:T(8,128)(2,1)}), bf16[8,136,2048]{2,1,0:T(8,128)(2,1)}, u32[]{:S(2)}, u32[]{:S(2)}) async-start(bf16[8,136,2048]{2,1,0:T(8,128)(2,1)} %bitcast.299), calls=%async_computation.8 | async-start | bytes 8912896 | tf_op jit(solution)/shard_map/all_to_all | solution.py:586
  261.7 26.2 %collective-permute-start.23 = (bf16[256,2048]{1,0:T(8,128)(2,1)}, bf16[256,2048]{1,0:T(8,128)(2,1)}, u32[]{:S(2)}, u32[]{:S(2)}) collective-permute-start(bf16[256,2048]{1,0:T(8,128)(2,1)} %get-tuple-element.559), channel_id=1, source_target_pairs={{0,1},{1,2},{2,3},{3,0},{4,5},{5,6},{6,7},{7,4},{8,9},{9,10},{10,1... | collective-permute-start | bytes 3145736 | tf_op jit(solution)/shard_map/ppermute | solution.py:71
  287.9 25.1 %collective-permute-start.24 = (bf16[256,2048]{1,0:T(8,128)(2,1)}, bf16[256,2048]{1,0:T(8,128)(2,1)}, u32[]{:S(2)}, u32[]{:S(2)}) collective-permute-start(bf16[256,2048]{1,0:T(8,128)(2,1)} %collective-permute-done.23), channel_id=1, source_target_pairs={{0,1},{1,2},{2,3},{3,0},{4,5},{5,6},{6,7},{7,4},{8,9},{9,10},{10,1... | collective-permute-start | bytes 3145736 | tf_op jit(solution)/shard_map/ppermute | solution.py:71
  294.1 56.5 %all-to-all-start.6 = ((bf16[8,136,2048]{2,1,0:T(8,128)(2,1)}), bf16[8,136,2048]{2,1,0:T(8,128)(2,1)}, u32[]{:S(2)}, u32[]{:S(2)}) async-start(bf16[8,136,2048]{2,1,0:T(8,128)(2,1)} %bitcast.301), calls=%async_computation.6 | async-start | bytes 8912896 | tf_op jit(solution)/shard_map/all_to_all | solution.py:586
  298.6 454.3 %all-gather.9.cloned.1.call-start = ((), (), s32[]{:S(2)}) async-start(), calls=%async_computation.15 | async-start | bytes 5242880 | tf_op jit(solution)/shard_map/all_gather | solution.py:657
  313.1 24.3 %collective-permute-start.25 = (bf16[256,2048]{1,0:T(8,128)(2,1)}, bf16[256,2048]{1,0:T(8,128)(2,1)S(1)}, u32[]{:S(2)}, u32[]{:S(2)}) collective-permute-start(bf16[256,2048]{1,0:T(8,128)(2,1)} %collective-permute-done.24), channel_id=1, source_target_pairs={{0,1},{1,2},{2,3},{3,0},{4,5},{5,6},{6,7},{7,4},{8,9},{9,10},{10,1... | collective-permute-start | bytes 3145736 | tf_op jit(solution)/shard_map/ppermute | solution.py:71
  350.6 56.9 %all-to-all-start.9 = ((bf16[8,136,2048]{2,1,0:T(8,128)(2,1)}), bf16[8,136,2048]{2,1,0:T(8,128)(2,1)}, u32[]{:S(2)}, u32[]{:S(2)}) async-start(bf16[8,136,2048]{2,1,0:T(8,128)(2,1)} %bitcast.302), calls=%async_computation.9 | async-start | bytes 8912896 | tf_op jit(solution)/shard_map/all_to_all | solution.py:586
  407.5 56.7 %all-to-all-start.7 = ((bf16[8,136,2048]{2,1,0:T(8,128)(2,1)}), bf16[8,136,2048]{2,1,0:T(8,128)(2,1)}, u32[]{:S(2)}, u32[]{:S(2)}) async-start(bf16[8,136,2048]{2,1,0:T(8,128)(2,1)} %bitcast.303), calls=%async_computation.7 | async-start | bytes 8912896 | tf_op jit(solution)/shard_map/all_to_all | solution.py:586
  464.2 56.7 %all-to-all-start.10 = ((bf16[8,136,2048]{2,1,0:T(8,128)(2,1)}), bf16[8,136,2048]{2,1,0:T(8,128)(2,1)}, u32[]{:S(2)}, u32[]{:S(2)}) async-start(bf16[8,136,2048]{2,1,0:T(8,128)(2,1)} %bitcast.300), calls=%async_computation.10 | async-start | bytes 8912896 | tf_op jit(solution)/shard_map/all_to_all | solution.py:586
  476.6 39.0 %collective-permute-start.26 = (bf16[256,2048]{1,0:T(8,128)(2,1)S(1)}, bf16[256,2048]{1,0:T(8,128)(2,1)S(1)}, u32[]{:S(2)}, u32[]{:S(2)}) collective-permute-start(bf16[256,2048]{1,0:T(8,128)(2,1)S(1)} %slice.402), channel_id=1, source_target_pairs={{0,1},{1,2},{2,3},{3,0},{4,5},{5,6},{6,7},{7,4},{8,9},{9,10},{10,1... | collective-permute-start | bytes 3145736 | tf_op jit(solution)/shard_map/ppermute | solution.py:71
  520.9 76.4 %copy-start.5 = (f32[1024,128]{1,0:T(8,128)S(1)}, f32[1024,128]{1,0:T(8,128)}, u32[]{:S(2)}) copy-start(f32[1024,128]{1,0:T(8,128)} %pad_maximum_fusion.4.cos_ref) | copy-start | bytes 1572868
  520.9 76.4 %copy-start.9 = (f32[1024,128]{1,0:T(8,128)S(1)}, f32[1024,128]{1,0:T(8,128)}, u32[]{:S(2)}) copy-start(f32[1024,128]{1,0:T(8,128)} %pad_maximum_fusion.5.sin_ref) | copy-start | bytes 1572868
  520.9 76.4 %copy-start.11 = (bf16[2048,256]{1,0:T(8,128)(2,1)S(1)}, bf16[2048,256]{1,0:T(8,128)(2,1)}, u32[]{:S(2)}) copy-start(bf16[2048,256]{1,0:T(8,128)(2,1)} %pad_maximum_fusion.2.kv_ref) | copy-start | bytes 3145732
  520.9 76.4 %copy-start.13 = (bf16[2048,128]{1,0:T(8,128)(2,1)S(1)}, bf16[2048,128]{1,0:T(8,128)(2,1)}, u32[]{:S(2)}) copy-start(bf16[2048,128]{1,0:T(8,128)(2,1)} %select_convert_fusion.ka_ref) | copy-start | bytes 1572868
  529.5 34.6 %collective-permute-start = (bf16[256,2048]{1,0:T(8,128)(2,1)}, bf16[256,2048]{1,0:T(8,128)(2,1)}, u32[]{:S(2)}, u32[]{:S(2)}) collective-permute-start(bf16[256,2048]{1,0:T(8,128)(2,1)} %fusion.3), channel_id=1, source_target_pairs={{0,1},{1,2},{2,3},{3,0},{4,5},{5,6},{6,7},{7,4},{8,9},{9,10},{10,1... | collective-permute-start | bytes 3145736 | tf_op jit(solution)/shard_map/cond/branch_1_fun/ppermute | solution.py:71
  529.5 67.6 %all-to-all-start = ((bf16[8,136,2048]{2,1,0:T(8,128)(2,1)}), bf16[8,136,2048]{2,1,0:T(8,128)(2,1)}, u32[]{:S(2)}, u32[]{:S(2)}) async-start(bf16[8,136,2048]{2,1,0:T(8,128)(2,1)} %bitcast.291), calls=%async_computation | async-start | bytes 8912896 | tf_op jit(solution)/shard_map/cond/branch_1_fun/all_to_all | solution.py:586
  565.8 27.6 %collective-permute-start.1 = (bf16[256,2048]{1,0:T(8,128)(2,1)S(1)}, bf16[256,2048]{1,0:T(8,128)(2,1)S(1)}, u32[]{:S(2)}, u32[]{:S(2)}) collective-permute-start(bf16[256,2048]{1,0:T(8,128)(2,1)S(1)} %fusion.4), channel_id=1, source_target_pairs={{0,1},{1,2},{2,3},{3,0},{4,5},{5,6},{6,7},{7,4},{8,9},{9,10},{10,1... | collective-permute-start | bytes 3145736 | tf_op jit(solution)/shard_map/cond/branch_1_fun/ppermute | solution.py:71
  597.4 33.6 %collective-permute-start.2 = (bf16[256,2048]{1,0:T(8,128)(2,1)}, bf16[256,2048]{1,0:T(8,128)(2,1)}, u32[]{:S(2)}, u32[]{:S(2)}) collective-permute-start(bf16[256,2048]{1,0:T(8,128)(2,1)} %get-tuple-element.303), channel_id=1, source_target_pairs={{0,1},{1,2},{2,3},{3,0},{4,5},{5,6},{6,7},{7,4},{8,9},{9,10},{10,1... | collective-permute-start | bytes 3145736 | tf_op jit(solution)/shard_map/cond/branch_1_fun/ppermute | solution.py:71
  598.6 32.4 %all-to-all-start.1 = ((f32[32,1,256]{2,1,0:T(1,128)}), f32[32,1,256]{2,1,0:T(1,128)S(1)}, u32[]{:S(2)}, u32[]{:S(2)}) async-start(f32[32,1,256]{2,1,0:T(1,128)} %all_to_all.28), calls=%async_computation.1 | async-start | bytes 65536 | tf_op jit(solution)/shard_map/cond/branch_1_fun/all_to_all | solution.py:767
  631.0 65.3 %all-to-all-start.11 = ((bf16[8,136,2048]{2,1,0:T(8,128)(2,1)}), bf16[8,136,2048]{2,1,0:T(8,128)(2,1)}, u32[]{:S(2)}, u32[]{:S(2)}) async-start(bf16[8,136,2048]{2,1,0:T(8,128)(2,1)} %bitcast.91), calls=%async_computation.11 | async-start | bytes 8912896 | tf_op jit(solution)/shard_map/all_to_all | solution.py:586
  635.6 290.3 %reduce-scatter.2.cloned.1.call-start = ((), (), s32[]{:S(2)}) async-start(), calls=%async_computation.16 | async-start | bytes 4718592 | tf_op jit(solution)/shard_map/reduce_scatter | solution.py:803
  641.6 27.5 %collective-permute-start.3 = (bf16[256,2048]{1,0:T(8,128)(2,1)}, bf16[256,2048]{1,0:T(8,128)(2,1)}, u32[]{:S(2)}, u32[]{:S(2)}) collective-permute-start(bf16[256,2048]{1,0:T(8,128)(2,1)} %get-tuple-element.326), channel_id=1, source_target_pairs={{0,1},{1,2},{2,3},{3,0},{4,5},{5,6},{6,7},{7,4},{8,9},{9,10},{10,1... | collective-permute-start | bytes 3145736 | tf_op jit(solution)/shard_map/cond/branch_1_fun/ppermute | solution.py:71
  669.1 27.1 %collective-permute-start.4 = (bf16[256,2048]{1,0:T(8,128)(2,1)}, bf16[256,2048]{1,0:T(8,128)(2,1)}, u32[]{:S(2)}, u32[]{:S(2)}) collective-permute-start(bf16[256,2048]{1,0:T(8,128)(2,1)} %get-tuple-element.343), channel_id=1, source_target_pairs={{0,1},{1,2},{2,3},{3,0},{4,5},{5,6},{6,7},{7,4},{8,9},{9,10},{10,1... | collective-permute-start | bytes 3145736 | tf_op jit(solution)/shard_map/cond/branch_1_fun/ppermute | solution.py:71
  704.7 34.2 %collective-permute-start.6 = (bf16[256,2048]{1,0:T(8,128)(2,1)}, bf16[256,2048]{1,0:T(8,128)(2,1)}, u32[]{:S(2)}, u32[]{:S(2)}) collective-permute-start(bf16[256,2048]{1,0:T(8,128)(2,1)} %slice.400), channel_id=1, source_target_pairs={{0,1},{1,2},{2,3},{3,0},{4,5},{5,6},{6,7},{7,4},{8,9},{9,10},{10,1... | collective-permute-start | bytes 3145736 | tf_op jit(solution)/shard_map/cond/branch_1_fun/ppermute | solution.py:71
  704.7 48.3 %collective-permute-start.5 = (bf16[256,2048]{1,0:T(8,128)(2,1)}, bf16[256,2048]{1,0:T(8,128)(2,1)}, u32[]{:S(2)}, u32[]{:S(2)}) collective-permute-start(bf16[256,2048]{1,0:T(8,128)(2,1)} %get-tuple-element.374), channel_id=1, source_target_pairs={{0,1},{1,2},{2,3},{3,0},{4,5},{5,6},{6,7},{7,4},{8,9},{9,10},{10,1... | collective-permute-start | bytes 3145736 | tf_op jit(solution)/shard_map/cond/branch_1_fun/ppermute | solution.py:71
  754.3 84.6 %copy-start.20 = (bf16[256,2048]{1,0:T(8,128)(2,1)S(1)}, bf16[256,2048]{1,0:T(8,128)(2,1)}, u32[]{:S(2)}) copy-start(bf16[256,2048]{1,0:T(8,128)(2,1)} %param.27) | copy-start | bytes 3145732
  754.3 84.6 %copy-start.69 = (f32[2048]{0:T(1024)S(1)}, f32[2048]{0:T(1024)}, u32[]{:S(2)}) copy-start(f32[2048]{0:T(1024)} %param.28) | copy-start | bytes 24580
  754.3 84.6 %copy-start.85 = (f32[256]{0:T(256)S(1)}, f32[256]{0:T(256)}, u32[]{:S(2)}) copy-start(f32[256]{0:T(256)} %copy-done.84) | copy-start | bytes 3076
  755.8 26.8 %collective-permute-start.9 = (bf16[1024,256]{1,0:T(8,128)(2,1)S(1)}, bf16[1024,256]{1,0:T(8,128)(2,1)S(1)}, u32[]{:S(2)}, u32[]{:S(2)}) collective-permute-start(bf16[1024,256]{1,0:T(8,128)(2,1)S(1)} %slice.401), channel_id=1, source_target_pairs={{4,0},{12,8},{20,16},{28,24},{5,1},{13,9},{21,17},{29,25},{6,2},{1... | collective-permute-start | bytes 1572872 | tf_op jit(solution)/shard_map/cond/branch_1_fun/ppermute | solution.py:811
  760.5 37.8 %collective-permute-start.7 = (bf16[256,2048]{1,0:T(8,128)(2,1)}, bf16[256,2048]{1,0:T(8,128)(2,1)}, u32[]{:S(2)}, u32[]{:S(2)}) collective-permute-start(bf16[256,2048]{1,0:T(8,128)(2,1)} %add_convert_fusion.1), channel_id=1, source_target_pairs={{0,1},{1,2},{2,3},{3,0},{4,5},{5,6},{6,7},{7,4},{8,9},{9,10},{10,1... | collective-permute-start | bytes 3145736 | tf_op jit(solution)/shard_map/cond/branch_1_fun/ppermute | solution.py:71
  768.2 66.2 %all-to-all-start.2 = ((bf16[8,256,1024]{2,1,0:T(8,128)(2,1)}), bf16[8,256,1024]{2,1,0:T(8,128)(2,1)}, u32[]{:S(2)}, u32[]{:S(2)}) async-start(bf16[8,256,1024]{2,1,0:T(8,128)(2,1)} %bitcast.304), calls=%async_computation.2 | async-start | bytes 8388608 | tf_op jit(solution)/shard_map/cond/branch_1_fun/all_to_all | solution.py:801
  785.9 22.4 %collective-permute-start.10 = (bf16[256,256]{1,0:T(8,128)(2,1)}, bf16[256,256]{1,0:T(8,128)(2,1)S(1)}, u32[]{:S(2)}, u32[]{:S(2)}) collective-permute-start(bf16[256,256]{1,0:T(8,128)(2,1)} %get-tuple-element.399), channel_id=1, source_target_pairs={{0,3},{1,0},{2,1},{3,2},{4,7},{5,4},{6,5},{7,6},{8,11},{9,8},{10,9... | collective-permute-start | bytes 393224 | tf_op jit(solution)/shard_map/cond/branch_1_fun/ppermute | solution.py:135
  792.3 16.1 %collective-permute-start.11 = (bf16[256,256]{1,0:T(8,128)(2,1)}, bf16[256,256]{1,0:T(8,128)(2,1)S(1)}, u32[]{:S(2)}, u32[]{:S(2)}) collective-permute-start(bf16[256,256]{1,0:T(8,128)(2,1)} %get-tuple-element.402), channel_id=1, source_target_pairs={{0,2},{1,3},{2,0},{3,1},{4,6},{5,7},{6,4},{7,5},{8,10},{9,11},{10,... | collective-permute-start | bytes 393224 | tf_op jit(solution)/shard_map/cond/branch_1_fun/ppermute | solution.py:135
  795.0 13.5 %collective-permute-start.12 = (bf16[256,256]{1,0:T(8,128)(2,1)}, bf16[256,256]{1,0:T(8,128)(2,1)S(1)}, u32[]{:S(2)}, u32[]{:S(2)}) collective-permute-start(bf16[256,256]{1,0:T(8,128)(2,1)} %get-tuple-element.405), channel_id=1, source_target_pairs={{0,1},{1,2},{2,3},{3,0},{4,5},{5,6},{6,7},{7,4},{8,9},{9,10},{10,1... | collective-permute-start | bytes 393224 | tf_op jit(solution)/shard_map/cond/branch_1_fun/ppermute | solution.py:135
  801.5 27.3 %collective-permute-start.8 = (bf16[256,2048]{1,0:T(8,128)(2,1)}, bf16[256,2048]{1,0:T(8,128)(2,1)S(1)}, u32[]{:S(2)}, u32[]{:S(2)}) collective-permute-start(bf16[256,2048]{1,0:T(8,128)(2,1)} %add_convert_fusion), channel_id=1, source_target_pairs={{0,1},{1,2},{2,3},{3,0},{4,5},{5,6},{6,7},{7,4},{8,9},{9,10},{10,1... | collective-permute-start | bytes 3145736 | tf_op jit(solution)/shard_map/cond/branch_1_fun/ppermute | solution.py:71
  839.6 1.3 collective-permute-start.29
  840.9 3.8 collective-permute-start.30
  843.5 9.9 %collective-permute-start.34 = (bf16[2,2,256,256]{3,2,1,0:T(8,128)(2,1)S(1)}, bf16[2,2,256,256]{3,2,1,0:T(8,128)(2,1)S(1)}, u32[]{:S(2)}, u32[]{:S(2)}) collective-permute-start(bf16[2,2,256,256]{3,2,1,0:T(8,128)(2,1)S(1)} %dynamic-slice_bitcast_fusion), channel_id=1, source_target_pairs={{0,4},{4,0},{8,12},{12,8},{16,20},{20,16},{24,28},{28,24},{1,5},{5... | collective-permute-start | bytes 1572872 | tf_op jit(solution)/shard_map/ppermute | solution.py:76
  844.8 4.4 collective-permute-start.31
  849.2 3.8 collective-permute-start.32
  849.7 54.0 %collective-permute-start.27 = (bf16[256,2048]{1,0:T(8,128)(2,1)S(1)}, bf16[256,2048]{1,0:T(8,128)(2,1)S(1)}, u32[]{:S(2)}, u32[]{:S(2)}) collective-permute-start(bf16[256,2048]{1,0:T(8,128)(2,1)S(1)} %add_convert_fusion.4), channel_id=1, source_target_pairs={{0,1},{1,2},{2,3},{3,0},{4,5},{5,6},{6,7},{7,4},{8,9},{9,10},{10,1... | collective-permute-start | bytes 3145736 | tf_op jit(solution)/shard_map/ppermute | solution.py:71
  853.0 26.7 %collective-permute-start.33 = (f32[4352]{0:T(1024)S(1)}, f32[4352]{0:T(1024)S(1)}, u32[]{:S(2)}, u32[]{:S(2)}) collective-permute-start(f32[4352]{0:T(1024)S(1)} %add.594), channel_id=1, source_target_pairs={{0,2},{1,3},{2,0},{3,1},{4,6},{5,7},{6,4},{7,5},{8,10},{9,11},{10,... | collective-permute-start | bytes 52232 | tf_op jit(solution)/shard_map/ppermute | solution.py:76
  854.6 25.9 %collective-permute-start.35 = (bf16[2,256,256]{2,1,0:T(8,128)(2,1)S(1)}, bf16[2,256,256]{2,1,0:T(8,128)(2,1)S(1)}, u32[]{:S(2)}, u32[]{:S(2)}) collective-permute-start(bf16[2,256,256]{2,1,0:T(8,128)(2,1)S(1)} %dynamic-slice_bitcast_fusion.1), channel_id=1, source_target_pairs={{0,8},{4,12},{8,0},{12,4},{16,24},{20,28},{24,16},{28,20},{1,9},{5... | collective-permute-start | bytes 786440 | tf_op jit(solution)/shard_map/ppermute | solution.py:76
  880.6 5.1 collective-permute-start.36
  905.8 18.7 %collective-permute-start.28 = (bf16[256,2048]{1,0:T(8,128)(2,1)S(1)}, bf16[256,2048]{1,0:T(8,128)(2,1)S(1)}, u32[]{:S(2)}, u32[]{:S(2)}) collective-permute-start(bf16[256,2048]{1,0:T(8,128)(2,1)S(1)} %add_convert_fusion.3), channel_id=1, source_target_pairs={{0,1},{1,2},{2,3},{3,0},{4,5},{5,6},{6,7},{7,4},{8,9},{9,10},{10,1... | collective-permute-start | bytes 3145736 | tf_op jit(solution)/shard_map/ppermute | solution.py:71
  (149 other events, 1354.8 us)
Sparse Core Ops, SparseCore 0:
  10.5 43.8 all-gather.4
  56.2 37.6 all-gather.6
  342.2 78.3 all-gather.8
  840.6 51.7 reduce-scatter.1

commit v4 on v3

--- a/solution.py
+++ b/solution.py
@@ -99,21 +99,14 @@
     return (array.astype(FULL) + sum(nought(o) for o in others)).astype(array.dtype)
 
 
-def sum_scatter_rows(rows, order):
-    me = lax.axis_index("dp")
-    count = len(order)
-    size = rows.shape[0] >> count
-    parts = rows.reshape((2,) * count + (size, rows.shape[1]))
-    axis_of = {bit: count - bit.bit_length() for bit in order}
-    left = sorted(order, reverse=True)
-    for bit in order:
-        axis = left.index(bit)
-        side = (me // bit) % 2
-        own = lax.dynamic_index_in_dim(parts, side, axis, keepdims=False)
-        other = lax.dynamic_index_in_dim(parts, 1 - side, axis, keepdims=False)
-        parts = (own.astype(FULL) + swap(other, "dp", bit).astype(FULL)).astype(LOW)
-        left.remove(bit)
-    return parts
+def half_rows(rows, bit):
+    side = (lax.axis_index("dp") // bit) % 2
+    size = lax.axis_size("dp")
+    parts = rows.reshape((-1, 2, rows.shape[0] * bit // size, rows.shape[1]))
+    own = lax.dynamic_index_in_dim(parts, side, 1, keepdims=False)
+    other = lax.dynamic_index_in_dim(parts, 1 - side, 1, keepdims=False)
+    total = own.astype(FULL) + swap(other, "dp", bit).astype(FULL)
+    return total.astype(LOW).reshape((-1, rows.shape[1]))
 
 
 def ring_sums(parts):
@@ -710,11 +703,16 @@
     outs = [expert_outs(g, late) for g in range(len(groups) - 1)]
     own_part = resid_parts[0]
 
+    def add_weights(k, tie=0.0):
+        left, right = pairs[k]
+        return row_major(contract_first(left[-1], right[-1]) + (weight_parts[k] + tie))
+
     def sum_work():
         first_out = plane_turn(outs[0][0])
         parts = place(came, len(groups) - 1)
         total = parts[0] + passed.astype(FULL)
         for part in parts[1:] + [own_part]:
+            tie = nought(total)
             total = part + ring_shift(total.astype(LOW)).astype(FULL)
         grad_norm, gain_part = norm_two_back(total)
         grad = cotangent.astype(FULL) + grad_norm
@@ -723,10 +721,7 @@
             grad.astype(LOW),
             gain_part,
             first_out,
-            [
-                row_major(contract_first(left[-1], right[-1]) + part)
-                for (left, right), part in zip(pairs, weight_parts)
-            ],
+            [add_weights(0), add_weights(1, tie), add_weights(2, tie)],
             expert_outs(len(groups) - 1, 0.0),
         )
 
@@ -738,36 +733,41 @@
     gate_grad_parts = [
         found[:, k * row_count : (k + 1) * row_count] for _, found in outs for k in range(group_size)
     ]
+    spread = jnp.stack(
+        [
+            sum(jnp.where(places[k] == p, gate_grad_parts[k], 0.0) for k in blocks)
+            for p in blocks
+        ],
+        axis=1,
+    ).reshape(expert_count, row_count)
 
     kv_grads = jnp.zeros((2 * sequence_length, 2 * head_width), FULL)
     query_low, input_parts = [], []
     query_gain_part = 0.0
     for b in blocks:
-        ended = b == mp_count - 1
-        spot = pinned(spots[b], *out_came[1:]) if ended else spots[b]
-
+        if b == mp_count - 1:
+
+            pin = sum(nought(rows) for rows in out_came[1:])
+
+            def out_weight_work():
+                return (
+                    contract_first(joined_rows(attended), joined_rows(back)).astype(LOW),
+                    ring_shift((input_parts[1] + pin).astype(LOW)),
+                    place(out_came[0], 0),
+                )
+
+            out_weight_part, input_passed, out_parts = stage(flag, out_weight_work)
+            out_weight_grad = lax.psum_scatter(
+                out_weight_part, "dp", scatter_dimension=1, tiled=True
+            )
         def block_work():
-            extra = ()
-            if not ended:
-                extra += (ring_shift(back[b]),)
+            if b < mp_count - 1:
+                sent = ring_shift(back[b])
             else:
-                extra += (ring_shift(input_parts[1].astype(LOW)),)
-                out_part = place(out_came[0], 0)
-                extra += (out_part[0], ring_shift(out_part[1].astype(LOW)))
-                extra += (contract_first(joined_rows(attended), joined_rows(back)).astype(LOW),)
-            if b == 0:
-                spread = jnp.stack(
-                    [
-                        sum(jnp.where(places[k] == p, gate_grad_parts[k], 0.0) for k in blocks)
-                        for p in blocks
-                    ],
-                    axis=1,
-                ).reshape(expert_count, row_count)
-                extra += (
-                    lax.all_to_all(spread, ("dp", "mp"), split_axis=0, concat_axis=0, tiled=True),
-                )
+                part = input_parts[2] + input_passed.astype(FULL)
+                sent = ring_shift(part.astype(LOW))
             low, kv, gain = attend_back(
-                spot,
+                spots[b],
                 queries[b],
                 augs[b],
                 contract_last(back[b], wo_whole).astype(LOW),
@@ -781,41 +781,30 @@
                 kv_grads,
                 score_scale,
             )
-            return (low, kv, gain, contract_last(low, wq_whole)) + extra
-
-        low_b, kv_b, gain_b, input_b, *extra = stage(flag, block_work)
-        kv_grads = kv_b
+            return low, kv, gain, contract_last(low, wq_whole), sent
+
+        low_b, kv_grads, gain_b, input_b, sent = stage(flag, block_work)
         query_low.append(low_b)
         input_parts.append(input_b)
         query_gain_part += gain_b[0]
-        if not ended:
-            back.append(extra[0])
-        if b == 0:
-            spread = extra[1]
-    input_passed, out_own, out_passed, out_weight_part = extra
-    gate_values_grad = jnp.stack(
-        [jnp.sum(jnp.where(picked[k], spread, 0.0), axis=0) for k in range(top_count)], axis=1
-    )
-
+        if b < mp_count - 1:
+            back.append(sent)
+    input_passed = sent
     def dp_turn(parts):
         return lax.all_to_all(parts, "dp", split_axis=0, concat_axis=0, tiled=True)
 
-    out_weight_grad = lax.psum_scatter(
-        out_weight_part, "dp", scatter_dimension=1, tiled=True
-    ).astype(FULL)
-    sequence_all = joined_rows(sequence)
-
-    def input_work():
-        weight_part = row_major(contract_first(sequence_all, joined_rows(query_low)).astype(LOW))
-        weight_came = dp_turn(weight_part.reshape(dp_count, shard_rows, local_width))
+    def key_work():
+        sent = input_passed
+        for part in input_parts[3:]:
+            sent = ring_shift((part + sent.astype(FULL)).astype(LOW))
         returned = lax.ppermute(
             kv_grads[:sequence_length].astype(LOW),
             "dp",
             [(i + 1, i) for i in range(0, dp_count, 2)],
         )
-        total = input_parts[2] + input_passed.astype(FULL)
-        for part in input_parts[3:] + [input_parts[0]]:
-            total = part + ring_shift(total.astype(LOW)).astype(FULL)
+        weight_part = row_major(
+            contract_first(joined_rows(sequence), joined_rows(query_low)).astype(LOW)
+        )
         kv_blocks, key_gain_part = [], 0.0
         for b in blocks:
             kv_low, gain_b = key_back(
@@ -832,54 +821,84 @@
             )
             kv_blocks.append(kv_low)
             key_gain_part += gain_b[0]
+        return sent, weight_part, kv_blocks, key_gain_part
+
+    input_passed, weight_part, kv_blocks, key_gain_part = stage(flag, key_work)
+    weight_came = dp_turn(weight_part.reshape(dp_count, shard_rows, local_width))
+
+    def input_work():
         kv_spread = jnp.zeros((mp_count, row_count, 2 * head_width), LOW)
         for b in blocks:
             kv_came = shift_by(kv_blocks[b], -b) if b else kv_blocks[0]
             kv_spread = lax.dynamic_update_index_in_dim(
                 kv_spread, kv_came, (mp_place + b) % mp_count, 0
             )
+        out_sent = ring_shift(out_parts[1].astype(LOW))
+        total = input_parts[0] + input_passed.astype(FULL)
         total += lax.dot_general(
             kv_spread.transpose(1, 0, 2).reshape(row_count, -1),
             kv_all_weights,
             (((1,), (1,)), ((), ())),
             preferred_element_type=FULL,
         )
-        out_parts = []
-        for g in range(1, len(groups)):
-            out_parts += place(out_came[g], g)
+        grad_norm, input_gain_part = norm_one_back(total)
+        gains = jnp.concatenate([moe_gain_part, query_gain_part, key_gain_part, input_gain_part])
+        kv_part = contract_first(joined_rows(sequence), joined_rows(kv_blocks)).astype(LOW)
         return (
-            row_major(weight_came),
+            row_major(grad_resid + grad_norm),
+            gains,
+            row_major(half_rows(kv_part, bits[0])),
+            [p for g in range(1, len(groups)) for p in place(out_came[g], g)],
+            out_sent,
+        )
+
+    tokens_grad, gains, kv_part, more_parts, out_passed = stage(flag, input_work)
+    out_parts += more_parts
+    out_total = out_parts[2] + out_passed.astype(FULL) + nought(out_weight_grad)
+
+    def token_work():
+        sent = ring_shift(out_total.astype(LOW))
+        total = gains
+        for bit in bits:
+            total += swap(total, "dp", bit)
+        kv_rows = kv_part
+        for bit in bits[1:]:
+            kv_rows = half_rows(kv_rows, bit)
+        return sent, total, row_major(kv_rows)
+
+    out_passed, gains, kv_rows = stage(flag, token_work)
+
+    def last_work():
+        own_cols = [kv_rows] + [shift_by(kv_rows, b) for b in blocks[1:]]
+        total = gains + sum(shift_by(gains, b) for b in blocks[1:])
+        found = lax.all_to_all(spread, ("dp", "mp"), split_axis=0, concat_axis=0, tiled=True)
+        sent = out_passed
+        for part in out_parts[3:]:
+            sent = ring_shift((part + sent.astype(FULL)).astype(LOW))
+        return (
+            row_major((resid + out_parts[0] + sent.astype(FULL)).astype(LOW)),
             total,
-            key_gain_part,
-            row_major(contract_first(sequence_all, joined_rows(kv_blocks)).astype(LOW)),
-            out_parts,
-        )
-
-    weight_came, grad_normed_one, key_gain_part, kv_part, out_parts = stage(flag, input_work)
-    out_total = out_parts[0] + out_passed.astype(FULL)
-    for part in out_parts[1:] + [out_own]:
-        out_total = part + ring_shift(out_total.astype(LOW)).astype(FULL)
-    block_out = (resid + out_total).astype(LOW)
-    grad_in_norm, input_gain_part = norm_one_back(grad_normed_one)
-    tokens_grad = grad_resid + grad_in_norm
-
-    query_weight_grad = jnp.sum(weight_came.astype(FULL), axis=0)
-    own_cols = lax.all_gather(sum_scatter_rows(kv_part, bits), "mp", axis=0).astype(FULL)
+            own_cols,
+            found,
+            row_major(jnp.sum(weight_came.astype(FULL), axis=0)),
+        )
+
+    block_out, gains, own_cols, spread, query_weight_grad = stage(flag, last_work)
+    cols_of = jnp.zeros((mp_count,) + own_cols[0].shape, LOW)
+    for b in blocks:
+        cols_of = lax.dynamic_update_index_in_dim(cols_of, own_cols[b], places[b], 0)
+    cols_of = cols_of.astype(FULL)
     kv_parts = [None] * (2 * kv_width // head_width)
     for m in blocks:
         for side in range(2):
             at = (kv_offsets[m] + side * kv_width) // head_width
-            term = own_cols[m, :, side * head_width : (side + 1) * head_width]
+            term = cols_of[m, :, side * head_width : (side + 1) * head_width]
             kv_parts[at] = term if kv_parts[at] is None else kv_parts[at] + term
     kv_weight_grad = jnp.concatenate(kv_parts, axis=1)
-
-    gains = jnp.concatenate([moe_gain_part, query_gain_part, key_gain_part, input_gain_part])
-    for bit in bits:
-        gains += swap(gains, "dp", bit)
-    step = 1
-    while step < mp_count:
-        gains += swap(gains, "mp", step)
-        step *= 2
+    gate_values_grad = jnp.stack(
+        [jnp.sum(jnp.where(picked[k], spread, 0.0), axis=0) for k in range(top_count)], axis=1
+    )
+
     ends = [model_width, model_width + head_width, model_width + 2 * head_width]
     return (
         block_out,
@@ -889,7 +908,7 @@
         kv_weight_grad,
         gains[ends[0] : ends[1]],
         gains[ends[1] : ends[2]],
-        out_weight_grad,
+        out_weight_grad.astype(FULL),
         gains[: ends[0]],
         gate_weight_grad[None],
         up_weight_grad[None],

time: 947 us -> 926 us (0.978)
  starting transfers between devices: 104 us -> 85.8 us
  blocking collectives: 17.7 us -> 0 us
  waiting for transfers between devices: 252 us -> 238 us
  local copies, waits for them, and re-layouts: 38.5 us -> 50.2 us
  other arithmetic: 100 us -> 111 us
    ppermute x24, waiting for transfers between devices: 183 us -> 151 us  [ring_shift(): lax.ppermute(shard, axis, [(i, (i + 1) % length) for i in range(length)])]
    ppermute x8 -> x6, starting transfers between devices: 25.5 us -> 5.51 us  [swap(): return lax.ppermute(shard, axis, [(i, i ^ bit) for i in range(length)])]
    all_gather x1 -> x0, blocking collectives: 17.7 us -> none  [on_device(): lax.all_gather(sum_scatter_rows(kv_part, bits), 'mp', axis=0).astype(FULL)]
    ppermute x3 -> x9, waiting for transfers between devices: 0.01 us -> 13.1 us  [shift_by(): lax.ppermute(shard, axis, [(i, (i + by) % length) for i in range(length)])]
    convert_element_type x12 -> x15, other arithmetic: 21.6 us -> 23.9 us  [the longest x1 3.57 us: token_work(): sent = ring_shift(out_total.astype(LOW))]
  transfers between devices with their start and end apart: 53 -> 57, of which waited for: 27 -> 32; matrix products, arithmetic and copies ran while one was open for 42% -> 46% of each run, Pallas kernels for 12% -> 12%
where the time goes in v4:
time: 926 us; the launch traced here: 913 us
  matrix products  288 us (31%)
  waiting for transfers between devices  238 us (26%)
  Pallas kernels  114 us (12%)
  other arithmetic  111 us (12%)
  starting transfers between devices  85.8 us (9%)
  local copies, waits for them, and re-layouts  50.2 us (5%)
  between operations  21.9 us (2%)
    ppermute x24, waiting for transfers between devices, ring_shift(): lax.ppermute(shard, axis, [(i, (i + 1) % length) for i in range(length)])  151 us
    dot_general x23, matrix products, matmul(): return jnp.dot(left, right, preferred_element_type=FULL)  113 us
    dot_general x13, matrix products, contract_first(): lax.dot_general(left, right, (((0,), (0,)), ((), ())), preferred_element_...  95.5 us
    dot_general x14, matrix products, contract_last(): lax.dot_general(left, right, (((1,), (1,)), ((), ())), preferred_element_...  67.1 us
    pallas_call x4, Pallas kernels, attend_back(): pl.pallas_call(functools.partial(attend_back_kernel, score_scale), out_sh...  59.5 us
    all_to_all x8, waiting for transfers between devices, plane_turn(): lax.all_to_all(rows.reshape(dp_count, group_rows, model_width), 'dp', spl...  58.9 us
    all_to_all x8, starting transfers between devices, plane_turn(): lax.all_to_all(rows.reshape(dp_count, group_rows, model_width), 'dp', spl...  38.9 us
    pallas_call x4, Pallas kernels, attend(): pl.pallas_call(functools.partial(attend_kernel, score_scale, docs), out_s...  33.9 us
  transfers between devices with their start and end apart: 57, of which 32 were waited for; matrix products, arithmetic and copies ran while one was open for 46% of the time, Pallas kernels for 12%

profile of v4, /device:TPU:0, one launch (start us, length us, event | category | flops | bytes accessed | tf_op | source)
XLA Modules:
  0.0 913.0 jit_solution(8753128279854918)
XLA Ops:
  32.8 11.5 %collective-permute-done.27 = bf16[256,2048]{1,0:T(8,128)(2,1)} collective-permute-done((bf16[256,2048]{1,0:T(8,128)(2,1)}, bf16[256,2048]{1,0:T(8,128)(2,1)}, u32[]{:S(2)}, u32[]{:S(2)}) %collective-permute-start.27) | collective-permute-done | bytes 1048608 | tf_op jit(solution)/shard_map/ppermute | solution.py:71
  46.4 6.1 all-to-all-start.3
  63.4 7.8 collective-permute-done.28
  92.6 5.8 collective-permute-done.29
  116.8 9.0 collective-permute-done.31
  125.8 5.8 convolution_convert_fusion.7
  133.6 8.7 shard_map.253
  155.2 8.6 shard_map.252
  164.4 15.2 %collective-permute-done.34 = bf16[256,2048]{1,0:T(8,128)(2,1)} collective-permute-done((bf16[256,2048]{1,0:T(8,128)(2,1)}, bf16[256,2048]{1,0:T(8,128)(2,1)}, u32[]{:S(2)}, u32[]{:S(2)}) %collective-permute-start.34) | collective-permute-done | bytes 1048608 | tf_op jit(solution)/shard_map/ppermute | solution.py:71
  187.7 14.3 %collective-permute-done.33 = bf16[256,2048]{1,0:T(8,128)(2,1)S(1)} collective-permute-done((bf16[256,2048]{1,0:T(8,128)(2,1)}, bf16[256,2048]{1,0:T(8,128)(2,1)S(1)}, u32[]{:S(2)}, u32[]{:S(2)}) %collective-permute-start.33) | collective-permute-done | bytes 1048608 | tf_op jit(solution)/shard_map/ppermute | solution.py:71
  204.2 8.7 shard_map.251
  212.9 11.4 %collective-permute-done.35 = bf16[256,2048]{1,0:T(8,128)(2,1)} collective-permute-done((bf16[256,2048]{1,0:T(8,128)(2,1)}, bf16[256,2048]{1,0:T(8,128)(2,1)}, u32[]{:S(2)}, u32[]{:S(2)}) %collective-permute-start.35) | collective-permute-done | bytes 1048608 | tf_op jit(solution)/shard_map/ppermute | solution.py:71
  229.1 5.8 convolution_convert_fusion.5
  241.0 7.9 shard_map.250
  249.0 7.1 collective-permute-done.36
  273.7 14.9 %collective-permute-done.37 = bf16[256,2048]{1,0:T(8,128)(2,1)} collective-permute-done((bf16[256,2048]{1,0:T(8,128)(2,1)}, bf16[256,2048]{1,0:T(8,128)(2,1)}, u32[]{:S(2)}, u32[]{:S(2)}) %collective-permute-start.37) | collective-permute-done | bytes 1048608 | tf_op jit(solution)/shard_map/ppermute | solution.py:71
  288.6 6.1 convolution_convert_fusion.6
  299.3 8.7 fusion.219
  308.0 5.7 collective-permute-done.38
  322.3 5.4 fusion.217
  327.8 10.2 %collective-permute-done.39 = bf16[256,2048]{1,0:T(8,128)(2,1)S(1)} collective-permute-done((bf16[256,2048]{1,0:T(8,128)(2,1)}, bf16[256,2048]{1,0:T(8,128)(2,1)S(1)}, u32[]{:S(2)}, u32[]{:S(2)}) %collective-permute-start.39) | collective-permute-done | bytes 1048608 | tf_op jit(solution)/shard_map/ppermute | solution.py:71
  342.7 6.3 convolution_convert_fusion.4
  356.2 6.5 fusion.87
  362.8 7.3 multiply_convert_fusion.10
  373.9 5.9 fusion.215
  379.8 5.3 fusion.74
  385.0 23.1 %all-to-all-done.8 = bf16[8,136,2048]{2,1,0:T(8,128)(2,1)} async-done(((bf16[8,136,2048]{2,1,0:T(8,128)(2,1)}), bf16[8,136,2048]{2,1,0:T(8,128)(2,1)}, u32[]{:S(2)}, u32[]{:S(2)}) %all-to-all-start.8) | async-done | bytes 4456480 | tf_op jit(solution)/shard_map/all_to_all | solution.py:579
  412.9 6.5 fusion.83
  419.5 8.5 multiply_convert_fusion.9
  431.7 5.3 fusion.75
  437.0 27.9 %all-to-all-done.6 = bf16[8,136,2048]{2,1,0:T(8,128)(2,1)} async-done(((bf16[8,136,2048]{2,1,0:T(8,128)(2,1)}), bf16[8,136,2048]{2,1,0:T(8,128)(2,1)}, u32[]{:S(2)}, u32[]{:S(2)}) %all-to-all-start.6) | async-done | bytes 4456480 | tf_op jit(solution)/shard_map/all_to_all | solution.py:579
  480.8 8.5 convolution_add_fusion.3
  489.3 11.6 %multiply_reduce_fusion.5 = (f32[1088]{0:T(1024)}, f32[1088,2048]{1,0:T(8,128)}, bf16[1088,2048]{1,0:T(8,128)(2,1)}) fusion(f32[1088,2048]{1,0:T(8,128)} %fusion.215, bf16[1088,2048]{1,0:T(8,128)(2,1)} %bitcast.221, f32[1088]{0:T(1024)S(1)} %broadcast_add_fusion), kind=kLoop, calls=%fused_computation.121 | loop fusion | flops 11140032 | bytes 26747392 | tf_op jit(solution)/shard_map/reduce_sum | solution.py:694
  500.9 8.6 convolution_add_fusion.4
  509.5 6.4 fusion.78
  515.9 5.7 all-to-all-done.9
  522.2 68.6 %conditional.10 = (f32[256,2048]{1,0:T(8,128)}, bf16[256,2048]{1,0:T(8,128)(2,1)}, f32[2048]{0:T(1024)S(1)}, bf16[1088,2048]{1,0:T(8,128)(2,1)}, bf16[1088,2048]...) conditional(s32[]{:T(128)} %bitcast.39, () %tuple.120, ...), branch_computations={%region_14.15_spmd, %region_15.20_spmd} | conditional | flops 16057010176 | bytes 235954496 | solution.py:93
  536.7 9.7 %multiply_reduce_fusion = (f32[1088]{0:T(1024)S(1)}, bf16[1088,2048]{1,0:T(8,128)(2,1)}) fusion(bf16[1088,2048]{1,0:T(8,128)(2,1)} %get-tuple-element.393, f32[1088]{0:T(1024)S(1)} %get-tuple-element.389, bf16[1088,768]{1,0:T(8,128)(2,1)} %get-tuple-element.390, bf16[768,2048]{1,0:T(8,128)(2,1)} %get-tuple-element.391), kind=kOutput, calls=%fused_computation | convolution fusion | flops 3433692160 | bytes 13738496 | tf_op jit(solution)/shard_map/cond/branch_1_fun/dot_general | solution.py:58
  547.5 6.5 add_bitcast_fusion.2
  560.4 11.7 %add_bitcast_fusion = f32[1,2048,768]{2,1,0:T(8,128)} fusion(f32[2048,768]{1,0:T(8,128)} %get-tuple-element.401, bf16[1088,2048]{1,0:T(8,128)(2,1)} %get-tuple-element.397, bf16[1088,768]{1,0:T(8,128)(2,1)} %get-tuple-element.400, f32[]{:T(128)S(6)} %min.24), kind=kOutput, calls=%fused_computation.2 | convolution fusion | flops 3425697792 | bytes 18710532 | tf_op jit(solution)/shard_map/cond/branch_1_fun/dot_general | solution.py:66
  572.1 9.9 %add_bitcast_fusion.1 = f32[1,2048,768]{2,1,0:T(8,128)} fusion(f32[2048,768]{1,0:T(8,128)} %get-tuple-element.399, bf16[1088,2048]{1,0:T(8,128)(2,1)} %get-tuple-element.397, bf16[1088,768]{1,0:T(8,128)(2,1)S(1)} %copy-done.144, f32[]{:T(128)S(6)} %min.24), kind=kOutput, calls=%fused_computation.3 | convolution fusion | flops 3425697792 | bytes 18710532 | tf_op jit(solution)/shard_map/cond/branch_1_fun/dot_general | solution.py:66
  590.8 5.9 all-to-all-start.10
  601.7 27.7 %conditional.11 = (bf16[256,1024]{1,0:T(8,128)(2,1)}, f32[2048,256]{1,0:T(8,128)S(1)}, f32[256,2048]{1,0:T(8,128)}, bf16[256,2048]{1,0:T(8,128)(2,1)}, f32[128]{0:T(128)}) conditional(s32[]{:T(128)} %bitcast.39, () %tuple.122, (bf16[256,2048]{1,0:T(8,128)(2,1)}, bf16[1024,2048]{1,0:T(8,128)(2,1)}, s32[1]{0:T(128)}, ...), branch_computations={%region_20.21_spmd, %region_21.22_spmd} | conditional | flops 2147745792 | bytes 18874452 | solution.py:93
  607.8 14.7 %branch_1_fun.8 = (bf16[256,1024]{1,0:T(8,128)(2,1)}, f32[2048,256]{1,0:T(8,128)S(1)}, f32[1,128]{1,0:T(1,128)}) custom-call(s32[1]{0:T(128)} %get-tuple-element.402.at_ref, bf16[256,1024]{1,0:T(8,128)(2,1)S(1)} %get-tuple-element.403.q_ref, bf16[256,1024]{1,0:T(8,128)(2,1)S(1)} %get-tuple-element.404.qa_ref, ...), custom_call_target="tpu_custom_call" | custom-call | flops 1 | bytes 1 | tf_op jit(solution)/shard_map/cond/branch_1_fun/pallas_call | solution.py:367
  629.4 26.8 %conditional.12 = (bf16[256,1024]{1,0:T(8,128)(2,1)}, f32[2048,256]{1,0:T(8,128)}, f32[256,2048]{1,0:T(8,128)S(1)}, bf16[256,2048]{1,0:T(8,128)(2,1)}, f32[128]{0:T(128)}) conditional(s32[]{:T(128)} %bitcast.39, () %tuple.124, (bf16[256,2048]{1,0:T(8,128)(2,1)}, bf16[1024,2048]{1,0:T(8,128)(2,1)}, s32[1]{0:T(128)}, bf16[256,1024]{1,0:T(8,128)(2,1)}, ...), branch_computations={%region_22.23_spmd, %region_23.24_spmd} | conditional | flops 2147745792 | bytes 28311744 | solution.py:93
  634.2 14.5 %branch_1_fun.9 = (bf16[256,1024]{1,0:T(8,128)(2,1)}, f32[2048,256]{1,0:T(8,128)}, f32[1,128]{1,0:T(1,128)}) custom-call(s32[1]{0:T(128)} %get-tuple-element.418.at_ref, bf16[256,1024]{1,0:T(8,128)(2,1)S(1)} %copy-done.46, bf16[256,1024]{1,0:T(8,128)(2,1)S(1)} %copy-done.63, bf16[256,1024]{1,0:T(8,128)(2,1)} %convolution_convert_fusion.1.grad_ref, ...), custom_call_target="tpu_custom_call" | custom-call | flops 1 | bytes 1 | tf_op jit(solution)/shard_map/cond/branch_1_fun/pallas_call | solution.py:367
  657.6 26.4 %conditional.13 = (bf16[256,1024]{1,0:T(8,128)(2,1)}, f32[2048,256]{1,0:T(8,128)}, f32[256,2048]{1,0:T(8,128)}, bf16[256,2048]{1,0:T(8,128)(2,1)}, f32[128]{0:T(128)}) conditional(s32[]{:T(128)} %bitcast.39, () %tuple.126, (bf16[256,2048]{1,0:T(8,128)(2,1)}, bf16[1024,2048]{1,0:T(8,128)(2,1)}, s32[1]{0:T(128)}, bf16[256,1024]{1,0:T(8,128)(2,1)S(1)}, ...), branch_computations={%region_24.25_spmd, %region_25.26_spmd} | conditional | flops 2147745792 | bytes 26214564 | solution.py:93
  662.5 15.4 %branch_1_fun.10 = (bf16[256,1024]{1,0:T(8,128)(2,1)}, f32[2048,256]{1,0:T(8,128)}, f32[1,128]{1,0:T(1,128)}) custom-call(s32[1]{0:T(128)} %get-tuple-element.435.at_ref, bf16[256,1024]{1,0:T(8,128)(2,1)S(1)} %get-tuple-element.436.q_ref, bf16[256,1024]{1,0:T(8,128)(2,1)S(1)} %copy-done.62, bf16[256,1024]{1,0:T(8,128)(2,1)} %convolution_convert_fusion.2.grad_ref, ...), custom_call_target="tpu_custom_call" | custom-call | flops 1 | bytes 1 | tf_op jit(solution)/shard_map/cond/branch_1_fun/pallas_call | solution.py:367
  684.6 28.1 %conditional.14 = (bf16[1024,2048]{1,0:T(8,128)(2,1)}, bf16[256,2048]{1,0:T(8,128)(2,1)}, f32[256,2048]{1,0:T(8,128)}, f32[256,2048]{1,0:T(8,128)}) conditional(s32[]{:T(128)} %bitcast.39, () %tuple.119, (bf16[256,1024]{1,0:T(8,128)(2,1)}, bf16[256,1024]{1,0:T(8,128)(2,1)}, bf16[256,1024]{1,0:T(8,128)(2,1)}, bf16[256,1024]{1,0:T(8,128)(2,1)}, ...), branch_computations={%region_26.27_spmd, %region_27.29_spmd} | conditional | flops 6604984320 | bytes 48832744 | solution.py:93
  694.9 8.8 fusion.20
  703.7 9.1 collective-permute-done.20
  712.8 26.4 %conditional.15 = (bf16[256,1024]{1,0:T(8,128)(2,1)}, f32[2048,256]{1,0:T(8,128)S(1)}, f32[256,2048]{1,0:T(8,128)S(1)}, bf16[256,2048]{1,0:T(8,128)(2,1)}, f32[128]{0:T(128)}) conditional(s32[]{:T(128)} %bitcast.39, () %tuple.132, (bf16[256,2048]{1,0:T(8,128)(2,1)}, bf16[1024,2048]{1,0:T(8,128)(2,1)}, s32[1]{0:T(128)}, ...), branch_computations={%region_29.30_spmd, %region_30.31_spmd} | conditional | flops 2149318656 | bytes 47186112 | solution.py:93
  719.7 14.8 %branch_1_fun.11 = (bf16[256,1024]{1,0:T(8,128)(2,1)}, f32[2048,256]{1,0:T(8,128)S(1)}, f32[1,128]{1,0:T(1,128)}) custom-call(s32[1]{0:T(128)} %get-tuple-element.464.at_ref, bf16[256,1024]{1,0:T(8,128)(2,1)S(1)} %copy-done.44, bf16[256,1024]{1,0:T(8,128)(2,1)} %get-tuple-element.466.qa_ref, bf16[256,1024]{1,0:T(8,128)(2,1)} %convolution_convert_fusion.3.grad_ref, ...), custom_call_target="tpu_custom_call" | custom-call | flops 1 | bytes 1 | tf_op jit(solution)/shard_map/cond/branch_1_fun/pallas_call | solution.py:367
  739.2 31.2 %conditional.16 = (bf16[256,2048]{1,0:T(8,128)(2,1)}, bf16[2048,1024]{1,0:T(8,128)(2,1)}, bf16[256,256]{1,0:T(8,128)(2,1)S(1)}, bf16[256,256]{1,0:T(8,128)(2,1)}...) conditional(s32[]{:T(128)} %bitcast.39, () %tuple.131, ...), branch_computations={%region_31.32_spmd, %region_32.33_spmd} | conditional | flops 4323803648 | bytes 45097888 | solution.py:93
  742.6 9.5 %fusion.39 = bf16[2048,1024]{1,0:T(8,128)(2,1)} fusion(bf16[256,2048]{1,0:T(8,128)(2,1)} %get-tuple-element.488, bf16[256,2048]{1,0:T(8,128)(2,1)} %get-tuple-element.487, bf16[256,2048]{1,0:T(8,128)(2,1)} %get-tuple-element.486, bf16[256,2048]{1,0:T(8,128)(2,1)} %get-tuple-element.485, bf16[256,1024]{1,0:T(8,128)(2,1)} %get-tuple-element.492, ...), kind=kOutput, calls=%fused_computation.56 | convolution fusion | flops 4322230272 | bytes 10485760 | tf_op jit(solution)/shard_map/cond/branch_1_fun/dot_general | solution.py:66
  764.8 5.5 collective-permute-done
  778.6 43.5 %conditional.17 = (f32[256,2048]{1,0:T(8,128)}, f32[4352]{0:T(1024)S(1)}, bf16[1024,256]{1,0:T(8,128)(2,1)S(1)}, f32[256,2048]{1,0:T(8,128)}, f32[256,2048]{1,0:T(8,128)}, /*index=5*/f32[256,2048]{1,0:T(8,128)S(1)}) conditional(s32[]{:T(128)} %bitcast.39, () %tuple.130, (bf16[256,2048]{1,0:T(8,128)(2,1)}, f32[256,2048]{1,0:T(8,128)}, ...), branch_computations={%region_34.35_spmd, %region_35.38_spmd} | conditional | flops 4458033152 | bytes 91102872 | solution.py:93
  795.0 7.5 fusion.240
  805.3 5.7 multiply_reduce_fusion.3
  823.5 31.8 %conditional.18 = (bf16[256,2048]{1,0:T(8,128)(2,1)}, f32[4352]{0:T(1024)}, bf16[256,256]{1,0:T(8,128)(2,1)S(1)}) conditional(s32[]{:T(128)} %bitcast.39, () %tuple.129, (f32[256,2048]{1,0:T(8,128)}, f32[256,2048]{1,0:T(8,128)}, f32[16,128]{1,0:T(8,128)S(1)}, f32[4352]{0:T(1024)S(1)}, bf16[1024,256]{1,0:T(8,128)(2,1)S(1)}) %tuple.273), branch_computations={%region_39.40_spmd, %region_40.42_spmd} | conditional | flops 2376512 | bytes 13350851 | solution.py:93
  830.5 6.1 collective-permute-done.6
  847.9 7.4 collective-permute-done.2
  855.3 41.9 %conditional.19 = (bf16[256,2048]{1,0:T(8,128)(2,1)S(1)}, f32[4352]{0:T(1024)}, f32[32,256]{1,0:T(8,128)S(1)}, f32[256,1024]{1,0:T(8,128)}, f32[2048]{0:T(1024)S...) conditional(s32[]{:T(128)} %bitcast.39, () %tuple.118, ...), branch_computations={%region_43.44_spmd, %region_44.46_spmd} | conditional | flops 7615232 | bytes 26578356 | solution.py:93
  874.4 13.1 %collective-permute-done.10 = f32[4352]{0:T(1024)S(1)} collective-permute-done((f32[4352]{0:T(1024)}, f32[4352]{0:T(1024)S(1)}, u32[]{:S(2)}, u32[]{:S(2)}) %collective-permute-start.10) | collective-permute-done | bytes 17440 | tf_op jit(solution)/shard_map/cond/branch_1_fun/ppermute | solution.py:128
  (611 shorter events, 383.8 us)
Async XLA Ops:
  7.2 355.6 %copy-start = (bf16[1,2048,768]{2,1,0:T(8,128)(2,1)S(1)}, bf16[1,2048,768]{2,1,0:T(8,128)(2,1)}, u32[]{:S(2)}) copy-start(bf16[1,2048,768]{2,1,0:T(8,128)(2,1)} %param.44) | copy-start | bytes 9437188
  7.2 47.1 %all-gather.4.cloned.1.call-start = ((), (), s32[]{:S(2)}) async-start(), calls=%async_computation.13 | async-start | bytes 5898240 | tf_op jit(solution)/shard_map/all_gather | solution.py:502
  15.6 28.7 %collective-permute-start.27 = (bf16[256,2048]{1,0:T(8,128)(2,1)}, bf16[256,2048]{1,0:T(8,128)(2,1)}, u32[]{:S(2)}, u32[]{:S(2)}) collective-permute-start(bf16[256,2048]{1,0:T(8,128)(2,1)} %get-tuple-element.929), channel_id=1, source_target_pairs={{0,1},{1,2},{2,3},{3,0},{4,5},{5,6},{6,7},{7,4},{8,9},{9,10},{10,1... | collective-permute-start | bytes 3145736 | tf_op jit(solution)/shard_map/ppermute | solution.py:71
  19.5 27.0 %all-to-all-start.2 = ((bf16[4,8,256]{2,1,0:T(8,128)(2,1)}), bf16[4,8,256]{2,1,0:T(8,128)(2,1)S(1)}, u32[]{:S(2)}, u32[]{:S(2)}) async-start(bf16[4,8,256]{2,1,0:T(8,128)(2,1)} %bitcast.298), calls=%async_computation.2 | async-start | bytes 32768 | tf_op jit(solution)/shard_map/all_to_all | solution.py:536
  23.3 123.6 %all-gather.6.cloned.1.call-start = ((), (), s32[]{:S(2)}) async-start(), calls=%async_computation.14 | async-start | bytes 4718592 | tf_op jit(solution)/shard_map/all_gather | solution.py:516
  25.2 240.8 %copy-start.103 = (pred[1088]{0:T(1024)(128)(4,1)}, pred[1088]{0:T(1024)(128)(4,1)S(1)}, u32[]{:S(2)}) copy-start(pred[1088]{0:T(1024)(128)(4,1)S(1)} %get-tuple-element.974) | copy-start | bytes 3268
  25.2 240.8 %copy-start.79 = (s32[1088]{0:T(1024)}, s32[1088]{0:T(1024)S(1)}, u32[]{:S(2)}) copy-start(s32[1088]{0:T(1024)S(1)} %broadcast_add_fusion.1) | copy-start | bytes 13060
  25.2 240.8 %copy-start.81 = (s32[1088]{0:T(1024)}, s32[1088]{0:T(1024)S(1)}, u32[]{:S(2)}) copy-start(s32[1088]{0:T(1024)S(1)} %iota_divide_fusion) | copy-start | bytes 13060
  44.3 26.9 %collective-permute-start.28 = (bf16[256,2048]{1,0:T(8,128)(2,1)}, bf16[256,2048]{1,0:T(8,128)(2,1)}, u32[]{:S(2)}, u32[]{:S(2)}) collective-permute-start(bf16[256,2048]{1,0:T(8,128)(2,1)} %collective-permute-done.27), channel_id=1, source_target_pairs={{0,1},{1,2},{2,3},{3,0},{4,5},{5,6},{6,7},{7,4},{8,9},{9,10},{10,1... | collective-permute-start | bytes 3145736 | tf_op jit(solution)/shard_map/ppermute | solution.py:71
  46.4 95.9 %all-to-all-start.3 = ((f32[32,2,256]{2,1,0:T(2,128)}), f32[32,2,256]{2,1,0:T(2,128)S(1)}, u32[]{:S(2)}, u32[]{:S(2)}) async-start(f32[32,2,256]{2,1,0:T(2,128)} %copy.63), calls=%async_computation.3 | async-start | bytes 131072 | tf_op jit(solution)/shard_map/all_to_all | solution.py:543
  73.6 24.8 %collective-permute-start.29 = (bf16[256,2048]{1,0:T(8,128)(2,1)}, bf16[256,2048]{1,0:T(8,128)(2,1)}, u32[]{:S(2)}, u32[]{:S(2)}) collective-permute-start(bf16[256,2048]{1,0:T(8,128)(2,1)} %add_convert_fusion.9), channel_id=1, source_target_pairs={{0,1},{1,2},{2,3},{3,0},{4,5},{5,6},{6,7},{7,4},{8,9},{9,10},{10,1... | collective-permute-start | bytes 3145736 | tf_op jit(solution)/shard_map/ppermute | solution.py:71
  101.9 24.0 %collective-permute-start.31 = (bf16[256,2048]{1,0:T(8,128)(2,1)S(1)}, bf16[256,2048]{1,0:T(8,128)(2,1)}, u32[]{:S(2)}, u32[]{:S(2)}) collective-permute-start(bf16[256,2048]{1,0:T(8,128)(2,1)S(1)} %add_convert_fusion.8), channel_id=1, source_target_pairs={{0,1},{1,2},{2,3},{3,0},{4,5},{5,6},{6,7},{7,4},{8,9},{9,10},{10,1... | collective-permute-start | bytes 3145736 | tf_op jit(solution)/shard_map/ppermute | solution.py:71
  110.7 3.8 collective-permute-start.30
  125.8 27.4 %collective-permute-start.32 = (bf16[256,2048]{1,0:T(8,128)(2,1)}, bf16[256,2048]{1,0:T(8,128)(2,1)}, u32[]{:S(2)}, u32[]{:S(2)}) collective-permute-start(bf16[256,2048]{1,0:T(8,128)(2,1)} %collective-permute-done.31), channel_id=1, source_target_pairs={{0,1},{1,2},{2,3},{3,0},{4,5},{5,6},{6,7},{7,4},{8,9},{9,10},{10,1... | collective-permute-start | bytes 3145736 | tf_op jit(solution)/shard_map/ppermute | solution.py:71
  142.3 92.6 %all-to-all-start.4 = ((bf16[8,136,2048]{2,1,0:T(8,128)(2,1)}), bf16[8,136,2048]{2,1,0:T(8,128)(2,1)}, u32[]{:S(2)}, u32[]{:S(2)}) async-start(bf16[8,136,2048]{2,1,0:T(8,128)(2,1)} %bitcast.306), calls=%async_computation.4 | async-start | bytes 8912896 | tf_op jit(solution)/shard_map/all_to_all | solution.py:579
  151.5 28.1 %collective-permute-start.34 = (bf16[256,2048]{1,0:T(8,128)(2,1)}, bf16[256,2048]{1,0:T(8,128)(2,1)}, u32[]{:S(2)}, u32[]{:S(2)}) collective-permute-start(bf16[256,2048]{1,0:T(8,128)(2,1)} %convolution_convert_fusion.8), channel_id=1, source_target_pairs={{0,1},{1,2},{2,3},{3,0},{4,5},{5,6},{6,7},{7,4},{8,9},{9,10},{10,1... | collective-permute-start | bytes 3145736 | tf_op jit(solution)/shard_map/ppermute | solution.py:71
  163.9 38.1 %collective-permute-start.33 = (bf16[256,2048]{1,0:T(8,128)(2,1)}, bf16[256,2048]{1,0:T(8,128)(2,1)S(1)}, u32[]{:S(2)}, u32[]{:S(2)}) collective-permute-start(bf16[256,2048]{1,0:T(8,128)(2,1)} %collective-permute-done.32), channel_id=1, source_target_pairs={{0,1},{1,2},{2,3},{3,0},{4,5},{5,6},{6,7},{7,4},{8,9},{9,10},{10,1... | collective-permute-start | bytes 3145736 | tf_op jit(solution)/shard_map/ppermute | solution.py:71
  184.4 39.9 %collective-permute-start.35 = (bf16[256,2048]{1,0:T(8,128)(2,1)}, bf16[256,2048]{1,0:T(8,128)(2,1)}, u32[]{:S(2)}, u32[]{:S(2)}) collective-permute-start(bf16[256,2048]{1,0:T(8,128)(2,1)} %fusion.97), channel_id=1, source_target_pairs={{0,1},{1,2},{2,3},{3,0},{4,5},{5,6},{6,7},{7,4},{8,9},{9,10},{10,1... | collective-permute-start | bytes 3145736 | tf_op jit(solution)/shard_map/ppermute | solution.py:71
  229.1 27.0 %collective-permute-start.36 = (bf16[256,2048]{1,0:T(8,128)(2,1)}, bf16[256,2048]{1,0:T(8,128)(2,1)}, u32[]{:S(2)}, u32[]{:S(2)}) collective-permute-start(bf16[256,2048]{1,0:T(8,128)(2,1)} %fusion.96), channel_id=1, source_target_pairs={{0,1},{1,2},{2,3},{3,0},{4,5},{5,6},{6,7},{7,4},{8,9},{9,10},{10,1... | collective-permute-start | bytes 3145736 | tf_op jit(solution)/shard_map/ppermute | solution.py:71
  234.9 59.8 %all-to-all-start.7 = ((bf16[8,136,2048]{2,1,0:T(8,128)(2,1)}), bf16[8,136,2048]{2,1,0:T(8,128)(2,1)}, u32[]{:S(2)}, u32[]{:S(2)}) async-start(bf16[8,136,2048]{2,1,0:T(8,128)(2,1)} %bitcast.307), calls=%async_computation.7 | async-start | bytes 8912896 | tf_op jit(solution)/shard_map/all_to_all | solution.py:579
  262.3 26.2 %collective-permute-start.37 = (bf16[256,2048]{1,0:T(8,128)(2,1)}, bf16[256,2048]{1,0:T(8,128)(2,1)}, u32[]{:S(2)}, u32[]{:S(2)}) collective-permute-start(bf16[256,2048]{1,0:T(8,128)(2,1)} %get-tuple-element.897), channel_id=1, source_target_pairs={{0,1},{1,2},{2,3},{3,0},{4,5},{5,6},{6,7},{7,4},{8,9},{9,10},{10,1... | collective-permute-start | bytes 3145736 | tf_op jit(solution)/shard_map/ppermute | solution.py:71
  268.4 45.5 %copy-start.77 = (f32[1088]{0:T(1024)}, f32[1088]{0:T(1024)S(1)}, u32[]{:S(2)}) copy-start(f32[1088]{0:T(1024)S(1)} %fusion.117) | copy-start | bytes 13060
  288.6 25.1 %collective-permute-start.38 = (bf16[256,2048]{1,0:T(8,128)(2,1)}, bf16[256,2048]{1,0:T(8,128)(2,1)}, u32[]{:S(2)}, u32[]{:S(2)}) collective-permute-start(bf16[256,2048]{1,0:T(8,128)(2,1)} %collective-permute-done.37), channel_id=1, source_target_pairs={{0,1},{1,2},{2,3},{3,0},{4,5},{5,6},{6,7},{7,4},{8,9},{9,10},{10,1... | collective-permute-start | bytes 3145736 | tf_op jit(solution)/shard_map/ppermute | solution.py:71
  294.7 56.5 %all-to-all-start.5 = ((bf16[8,136,2048]{2,1,0:T(8,128)(2,1)}), bf16[8,136,2048]{2,1,0:T(8,128)(2,1)}, u32[]{:S(2)}, u32[]{:S(2)}) async-start(bf16[8,136,2048]{2,1,0:T(8,128)(2,1)} %bitcast.308), calls=%async_computation.5 | async-start | bytes 8912896 | tf_op jit(solution)/shard_map/all_to_all | solution.py:579
  299.3 479.2 %all-gather.8.cloned.1.call-start = ((), (), s32[]{:S(2)}) async-start(), calls=%async_computation.15 | async-start | bytes 5242880 | tf_op jit(solution)/shard_map/all_gather | solution.py:650
  313.7 24.3 %collective-permute-start.39 = (bf16[256,2048]{1,0:T(8,128)(2,1)}, bf16[256,2048]{1,0:T(8,128)(2,1)S(1)}, u32[]{:S(2)}, u32[]{:S(2)}) collective-permute-start(bf16[256,2048]{1,0:T(8,128)(2,1)} %collective-permute-done.38), channel_id=1, source_target_pairs={{0,1},{1,2},{2,3},{3,0},{4,5},{5,6},{6,7},{7,4},{8,9},{9,10},{10,1... | collective-permute-start | bytes 3145736 | tf_op jit(solution)/shard_map/ppermute | solution.py:71
  351.2 56.9 %all-to-all-start.8 = ((bf16[8,136,2048]{2,1,0:T(8,128)(2,1)}), bf16[8,136,2048]{2,1,0:T(8,128)(2,1)}, u32[]{:S(2)}, u32[]{:S(2)}) async-start(bf16[8,136,2048]{2,1,0:T(8,128)(2,1)} %bitcast.310), calls=%async_computation.8 | async-start | bytes 8912896 | tf_op jit(solution)/shard_map/all_to_all | solution.py:579
  408.1 56.7 %all-to-all-start.6 = ((bf16[8,136,2048]{2,1,0:T(8,128)(2,1)}), bf16[8,136,2048]{2,1,0:T(8,128)(2,1)}, u32[]{:S(2)}, u32[]{:S(2)}) async-start(bf16[8,136,2048]{2,1,0:T(8,128)(2,1)} %bitcast.311), calls=%async_computation.6 | async-start | bytes 8912896 | tf_op jit(solution)/shard_map/all_to_all | solution.py:579
  464.9 56.7 %all-to-all-start.9 = ((bf16[8,136,2048]{2,1,0:T(8,128)(2,1)}), bf16[8,136,2048]{2,1,0:T(8,128)(2,1)}, u32[]{:S(2)}, u32[]{:S(2)}) async-start(bf16[8,136,2048]{2,1,0:T(8,128)(2,1)} %bitcast.309), calls=%async_computation.9 | async-start | bytes 8912896 | tf_op jit(solution)/shard_map/all_to_all | solution.py:579
  480.6 35.3 %collective-permute-start.40 = (bf16[256,2048]{1,0:T(8,128)(2,1)}, bf16[256,2048]{1,0:T(8,128)(2,1)}, u32[]{:S(2)}, u32[]{:S(2)}) collective-permute-start(bf16[256,2048]{1,0:T(8,128)(2,1)} %slice.420), channel_id=1, source_target_pairs={{0,1},{1,2},{2,3},{3,0},{4,5},{5,6},{6,7},{7,4},{8,9},{9,10},{10,1... | collective-permute-start | bytes 3145736 | tf_op jit(solution)/shard_map/ppermute | solution.py:71
  531.7 24.3 %collective-permute-start.15 = (bf16[256,2048]{1,0:T(8,128)(2,1)}, bf16[256,2048]{1,0:T(8,128)(2,1)}, u32[]{:S(2)}, u32[]{:S(2)}) collective-permute-start(bf16[256,2048]{1,0:T(8,128)(2,1)} %fusion.3), channel_id=1, source_target_pairs={{0,1},{1,2},{2,3},{3,0},{4,5},{5,6},{6,7},{7,4},{8,9},{9,10},{10,1... | collective-permute-start | bytes 3145736 | tf_op jit(solution)/shard_map/cond/branch_1_fun/ppermute | solution.py:71
  531.7 58.9 %all-to-all-start.1 = ((bf16[8,136,2048]{2,1,0:T(8,128)(2,1)}), bf16[8,136,2048]{2,1,0:T(8,128)(2,1)}, u32[]{:S(2)}, u32[]{:S(2)}) async-start(bf16[8,136,2048]{2,1,0:T(8,128)(2,1)} %bitcast.301), calls=%async_computation.1 | async-start | bytes 8912896 | tf_op jit(solution)/shard_map/cond/branch_1_fun/all_to_all | solution.py:579
  558.6 26.3 %collective-permute-start.16 = (bf16[256,2048]{1,0:T(8,128)(2,1)}, bf16[256,2048]{1,0:T(8,128)(2,1)}, u32[]{:S(2)}, u32[]{:S(2)}) collective-permute-start(bf16[256,2048]{1,0:T(8,128)(2,1)} %get-tuple-element.893), channel_id=1, source_target_pairs={{0,1},{1,2},{2,3},{3,0},{4,5},{5,6},{6,7},{7,4},{8,9},{9,10},{10,1... | collective-permute-start | bytes 3145736 | tf_op jit(solution)/shard_map/cond/branch_1_fun/ppermute | solution.py:71
  590.8 93.2 %all-to-all-start.10 = ((bf16[8,136,2048]{2,1,0:T(8,128)(2,1)}), bf16[8,136,2048]{2,1,0:T(8,128)(2,1)}, u32[]{:S(2)}, u32[]{:S(2)}) async-start(bf16[8,136,2048]{2,1,0:T(8,128)(2,1)} %bitcast.102), calls=%async_computation.10 | async-start | bytes 8912896 | tf_op jit(solution)/shard_map/all_to_all | solution.py:579
  596.7 225.5 %reduce-scatter.2.cloned.1.call-start = ((), (), s32[]{:S(2)}) async-start(), calls=%async_computation.16 | async-start | bytes 4718592 | tf_op jit(solution)/shard_map/reduce_scatter | solution.py:760
  601.7 27.7 %collective-permute-start.17 = (bf16[256,2048]{1,0:T(8,128)(2,1)}, bf16[256,2048]{1,0:T(8,128)(2,1)}, u32[]{:S(2)}, u32[]{:S(2)}) collective-permute-start(bf16[256,2048]{1,0:T(8,128)(2,1)} %get-tuple-element.405), channel_id=1, source_target_pairs={{0,1},{1,2},{2,3},{3,0},{4,5},{5,6},{6,7},{7,4},{8,9},{9,10},{10,1... | collective-permute-start | bytes 3145736 | tf_op jit(solution)/shard_map/cond/branch_1_fun/ppermute | solution.py:71
  629.4 26.8 %collective-permute-start.18 = (bf16[256,2048]{1,0:T(8,128)(2,1)}, bf16[256,2048]{1,0:T(8,128)(2,1)}, u32[]{:S(2)}, u32[]{:S(2)}) collective-permute-start(bf16[256,2048]{1,0:T(8,128)(2,1)} %get-tuple-element.421), channel_id=1, source_target_pairs={{0,1},{1,2},{2,3},{3,0},{4,5},{5,6},{6,7},{7,4},{8,9},{9,10},{10,1... | collective-permute-start | bytes 3145736 | tf_op jit(solution)/shard_map/cond/branch_1_fun/ppermute | solution.py:71
  657.6 26.1 %collective-permute-start.19 = (bf16[256,2048]{1,0:T(8,128)(2,1)}, bf16[256,2048]{1,0:T(8,128)(2,1)}, u32[]{:S(2)}, u32[]{:S(2)}) collective-permute-start(bf16[256,2048]{1,0:T(8,128)(2,1)} %get-tuple-element.438), channel_id=1, source_target_pairs={{0,1},{1,2},{2,3},{3,0},{4,5},{5,6},{6,7},{7,4},{8,9},{9,10},{10,1... | collective-permute-start | bytes 3145736 | tf_op jit(solution)/shard_map/cond/branch_1_fun/ppermute | solution.py:71
  687.8 25.0 %collective-permute-start.20 = (bf16[256,2048]{1,0:T(8,128)(2,1)S(1)}, bf16[256,2048]{1,0:T(8,128)(2,1)}, u32[]{:S(2)}, u32[]{:S(2)}) collective-permute-start(bf16[256,2048]{1,0:T(8,128)(2,1)S(1)} %add_convert_fusion), channel_id=1, source_target_pairs={{0,1},{1,2},{2,3},{3,0},{4,5},{5,6},{6,7},{7,4},{8,9},{9,10},{10,1... | collective-permute-start | bytes 3145736 | tf_op jit(solution)/shard_map/cond/branch_1_fun/ppermute | solution.py:71
  715.1 24.1 %collective-permute-start.21 = (bf16[256,2048]{1,0:T(8,128)(2,1)S(1)}, bf16[256,2048]{1,0:T(8,128)(2,1)}, u32[]{:S(2)}, u32[]{:S(2)}) collective-permute-start(bf16[256,2048]{1,0:T(8,128)(2,1)S(1)} %add_convert_fusion.1), channel_id=1, source_target_pairs={{0,1},{1,2},{2,3},{3,0},{4,5},{5,6},{6,7},{7,4},{8,9},{9,10},{10,1... | collective-permute-start | bytes 3145736 | tf_op jit(solution)/shard_map/cond/branch_1_fun/ppermute | solution.py:71
  739.3 14.0 %collective-permute-start.1 = (bf16[1024,256]{1,0:T(8,128)(2,1)S(1)}, bf16[1024,256]{1,0:T(8,128)(2,1)S(1)}, u32[]{:S(2)}, u32[]{:S(2)}) collective-permute-start(bf16[1024,256]{1,0:T(8,128)(2,1)S(1)} %slice.419), channel_id=1, source_target_pairs={{4,0},{12,8},{20,16},{28,24},{5,1},{13,9},{21,17},{29,25},{6,2},{1... | collective-permute-start | bytes 1572872 | tf_op jit(solution)/shard_map/cond/branch_1_fun/ppermute | solution.py:800
  742.6 27.8 %collective-permute-start = (bf16[256,2048]{1,0:T(8,128)(2,1)S(1)}, bf16[256,2048]{1,0:T(8,128)(2,1)}, u32[]{:S(2)}, u32[]{:S(2)}) collective-permute-start(bf16[256,2048]{1,0:T(8,128)(2,1)S(1)} %add_convert_fusion.2), channel_id=1, source_target_pairs={{0,1},{1,2},{2,3},{3,0},{4,5},{5,6},{6,7},{7,4},{8,9},{9,10},{10,1... | collective-permute-start | bytes 3145736 | tf_op jit(solution)/shard_map/cond/branch_1_fun/ppermute | solution.py:71
  771.0 84.3 %all-to-all-start.11 = ((bf16[8,256,1024]{2,1,0:T(8,128)(2,1)}), bf16[8,256,1024]{2,1,0:T(8,128)(2,1)}, u32[]{:S(2)}, u32[]{:S(2)}) async-start(bf16[8,256,1024]{2,1,0:T(8,128)(2,1)} %bitcast.108), calls=%async_computation.12 | async-start | bytes 8388608 | tf_op jit(solution)/shard_map/all_to_all | solution.py:794
  780.3 22.2 %collective-permute-start.22 = (bf16[256,256]{0,1:T(8,128)(2,1)}, bf16[256,256]{0,1:T(8,128)(2,1)}, u32[]{:S(2)}, u32[]{:S(2)}) collective-permute-start(bf16[256,256]{0,1:T(8,128)(2,1)} %copy.69), channel_id=1, source_target_pairs={{0,3},{1,0},{2,1},{3,2},{4,7},{5,4},{6,5},{7,6},{8,11},{9,8},{10,9... | collective-permute-start | bytes 393224 | tf_op jit(solution)/shard_map/cond/branch_1_fun/ppermute | solution.py:128
  782.5 21.0 %collective-permute-start.23 = (bf16[256,256]{0,1:T(8,128)(2,1)}, bf16[256,256]{0,1:T(8,128)(2,1)}, u32[]{:S(2)}, u32[]{:S(2)}) collective-permute-start(bf16[256,256]{0,1:T(8,128)(2,1)} %copy.70), channel_id=1, source_target_pairs={{0,2},{1,3},{2,0},{3,1},{4,6},{5,7},{6,4},{7,5},{8,10},{9,11},{10,... | collective-permute-start | bytes 393224 | tf_op jit(solution)/shard_map/cond/branch_1_fun/ppermute | solution.py:128
  784.1 20.2 %collective-permute-start.24 = (bf16[256,256]{0,1:T(8,128)(2,1)}, bf16[256,256]{0,1:T(8,128)(2,1)}, u32[]{:S(2)}, u32[]{:S(2)}) collective-permute-start(bf16[256,256]{0,1:T(8,128)(2,1)} %copy.71), channel_id=1, source_target_pairs={{0,1},{1,2},{2,3},{3,0},{4,5},{5,6},{6,7},{7,4},{8,9},{9,10},{10,1... | collective-permute-start | bytes 393224 | tf_op jit(solution)/shard_map/cond/branch_1_fun/ppermute | solution.py:128
  790.3 25.9 %collective-permute-start.25 = (bf16[4,256,256]{2,1,0:T(8,128)(2,1)}, bf16[4,256,256]{2,1,0:T(8,128)(2,1)}, u32[]{:S(2)}, u32[]{:S(2)}) collective-permute-start(bf16[4,256,256]{2,1,0:T(8,128)(2,1)} %dynamic-slice_bitcast_fusion), channel_id=1, source_target_pairs={{0,4},{4,0},{8,12},{12,8},{16,20},{20,16},{24,28},{28,24},{1,5},{5... | collective-permute-start | bytes 1572872 | tf_op jit(solution)/shard_map/cond/branch_1_fun/ppermute | solution.py:76
  793.0 27.7 %collective-permute-start.26 = (bf16[256,2048]{1,0:T(8,128)(2,1)}, bf16[256,2048]{1,0:T(8,128)(2,1)}, u32[]{:S(2)}, u32[]{:S(2)}) collective-permute-start(bf16[256,2048]{1,0:T(8,128)(2,1)} %convert_element_type.283), channel_id=1, source_target_pairs={{0,1},{1,2},{2,3},{3,0},{4,5},{5,6},{6,7},{7,4},{8,9},{9,10},{10,1... | collective-permute-start | bytes 3145736 | tf_op jit(solution)/shard_map/cond/branch_1_fun/ppermute | solution.py:71
  828.4 26.9 %collective-permute-start.2 = (bf16[256,2048]{1,0:T(8,128)(2,1)}, bf16[256,2048]{1,0:T(8,128)(2,1)}, u32[]{:S(2)}, u32[]{:S(2)}) collective-permute-start(bf16[256,2048]{1,0:T(8,128)(2,1)} %add_convert_fusion.3), channel_id=1, source_target_pairs={{0,1},{1,2},{2,3},{3,0},{4,5},{5,6},{6,7},{7,4},{8,9},{9,10},{10,1... | collective-permute-start | bytes 3145736 | tf_op jit(solution)/shard_map/cond/branch_1_fun/ppermute | solution.py:71
  828.5 8.0 collective-permute-start.6
  836.7 11.2 %collective-permute-start.7 = (bf16[1,256,256]{2,1,0:T(8,128)(2,1)S(1)}, bf16[1,256,256]{2,1,0:T(8,128)(2,1)S(1)}, u32[]{:S(2)}, u32[]{:S(2)}) collective-permute-start(bf16[1,256,256]{2,1,0:T(8,128)(2,1)S(1)} %constant_dynamic-slice_fusion), channel_id=1, source_target_pairs={{0,16},{4,20},{8,24},{12,28},{16,0},{20,4},{24,8},{28,12},{1,17},{... | collective-permute-start | bytes 393224 | tf_op jit(solution)/shard_map/cond/branch_1_fun/ppermute | solution.py:76
  838.5 1.2 collective-permute-start.3
  839.7 3.8 collective-permute-start.4
  843.5 3.8 collective-permute-start.5
  855.3 43.0 %copy-start.92 = (s32[1,256]{1,0:T(1,128)S(1)}, s32[1,256]{1,0:T(1,128)}, u32[]{:S(2)}) copy-start(s32[1,256]{1,0:T(1,128)} %copy-done.91) | copy-start | bytes 3076
  855.3 43.0 %copy-start.94 = (s32[1,256]{1,0:T(1,128)S(1)}, s32[1,256]{1,0:T(1,128)}, u32[]{:S(2)}) copy-start(s32[1,256]{1,0:T(1,128)} %copy-done.93) | copy-start | bytes 3076
  858.5 35.1 %collective-permute-start.8 = (bf16[256,2048]{1,0:T(8,128)(2,1)}, bf16[256,2048]{1,0:T(8,128)(2,1)S(1)}, u32[]{:S(2)}, u32[]{:S(2)}) collective-permute-start(bf16[256,2048]{1,0:T(8,128)(2,1)} %add_convert_fusion.6), channel_id=1, source_target_pairs={{0,1},{1,2},{2,3},{3,0},{4,5},{5,6},{6,7},{7,4},{8,9},{9,10},{10,1... | collective-permute-start | bytes 3145736 | tf_op jit(solution)/shard_map/cond/branch_1_fun/ppermute | solution.py:71
  858.7 28.7 %collective-permute-start.10 = (f32[4352]{0:T(1024)}, f32[4352]{0:T(1024)S(1)}, u32[]{:S(2)}, u32[]{:S(2)}) collective-permute-start(f32[4352]{0:T(1024)} %get-tuple-element.552), channel_id=1, source_target_pairs={{0,2},{1,3},{2,0},{3,1},{4,6},{5,7},{6,4},{7,5},{8,10},{9,11},{10,... | collective-permute-start | bytes 52232 | tf_op jit(solution)/shard_map/cond/branch_1_fun/ppermute | solution.py:128
  858.8 28.6 %collective-permute-start.11 = (f32[4352]{0:T(1024)}, f32[4352]{0:T(1024)S(1)}, u32[]{:S(2)}, u32[]{:S(2)}) collective-permute-start(f32[4352]{0:T(1024)} %get-tuple-element.552), channel_id=1, source_target_pairs={{0,3},{1,0},{2,1},{3,2},{4,7},{5,4},{6,5},{7,6},{8,11},{9,8},{10,9... | collective-permute-start | bytes 52232 | tf_op jit(solution)/shard_map/cond/branch_1_fun/ppermute | solution.py:128
  862.5 27.7 %collective-permute-start.9 = (f32[4352]{0:T(1024)}, f32[4352]{0:T(1024)S(1)}, u32[]{:S(2)}, u32[]{:S(2)}) collective-permute-start(f32[4352]{0:T(1024)} %get-tuple-element.552), channel_id=1, source_target_pairs={{0,1},{1,2},{2,3},{3,0},{4,5},{5,6},{6,7},{7,4},{8,9},{9,10},{10,1... | collective-permute-start | bytes 52232 | tf_op jit(solution)/shard_map/cond/branch_1_fun/ppermute | solution.py:128
  863.1 33.9 %collective-permute-start.12 = (bf16[256,256]{1,0:T(8,128)(2,1)S(1)}, bf16[256,256]{1,0:T(8,128)(2,1)}, u32[]{:S(2)}, u32[]{:S(2)}) collective-permute-start(bf16[256,256]{1,0:T(8,128)(2,1)S(1)} %get-tuple-element.555), channel_id=1, source_target_pairs={{0,1},{1,2},{2,3},{3,0},{4,5},{5,6},{6,7},{7,4},{8,9},{9,10},{10,1... | collective-permute-start | bytes 393224 | tf_op jit(solution)/shard_map/cond/branch_1_fun/ppermute | solution.py:128
  865.8 27.8 %all-to-all-start = ((f32[32,1,256]{2,1,0:T(1,128)}), f32[32,1,256]{2,1,0:T(1,128)S(1)}, u32[]{:S(2)}, u32[]{:S(2)}) async-start(f32[32,1,256]{2,1,0:T(1,128)} %all_to_all.28), calls=%async_computation | async-start | bytes 65536 | tf_op jit(solution)/shard_map/cond/branch_1_fun/all_to_all | solution.py:874
  887.5 9.6 %collective-permute-start.13 = (bf16[256,256]{1,0:T(8,128)(2,1)S(1)}, bf16[256,256]{1,0:T(8,128)(2,1)}, u32[]{:S(2)}, u32[]{:S(2)}) collective-permute-start(bf16[256,256]{1,0:T(8,128)(2,1)S(1)} %get-tuple-element.555), channel_id=1, source_target_pairs={{0,2},{1,3},{2,0},{3,1},{4,6},{5,7},{6,4},{7,5},{8,10},{9,11},{10,... | collective-permute-start | bytes 393224 | tf_op jit(solution)/shard_map/cond/branch_1_fun/ppermute | solution.py:128
  887.5 9.6 %collective-permute-start.14 = (bf16[256,256]{1,0:T(8,128)(2,1)S(1)}, bf16[256,256]{1,0:T(8,128)(2,1)}, u32[]{:S(2)}, u32[]{:S(2)}) collective-permute-start(bf16[256,256]{1,0:T(8,128)(2,1)S(1)} %get-tuple-element.555), channel_id=1, source_target_pairs={{0,3},{1,0},{2,1},{3,2},{4,7},{5,4},{6,5},{7,6},{8,11},{9,8},{10,9... | collective-permute-start | bytes 393224 | tf_op jit(solution)/shard_map/cond/branch_1_fun/ppermute | solution.py:128
  (155 other events, 1138.0 us)
Sparse Core Ops, SparseCore 0:
  10.5 43.8 all-gather.3
  56.2 37.7 all-gather.5
  342.8 78.3 all-gather.7
  712.9 50.0 reduce-scatter.1

commit v5 on v4

--- a/solution.py
+++ b/solution.py
@@ -512,7 +512,6 @@
         axis=0,
         tiled=True,
     )
-    wq_whole = own_whole[:, :local_width]
     wo_whole = lax.all_gather(out_weight, "dp", axis=1, tiled=True)
 
     top_count = routes.shape[1]
@@ -723,9 +722,12 @@
             first_out,
             [add_weights(0), add_weights(1, tie), add_weights(2, tie)],
             expert_outs(len(groups) - 1, 0.0),
-        )
-
-    grad_resid, back_own, moe_gain_part, first_out, weight_grads, last_outs = stage(flag, sum_work)
+            own_whole[:, :local_width],
+        )
+
+    grad_resid, back_own, moe_gain_part, first_out, weight_grads, last_outs, wq_whole = stage(
+        flag, sum_work
+    )
     down_weight_grad, gate_weight_grad, up_weight_grad = weight_grads
     outs.append(last_outs)
     back = [back_own]
@@ -864,12 +866,12 @@
         kv_rows = kv_part
         for bit in bits[1:]:
             kv_rows = half_rows(kv_rows, bit)
-        return sent, total, row_major(kv_rows)
-
-    out_passed, gains, kv_rows = stage(flag, token_work)
+        own_cols = [kv_rows] + [shift_by(kv_rows, b) for b in blocks[1:]]
+        return sent, total, own_cols
+
+    out_passed, gains, own_cols = stage(flag, token_work)
 
     def last_work():
-        own_cols = [kv_rows] + [shift_by(kv_rows, b) for b in blocks[1:]]
         total = gains + sum(shift_by(gains, b) for b in blocks[1:])
         found = lax.all_to_all(spread, ("dp", "mp"), split_axis=0, concat_axis=0, tiled=True)
         sent = out_passed
@@ -878,12 +880,11 @@
         return (
             row_major((resid + out_parts[0] + sent.astype(FULL)).astype(LOW)),
             total,
-            own_cols,
             found,
             row_major(jnp.sum(weight_came.astype(FULL), axis=0)),
         )
 
-    block_out, gains, own_cols, spread, query_weight_grad = stage(flag, last_work)
+    block_out, gains, spread, query_weight_grad = stage(flag, last_work)
     cols_of = jnp.zeros((mp_count,) + own_cols[0].shape, LOW)
     for b in blocks:
         cols_of = lax.dynamic_update_index_in_dim(cols_of, own_cols[b], places[b], 0)

time: 926 us -> 929 us (level)
    ppermute x9, waiting for transfers between devices: 13.1 us -> 28.6 us  [shift_by(): lax.ppermute(shard, axis, [(i, (i + by) % length) for i in range(length)])]
    ppermute x24, waiting for transfers between devices: 151 us -> 141 us  [ring_shift(): lax.ppermute(shard, axis, [(i, (i + 1) % length) for i in range(length)])]
  transfers between devices with their start and end apart: 57 -> 57, of which waited for: 32 -> 33; matrix products, arithmetic and copies ran while one was open for 46% -> 46% of each run, Pallas kernels for 12% -> 12%
where the time goes in v5:
time: 929 us; the launch traced here: 917 us
  matrix products  290 us (31%)
  waiting for transfers between devices  240 us (26%)
  Pallas kernels  114 us (12%)
  other arithmetic  110 us (12%)
  starting transfers between devices  88.8 us (10%)
  local copies, waits for them, and re-layouts  47.7 us (5%)
  between operations  21.9 us (2%)
    ppermute x24, waiting for transfers between devices, ring_shift(): lax.ppermute(shard, axis, [(i, (i + 1) % length) for i in range(length)])  141 us
    dot_general x23, matrix products, matmul(): return jnp.dot(left, right, preferred_element_type=FULL)  113 us
    dot_general x13, matrix products, contract_first(): lax.dot_general(left, right, (((0,), (0,)), ((), ())), preferred_element_...  97.6 us
    dot_general x14, matrix products, contract_last(): lax.dot_general(left, right, (((1,), (1,)), ((), ())), preferred_element_...  67.2 us
    pallas_call x4, Pallas kernels, attend_back(): pl.pallas_call(functools.partial(attend_back_kernel, score_scale), out_sh...  59.4 us
    all_to_all x8, waiting for transfers between devices, plane_turn(): lax.all_to_all(rows.reshape(dp_count, group_rows, model_width), 'dp', spl...  58.6 us
    all_to_all x8, starting transfers between devices, plane_turn(): lax.all_to_all(rows.reshape(dp_count, group_rows, model_width), 'dp', spl...  38.1 us
    pallas_call x4, Pallas kernels, attend(): pl.pallas_call(functools.partial(attend_kernel, score_scale, docs), out_s...  33.9 us
  transfers between devices with their start and end apart: 57, of which 33 were waited for; matrix products, arithmetic and copies ran while one was open for 46% of the time, Pallas kernels for 12%

profile of v5, /device:TPU:0, one launch (start us, length us, event | category | flops | bytes accessed | tf_op | source)
XLA Modules:
  0.0 916.9 jit_solution(5589970929290763759)
XLA Ops:
  32.8 11.5 %collective-permute-done.27 = bf16[256,2048]{1,0:T(8,128)(2,1)} collective-permute-done((bf16[256,2048]{1,0:T(8,128)(2,1)}, bf16[256,2048]{1,0:T(8,128)(2,1)}, u32[]{:S(2)}, u32[]{:S(2)}) %collective-permute-start.27) | collective-permute-done | bytes 1048608 | tf_op jit(solution)/shard_map/ppermute | solution.py:71
  46.5 6.1 all-to-all-start.3
  63.4 7.8 collective-permute-done.28
  92.6 5.8 collective-permute-done.29
  116.8 9.1 collective-permute-done.31
  125.9 5.8 convolution_convert_fusion.7
  133.6 8.7 shard_map.253
  155.2 8.7 shard_map.252
  164.4 15.1 %collective-permute-done.34 = bf16[256,2048]{1,0:T(8,128)(2,1)} collective-permute-done((bf16[256,2048]{1,0:T(8,128)(2,1)}, bf16[256,2048]{1,0:T(8,128)(2,1)}, u32[]{:S(2)}, u32[]{:S(2)}) %collective-permute-start.34) | collective-permute-done | bytes 1048608 | tf_op jit(solution)/shard_map/ppermute | solution.py:71
  187.6 14.3 %collective-permute-done.33 = bf16[256,2048]{1,0:T(8,128)(2,1)S(1)} collective-permute-done((bf16[256,2048]{1,0:T(8,128)(2,1)}, bf16[256,2048]{1,0:T(8,128)(2,1)S(1)}, u32[]{:S(2)}, u32[]{:S(2)}) %collective-permute-start.33) | collective-permute-done | bytes 1048608 | tf_op jit(solution)/shard_map/ppermute | solution.py:71
  204.2 8.7 shard_map.251
  212.8 11.4 %collective-permute-done.35 = bf16[256,2048]{1,0:T(8,128)(2,1)} collective-permute-done((bf16[256,2048]{1,0:T(8,128)(2,1)}, bf16[256,2048]{1,0:T(8,128)(2,1)}, u32[]{:S(2)}, u32[]{:S(2)}) %collective-permute-start.35) | collective-permute-done | bytes 1048608 | tf_op jit(solution)/shard_map/ppermute | solution.py:71
  229.1 5.8 convolution_convert_fusion.5
  241.0 7.9 shard_map.250
  249.0 7.1 collective-permute-done.36
  268.5 5.2 multiply_convert_fusion.5
  273.7 15.0 %collective-permute-done.37 = bf16[256,2048]{1,0:T(8,128)(2,1)} collective-permute-done((bf16[256,2048]{1,0:T(8,128)(2,1)}, bf16[256,2048]{1,0:T(8,128)(2,1)}, u32[]{:S(2)}, u32[]{:S(2)}) %collective-permute-start.37) | collective-permute-done | bytes 1048608 | tf_op jit(solution)/shard_map/ppermute | solution.py:71
  288.7 6.1 convolution_convert_fusion.6
  299.4 8.6 fusion.218
  308.1 5.8 collective-permute-done.38
  314.1 5.2 multiply_convert_fusion.2
  322.6 5.4 fusion.216
  328.0 10.3 %collective-permute-done.39 = bf16[256,2048]{1,0:T(8,128)(2,1)S(1)} collective-permute-done((bf16[256,2048]{1,0:T(8,128)(2,1)}, bf16[256,2048]{1,0:T(8,128)(2,1)S(1)}, u32[]{:S(2)}, u32[]{:S(2)}) %collective-permute-start.39) | collective-permute-done | bytes 1048608 | tf_op jit(solution)/shard_map/ppermute | solution.py:71
  343.0 6.3 convolution_convert_fusion.4
  356.3 6.5 fusion.86
  362.9 7.3 multiply_convert_fusion.10
  374.0 6.0 fusion.214
  380.0 5.3 fusion.73
  385.2 23.0 %all-to-all-done.8 = bf16[8,136,2048]{2,1,0:T(8,128)(2,1)} async-done(((bf16[8,136,2048]{2,1,0:T(8,128)(2,1)}), bf16[8,136,2048]{2,1,0:T(8,128)(2,1)}, u32[]{:S(2)}, u32[]{:S(2)}) %all-to-all-start.8) | async-done | bytes 4456480 | tf_op jit(solution)/shard_map/all_to_all | solution.py:578
  413.0 6.5 fusion.82
  419.6 8.5 multiply_convert_fusion.9
  431.8 5.3 fusion.74
  437.0 27.9 %all-to-all-done.6 = bf16[8,136,2048]{2,1,0:T(8,128)(2,1)} async-done(((bf16[8,136,2048]{2,1,0:T(8,128)(2,1)}), bf16[8,136,2048]{2,1,0:T(8,128)(2,1)}, u32[]{:S(2)}, u32[]{:S(2)}) %all-to-all-start.6) | async-done | bytes 4456480 | tf_op jit(solution)/shard_map/all_to_all | solution.py:578
  480.9 8.5 convolution_add_fusion.3
  489.3 11.6 %multiply_reduce_fusion.5 = (f32[1088]{0:T(1024)}, f32[1088,2048]{1,0:T(8,128)}, bf16[1088,2048]{1,0:T(8,128)(2,1)}) fusion(f32[1088,2048]{1,0:T(8,128)} %fusion.214, bf16[1088,2048]{1,0:T(8,128)(2,1)} %bitcast.217, f32[1088]{0:T(1024)S(1)} %broadcast_add_fusion), kind=kLoop, calls=%fused_computation.120 | loop fusion | flops 11140032 | bytes 26747392 | tf_op jit(solution)/shard_map/reduce_sum | solution.py:693
  500.9 8.6 convolution_add_fusion.4
  509.6 6.5 fusion.77
  516.1 5.6 all-to-all-done.9
  521.7 72.9 %conditional.10 = (f32[256,2048]{1,0:T(8,128)}, bf16[256,2048]{1,0:T(8,128)(2,1)}, f32[2048]{0:T(1024)S(1)}, bf16[1088,2048]{1,0:T(8,128)(2,1)}, bf16[1088,2048]...) conditional(s32[]{:T(128)} %bitcast.38, () %tuple.120, ...), branch_computations={%region_14.15_spmd, %region_15.20_spmd} | conditional | flops 16057010176 | bytes 241197392 | solution.py:93
  536.3 9.7 %multiply_reduce_fusion = (f32[1088]{0:T(1024)S(1)}, bf16[1088,2048]{1,0:T(8,128)(2,1)}) fusion(bf16[1088,2048]{1,0:T(8,128)(2,1)} %get-tuple-element.393, f32[1088]{0:T(1024)S(1)} %get-tuple-element.389, bf16[1088,768]{1,0:T(8,128)(2,1)} %get-tuple-element.390, bf16[768,2048]{1,0:T(8,128)(2,1)} %get-tuple-element.391), kind=kOutput, calls=%fused_computation | convolution fusion | flops 3433692160 | bytes 13738496 | tf_op jit(solution)/shard_map/cond/branch_1_fun/dot_general | solution.py:58
  549.8 8.3 add_bitcast_fusion.2
  562.8 11.8 %add_bitcast_fusion = f32[1,2048,768]{2,1,0:T(8,128)} fusion(f32[2048,768]{1,0:T(8,128)} %get-tuple-element.402, bf16[1088,2048]{1,0:T(8,128)(2,1)} %get-tuple-element.398, bf16[1088,768]{1,0:T(8,128)(2,1)} %get-tuple-element.401, f32[]{:T(128)S(6)} %min.24), kind=kOutput, calls=%fused_computation.2 | convolution fusion | flops 3425697792 | bytes 18710532 | tf_op jit(solution)/shard_map/cond/branch_1_fun/dot_general | solution.py:66
  574.5 9.9 %add_bitcast_fusion.1 = f32[1,2048,768]{2,1,0:T(8,128)} fusion(f32[2048,768]{1,0:T(8,128)} %get-tuple-element.400, bf16[1088,2048]{1,0:T(8,128)(2,1)} %get-tuple-element.398, bf16[1088,768]{1,0:T(8,128)(2,1)S(1)} %copy-done.137, f32[]{:T(128)S(6)} %min.24), kind=kOutput, calls=%fused_computation.3 | convolution fusion | flops 3425697792 | bytes 18710532 | tf_op jit(solution)/shard_map/cond/branch_1_fun/dot_general | solution.py:66
  599.6 27.6 %conditional.11 = (bf16[256,1024]{1,0:T(8,128)(2,1)}, f32[2048,256]{1,0:T(8,128)S(1)}, f32[256,2048]{1,0:T(8,128)}, bf16[256,2048]{1,0:T(8,128)(2,1)}, f32[128]{0:T(128)S(1)}) conditional(s32[]{:T(128)} %bitcast.38, () %tuple.122, (bf16[256,2048]{1,0:T(8,128)(2,1)}, bf16[1024,2048]{1,0:T(8,128)(2,1)}, s32[1]{0:T(128)}, ...), branch_computations={%region_20.21_spmd, %region_21.22_spmd} | conditional | flops 2147745792 | bytes 28311720 | solution.py:93
  606.3 14.7 %branch_1_fun.8 = (bf16[256,1024]{1,0:T(8,128)(2,1)}, f32[2048,256]{1,0:T(8,128)S(1)}, f32[1,128]{1,0:T(1,128)S(1)}) custom-call(s32[1]{0:T(128)} %get-tuple-element.403.at_ref, bf16[256,1024]{1,0:T(8,128)(2,1)S(1)} %get-tuple-element.404.q_ref, bf16[256,1024]{1,0:T(8,128)(2,1)S(1)} %copy-done.67, bf16[256,1024]{1,0:T(8,128)(2,1)} %convolution_convert_fusion.grad_ref, ...), custom_call_target="tpu_custom_call" | custom-call | flops 1 | bytes 1 | tf_op jit(solution)/shard_map/cond/branch_1_fun/pallas_call | solution.py:367
  627.2 26.7 %conditional.12 = (bf16[256,1024]{1,0:T(8,128)(2,1)}, f32[2048,256]{1,0:T(8,128)}, f32[256,2048]{1,0:T(8,128)S(1)}, bf16[256,2048]{1,0:T(8,128)(2,1)}, f32[128]{0:T(128)S(1)}) conditional(s32[]{:T(128)} %bitcast.38, () %tuple.124, (bf16[256,2048]{1,0:T(8,128)(2,1)}, bf16[1024,2048]{1,0:T(8,128)(2,1)}, s32[1]{0:T(128)}, ...), branch_computations={%region_22.23_spmd, %region_23.24_spmd} | conditional | flops 2147745792 | bytes 28311744 | solution.py:93
  633.3 14.5 %branch_1_fun.9 = (bf16[256,1024]{1,0:T(8,128)(2,1)}, f32[2048,256]{1,0:T(8,128)}, f32[1,128]{1,0:T(1,128)S(1)}) custom-call(s32[1]{0:T(128)} %get-tuple-element.419.at_ref, bf16[256,1024]{1,0:T(8,128)(2,1)S(1)} %copy-done.46, bf16[256,1024]{1,0:T(8,128)(2,1)S(1)} %copy-done.63, bf16[256,1024]{1,0:T(8,128)(2,1)} %convolution_convert_fusion.1.grad_ref, ...), custom_call_target="tpu_custom_call" | custom-call | flops 1 | bytes 1 | tf_op jit(solution)/shard_map/cond/branch_1_fun/pallas_call | solution.py:367
  655.3 26.5 %conditional.13 = (bf16[256,1024]{1,0:T(8,128)(2,1)}, f32[2048,256]{1,0:T(8,128)}, f32[256,2048]{1,0:T(8,128)}, bf16[256,2048]{1,0:T(8,128)(2,1)}, f32[128]{0:T(128)S(1)}) conditional(s32[]{:T(128)} %bitcast.38, () %tuple.126, (bf16[256,2048]{1,0:T(8,128)(2,1)}, bf16[1024,2048]{1,0:T(8,128)(2,1)}, s32[1]{0:T(128)}, ...), branch_computations={%region_24.25_spmd, %region_25.26_spmd} | conditional | flops 2147745792 | bytes 26214564 | solution.py:93
  660.4 15.4 %branch_1_fun.10 = (bf16[256,1024]{1,0:T(8,128)(2,1)}, f32[2048,256]{1,0:T(8,128)}, f32[1,128]{1,0:T(1,128)S(1)}) custom-call(s32[1]{0:T(128)} %get-tuple-element.436.at_ref, bf16[256,1024]{1,0:T(8,128)(2,1)S(1)} %get-tuple-element.437.q_ref, bf16[256,1024]{1,0:T(8,128)(2,1)S(1)} %copy-done.62, bf16[256,1024]{1,0:T(8,128)(2,1)} %convolution_convert_fusion.2.grad_ref, ...), custom_call_target="tpu_custom_call" | custom-call | flops 1 | bytes 1 | tf_op jit(solution)/shard_map/cond/branch_1_fun/pallas_call | solution.py:367
  682.5 28.4 %conditional.14 = (bf16[1024,2048]{1,0:T(8,128)(2,1)}, bf16[256,2048]{1,0:T(8,128)(2,1)}, f32[256,2048]{1,0:T(8,128)}, f32[256,2048]{1,0:T(8,128)}) conditional(s32[]{:T(128)} %bitcast.38, () %tuple.119, (bf16[256,1024]{1,0:T(8,128)(2,1)}, bf16[256,1024]{1,0:T(8,128)(2,1)}, bf16[256,1024]{1,0:T(8,128)(2,1)}, bf16[256,1024]{1,0:T(8,128)(2,1)}, ...), branch_computations={%region_26.27_spmd, %region_27.29_spmd} | conditional | flops 6604984320 | bytes 48832744 | solution.py:93
  692.8 8.8 fusion.20
  701.6 9.3 %collective-permute-done.20 = bf16[256,2048]{1,0:T(8,128)(2,1)} collective-permute-done((bf16[256,2048]{1,0:T(8,128)(2,1)S(1)}, bf16[256,2048]{1,0:T(8,128)(2,1)}, u32[]{:S(2)}, u32[]{:S(2)}) %collective-permute-start.20) | collective-permute-done | bytes 1048608 | tf_op jit(solution)/shard_map/cond/branch_1_fun/ppermute | solution.py:71
  711.0 26.7 %conditional.15 = (bf16[256,1024]{1,0:T(8,128)(2,1)}, f32[2048,256]{1,0:T(8,128)S(1)}, f32[256,2048]{1,0:T(8,128)S(1)}, bf16[256,2048]{1,0:T(8,128)(2,1)}, f32[128]{0:T(128)S(1)}) conditional(s32[]{:T(128)} %bitcast.38, () %tuple.132, (bf16[256,2048]{1,0:T(8,128)(2,1)}, bf16[1024,2048]{1,0:T(8,128)(2,1)}, s32[1]{0:T(128)}, ...), branch_computations={%region_29.30_spmd, %region_30.31_spmd} | conditional | flops 2149318656 | bytes 47186112 | solution.py:93
  717.8 14.9 %branch_1_fun.11 = (bf16[256,1024]{1,0:T(8,128)(2,1)}, f32[2048,256]{1,0:T(8,128)S(1)}, f32[1,128]{1,0:T(1,128)S(1)}) custom-call(s32[1]{0:T(128)} %get-tuple-element.465.at_ref, bf16[256,1024]{1,0:T(8,128)(2,1)S(1)} %copy-done.44, bf16[256,1024]{1,0:T(8,128)(2,1)} %get-tuple-element.467.qa_ref, bf16[256,1024]{1,0:T(8,128)(2,1)} %convolution_convert_fusion.3.grad_ref, ...), custom_call_target="tpu_custom_call" | custom-call | flops 1 | bytes 1 | tf_op jit(solution)/shard_map/cond/branch_1_fun/pallas_call | solution.py:367
  737.7 31.0 %conditional.16 = (bf16[256,2048]{1,0:T(8,128)(2,1)}, bf16[2048,1024]{1,0:T(8,128)(2,1)}, bf16[256,256]{1,0:T(8,128)(2,1)S(1)}, bf16[256,256]{1,0:T(8,128)(2,1)}...) conditional(s32[]{:T(128)} %bitcast.38, () %tuple.131, ...), branch_computations={%region_31.32_spmd, %region_32.33_spmd} | conditional | flops 4323803648 | bytes 45097888 | solution.py:93
  740.8 9.5 %fusion.39 = bf16[2048,1024]{1,0:T(8,128)(2,1)} fusion(bf16[256,2048]{1,0:T(8,128)(2,1)} %get-tuple-element.489, bf16[256,2048]{1,0:T(8,128)(2,1)} %get-tuple-element.488, bf16[256,2048]{1,0:T(8,128)(2,1)} %get-tuple-element.487, bf16[256,2048]{1,0:T(8,128)(2,1)} %get-tuple-element.486, bf16[256,1024]{1,0:T(8,128)(2,1)} %get-tuple-element.493, ...), kind=kOutput, calls=%fused_computation.56 | convolution fusion | flops 4322230272 | bytes 10485760 | tf_op jit(solution)/shard_map/cond/branch_1_fun/dot_general | solution.py:66
  763.2 5.2 collective-permute-done
  776.4 43.5 %conditional.17 = (f32[256,2048]{1,0:T(8,128)}, f32[4352]{0:T(1024)S(1)}, bf16[1024,256]{1,0:T(8,128)(2,1)S(1)}, f32[256,2048]{1,0:T(8,128)}, f32[256,2048]{1,0:T(8,128)}, /*index=5*/f32[256,2048]{1,0:T(8,128)S(1)}) conditional(s32[]{:T(128)} %bitcast.38, () %tuple.130, (bf16[256,2048]{1,0:T(8,128)(2,1)}, f32[256,2048]{1,0:T(8,128)}, ...), branch_computations={%region_34.35_spmd, %region_35.38_spmd} | conditional | flops 4458033152 | bytes 91102872 | solution.py:93
  792.5 7.5 fusion.239
  802.8 5.7 multiply_reduce_fusion.3
  821.3 42.0 %conditional.18 = (bf16[256,2048]{1,0:T(8,128)(2,1)}, f32[4352]{0:T(1024)S(1)}, bf16[1,256,256]{2,1,0:T(8,128)(2,1)}, bf16[1,256,256]{2,1,0:T(8,128)(2,1)}, bf16...) conditional(s32[]{:T(128)} %bitcast.38, () %tuple.129, (f32[256,2048]{1,0:T(8,128)}, ...), branch_computations={%region_39.40_spmd, %region_40.42_spmd} | conditional | flops 2376512 | bytes 14923859 | solution.py:93
  848.1 11.1 %collective-permute-done.8 = bf16[256,256]{1,0:T(8,128)(2,1)} collective-permute-done((bf16[256,256]{1,0:T(8,128)(2,1)}, bf16[256,256]{1,0:T(8,128)(2,1)}, u32[]{:S(2)}, u32[]{:S(2)}) %collective-permute-start.8) | collective-permute-done | bytes 131104 | tf_op jit(solution)/shard_map/cond/branch_1_fun/ppermute | solution.py:128
  863.4 37.8 %conditional.19 = (bf16[256,2048]{1,0:T(8,128)(2,1)S(1)}, f32[4352]{0:T(1024)}, f32[32,256]{1,0:T(8,128)S(1)}, f32[256,1024]{1,0:T(8,128)}, f32[2048]{0:T(1024)S...) conditional(s32[]{:T(128)} %bitcast.38, () %tuple.118, (f32[256,2048]{1,0:T(8,128)S(1)}, ...), branch_computations={%region_43.44_spmd, %region_44.46_spmd} | conditional | flops 7615232 | bytes 24743196 | solution.py:93
  882.0 13.0 %collective-permute-done.12 = f32[4352]{0:T(1024)S(1)} collective-permute-done((f32[4352]{0:T(1024)S(1)}, f32[4352]{0:T(1024)S(1)}, u32[]{:S(2)}, u32[]{:S(2)}) %collective-permute-start.12) | collective-permute-done | bytes 17440 | tf_op jit(solution)/shard_map/cond/branch_1_fun/ppermute | solution.py:128
  (596 shorter events, 382.9 us)
Async XLA Ops:
  7.2 355.7 %copy-start = (bf16[1,2048,768]{2,1,0:T(8,128)(2,1)S(1)}, bf16[1,2048,768]{2,1,0:T(8,128)(2,1)}, u32[]{:S(2)}) copy-start(bf16[1,2048,768]{2,1,0:T(8,128)(2,1)} %param.44) | copy-start | bytes 9437188
  7.2 47.1 %all-gather.4.cloned.1.call-start = ((), (), s32[]{:S(2)}) async-start(), calls=%async_computation.13 | async-start | bytes 5898240 | tf_op jit(solution)/shard_map/all_gather | solution.py:502
  15.6 28.7 %collective-permute-start.27 = (bf16[256,2048]{1,0:T(8,128)(2,1)}, bf16[256,2048]{1,0:T(8,128)(2,1)}, u32[]{:S(2)}, u32[]{:S(2)}) collective-permute-start(bf16[256,2048]{1,0:T(8,128)(2,1)} %get-tuple-element.924), channel_id=1, source_target_pairs={{0,1},{1,2},{2,3},{3,0},{4,5},{5,6},{6,7},{7,4},{8,9},{9,10},{10,1... | collective-permute-start | bytes 3145736 | tf_op jit(solution)/shard_map/ppermute | solution.py:71
  19.5 27.0 %all-to-all-start.2 = ((bf16[4,8,256]{2,1,0:T(8,128)(2,1)}), bf16[4,8,256]{2,1,0:T(8,128)(2,1)S(1)}, u32[]{:S(2)}, u32[]{:S(2)}) async-start(bf16[4,8,256]{2,1,0:T(8,128)(2,1)} %bitcast.294), calls=%async_computation.2 | async-start | bytes 32768 | tf_op jit(solution)/shard_map/all_to_all | solution.py:535
  23.3 123.6 %all-gather.6.cloned.1.call-start = ((), (), s32[]{:S(2)}) async-start(), calls=%async_computation.14 | async-start | bytes 4718592 | tf_op jit(solution)/shard_map/all_gather | solution.py:515
  25.2 240.8 %copy-start.106 = (pred[1088]{0:T(1024)(128)(4,1)}, pred[1088]{0:T(1024)(128)(4,1)S(1)}, u32[]{:S(2)}) copy-start(pred[1088]{0:T(1024)(128)(4,1)S(1)} %get-tuple-element.969) | copy-start | bytes 3268
  25.2 240.8 %copy-start.79 = (s32[1088]{0:T(1024)}, s32[1088]{0:T(1024)S(1)}, u32[]{:S(2)}) copy-start(s32[1088]{0:T(1024)S(1)} %broadcast_add_fusion.1) | copy-start | bytes 13060
  25.2 240.8 %copy-start.81 = (s32[1088]{0:T(1024)}, s32[1088]{0:T(1024)S(1)}, u32[]{:S(2)}) copy-start(s32[1088]{0:T(1024)S(1)} %iota_divide_fusion) | copy-start | bytes 13060
  44.3 26.9 %collective-permute-start.28 = (bf16[256,2048]{1,0:T(8,128)(2,1)}, bf16[256,2048]{1,0:T(8,128)(2,1)}, u32[]{:S(2)}, u32[]{:S(2)}) collective-permute-start(bf16[256,2048]{1,0:T(8,128)(2,1)} %collective-permute-done.27), channel_id=1, source_target_pairs={{0,1},{1,2},{2,3},{3,0},{4,5},{5,6},{6,7},{7,4},{8,9},{9,10},{10,1... | collective-permute-start | bytes 3145736 | tf_op jit(solution)/shard_map/ppermute | solution.py:71
  46.5 95.9 %all-to-all-start.3 = ((f32[32,2,256]{2,1,0:T(2,128)}), f32[32,2,256]{2,1,0:T(2,128)S(1)}, u32[]{:S(2)}, u32[]{:S(2)}) async-start(f32[32,2,256]{2,1,0:T(2,128)} %copy.59), calls=%async_computation.3 | async-start | bytes 131072 | tf_op jit(solution)/shard_map/all_to_all | solution.py:542
  73.6 24.8 %collective-permute-start.29 = (bf16[256,2048]{1,0:T(8,128)(2,1)}, bf16[256,2048]{1,0:T(8,128)(2,1)}, u32[]{:S(2)}, u32[]{:S(2)}) collective-permute-start(bf16[256,2048]{1,0:T(8,128)(2,1)} %add_convert_fusion.9), channel_id=1, source_target_pairs={{0,1},{1,2},{2,3},{3,0},{4,5},{5,6},{6,7},{7,4},{8,9},{9,10},{10,1... | collective-permute-start | bytes 3145736 | tf_op jit(solution)/shard_map/ppermute | solution.py:71
  101.9 24.0 %collective-permute-start.31 = (bf16[256,2048]{1,0:T(8,128)(2,1)S(1)}, bf16[256,2048]{1,0:T(8,128)(2,1)}, u32[]{:S(2)}, u32[]{:S(2)}) collective-permute-start(bf16[256,2048]{1,0:T(8,128)(2,1)S(1)} %add_convert_fusion.8), channel_id=1, source_target_pairs={{0,1},{1,2},{2,3},{3,0},{4,5},{5,6},{6,7},{7,4},{8,9},{9,10},{10,1... | collective-permute-start | bytes 3145736 | tf_op jit(solution)/shard_map/ppermute | solution.py:71
  110.7 3.8 collective-permute-start.30
  125.9 27.4 %collective-permute-start.32 = (bf16[256,2048]{1,0:T(8,128)(2,1)}, bf16[256,2048]{1,0:T(8,128)(2,1)}, u32[]{:S(2)}, u32[]{:S(2)}) collective-permute-start(bf16[256,2048]{1,0:T(8,128)(2,1)} %collective-permute-done.31), channel_id=1, source_target_pairs={{0,1},{1,2},{2,3},{3,0},{4,5},{5,6},{6,7},{7,4},{8,9},{9,10},{10,1... | collective-permute-start | bytes 3145736 | tf_op jit(solution)/shard_map/ppermute | solution.py:71
  142.3 92.6 %all-to-all-start.4 = ((bf16[8,136,2048]{2,1,0:T(8,128)(2,1)}), bf16[8,136,2048]{2,1,0:T(8,128)(2,1)}, u32[]{:S(2)}, u32[]{:S(2)}) async-start(bf16[8,136,2048]{2,1,0:T(8,128)(2,1)} %bitcast.302), calls=%async_computation.4 | async-start | bytes 8912896 | tf_op jit(solution)/shard_map/all_to_all | solution.py:578
  151.5 28.0 %collective-permute-start.34 = (bf16[256,2048]{1,0:T(8,128)(2,1)}, bf16[256,2048]{1,0:T(8,128)(2,1)}, u32[]{:S(2)}, u32[]{:S(2)}) collective-permute-start(bf16[256,2048]{1,0:T(8,128)(2,1)} %convolution_convert_fusion.8), channel_id=1, source_target_pairs={{0,1},{1,2},{2,3},{3,0},{4,5},{5,6},{6,7},{7,4},{8,9},{9,10},{10,1... | collective-permute-start | bytes 3145736 | tf_op jit(solution)/shard_map/ppermute | solution.py:71
  163.9 38.0 %collective-permute-start.33 = (bf16[256,2048]{1,0:T(8,128)(2,1)}, bf16[256,2048]{1,0:T(8,128)(2,1)S(1)}, u32[]{:S(2)}, u32[]{:S(2)}) collective-permute-start(bf16[256,2048]{1,0:T(8,128)(2,1)} %collective-permute-done.32), channel_id=1, source_target_pairs={{0,1},{1,2},{2,3},{3,0},{4,5},{5,6},{6,7},{7,4},{8,9},{9,10},{10,1... | collective-permute-start | bytes 3145736 | tf_op jit(solution)/shard_map/ppermute | solution.py:71
  184.3 40.0 %collective-permute-start.35 = (bf16[256,2048]{1,0:T(8,128)(2,1)}, bf16[256,2048]{1,0:T(8,128)(2,1)}, u32[]{:S(2)}, u32[]{:S(2)}) collective-permute-start(bf16[256,2048]{1,0:T(8,128)(2,1)} %fusion.96), channel_id=1, source_target_pairs={{0,1},{1,2},{2,3},{3,0},{4,5},{5,6},{6,7},{7,4},{8,9},{9,10},{10,1... | collective-permute-start | bytes 3145736 | tf_op jit(solution)/shard_map/ppermute | solution.py:71
  229.1 27.0 %collective-permute-start.36 = (bf16[256,2048]{1,0:T(8,128)(2,1)}, bf16[256,2048]{1,0:T(8,128)(2,1)}, u32[]{:S(2)}, u32[]{:S(2)}) collective-permute-start(bf16[256,2048]{1,0:T(8,128)(2,1)} %fusion.95), channel_id=1, source_target_pairs={{0,1},{1,2},{2,3},{3,0},{4,5},{5,6},{6,7},{7,4},{8,9},{9,10},{10,1... | collective-permute-start | bytes 3145736 | tf_op jit(solution)/shard_map/ppermute | solution.py:71
  234.9 59.9 %all-to-all-start.7 = ((bf16[8,136,2048]{2,1,0:T(8,128)(2,1)}), bf16[8,136,2048]{2,1,0:T(8,128)(2,1)}, u32[]{:S(2)}, u32[]{:S(2)}) async-start(bf16[8,136,2048]{2,1,0:T(8,128)(2,1)} %bitcast.303), calls=%async_computation.7 | async-start | bytes 8912896 | tf_op jit(solution)/shard_map/all_to_all | solution.py:578
  262.4 26.3 %collective-permute-start.37 = (bf16[256,2048]{1,0:T(8,128)(2,1)}, bf16[256,2048]{1,0:T(8,128)(2,1)}, u32[]{:S(2)}, u32[]{:S(2)}) collective-permute-start(bf16[256,2048]{1,0:T(8,128)(2,1)} %get-tuple-element.892), channel_id=1, source_target_pairs={{0,1},{1,2},{2,3},{3,0},{4,5},{5,6},{6,7},{7,4},{8,9},{9,10},{10,1... | collective-permute-start | bytes 3145736 | tf_op jit(solution)/shard_map/ppermute | solution.py:71
  268.4 45.7 %copy-start.77 = (f32[1088]{0:T(1024)}, f32[1088]{0:T(1024)S(1)}, u32[]{:S(2)}) copy-start(f32[1088]{0:T(1024)S(1)} %fusion.116) | copy-start | bytes 13060
  288.7 25.2 %collective-permute-start.38 = (bf16[256,2048]{1,0:T(8,128)(2,1)}, bf16[256,2048]{1,0:T(8,128)(2,1)}, u32[]{:S(2)}, u32[]{:S(2)}) collective-permute-start(bf16[256,2048]{1,0:T(8,128)(2,1)} %collective-permute-done.37), channel_id=1, source_target_pairs={{0,1},{1,2},{2,3},{3,0},{4,5},{5,6},{6,7},{7,4},{8,9},{9,10},{10,1... | collective-permute-start | bytes 3145736 | tf_op jit(solution)/shard_map/ppermute | solution.py:71
  294.8 56.5 %all-to-all-start.5 = ((bf16[8,136,2048]{2,1,0:T(8,128)(2,1)}), bf16[8,136,2048]{2,1,0:T(8,128)(2,1)}, u32[]{:S(2)}, u32[]{:S(2)}) async-start(bf16[8,136,2048]{2,1,0:T(8,128)(2,1)} %bitcast.304), calls=%async_computation.5 | async-start | bytes 8912896 | tf_op jit(solution)/shard_map/all_to_all | solution.py:578
  299.4 476.9 %all-gather.8.cloned.1.call-start = ((), (), s32[]{:S(2)}) async-start(), calls=%async_computation.15 | async-start | bytes 5242880 | tf_op jit(solution)/shard_map/all_gather | solution.py:649
  313.9 24.4 %collective-permute-start.39 = (bf16[256,2048]{1,0:T(8,128)(2,1)}, bf16[256,2048]{1,0:T(8,128)(2,1)S(1)}, u32[]{:S(2)}, u32[]{:S(2)}) collective-permute-start(bf16[256,2048]{1,0:T(8,128)(2,1)} %collective-permute-done.38), channel_id=1, source_target_pairs={{0,1},{1,2},{2,3},{3,0},{4,5},{5,6},{6,7},{7,4},{8,9},{9,10},{10,1... | collective-permute-start | bytes 3145736 | tf_op jit(solution)/shard_map/ppermute | solution.py:71
  351.3 56.9 %all-to-all-start.8 = ((bf16[8,136,2048]{2,1,0:T(8,128)(2,1)}), bf16[8,136,2048]{2,1,0:T(8,128)(2,1)}, u32[]{:S(2)}, u32[]{:S(2)}) async-start(bf16[8,136,2048]{2,1,0:T(8,128)(2,1)} %bitcast.306), calls=%async_computation.8 | async-start | bytes 8912896 | tf_op jit(solution)/shard_map/all_to_all | solution.py:578
  408.3 56.7 %all-to-all-start.6 = ((bf16[8,136,2048]{2,1,0:T(8,128)(2,1)}), bf16[8,136,2048]{2,1,0:T(8,128)(2,1)}, u32[]{:S(2)}, u32[]{:S(2)}) async-start(bf16[8,136,2048]{2,1,0:T(8,128)(2,1)} %bitcast.307), calls=%async_computation.6 | async-start | bytes 8912896 | tf_op jit(solution)/shard_map/all_to_all | solution.py:578
  465.0 56.7 %all-to-all-start.9 = ((bf16[8,136,2048]{2,1,0:T(8,128)(2,1)}), bf16[8,136,2048]{2,1,0:T(8,128)(2,1)}, u32[]{:S(2)}, u32[]{:S(2)}) async-start(bf16[8,136,2048]{2,1,0:T(8,128)(2,1)} %bitcast.305), calls=%async_computation.9 | async-start | bytes 8912896 | tf_op jit(solution)/shard_map/all_to_all | solution.py:578
  480.6 35.4 %collective-permute-start.40 = (bf16[256,2048]{1,0:T(8,128)(2,1)}, bf16[256,2048]{1,0:T(8,128)(2,1)}, u32[]{:S(2)}, u32[]{:S(2)}) collective-permute-start(bf16[256,2048]{1,0:T(8,128)(2,1)} %slice.418), channel_id=1, source_target_pairs={{0,1},{1,2},{2,3},{3,0},{4,5},{5,6},{6,7},{7,4},{8,9},{9,10},{10,1... | collective-permute-start | bytes 3145736 | tf_op jit(solution)/shard_map/ppermute | solution.py:71
  531.3 26.8 %collective-permute-start.15 = (bf16[256,2048]{1,0:T(8,128)(2,1)}, bf16[256,2048]{1,0:T(8,128)(2,1)}, u32[]{:S(2)}, u32[]{:S(2)}) collective-permute-start(bf16[256,2048]{1,0:T(8,128)(2,1)} %fusion.3), channel_id=1, source_target_pairs={{0,1},{1,2},{2,3},{3,0},{4,5},{5,6},{6,7},{7,4},{8,9},{9,10},{10,1... | collective-permute-start | bytes 3145736 | tf_op jit(solution)/shard_map/cond/branch_1_fun/ppermute | solution.py:71
  531.3 63.1 %all-to-all-start.1 = ((bf16[8,136,2048]{2,1,0:T(8,128)(2,1)}), bf16[8,136,2048]{2,1,0:T(8,128)(2,1)}, u32[]{:S(2)}, u32[]{:S(2)}) async-start(bf16[8,136,2048]{2,1,0:T(8,128)(2,1)} %bitcast.297), calls=%async_computation.1 | async-start | bytes 8912896 | tf_op jit(solution)/shard_map/cond/branch_1_fun/all_to_all | solution.py:578
  560.7 28.0 %collective-permute-start.16 = (bf16[256,2048]{1,0:T(8,128)(2,1)}, bf16[256,2048]{1,0:T(8,128)(2,1)}, u32[]{:S(2)}, u32[]{:S(2)}) collective-permute-start(bf16[256,2048]{1,0:T(8,128)(2,1)} %get-tuple-element.888), channel_id=1, source_target_pairs={{0,1},{1,2},{2,3},{3,0},{4,5},{5,6},{6,7},{7,4},{8,9},{9,10},{10,1... | collective-permute-start | bytes 3145736 | tf_op jit(solution)/shard_map/cond/branch_1_fun/ppermute | solution.py:71
  594.7 87.1 %all-to-all-start.10 = ((bf16[8,136,2048]{2,1,0:T(8,128)(2,1)}), bf16[8,136,2048]{2,1,0:T(8,128)(2,1)}, u32[]{:S(2)}, u32[]{:S(2)}) async-start(bf16[8,136,2048]{2,1,0:T(8,128)(2,1)} %bitcast.101), calls=%async_computation.10 | async-start | bytes 8912896 | tf_op jit(solution)/shard_map/all_to_all | solution.py:578
  599.5 220.4 %reduce-scatter.2.cloned.1.call-start = ((), (), s32[]{:S(2)}) async-start(), calls=%async_computation.16 | async-start | bytes 4718592 | tf_op jit(solution)/shard_map/reduce_scatter | solution.py:762
  599.7 27.6 %collective-permute-start.17 = (bf16[256,2048]{1,0:T(8,128)(2,1)}, bf16[256,2048]{1,0:T(8,128)(2,1)}, u32[]{:S(2)}, u32[]{:S(2)}) collective-permute-start(bf16[256,2048]{1,0:T(8,128)(2,1)} %get-tuple-element.406), channel_id=1, source_target_pairs={{0,1},{1,2},{2,3},{3,0},{4,5},{5,6},{6,7},{7,4},{8,9},{9,10},{10,1... | collective-permute-start | bytes 3145736 | tf_op jit(solution)/shard_map/cond/branch_1_fun/ppermute | solution.py:71
  627.2 26.7 %collective-permute-start.18 = (bf16[256,2048]{1,0:T(8,128)(2,1)}, bf16[256,2048]{1,0:T(8,128)(2,1)}, u32[]{:S(2)}, u32[]{:S(2)}) collective-permute-start(bf16[256,2048]{1,0:T(8,128)(2,1)} %get-tuple-element.422), channel_id=1, source_target_pairs={{0,1},{1,2},{2,3},{3,0},{4,5},{5,6},{6,7},{7,4},{8,9},{9,10},{10,1... | collective-permute-start | bytes 3145736 | tf_op jit(solution)/shard_map/cond/branch_1_fun/ppermute | solution.py:71
  655.3 26.0 %collective-permute-start.19 = (bf16[256,2048]{1,0:T(8,128)(2,1)}, bf16[256,2048]{1,0:T(8,128)(2,1)}, u32[]{:S(2)}, u32[]{:S(2)}) collective-permute-start(bf16[256,2048]{1,0:T(8,128)(2,1)} %get-tuple-element.439), channel_id=1, source_target_pairs={{0,1},{1,2},{2,3},{3,0},{4,5},{5,6},{6,7},{7,4},{8,9},{9,10},{10,1... | collective-permute-start | bytes 3145736 | tf_op jit(solution)/shard_map/cond/branch_1_fun/ppermute | solution.py:71
  685.6 25.3 %collective-permute-start.20 = (bf16[256,2048]{1,0:T(8,128)(2,1)S(1)}, bf16[256,2048]{1,0:T(8,128)(2,1)}, u32[]{:S(2)}, u32[]{:S(2)}) collective-permute-start(bf16[256,2048]{1,0:T(8,128)(2,1)S(1)} %add_convert_fusion), channel_id=1, source_target_pairs={{0,1},{1,2},{2,3},{3,0},{4,5},{5,6},{6,7},{7,4},{8,9},{9,10},{10,1... | collective-permute-start | bytes 3145736 | tf_op jit(solution)/shard_map/cond/branch_1_fun/ppermute | solution.py:71
  713.3 24.4 %collective-permute-start.21 = (bf16[256,2048]{1,0:T(8,128)(2,1)S(1)}, bf16[256,2048]{1,0:T(8,128)(2,1)}, u32[]{:S(2)}, u32[]{:S(2)}) collective-permute-start(bf16[256,2048]{1,0:T(8,128)(2,1)S(1)} %add_convert_fusion.1), channel_id=1, source_target_pairs={{0,1},{1,2},{2,3},{3,0},{4,5},{5,6},{6,7},{7,4},{8,9},{9,10},{10,1... | collective-permute-start | bytes 3145736 | tf_op jit(solution)/shard_map/cond/branch_1_fun/ppermute | solution.py:71
  737.7 13.9 %collective-permute-start.1 = (bf16[1024,256]{1,0:T(8,128)(2,1)S(1)}, bf16[1024,256]{1,0:T(8,128)(2,1)S(1)}, u32[]{:S(2)}, u32[]{:S(2)}) collective-permute-start(bf16[1024,256]{1,0:T(8,128)(2,1)S(1)} %slice.417), channel_id=1, source_target_pairs={{4,0},{12,8},{20,16},{28,24},{5,1},{13,9},{21,17},{29,25},{6,2},{1... | collective-permute-start | bytes 1572872 | tf_op jit(solution)/shard_map/cond/branch_1_fun/ppermute | solution.py:802
  740.7 27.8 %collective-permute-start = (bf16[256,2048]{1,0:T(8,128)(2,1)S(1)}, bf16[256,2048]{1,0:T(8,128)(2,1)}, u32[]{:S(2)}, u32[]{:S(2)}) collective-permute-start(bf16[256,2048]{1,0:T(8,128)(2,1)S(1)} %add_convert_fusion.2), channel_id=1, source_target_pairs={{0,1},{1,2},{2,3},{3,0},{4,5},{5,6},{6,7},{7,4},{8,9},{9,10},{10,1... | collective-permute-start | bytes 3145736 | tf_op jit(solution)/shard_map/cond/branch_1_fun/ppermute | solution.py:71
  768.7 94.6 %all-to-all-start.11 = ((bf16[8,256,1024]{2,1,0:T(8,128)(2,1)}), bf16[8,256,1024]{2,1,0:T(8,128)(2,1)}, u32[]{:S(2)}, u32[]{:S(2)}) async-start(bf16[8,256,1024]{2,1,0:T(8,128)(2,1)} %bitcast.107), calls=%async_computation.12 | async-start | bytes 8388608 | tf_op jit(solution)/shard_map/all_to_all | solution.py:796
  778.1 22.0 %collective-permute-start.22 = (bf16[256,256]{0,1:T(8,128)(2,1)}, bf16[256,256]{0,1:T(8,128)(2,1)}, u32[]{:S(2)}, u32[]{:S(2)}) collective-permute-start(bf16[256,256]{0,1:T(8,128)(2,1)} %copy.65), channel_id=1, source_target_pairs={{0,3},{1,0},{2,1},{3,2},{4,7},{5,4},{6,5},{7,6},{8,11},{9,8},{10,9... | collective-permute-start | bytes 393224 | tf_op jit(solution)/shard_map/cond/branch_1_fun/ppermute | solution.py:128
  780.0 21.0 %collective-permute-start.23 = (bf16[256,256]{0,1:T(8,128)(2,1)}, bf16[256,256]{0,1:T(8,128)(2,1)}, u32[]{:S(2)}, u32[]{:S(2)}) collective-permute-start(bf16[256,256]{0,1:T(8,128)(2,1)} %copy.66), channel_id=1, source_target_pairs={{0,2},{1,3},{2,0},{3,1},{4,6},{5,7},{6,4},{7,5},{8,10},{9,11},{10,... | collective-permute-start | bytes 393224 | tf_op jit(solution)/shard_map/cond/branch_1_fun/ppermute | solution.py:128
  781.6 20.2 %collective-permute-start.24 = (bf16[256,256]{0,1:T(8,128)(2,1)}, bf16[256,256]{0,1:T(8,128)(2,1)}, u32[]{:S(2)}, u32[]{:S(2)}) collective-permute-start(bf16[256,256]{0,1:T(8,128)(2,1)} %copy.67), channel_id=1, source_target_pairs={{0,1},{1,2},{2,3},{3,0},{4,5},{5,6},{6,7},{7,4},{8,9},{9,10},{10,1... | collective-permute-start | bytes 393224 | tf_op jit(solution)/shard_map/cond/branch_1_fun/ppermute | solution.py:128
  788.0 25.6 %collective-permute-start.25 = (bf16[4,256,256]{2,1,0:T(8,128)(2,1)}, bf16[4,256,256]{2,1,0:T(8,128)(2,1)}, u32[]{:S(2)}, u32[]{:S(2)}) collective-permute-start(bf16[4,256,256]{2,1,0:T(8,128)(2,1)} %dynamic-slice_bitcast_fusion), channel_id=1, source_target_pairs={{0,4},{4,0},{8,12},{12,8},{16,20},{20,16},{24,28},{28,24},{1,5},{5... | collective-permute-start | bytes 1572872 | tf_op jit(solution)/shard_map/cond/branch_1_fun/ppermute | solution.py:76
  790.8 27.7 %collective-permute-start.26 = (bf16[256,2048]{1,0:T(8,128)(2,1)}, bf16[256,2048]{1,0:T(8,128)(2,1)}, u32[]{:S(2)}, u32[]{:S(2)}) collective-permute-start(bf16[256,2048]{1,0:T(8,128)(2,1)} %convert_element_type.283), channel_id=1, source_target_pairs={{0,1},{1,2},{2,3},{3,0},{4,5},{5,6},{6,7},{7,4},{8,9},{9,10},{10,1... | collective-permute-start | bytes 3145736 | tf_op jit(solution)/shard_map/cond/branch_1_fun/ppermute | solution.py:71
  821.3 42.0 %copy-start.16 = (f32[256,2048]{1,0:T(8,128)S(1)}, f32[256,2048]{1,0:T(8,128)}, u32[]{:S(2)}) copy-start(f32[256,2048]{1,0:T(8,128)} %copy-done.14) | copy-start | bytes 6291460
  821.3 8.1 collective-permute-start.6
  828.1 35.2 %collective-permute-start.2 = (bf16[256,2048]{1,0:T(8,128)(2,1)}, bf16[256,2048]{1,0:T(8,128)(2,1)}, u32[]{:S(2)}, u32[]{:S(2)}) collective-permute-start(bf16[256,2048]{1,0:T(8,128)(2,1)} %add_convert_fusion.3), channel_id=1, source_target_pairs={{0,1},{1,2},{2,3},{3,0},{4,5},{5,6},{6,7},{7,4},{8,9},{9,10},{10,1... | collective-permute-start | bytes 3145736 | tf_op jit(solution)/shard_map/cond/branch_1_fun/ppermute | solution.py:71
  829.6 5.0 collective-permute-start.7
  835.3 23.9 %collective-permute-start.8 = (bf16[256,256]{1,0:T(8,128)(2,1)}, bf16[256,256]{1,0:T(8,128)(2,1)}, u32[]{:S(2)}, u32[]{:S(2)}) collective-permute-start(bf16[256,256]{1,0:T(8,128)(2,1)} %bitcast.34), channel_id=1, source_target_pairs={{0,1},{1,2},{2,3},{3,0},{4,5},{5,6},{6,7},{7,4},{8,9},{9,10},{10,1... | collective-permute-start | bytes 393224 | tf_op jit(solution)/shard_map/cond/branch_1_fun/ppermute | solution.py:128
  835.6 27.7 %collective-permute-start.9 = (bf16[256,256]{1,0:T(8,128)(2,1)}, bf16[256,256]{1,0:T(8,128)(2,1)}, u32[]{:S(2)}, u32[]{:S(2)}) collective-permute-start(bf16[256,256]{1,0:T(8,128)(2,1)} %bitcast.34), channel_id=1, source_target_pairs={{0,2},{1,3},{2,0},{3,1},{4,6},{5,7},{6,4},{7,5},{8,10},{9,11},{10,... | collective-permute-start | bytes 393224 | tf_op jit(solution)/shard_map/cond/branch_1_fun/ppermute | solution.py:128
  838.3 25.0 %collective-permute-start.10 = (bf16[256,256]{1,0:T(8,128)(2,1)}, bf16[256,256]{1,0:T(8,128)(2,1)}, u32[]{:S(2)}, u32[]{:S(2)}) collective-permute-start(bf16[256,256]{1,0:T(8,128)(2,1)} %bitcast.34), channel_id=1, source_target_pairs={{0,3},{1,0},{2,1},{3,2},{4,7},{5,4},{6,5},{7,6},{8,11},{9,8},{10,9... | collective-permute-start | bytes 393224 | tf_op jit(solution)/shard_map/cond/branch_1_fun/ppermute | solution.py:128
  839.4 1.2 collective-permute-start.3
  840.5 3.8 collective-permute-start.4
  844.3 3.8 collective-permute-start.5
  863.3 38.0 %copy-start.90 = (s32[1,256]{1,0:T(1,128)S(1)}, s32[1,256]{1,0:T(1,128)}, u32[]{:S(2)}) copy-start(s32[1,256]{1,0:T(1,128)} %copy-done.89) | copy-start | bytes 3076
  866.8 30.7 %collective-permute-start.11 = (bf16[256,2048]{1,0:T(8,128)(2,1)}, bf16[256,2048]{1,0:T(8,128)(2,1)S(1)}, u32[]{:S(2)}, u32[]{:S(2)}) collective-permute-start(bf16[256,2048]{1,0:T(8,128)(2,1)} %add_convert_fusion.6), channel_id=1, source_target_pairs={{0,1},{1,2},{2,3},{3,0},{4,5},{5,6},{6,7},{7,4},{8,9},{9,10},{10,1... | collective-permute-start | bytes 3145736 | tf_op jit(solution)/shard_map/cond/branch_1_fun/ppermute | solution.py:71
  870.1 25.0 %collective-permute-start.12 = (f32[4352]{0:T(1024)S(1)}, f32[4352]{0:T(1024)S(1)}, u32[]{:S(2)}, u32[]{:S(2)}) collective-permute-start(f32[4352]{0:T(1024)S(1)} %get-tuple-element.553), channel_id=1, source_target_pairs={{0,1},{1,2},{2,3},{3,0},{4,5},{5,6},{6,7},{7,4},{8,9},{9,10},{10,1... | collective-permute-start | bytes 52232 | tf_op jit(solution)/shard_map/cond/branch_1_fun/ppermute | solution.py:128
  870.1 25.3 %collective-permute-start.13 = (f32[4352]{0:T(1024)S(1)}, f32[4352]{0:T(1024)S(1)}, u32[]{:S(2)}, u32[]{:S(2)}) collective-permute-start(f32[4352]{0:T(1024)S(1)} %get-tuple-element.553), channel_id=1, source_target_pairs={{0,2},{1,3},{2,0},{3,1},{4,6},{5,7},{6,4},{7,5},{8,10},{9,11},{10,... | collective-permute-start | bytes 52232 | tf_op jit(solution)/shard_map/cond/branch_1_fun/ppermute | solution.py:128
  871.2 24.2 %collective-permute-start.14 = (f32[4352]{0:T(1024)S(1)}, f32[4352]{0:T(1024)S(1)}, u32[]{:S(2)}, u32[]{:S(2)}) collective-permute-start(f32[4352]{0:T(1024)S(1)} %get-tuple-element.553), channel_id=1, source_target_pairs={{0,3},{1,0},{2,1},{3,2},{4,7},{5,4},{6,5},{7,6},{8,11},{9,8},{10,9... | collective-permute-start | bytes 52232 | tf_op jit(solution)/shard_map/cond/branch_1_fun/ppermute | solution.py:128
  874.6 23.0 %all-to-all-start = ((f32[32,1,256]{2,1,0:T(1,128)}), f32[32,1,256]{2,1,0:T(1,128)S(1)}, u32[]{:S(2)}, u32[]{:S(2)}) async-start(f32[32,1,256]{2,1,0:T(1,128)} %all_to_all.28), calls=%async_computation | async-start | bytes 65536 | tf_op jit(solution)/shard_map/cond/branch_1_fun/all_to_all | solution.py:876
  (148 other events, 1219.4 us)
Sparse Core Ops, SparseCore 0:
  10.5 43.8 all-gather.3
  56.2 37.7 all-gather.5
  343.1 77.8 all-gather.7
  711.1 50.1 reduce-scatter.1
